TPU v7x, 32 devices: a whole 2x2x4 slice. The times are simulated.
32 devices in a mesh: dp: 4 (over y, x), ctx: 2 (over core), tp: 4 (over z).
Axes of the slice: x: 2, y: 2, z: 4, core: 2. Of those that a mesh axis runs over, the one named last changes fastest.
Arguments:
- tokens: bfloat16 [16384, 1024], P(('dp', 'ctx')), may hold values from -6 to 6
- cotangent: bfloat16 [16384, 1024], P(('dp', 'ctx')), may hold values from -6 to 6
- lengths: int32 [4], P('dp'), may hold values from 2049 to 4096, as said below
- query_key_weight: float32 [2, 1024, 512], P(None, ('dp', 'ctx'), 'tp'), may hold values from -0.1875 to 0.1875
- query_key_mean: float32 [2, 1024, 512], P(None, ('dp', 'ctx'), 'tp'), may hold values from -40 to 40
- query_key_square: float32 [2, 1024, 512], P(None, ('dp', 'ctx'), 'tp'), may hold values from 108.1344 to 1638.4
- value_gate_weight: float32 [2, 1024, 1024], P(None, ('dp', 'ctx'), 'tp'), may hold values from -0.1875 to 0.1875
- value_gate_mean: float32 [2, 1024, 1024], P(None, ('dp', 'ctx'), 'tp'), may hold values from -40 to 40
- value_gate_square: float32 [2, 1024, 1024], P(None, ('dp', 'ctx'), 'tp'), may hold values from 108.1344 to 1638.4
- decay_in_weight: float32 [1024, 16], P(('dp', 'ctx')), may hold values from -0.1875 to 0.1875
- decay_in_mean: float32 [1024, 16], P(('dp', 'ctx')), may hold values from -40 to 40
- decay_in_square: float32 [1024, 16], P(('dp', 'ctx')), may hold values from 108.1344 to 1638.4
- decay_out_weight: float32 [16, 512], P(None, 'tp'), may hold values from -1.5 to 1.5
- decay_out_mean: float32 [16, 512], P(None, 'tp'), may hold values from -40 to 40
- decay_out_square: float32 [16, 512], P(None, 'tp'), may hold values from 108.1344 to 1638.4
- decay_bias: float32 [512], P('tp'), may hold values from 0 to 9
- decay_bias_mean: float32 [512], P('tp'), may hold values from -40 to 40
- decay_bias_square: float32 [512], P('tp'), may hold values from 108.1344 to 1638.4
- output_weight: float32 [1024, 1024], P('tp', ('dp', 'ctx')), may hold values from -0.1875 to 0.1875
- output_mean: float32 [1024, 1024], P('tp', ('dp', 'ctx')), may hold values from -40 to 40
- output_square: float32 [1024, 1024], P('tp', ('dp', 'ctx')), may hold values from 108.1344 to 1638.4
- gate_up_weight: float32 [2, 1024, 2816], P(None, ('dp', 'ctx'), 'tp'), may hold values from -0.1875 to 0.1875
- gate_up_mean: float32 [2, 1024, 2816], P(None, ('dp', 'ctx'), 'tp'), may hold values from -40 to 40
- gate_up_square: float32 [2, 1024, 2816], P(None, ('dp', 'ctx'), 'tp'), may hold values from 108.1344 to 1638.4
- down_weight: float32 [2816, 1024], P('tp', ('dp', 'ctx')), may hold values from -0.109375 to 0.109375
- down_mean: float32 [2816, 1024], P('tp', ('dp', 'ctx')), may hold values from -40 to 40
- down_square: float32 [2816, 1024], P('tp', ('dp', 'ctx')), may hold values from 108.1344 to 1638.4
- gains: float32 [2304], replicated, may hold values from 0.5 to 1.5
- gains_mean: float32 [2304], replicated, may hold values from -40 to 40
- gains_square: float32 [2304], replicated, may hold values from 108.1344 to 1638.4
Outputs:
- layer_out: bfloat16 [16384, 1024], P(('dp', 'ctx'))
- input_grad: float32 [16384, 1024], P(('dp', 'ctx'))
- query_key_mean_new: float32 [2, 1024, 512], P(None, ('dp', 'ctx'), 'tp')
- query_key_square_new: float32 [2, 1024, 512], P(None, ('dp', 'ctx'), 'tp')
- query_key_new: float32 [2, 1024, 512], P(None, ('dp', 'ctx'), 'tp')
- value_gate_mean_new: float32 [2, 1024, 1024], P(None, ('dp', 'ctx'), 'tp')
- value_gate_square_new: float32 [2, 1024, 1024], P(None, ('dp', 'ctx'), 'tp')
- value_gate_new: float32 [2, 1024, 1024], P(None, ('dp', 'ctx'), 'tp')
- decay_in_mean_new: float32 [1024, 16], P(('dp', 'ctx'))
- decay_in_square_new: float32 [1024, 16], P(('dp', 'ctx'))
- decay_in_new: float32 [1024, 16], P(('dp', 'ctx'))
- decay_out_mean_new: float32 [16, 512], P(None, 'tp')
- decay_out_square_new: float32 [16, 512], P(None, 'tp')
- decay_out_new: float32 [16, 512], P(None, 'tp')
- decay_bias_mean_new: float32 [512], P('tp')
- decay_bias_square_new: float32 [512], P('tp')
- decay_bias_new: float32 [512], P('tp')
- output_mean_new: float32 [1024, 1024], P('tp', ('dp', 'ctx'))
- output_square_new: float32 [1024, 1024], P('tp', ('dp', 'ctx'))
- output_new: float32 [1024, 1024], P('tp', ('dp', 'ctx'))
- gate_up_mean_new: float32 [2, 1024, 2816], P(None, ('dp', 'ctx'), 'tp')
- gate_up_square_new: float32 [2, 1024, 2816], P(None, ('dp', 'ctx'), 'tp')
- gate_up_new: float32 [2, 1024, 2816], P(None, ('dp', 'ctx'), 'tp')
- down_mean_new: float32 [2816, 1024], P('tp', ('dp', 'ctx'))
- down_square_new: float32 [2816, 1024], P('tp', ('dp', 'ctx'))
- down_new: float32 [2816, 1024], P('tp', ('dp', 'ctx'))
- gains_mean_new: float32 [2304], replicated
- gains_square_new: float32 [2304], replicated
- gains_new: float32 [2304], replicated
Inputs may be any that keep to these rules, and one draw needn't show every extreme that they name: `lengths`: 4096 in some sequence in every draw.
All inputs are finite; a program needn't handle non-finite values.
Results may differ from a plain program's by a relative error of at most 0.012.
The roundings to bfloat16 on the way count: a program that leaves them out, or rounds other values in their place, can miss the bound.
Values may be sent and summed in bfloat16 or wider, within the bound.
No kernel may reach another device: no remote copies, remote signals or barrier semaphores. Data moves between devices by JAX's collectives and lax.ppermute only.
A program may use at most 192 MiB of HBM per device.

v0:
```python
import jax
import jax.numpy as jnp
from jax import lax
from jax.sharding import PartitionSpec as P

HK = 128
HV = 256
C = 64
STEP = 10


NORM_EPS = 1e-06
HEAD_EPS = 1e-05
GATE_SCALE = 16.0
BETA_ONE = 0.9
BETA_TWO = 0.95
ADAM_EPS = 1e-08
WEIGHT_DECAY = 0.1
RATE_MATRIX = 0.03
RATE_RANK = 0.1
RATE_BIAS = 1.5
RATE_GAIN = 0.3
BEST_PRECISION = lax.Precision.HIGHEST


def from_behind(value, axis, steps):
    count = lax.axis_size(axis)
    first, last = (max(0, -steps), min(count, count - steps))
    return lax.ppermute(value, axis, [(source, source + steps) for source in range(first, last)])


def norm_apply(values, gain, epsilon):
    return values * lax.rsqrt(jnp.mean(values * values, axis=-1, keepdims=True) + epsilon) * gain


def silu_fn(values):
    return values * jax.nn.sigmoid(values)


def gla_head(query_matrix, key_rows, value_rows, log_decay, start_state):
    total = query_matrix.shape[0]
    blocks = total // C
    query_blocks = query_matrix.reshape(blocks, C, -1)
    key_blocks = key_rows.reshape(blocks, C, -1)
    value_block_list = value_rows.reshape(blocks, C, -1)
    cumulative = jnp.cumsum(log_decay.reshape(blocks, C, -1), axis=1)
    block_total = cumulative[:, -1]
    scaled_query_rows = query_blocks * jnp.exp(cumulative)
    key_scaled = key_blocks * jnp.exp(-cumulative)
    carried_key_rows = key_blocks * jnp.exp(block_total[:, None, :] - cumulative)
    causal = (jnp.arange(C)[:, None] >= jnp.arange(C)[None, :]).astype(jnp.float32)
    scores = (
        jnp.einsum("nck,nsk->ncs", scaled_query_rows, key_scaled, precision=BEST_PRECISION) * causal
    )
    inner = jnp.einsum("ncs,nsv->ncv", scores, value_block_list, precision=BEST_PRECISION)
    update_terms = jnp.einsum(
        "tfl,tfd->tld", carried_key_rows, value_block_list, precision=BEST_PRECISION
    )

    def advance(state, item):
        return (jnp.exp(item[0])[:, None] * state + item[1], state)

    final_state, start_offsets = lax.scan(advance, start_state, (block_total, update_terms))
    outer_product = jnp.einsum(
        "max,mxd->mad", scaled_query_rows, start_offsets, precision=BEST_PRECISION
    )
    return ((inner + outer_product).reshape(total, -1), final_state)


def mix_heads(query_matrix, key_rows, value_rows, log_decay, start_state):
    return jax.vmap(gla_head, in_axes=(1, 1, 1, 1, 0), out_axes=(1, 0))(
        query_matrix, key_rows, value_rows, log_decay, start_state
    )


def adamw(weight_now, grad_now, mean_now, square_now, rate_value, decay_value):
    mean_new = BETA_ONE * mean_now + (1.0 - BETA_ONE) * grad_now
    square_new = BETA_TWO * square_now + (1.0 - BETA_TWO) * grad_now * grad_now
    mean_hat = mean_new / (1.0 - BETA_ONE**STEP)
    square_hat = square_new / (1.0 - BETA_TWO**STEP)
    weight_new = weight_now - rate_value * (
        mean_hat / (jnp.sqrt(square_hat) + ADAM_EPS) + decay_value * weight_now
    )
    return (mean_new, square_new, weight_new)


def carry_states(local_state, device_decay):

    def advance_once(step_index, incoming):
        return from_behind(device_decay[..., None] * incoming + local_state, "ctx", 1)

    return lax.fori_loop(0, lax.axis_size("ctx") - 1, advance_once, jnp.zeros_like(local_state))


def carry_grads(local_grad, device_decay):

    def advance_once(step_index, incoming):
        return from_behind(
            (device_decay[..., None] * incoming + local_grad).astype(jnp.bfloat16), "ctx", -1
        ).astype(jnp.float32)

    return lax.fori_loop(0, lax.axis_size("ctx") - 1, advance_once, jnp.zeros_like(local_grad))


def tensor_total(term_fn, row_count):
    return lax.psum(term_fn(0, row_count), "tp")


def norm_plain(values, gain):
    return norm_apply(values, gain, NORM_EPS)


def gate_piece(mixed_in, gate_in, gain_in):
    return norm_apply(mixed_in, gain_in, HEAD_EPS) * silu_fn(gate_in)


def swish_product(gate_in, upward_in):
    return silu_fn(gate_in) * upward_in


def dot_float(left, right):
    return jnp.dot(left, right, preferred_element_type=jnp.float32)


def body(
    tokens,
    cotangent,
    lengths,
    query_key_weight,
    query_key_mean,
    query_key_square,
    value_gate_weight,
    value_gate_mean,
    value_gate_square,
    decay_in_weight,
    decay_in_mean,
    decay_in_square,
    decay_out_weight,
    decay_out_mean,
    decay_out_square,
    decay_bias,
    decay_bias_mean,
    decay_bias_square,
    output_weight,
    output_mean,
    output_square,
    gate_up_weight,
    gate_up_mean,
    gate_up_square,
    down_weight,
    down_mean,
    down_square,
    gains,
    gains_mean,
    gains_square,
):
    row_count = tokens.shape[0]
    width = tokens.shape[1]
    head_count = query_key_weight.shape[2] // HK
    query_scale = HK ** (-0.5)
    inputs = tokens.astype(jnp.float32)
    gain_one = gains[:width]
    gain_two = gains[width : 2 * width]
    gain_head = gains[2 * width :]
    normed_float, norm_back_one = jax.vjp(norm_plain, inputs, gain_one)
    normed = normed_float.astype(jnp.bfloat16)
    query_key_full, value_gate_full, decay_in_full, output_full = (
        lax.all_gather(query_key_weight.astype(jnp.bfloat16), ("dp", "ctx"), axis=1, tiled=True),
        lax.all_gather(value_gate_weight.astype(jnp.bfloat16), ("dp", "ctx"), axis=1, tiled=True),
        lax.all_gather(decay_in_weight.astype(jnp.bfloat16), ("dp", "ctx"), axis=0, tiled=True),
        lax.all_gather(output_weight.astype(jnp.bfloat16), ("dp", "ctx"), axis=1, tiled=True),
    )
    query_matrix = (
        dot_float(normed, query_key_full[0]).reshape(row_count, head_count, HK) * query_scale
    )
    key_rows = dot_float(normed, query_key_full[1]).reshape(row_count, head_count, HK)
    value_rows = dot_float(normed, value_gate_full[0]).reshape(row_count, head_count, HV)
    out_gate = dot_float(normed, value_gate_full[1]).reshape(row_count, head_count, HV)
    decay_rank = dot_float(normed, decay_in_full)
    logits = jnp.dot(decay_rank, decay_out_weight, precision=BEST_PRECISION) + decay_bias
    log_decay = (jax.nn.log_sigmoid(logits) / GATE_SCALE).reshape(row_count, head_count, HK)
    running_total = jnp.cumsum(log_decay, axis=0)
    device_decay = jnp.exp(running_total[-1])
    local_state = jnp.einsum(
        "sng,sni->ngi",
        key_rows * jnp.exp(running_total[-1] - running_total),
        value_rows,
        precision=BEST_PRECISION,
    )
    start_state = carry_states(local_state, device_decay)
    (mixed_out, end_states), mix_back = jax.vjp(
        mix_heads, query_matrix, key_rows, value_rows, log_decay, start_state
    )
    gated_float, gate_back = jax.vjp(gate_piece, mixed_out, out_gate, gain_head)
    gated = gated_float.reshape(row_count, -1).astype(jnp.bfloat16)

    def attn_term(start, count):
        return dot_float(gated, output_full)

    attn_total = tensor_total(attn_term, row_count)
    middle = inputs + attn_total
    normed_two_float, norm_back_two = jax.vjp(norm_plain, middle, gain_two)
    normed_two = normed_two_float.astype(jnp.bfloat16)
    gate_up_full, down_full = (
        lax.all_gather(gate_up_weight.astype(jnp.bfloat16), ("dp", "ctx"), axis=1, tiled=True),
        lax.all_gather(down_weight.astype(jnp.bfloat16), ("dp", "ctx"), axis=1, tiled=True),
    )
    gate_values = dot_float(normed_two, gate_up_full[0])
    upward = dot_float(normed_two, gate_up_full[1])
    active_float, active_back = jax.vjp(swish_product, gate_values, upward)
    active = active_float.astype(jnp.bfloat16)
    ffn_sum = lax.psum(dot_float(active, down_full).astype(jnp.bfloat16), "tp").astype(jnp.float32)
    layer_out = (middle + ffn_sum).astype(jnp.bfloat16)
    position = lax.axis_index("ctx") * row_count + jnp.arange(row_count, dtype=jnp.int32)
    live_rows = (position < lengths[0]).astype(jnp.float32)
    back_out = cotangent.astype(jnp.float32) * live_rows[:, None]
    back_ffn = back_out.astype(jnp.bfloat16)
    back_active = dot_float(back_ffn, down_full.T)
    down_grad = dot_float(active.T, back_ffn)
    back_gate_float, back_up_float = active_back(back_active)
    back_gate = back_gate_float.astype(jnp.bfloat16)
    back_up = back_up_float.astype(jnp.bfloat16)
    gate_up_grad = jnp.stack([dot_float(normed_two.T, back_gate), dot_float(normed_two.T, back_up)])

    def ffn_back_term(start, count):
        return dot_float(back_gate, gate_up_full[0].T) + dot_float(back_up, gate_up_full[1].T)

    back_normed_two = tensor_total(ffn_back_term, row_count)
    back_middle_norm, gain_two_part = norm_back_two(back_normed_two)
    back_middle = back_out + back_middle_norm
    back_attn = back_middle.astype(jnp.bfloat16)
    back_gated = dot_float(back_attn, output_full.T).reshape(row_count, head_count, HV)
    output_grad = dot_float(gated.T, back_attn)
    mixed_gradient, back_gate_in, head_gain_part = gate_back(back_gated)
    collected = jnp.einsum(
        "sng,sni->ngi",
        query_matrix * jnp.exp(running_total),
        mixed_gradient,
        precision=BEST_PRECISION,
    )
    back_end = carry_grads(collected, device_decay)
    back_query, back_keys, back_values, back_log_decay, back_start = mix_back(
        (mixed_gradient, back_end)
    )
    query_back = (back_query * query_scale).reshape(row_count, -1).astype(jnp.bfloat16)
    keys_back = back_keys.reshape(row_count, -1).astype(jnp.bfloat16)
    values_back = back_values.reshape(row_count, -1).astype(jnp.bfloat16)
    out_gate_back = back_gate_in.reshape(row_count, -1).astype(jnp.bfloat16)
    back_logits = back_log_decay.reshape(row_count, -1) * jax.nn.sigmoid(-logits) / GATE_SCALE
    bias_grad = jnp.sum(back_logits, axis=0)
    decay_out_grad = jnp.dot(decay_rank.T, back_logits, precision=BEST_PRECISION)
    rank_part = jnp.dot(back_logits, decay_out_weight.T, precision=BEST_PRECISION)
    normed_part = (
        dot_float(query_back, query_key_full[0].T)
        + dot_float(keys_back, query_key_full[1].T)
        + dot_float(values_back, value_gate_full[0].T)
        + dot_float(out_gate_back, value_gate_full[1].T)
    )
    back_normed, back_rank, head_gain_grad = (
        lax.psum(normed_part.astype(jnp.bfloat16), "tp").astype(jnp.float32),
        lax.psum(rank_part.astype(jnp.bfloat16), "tp").astype(jnp.float32),
        lax.psum(head_gain_part.astype(jnp.bfloat16), "tp").astype(jnp.float32),
    )
    rank_back = back_rank.astype(jnp.bfloat16)
    back_normed = back_normed + dot_float(rank_back, decay_in_full.T)
    decay_in_grad = dot_float(normed.T, rank_back)
    query_key_grad = jnp.stack([dot_float(normed.T, query_back), dot_float(normed.T, keys_back)])
    value_gate_grad = jnp.stack(
        [dot_float(normed.T, values_back), dot_float(normed.T, out_gate_back)]
    )
    query_key_share, value_gate_share, decay_in_share, output_share, gate_up_share, down_share = (
        lax.psum_scatter(query_key_grad, ("dp", "ctx"), scatter_dimension=1, tiled=True),
        lax.psum_scatter(value_gate_grad, ("dp", "ctx"), scatter_dimension=1, tiled=True),
        lax.psum_scatter(decay_in_grad, ("dp", "ctx"), scatter_dimension=0, tiled=True),
        lax.psum_scatter(output_grad, ("dp", "ctx"), scatter_dimension=1, tiled=True),
        lax.psum_scatter(gate_up_grad, ("dp", "ctx"), scatter_dimension=1, tiled=True),
        lax.psum_scatter(down_grad, ("dp", "ctx"), scatter_dimension=1, tiled=True),
    )
    back_input_norm, gain_one_grad = norm_back_one(back_normed)
    input_grad = back_middle + back_input_norm
    gains_grad, decay_out_total, bias_total = lax.psum(
        (
            jnp.concatenate([gain_one_grad, gain_two_part, head_gain_grad]),
            decay_out_grad,
            bias_grad,
        ),
        ("dp", "ctx"),
    )
    updated = adamw(
        query_key_weight,
        query_key_share,
        query_key_mean,
        query_key_square,
        RATE_MATRIX,
        WEIGHT_DECAY,
    )
    updated = updated + adamw(
        value_gate_weight,
        value_gate_share,
        value_gate_mean,
        value_gate_square,
        RATE_MATRIX,
        WEIGHT_DECAY,
    )
    updated = updated + adamw(
        decay_in_weight, decay_in_share, decay_in_mean, decay_in_square, RATE_MATRIX, WEIGHT_DECAY
    )
    updated = updated + adamw(
        decay_out_weight, decay_out_total, decay_out_mean, decay_out_square, RATE_RANK, WEIGHT_DECAY
    )
    updated = updated + adamw(
        decay_bias, bias_total, decay_bias_mean, decay_bias_square, RATE_BIAS, 0.0
    )
    updated = updated + adamw(
        output_weight, output_share, output_mean, output_square, RATE_MATRIX, WEIGHT_DECAY
    )
    updated = updated + adamw(
        gate_up_weight, gate_up_share, gate_up_mean, gate_up_square, RATE_MATRIX, WEIGHT_DECAY
    )
    updated = updated + adamw(
        down_weight, down_share, down_mean, down_square, RATE_MATRIX, WEIGHT_DECAY
    )
    updated = updated + adamw(gains, gains_grad, gains_mean, gains_square, RATE_GAIN, 0.0)
    return (layer_out, input_grad) + updated


def solution(mesh):
    placed = (
        P(("dp", "ctx"), None),
        P(("dp", "ctx"), None),
        P("dp"),
        P(None, ("dp", "ctx"), "tp"),
        P(None, ("dp", "ctx"), "tp"),
        P(None, ("dp", "ctx"), "tp"),
        P(None, ("dp", "ctx"), "tp"),
        P(None, ("dp", "ctx"), "tp"),
        P(None, ("dp", "ctx"), "tp"),
        P(("dp", "ctx"), None),
        P(("dp", "ctx"), None),
        P(("dp", "ctx"), None),
        P(None, "tp"),
        P(None, "tp"),
        P(None, "tp"),
        P("tp"),
        P("tp"),
        P("tp"),
        P("tp", ("dp", "ctx")),
        P("tp", ("dp", "ctx")),
        P("tp", ("dp", "ctx")),
        P(None, ("dp", "ctx"), "tp"),
        P(None, ("dp", "ctx"), "tp"),
        P(None, ("dp", "ctx"), "tp"),
        P("tp", ("dp", "ctx")),
        P("tp", ("dp", "ctx")),
        P("tp", ("dp", "ctx")),
        P(),
        P(),
        P(),
    )
    return jax.shard_map(
        body,
        mesh=mesh,
        in_specs=placed,
        out_specs=(
            P(("dp", "ctx"), None),
            P(("dp", "ctx"), None),
            P(None, ("dp", "ctx"), "tp"),
            P(None, ("dp", "ctx"), "tp"),
            P(None, ("dp", "ctx"), "tp"),
            P(None, ("dp", "ctx"), "tp"),
            P(None, ("dp", "ctx"), "tp"),
            P(None, ("dp", "ctx"), "tp"),
            P(("dp", "ctx"), None),
            P(("dp", "ctx"), None),
            P(("dp", "ctx"), None),
            P(None, "tp"),
            P(None, "tp"),
            P(None, "tp"),
            P("tp"),
            P("tp"),
            P("tp"),
            P("tp", ("dp", "ctx")),
            P("tp", ("dp", "ctx")),
            P("tp", ("dp", "ctx")),
            P(None, ("dp", "ctx"), "tp"),
            P(None, ("dp", "ctx"), "tp"),
            P(None, ("dp", "ctx"), "tp"),
            P("tp", ("dp", "ctx")),
            P("tp", ("dp", "ctx")),
            P("tp", ("dp", "ctx")),
            P(),
            P(),
            P(),
        ),
        check_vma=False,
    )
```

profile of v0, /device:TPU:0, one launch (start us, length us, event | category | flops | bytes accessed | tf_op | source)
XLA Modules:
  0.0 1475.3 jit_solution(2634122692577038377)
XLA Ops:
  9.0 3.2 fusion.11
  12.3 10.3 all_gather.19
  25.0 3.1 fusion.58
  29.5 10.6 all_gather.18
  40.7 10.3 all_gather.21
  51.1 3.6 convolution_multiply_fusion
  56.3 2.2 fusion.94
  58.6 3.4 convolution_multiply_fusion.2
  61.9 3.8 fusion.82
  65.7 2.0 fusion.54
  67.7 2.7 collective-permute-start
  70.5 3.2 fusion.120
  73.7 6.0 convolution_bitcast_fusion.1
  79.6 2.5 broadcast.233.clone
  82.1 70.5 %while.42 = (s32[]{:T(128)}, f32[1,128,256]{2,1,0:T(8,128)S(1)}, f32[32,1,128,256]{3,2,1,0:T(8,128)}, f32[32,1,128]{2,1,0:T(1,128)S(1)}, f32[32,1,128,1]{2,3,1,0...) while((s32[]{:T(128)}, f32[1,128,256]{2,1,0:T(8,128)S(1)}, ...), condition=%wide.region_5.6_spmd, body=%wide.region_4.5_spmd.sunk | while | flops 65538 | bytes 659549 | solution.py:63
  152.7 6.8 multiply_reduce_fusion.4
  159.5 6.0 multiply_convert_fusion.3
  166.4 4.7 fusion.121
  174.6 287.7 %all-reduce.7.cloned.1.call-done = f32[2048,1024]{1,0:T(8,128)} async-done(((f32[2048,1024]{1,0:T(8,128)}), f32[2048,1024]{1,0:T(8,128)}) %all-reduce.7.cloned.1.call-update) | async-done | bytes 8388624 | tf_op jit(solution)/shard_map/psum | solution.py:106
  462.4 5.7 multiply_reduce_fusion.2
  468.1 3.4 copy-done.5
  471.5 2.6 multiply_convert_fusion
  474.1 21.5 %all-gather.6.cloned.1.call-done = bf16[2,1024,704]{1,2,0:T(8,128)(2,1)} async-done(((bf16[2,128,704]{1,2,0:T(8,128)(2,1)}), bf16[2,1024,704]{1,2,0:T(8,128)(2,1)}) %all-gather.6.cloned.1.call-update) | async-done | bytes 2883600 | tf_op jit(solution)/shard_map/all_gather | solution.py:205
  495.5 8.5 fusion.52
  504.0 5.0 fusion.53
  509.0 14.2 all-gather.8.cloned.1.call-done
  523.2 12.0 multiply_convert_fusion.1
  535.2 3.6 fusion.51
  538.8 6.0 convolution_add_fusion
  545.3 7.9 fusion.36
  553.3 5.9 convolution_bitcast_fusion.2
  559.2 3.2 convolution_bitcast_fusion.3
  562.4 3.1 pad_maximum_fusion
  565.6 7.8 convolution_convert_fusion
  573.3 262.5 %all-reduce.9.cloned.1.call-done = f32[2048,1024]{1,0:T(8,128)} async-done(((f32[2048,1024]{1,0:T(8,128)}), f32[2048,1024]{1,0:T(8,128)}) %all-reduce.9.cloned.1.call-update) | async-done | bytes 8388624 | tf_op jit(solution)/shard_map/psum | solution.py:106
  835.8 7.0 multiply_reduce_fusion
  844.3 7.2 fusion.9
  851.6 3.6 multiply_reduce_fusion.3
  860.2 2.1 convolution_multiply_fusion.1
  862.3 2.8 fusion.122
  866.9 3.4 fusion.123
  870.3 5.8 multiply_convert_fusion.4
  876.1 2.3 convolution_bitcast_fusion.7
  878.4 2.3 fusion.30
  880.6 10.2 convolution_bitcast_fusion
  890.9 2.5 broadcast.233
  893.4 129.1 %while.43 = (s32[]{:T(128)}, f32[1,128,256]{2,1,0:T(8,128)S(1)}, f32[32,1,128]{2,1,0:T(1,128)S(1)}, f32[32,1,128,256]{3,2,1,0:T(8,128)}, f32[32,1,128,256]{2,3,0...) while((s32[]{:T(128)}, f32[1,128,256]{2,1,0:T(8,128)S(1)}, ...), condition=%wide.region_15.16_spmd, body=%wide.region_13.15_spmd.sunk | while | flops 131075 | bytes 1314437 | solution.py:63
  1022.5 8.0 fusion.95
  1030.6 2.1 fusion.60
  1035.8 3.9 convolution_bitcast_fusion.4
  1040.3 3.2 add_convert_fusion.2
  1051.9 4.5 fusion.93
  1056.4 4.6 fusion.81
  1061.1 9.8 add_convert_fusion
  1071.9 2.3 multiply_subtract_fusion.1
  1074.2 9.3 psum.70
  1084.2 3.1 multiply_subtract_fusion
  1090.9 24.3 %reduce-scatter.9.cloned.1.call-done = f32[2,128,256]{2,1,0:T(8,128)} async-done(((f32[2,1024,256]{2,1,0:T(8,128)}), f32[2,128,256]{2,1,0:T(8,128)}) %reduce-scatter.9.cloned.1.call-update) | async-done | bytes 262160 | tf_op jit(solution)/shard_map/reduce_scatter | solution.py:273
  1115.2 2.1 multiply_subtract_fusion.2
  1117.3 295.3 %all-reduce.11.cloned.1.call-done = (bf16[2048,1024]{1,0:T(8,128)(2,1)}, bf16[2048,1024]{1,0:T(8,128)(2,1)}, bf16[2048,16]{0,1:T(8,128)(2,1)}) async-done(((bf16[2048,1024]{1,0:T(8,128)(2,1)}, bf16[2048,1024]{1,0:T(8,128)(2,1)}, bf16[2048,16]{0,1:T(8,128)(2,1)}), (bf16[2048,1024]{1,0:T(8,128)(2,1)}, bf16[2048,1024]{1,0:T(8,128)(2,1)}, bf16[2048,16]{0,1:T(8,128)(2,1)})) %all-reduce.11.cloned.1.call-update) | async-done | bytes 8454160 | tf_op jit(solution)/shard_map/psum | solution.py:212
  1412.6 3.5 fusion.125
  1416.3 7.3 fusion.8
  1423.6 24.0 %all-reduce.1 = (f32[16,128]{1,0:T(8,128)S(1)}, f32[128]{0:T(128)S(1)}, f32[2304]{0:T(1024)S(1)}) all-reduce(f32[16,128]{1,0:T(8,128)S(1)} %fusion.124, f32[128]{0:T(128)S(1)} %get-tuple-element.333, f32[2304]{0:T(1024)S(1)} %pad_maximum_fusion.3), channel_id=1, replica_groups=mesh['dp'=4,'ctx'=2,'tp'=4] {'dp','ctx'}, use_global_device_ids=true, to_apply=%region_24.25 | all-reduce | flops 4480 | bytes 35840 | tf_op jit(solution)/shard_map/psum | solution.py:281
  1449.0 17.4 %fusion.10 = (f32[2048,1024]{1,0:T(8,128)}, bf16[2048,1024]{1,0:T(8,128)(2,1)}) fusion(f32[2048,1024]{1,0:T(8,128)} %copy-done.7, bf16[2048,1024]{1,0:T(8,128)(2,1)} %param.34, f32[2048,1024]{1,0:T(8,128)} %get-tuple-element.371, f32[2048]{0:T(1024)S(1)} %multiply_multiply_fusion.9, f32[1024]{0:T(1024)S(1)} %copy-done.68, f32[2048]{0:T(1024)S(1)} %copy-done.63, ...), kind=kLoop, calls=%fused_computation.30 | loop fusion | flops 20971520 | bytes 46157824 | tf_op jit(solution)/shard_map/add | solution.py:280
  (596 shorter events, 239.6 us)
Async XLA Ops:
  7.2 54.7 %all-gather.4.cloned.1.call-start = ((), (), s32[]{:S(2)}) async-start(), calls=%async_computation.6 | async-start | bytes 1179648 | tf_op jit(solution)/shard_map/all_gather | solution.py:169
  8.9 453.4 %all-reduce.7.cloned.1.call-start = ((), (), s32[]{:S(2)}) async-start(), calls=%async_computation.7 | async-start | bytes 16777216 | tf_op jit(solution)/shard_map/psum | solution.py:106
  9.0 13.7 copy-start.8
  12.2 11.5 copy-start.60
  12.2 11.5 copy-start.62
  12.3 11.5 copy-start.67
  28.8 11.8 copy-start.51
  29.4 21.6 %copy-start.17 = (f32[2048,1,128]{2,0,1:T(8,128)}, f32[2048,1,128]{2,0,1:T(8,128)S(1)}, u32[]{:S(2)}) copy-start(f32[2048,1,128]{2,0,1:T(8,128)S(1)} %fusion.64) | copy-start | bytes 3145732
  29.4 36.3 %copy-start.82 = (f32[128]{0:T(128)}, f32[128]{0:T(128)S(1)}, u32[]{:S(2)}) copy-start(f32[128]{0:T(128)S(1)} %exponential_multiply_fusion) | copy-start | bytes 1540
  40.0 14.6 copy-start.30
  51.0 22.6 %copy-start.55 = (f32[32,128]{1,0:T(8,128)}, f32[32,128]{1,0:T(8,128)S(1)}, u32[]{:S(2)}) copy-start(f32[32,128]{1,0:T(8,128)S(1)} %get-tuple-element.356) | copy-start | bytes 49156
  61.9 8.5 copy-start.20
  65.7 7.9 copy-start.9
  67.7 11.9 collective-permute-start
  152.7 6.8 copy-start.75
  159.5 6.9 copy-start.39
  171.1 324.4 %all-gather.6.cloned.1.call-start = ((), (), s32[]{:S(2)}) async-start(), calls=%async_computation.8 | async-start | bytes 3244032 | tf_op jit(solution)/shard_map/all_gather | solution.py:205
  173.1 350.0 %all-gather.8.cloned.1.call-start = ((), (), s32[]{:S(2)}) async-start(), calls=%async_computation.9 | async-start | bytes 1622016 | tf_op jit(solution)/shard_map/all_gather | solution.py:206
  173.9 661.9 %all-reduce.9.cloned.1.call-start = ((), (), s32[]{:S(2)}) async-start(), calls=%async_computation.10 | async-start | bytes 16777216 | tf_op jit(solution)/shard_map/psum | solution.py:106
  495.5 8.5 copy-start.32
  495.5 8.5 copy-start.88
  523.2 12.0 copy-start.89
  544.8 526.2 %reduce-scatter.17.cloned.1.call-start = ((), (), s32[]{:S(2)}) async-start(), calls=%async_computation.16 | async-start | bytes 3244032 | tf_op jit(solution)/shard_map/reduce_scatter | solution.py:277
  553.2 530.9 %reduce-scatter.15.cloned.1.call-start = ((), (), s32[]{:S(2)}) async-start(), calls=%async_computation.15 | async-start | bytes 6488064 | tf_op jit(solution)/shard_map/reduce_scatter | solution.py:276
  553.3 6.0 copy-start.33
  565.5 521.8 %reduce-scatter.13.cloned.1.call-start = ((), (), s32[]{:S(2)}) async-start(), calls=%async_computation.14 | async-start | bytes 1179648 | tf_op jit(solution)/shard_map/reduce_scatter | solution.py:275
  835.8 8.5 copy-start.13
  844.3 7.3 copy-start.22
  844.3 7.3 copy-start.38
  844.3 7.3 copy-start.40
  844.3 7.3 copy-start.74
  851.5 26.8 %copy-start.7 = (f32[2048,1024]{1,0:T(8,128)}, f32[2048,1024]{1,0:T(8,128)S(1)}, u32[]{:S(2)}) copy-start(f32[2048,1024]{1,0:T(8,128)S(1)} %fusion.9) | copy-start | bytes 25165828
  856.8 13.5 copy-start.6
  858.7 32.2 %collective-permute-start.1 = (bf16[1,128,256]{2,1,0:T(8,128)(2,1)S(1)}, bf16[1,128,256]{2,1,0:T(8,128)(2,1)S(1)}, u32[]{:S(2)}, u32[]{:S(2)}) collective-permute-start(bf16[1,128,256]{2,1,0:T(8,128)(2,1)S(1)} %fusion.56), channel_id=1, source_target_pairs={{4,0},{5,1},{6,2},{7,3},{12,8},{13,9},{14,10},{15,11},{20,16},{21,... | collective-permute-start | bytes 196616 | tf_op jit(solution)/shard_map/while/body/eval_jaxpr/ppermute | solution.py:29
  890.8 198.3 %reduce-scatter.7.cloned.1.call-start = ((), (), s32[]{:S(2)}) async-start(), calls=%async_computation.11 | async-start | bytes 1179648 | tf_op jit(solution)/shard_map/reduce_scatter | solution.py:272
  893.4 129.1 %copy-start.56 = (f32[32,128]{1,0:T(8,128)S(1)}, f32[32,128]{1,0:T(8,128)}, u32[]{:S(2)}) copy-start(f32[32,128]{1,0:T(8,128)} %copy-done.55) | copy-start | bytes 49156
  1022.5 8.0 copy-start.16
  1022.5 8.0 copy-start.34
  1022.5 8.0 copy-start.35
  1035.4 79.9 %reduce-scatter.9.cloned.1.call-start = ((), (), s32[]{:S(2)}) async-start(), calls=%async_computation.12 | async-start | bytes 2359296 | tf_op jit(solution)/shard_map/reduce_scatter | solution.py:273
  1046.3 366.4 %all-reduce.11.cloned.1.call-start = ((), (), s32[]{:S(2)}) async-start(), calls=%async_computation.17 | async-start | bytes 16908288 | tf_op jit(solution)/shard_map/psum | solution.py:212
  1070.9 12.6 copy-start.49
  1070.9 13.3 copy-start.37
  1070.9 13.3 copy-start.50
  1070.9 16.3 %copy-start.52 = (f32[256,128]{1,0:T(8,128)S(1)}, f32[256,128]{1,0:T(8,128)}, u32[]{:S(2)}) copy-start(f32[256,128]{1,0:T(8,128)} %param.52) | copy-start | bytes 393220
  1070.9 396.0 %reduce-scatter.11.cloned.1.call-start = ((), (), s32[]{:S(2)}) async-start(), calls=%async_computation.13 | async-start | bytes 73728 | tf_op jit(solution)/shard_map/reduce_scatter | solution.py:274
  1074.2 14.9 %copy-start.54 = (f32[2,128,128]{2,1,0:T(8,128)S(1)}, f32[2,128,128]{2,1,0:T(8,128)}, u32[]{:S(2)}) copy-start(f32[2,128,128]{2,1,0:T(8,128)} %param.37) | copy-start | bytes 393220
  1074.2 14.9 %copy-start.59 = (f32[2,128,128]{2,1,0:T(8,128)S(1)}, f32[2,128,128]{2,1,0:T(8,128)}, u32[]{:S(2)}) copy-start(f32[2,128,128]{2,1,0:T(8,128)} %param.39) | copy-start | bytes 393220
  1074.2 41.0 %copy-start.45 = (f32[2,128,256]{2,1,0:T(8,128)S(1)}, f32[2,128,256]{2,1,0:T(8,128)}, u32[]{:S(2)}) copy-start(f32[2,128,256]{2,1,0:T(8,128)} %param.40) | copy-start | bytes 786436
  1087.2 329.0 %copy-start.58 = (bf16[1024,16]{0,1:T(8,128)(2,1)S(1)}, bf16[1024,16]{0,1:T(8,128)(2,1)}, u32[]{:S(2)}) copy-start(bf16[1024,16]{0,1:T(8,128)(2,1)} %copy-done.57) | copy-start | bytes 98308
  1087.2 329.0 %copy-start.63 = (f32[2048]{0:T(1024)S(1)}, f32[2048]{0:T(1024)}, u32[]{:S(2)}) copy-start(f32[2048]{0:T(1024)} %copy-done.62) | copy-start | bytes 24580
  1087.3 329.0 %copy-start.68 = (f32[1024]{0:T(1024)S(1)}, f32[1024]{0:T(1024)}, u32[]{:S(2)}) copy-start(f32[1024]{0:T(1024)} %copy-done.67) | copy-start | bytes 12292
  1416.2 7.4 copy-start.61
  1416.2 31.4 %copy-start.66 = (f32[2304]{0:T(1024)S(1)}, f32[2304]{0:T(1024)}, u32[]{:S(2)}) copy-start(f32[2304]{0:T(1024)} %param.61) | copy-start | bytes 27652
  1416.2 31.4 %copy-start.76 = (f32[2304]{0:T(1024)S(1)}, f32[2304]{0:T(1024)}, u32[]{:S(2)}) copy-start(f32[2304]{0:T(1024)} %param.63) | copy-start | bytes 27652
  1416.3 31.4 %copy-start.77 = (f32[2304]{0:T(1024)S(1)}, f32[2304]{0:T(1024)}, u32[]{:S(2)}) copy-start(f32[2304]{0:T(1024)} %param.62) | copy-start | bytes 27652
  1416.3 32.0 %copy-start.78 = (f32[16,128]{1,0:T(8,128)S(1)}, f32[16,128]{1,0:T(8,128)}, u32[]{:S(2)}) copy-start(f32[16,128]{1,0:T(8,128)} %param.48) | copy-start | bytes 24580
  1416.3 32.0 %copy-start.79 = (f32[16,128]{1,0:T(8,128)S(1)}, f32[16,128]{1,0:T(8,128)}, u32[]{:S(2)}) copy-start(f32[16,128]{1,0:T(8,128)} %param.47) | copy-start | bytes 24580
  1448.9 17.4 %copy-start.85 = (f32[128]{0:T(128)S(1)}, f32[128]{0:T(128)}, u32[]{:S(2)}) copy-start(f32[128]{0:T(128)} %param.49) | copy-start | bytes 1540
  1448.9 17.4 %copy-start.86 = (f32[128]{0:T(128)S(1)}, f32[128]{0:T(128)}, u32[]{:S(2)}) copy-start(f32[128]{0:T(128)} %param.51) | copy-start | bytes 1540
  1448.9 17.4 %copy-start.87 = (f32[128]{0:T(128)S(1)}, f32[128]{0:T(128)}, u32[]{:S(2)}) copy-start(f32[128]{0:T(128)} %param.50) | copy-start | bytes 1540
  1448.9 18.0 %copy-start.72 = (f32[128,16]{0,1:T(8,128)S(1)}, f32[128,16]{0,1:T(8,128)}, u32[]{:S(2)}) copy-start(f32[128,16]{0,1:T(8,128)} %param.43) | copy-start | bytes 24580
  1448.9 18.0 %copy-start.80 = (f32[128,16]{0,1:T(8,128)S(1)}, f32[128,16]{0,1:T(8,128)}, u32[]{:S(2)}) copy-start(f32[128,16]{0,1:T(8,128)} %param.45) | copy-start | bytes 24580
  1449.0 18.0 %copy-start.81 = (f32[128,16]{0,1:T(8,128)S(1)}, f32[128,16]{0,1:T(8,128)}, u32[]{:S(2)}) copy-start(f32[128,16]{0,1:T(8,128)} %param.44) | copy-start | bytes 24580
  (43 other events, 130.6 us)
Sparse Core Ops, SparseCore 0:
  10.5 26.8 all-gather.3
  171.2 291.0 all-reduce.6
  464.8 30.6 all-gather.5
  497.8 25.2 all-gather.7
  545.0 290.8 all-reduce.8
  839.0 43.9 reduce-scatter.16
  886.9 59.0 reduce-scatter.14
  949.1 36.0 reduce-scatter.12
  1035.5 35.3 reduce-scatter.6
  1074.0 41.1 reduce-scatter.8
  1118.3 294.3 all-reduce.10
  1423.7 30.4 reduce-scatter.10
where the time goes:
time: 1480 us
  waiting for transfers between devices  906 us (61%)
  matrix products  193 us (13%)
  other arithmetic  161 us (11%)
  local copies, waits for them, and re-layouts  128 us (9%)
  blocking collectives  64.5 us (4%)
  between operations  16.3 us (1%)
    psum x2, waiting for transfers between devices, tensor_total(): return lax.psum(term_fn(0, row_count), 'tp')  550 us
    psum x1, waiting for transfers between devices, body(): lax.psum(dot_float(active, down_full).astype(jnp.bfloat16), 'tp')  295 us
    dot_general x27, matrix products, dot_float(): return jnp.dot(left, right, preferred_element_type=jnp.float32)  127 us
    dynamic_update_slice x128, local copies, waits for them, and re-layouts, gla_head(): lax.scan(advance, start_state, (block_total, update_terms))  59.4 us
    reduce_sum x32, other arithmetic, advance(): return (jnp.exp(item[0])[:, None] * state + item[1], state)  32.6 us
    dynamic_slice x64, local copies, waits for them, and re-layouts, gla_head(): lax.scan(advance, start_state, (block_total, update_terms))  32.4 us
    add x32, other arithmetic, advance(): return (jnp.exp(item[0])[:, None] * state + item[1], state)  31.8 us
  transfers between devices with their start and end apart: 14, of which 6 were waited for; matrix products, arithmetic and copies ran while one was open for 23% of the time, Pallas kernels for 0%

commit v1 on v0

v1 whole, which is shorter than its diff:
```python
import functools

import jax
import jax.numpy as jnp
from jax import lax
from jax.experimental import pallas as pl
from jax.experimental.pallas import tpu as pltpu
from jax.sharding import PartitionSpec as P

HK = 128
HV = 256
BLOCK = 128
MID = 63
ROWS = 256
FFN_ROWS = 512
STEP = 10

NORM_EPS = 1e-06
HEAD_EPS = 1e-05
GATE_SCALE = 16.0
BETA_ONE = 0.9
BETA_TWO = 0.95
ADAM_EPS = 1e-08
WEIGHT_DECAY = 0.1
RATE_MATRIX = 0.03
RATE_RANK = 0.1
RATE_BIAS = 1.5
RATE_GAIN = 0.3
VMEM_LIMIT = 60 * 1024 * 1024

F32 = jnp.float32
BF16 = jnp.bfloat16
NN = (((1,), (0,)), ((), ()))
NT = (((1,), (1,)), ((), ()))
TN = (((0,), (0,)), ((), ()))


def dot(left, right, dims=NN):
    return lax.dot_general(left, right, dims, preferred_element_type=F32)


def split_two(values):
    high = values.astype(BF16)
    return high, (values - high.astype(F32)).astype(BF16)


def dot_split(left, right, dims=NN):
    return (
        dot(left[0], right[0], dims) + dot(left[0], right[1], dims) + dot(left[1], right[0], dims)
    )


def dot_exact(matrix, values):
    high = values.astype(BF16)
    rest = values - high.astype(F32)
    middle = rest.astype(BF16)
    low = (rest - middle.astype(F32)).astype(BF16)
    return dot(matrix, high) + dot(matrix, middle) + dot(matrix, low)


def lower_mask():
    rows = lax.broadcasted_iota(jnp.int32, (BLOCK, BLOCK), 0)
    columns = lax.broadcasted_iota(jnp.int32, (BLOCK, BLOCK), 1)
    return rows >= columns


def upper_mask():
    rows = lax.broadcasted_iota(jnp.int32, (BLOCK, BLOCK), 0)
    columns = lax.broadcasted_iota(jnp.int32, (BLOCK, BLOCK), 1)
    return rows <= columns


def as_ones(mask):
    return jnp.where(mask, 1.0, 0.0).astype(BF16)


def inverse_rms(values, epsilon):
    return lax.rsqrt(jnp.mean(values * values, axis=-1, keepdims=True) + epsilon)


def sigmoid(values):
    return 1.0 / (1.0 + jnp.exp(-values))


def project_kernel(
    tokens, gain, weight, rank_weight, decay_out, bias,
    normed_out, qkv_out, gate_out, rank_out, logits_out, cum_out, state_out, total_out,
):
    heads = weight.shape[0]

    @pl.when(pl.program_id(0) == 0)
    def _():
        state_out[...] = jnp.zeros_like(state_out)
        total_out[...] = jnp.zeros_like(total_out)

    inputs = tokens[...].astype(F32)
    normed = (inputs * inverse_rms(inputs, NORM_EPS) * gain[...]).astype(BF16)
    normed_out[...] = normed
    rank = dot(normed, rank_weight[0], NT)
    rank_out[...] = rank
    lower = as_ones(lower_mask())
    for head in range(heads):
        made = dot(normed, weight[head], NT)
        query = made[:, :HK] * HK ** (-0.5)
        keys = made[:, HK : 2 * HK]
        values = made[:, 2 * HK : 2 * HK + HV]
        qkv_out[head, :, :HK] = query
        qkv_out[head, :, HK : 2 * HK] = keys
        qkv_out[head, :, 2 * HK :] = values
        gate_out[head] = made[:, 2 * HK + HV :]
        logits = (
            lax.dot_general(
                rank, decay_out[head], NN, precision=lax.Precision.HIGHEST,
                preferred_element_type=F32,
            )
            + bias[head]
        )
        logits_out[head] = logits
        log_decay = (
            jnp.minimum(logits, 0.0) - jnp.log1p(jnp.exp(-jnp.abs(logits)))
        ) / GATE_SCALE
        state = state_out[head]
        for part in range(ROWS // BLOCK):
            span = slice(part * BLOCK, (part + 1) * BLOCK)
            cum = dot_exact(lower, log_decay[span])
            cum_out[head, span] = cum
            total = cum[BLOCK - 1 :]
            carried = split_two(keys[span] * jnp.exp(total - cum))
            state = state * jnp.exp(total) + dot_split(split_two(values[span]), carried, TN)
            total_out[head] += total
        state_out[head] = state


def mix_kernel(
    own, tokens, qkv, gate, cum_in, start, out_weight, head_gain, gain,
    mixed_out, state_out, gated_out, middle_out, normed_out,
    state_ref, gated_ref,
):
    heads = start.shape[0]

    @pl.when(pl.program_id(0) == 0)
    def _():
        state_ref[...] = start[...]

    causal = lower_mask()
    for part in range(ROWS // BLOCK):
        span = slice(part * BLOCK, (part + 1) * BLOCK)
        for head in range(heads):
            query = qkv[head, span, :HK]
            keys = qkv[head, span, HK : 2 * HK]
            values = split_two(qkv[head, span, 2 * HK :])
            cum = cum_in[head, span]
            center = cum[MID : MID + 1]
            total = cum[BLOCK - 1 :]
            query_mid = split_two(query * jnp.exp(cum - center))
            key_mid = split_two(keys * jnp.exp(center - cum))
            scores = split_two(jnp.where(causal, dot_split(query_mid, key_mid, NT), 0.0))
            state = state_ref[head]
            state_out[part, head] = state
            mixed = dot_split(scores, values) + dot_split(
                split_two(query * jnp.exp(cum)), split_two(state), NT
            )
            carried = split_two(keys * jnp.exp(total - cum))
            state_ref[head] = state * jnp.exp(total) + dot_split(values, carried, TN)
            mixed_out[head, span] = mixed
            out_gate = gate[head, span]
            gated = (
                mixed * inverse_rms(mixed, HEAD_EPS) * head_gain[...] * (out_gate * sigmoid(out_gate))
            ).astype(BF16)
            gated_ref[span, head * HV : (head + 1) * HV] = gated

            @pl.when(own[0] == head)
            def _():
                gated_out[span] = gated

    width = tokens.shape[1]
    middle = tokens[...].astype(F32) + dot(
        gated_ref[...], out_weight[...].reshape(heads * HV, width)
    )
    middle_out[...] = middle
    normed_out[...] = (middle * inverse_rms(middle, NORM_EPS) * gain[...]).astype(BF16)


def ffn_kernel(
    own, normed, back, middle, weight, gain,
    active_out, back_gate_out, back_up_out, layer_out, back_middle_out, back_attn_out, gain_out,
    ffn_ref, back_ref,
):
    step, piece = pl.program_id(0), pl.program_id(1)
    units = weight.shape[1] // 3

    @pl.when((step == 0) & (piece == 0))
    def _():
        gain_out[...] = jnp.zeros_like(gain_out)

    gate_weight = weight[0, :units]
    up_weight = weight[0, units : 2 * units]
    down_weight = weight[0, 2 * units :]
    gate_values = dot(normed[...], gate_weight, NT)
    upward = dot(normed[...], up_weight, NT)
    back_active = dot(back[...], down_weight, NT)
    share = sigmoid(gate_values)
    silu = gate_values * share
    active = (silu * upward).astype(BF16)
    back_gate = (back_active * upward * (share * (1.0 + gate_values * (1.0 - share)))).astype(BF16)
    back_up = (back_active * silu).astype(BF16)
    ffn = dot(active, down_weight)
    back_normed = dot(back_gate, gate_weight) + dot(back_up, up_weight)

    @pl.when(piece == own[0])
    def _():
        active_out[...] = active
        back_gate_out[...] = back_gate
        back_up_out[...] = back_up

    @pl.when(piece == 0)
    def _():
        ffn_ref[...] = ffn
        back_ref[...] = back_normed

    @pl.when(piece > 0)
    def _():
        ffn_ref[...] += ffn
        back_ref[...] += back_normed

    @pl.when(piece == pl.num_programs(1) - 1)
    def _():
        mid = middle[...]
        layer_out[...] = (mid + ffn_ref[...]).astype(BF16)
        inverse = inverse_rms(mid, NORM_EPS)
        unit = mid * inverse
        total = back_ref[...]
        weighted = total * gain[...]
        back_middle = back[...].astype(F32) + inverse * (
            weighted - unit * jnp.mean(weighted * unit, axis=-1, keepdims=True)
        )
        back_middle_out[...] = back_middle
        back_attn_out[...] = back_middle.astype(BF16)
        gain_out[...] += jnp.sum(total * unit, axis=0, keepdims=True)


def gate_back_kernel(
    back_attn, out_weight, mixed_in, gate, query_in, cum_in, head_gain,
    back_mixed_out, back_gate_out, gain_out, state_out,
):
    heads = gate.shape[0]

    @pl.when(pl.program_id(0) == 0)
    def _():
        gain_out[...] = jnp.zeros_like(gain_out)
        state_out[...] = jnp.zeros_like(state_out)

    for head in range(heads):
        back_gated = dot(back_attn[...], out_weight[head], NT)
        mixed = mixed_in[head]
        out_gate = gate[head]
        inverse = inverse_rms(mixed, HEAD_EPS)
        unit = mixed * inverse
        share = sigmoid(out_gate)
        silu = out_gate * share
        slope = share * (1.0 + out_gate * (1.0 - share))
        back_gate_out[head] = (back_gated * unit * head_gain[...] * slope).astype(BF16)
        gain_out[...] += jnp.sum(back_gated * unit * silu, axis=0, keepdims=True)
        weighted = back_gated * head_gain[...] * silu
        back_mixed = inverse * (
            weighted - unit * jnp.mean(weighted * unit, axis=-1, keepdims=True)
        )
        back_mixed_out[head] = back_mixed
        state = state_out[head]
        for part in reversed(range(ROWS // BLOCK)):
            span = slice(part * BLOCK, (part + 1) * BLOCK)
            cum = cum_in[head, span]
            scaled = split_two(query_in[head, span] * jnp.exp(cum))
            state = state * jnp.exp(cum[BLOCK - 1 :]) + dot_split(
                split_two(back_mixed[span]), scaled, TN
            )
        state_out[head] = state


def mix_back_kernel(
    own, tokens, back_middle, qkv, cum_in, logits_in, states, back_mixed, back_gate, back_end,
    weight, rank_weight, decay_out, rank, gain,
    grad_out, input_out, decay_grad_out, bias_out, gain_out,
    state_ref, back_ref,
):
    heads = weight.shape[0]

    @pl.when(pl.program_id(0) == 0)
    def _():
        state_ref[...] = back_end[...]
        decay_grad_out[...] = jnp.zeros_like(decay_grad_out)
        bias_out[...] = jnp.zeros_like(bias_out)
        gain_out[...] = jnp.zeros_like(gain_out)

    causal = lower_mask()
    upper = as_ones(upper_mask())
    for part in reversed(range(ROWS // BLOCK)):
        span = slice(part * BLOCK, (part + 1) * BLOCK)
        rank_back = jnp.zeros((BLOCK, rank.shape[1]), F32)
        for head in range(heads):
            query = qkv[head, span, :HK]
            keys = qkv[head, span, HK : 2 * HK]
            values = split_two(qkv[head, span, 2 * HK :])
            cum = cum_in[head, span]
            center = cum[MID : MID + 1]
            total = cum[BLOCK - 1 :]
            grow, shrink = jnp.exp(cum - center), jnp.exp(center - cum)
            since, until = jnp.exp(cum), jnp.exp(total - cum)
            query_mid, key_mid = split_two(query * grow), split_two(keys * shrink)
            carried = keys * until
            carried_split = split_two(carried)
            back = split_two(back_mixed[head, span])
            scores = split_two(jnp.where(causal, dot_split(query_mid, key_mid, NT), 0.0))
            back_scores = split_two(jnp.where(causal, dot_split(back, values, NT), 0.0))
            state = states[part, head]
            back_state = state_ref[head]
            back_state_split = split_two(back_state)
            back_values = dot_split(scores, back, TN) + dot_split(
                carried_split, back_state_split, NT
            )
            back_query = (
                dot_split(back_scores, key_mid) * grow
                + dot_split(back, split_two(state)) * since
            )
            back_carried = dot_split(values, back_state_split)
            back_keys = dot_split(back_scores, query_mid, TN) * shrink + back_carried * until
            decayed = back_state * jnp.exp(total)
            back_total = jnp.sum(back_carried * carried, axis=0, keepdims=True) + jnp.sum(
                decayed * state, axis=0, keepdims=True
            )
            state_ref[head] = decayed + dot_split(back, split_two(query * since), TN)
            back_decay = (
                dot_exact(upper, query * back_query - keys * back_keys) + back_total
            )
            back_logits = back_decay * sigmoid(-logits_in[head, span]) / GATE_SCALE
            bias_out[head] += jnp.sum(back_logits, axis=0, keepdims=True)
            rank_back += lax.dot_general(
                back_logits, decay_out[head], NT, precision=lax.Precision.HIGHEST,
                preferred_element_type=F32,
            )
            decay_grad_out[head] += dot_split(split_two(rank[span]), split_two(back_logits), TN)
            back_ref[head, span, :HK] = (back_query * HK ** (-0.5)).astype(BF16)
            back_ref[head, span, HK : 2 * HK] = back_keys.astype(BF16)
            back_ref[head, span, 2 * HK : 2 * HK + HV] = back_values.astype(BF16)
            back_ref[head, span, 2 * HK + HV :] = back_gate[head, span]
        grad_out[span, 2 * HK + 2 * HV :] = rank_back.astype(BF16)

    back_normed = dot(grad_out[:, 2 * HK + 2 * HV :], rank_weight[0])
    for head in range(heads):
        back_normed += dot(back_ref[head], weight[head])

        @pl.when(own[0] == head)
        def _():
            grad_out[:, : 2 * HK + 2 * HV] = back_ref[head]

    inputs = tokens[...].astype(F32)
    inverse = inverse_rms(inputs, NORM_EPS)
    unit = inputs * inverse
    weighted = back_normed * gain[...]
    input_out[...] = back_middle[...] + inverse * (
        weighted - unit * jnp.mean(weighted * unit, axis=-1, keepdims=True)
    )
    gain_out[...] += jnp.sum(back_normed * unit, axis=0, keepdims=True)


def shaped(shape, kind=F32):
    return jax.ShapeDtypeStruct(shape, kind)


def call(kernel, grid, in_specs, out_specs, out_shape, scratch, operands, prefetch, flops, moved):
    return pl.pallas_call(
        kernel,
        grid_spec=pltpu.PrefetchScalarGridSpec(
            num_scalar_prefetch=prefetch,
            grid=grid,
            in_specs=in_specs,
            out_specs=out_specs,
            scratch_shapes=scratch,
        ),
        out_shape=out_shape,
        compiler_params=pltpu.CompilerParams(
            vmem_limit_bytes=VMEM_LIMIT, dimension_semantics=("arbitrary",) * len(grid)
        ),
        cost_estimate=pl.CostEstimate(flops=flops, bytes_accessed=moved, transcendentals=0),
    )(*operands)


def from_behind(value, axis, steps):
    count = lax.axis_size(axis)
    first, last = (max(0, -steps), min(count, count - steps))
    return lax.ppermute(value, axis, [(source, source + steps) for source in range(first, last)])


def carry(local, decay, steps):
    incoming = jnp.zeros_like(local)
    for _ in range(lax.axis_size("ctx") - 1):
        incoming = from_behind(decay * incoming + local, "ctx", steps)
    return incoming


def gather_pack(pack):
    rows, share = pack.shape
    if share % 128 == 0:
        whole = lax.all_gather(pack, ("dp", "ctx", "tp"))
        whole = whole.reshape(-1, lax.axis_size("tp"), rows, share)
        return whole.transpose(1, 2, 0, 3).reshape(whole.shape[1], rows, -1)
    return lax.all_gather(
        lax.all_gather(pack, "tp"), ("dp", "ctx"), axis=2, tiled=True
    )


def total_over(value, axes):
    return lax.psum(value, axes)


def adamw(weight_now, grad_now, mean_now, square_now, rate_value, decay_value):
    mean_new = BETA_ONE * mean_now + (1.0 - BETA_ONE) * grad_now
    square_new = BETA_TWO * square_now + (1.0 - BETA_TWO) * grad_now * grad_now
    mean_hat = mean_new / (1.0 - BETA_ONE**STEP)
    square_hat = square_new / (1.0 - BETA_TWO**STEP)
    weight_new = weight_now - rate_value * (
        mean_hat / (jnp.sqrt(square_hat) + ADAM_EPS) + decay_value * weight_now
    )
    return (mean_new, square_new, weight_new)


def three_parts(value):
    high = lax.reduce_precision(value, 8, 7)
    rest = value - high
    middle = lax.reduce_precision(rest, 8, 7)
    low = lax.reduce_precision(rest - middle, 8, 7)
    return [part.astype(BF16) for part in (high, middle, low)]


def body(
    tokens,
    cotangent,
    lengths,
    query_key_weight,
    query_key_mean,
    query_key_square,
    value_gate_weight,
    value_gate_mean,
    value_gate_square,
    decay_in_weight,
    decay_in_mean,
    decay_in_square,
    decay_out_weight,
    decay_out_mean,
    decay_out_square,
    decay_bias,
    decay_bias_mean,
    decay_bias_square,
    output_weight,
    output_mean,
    output_square,
    gate_up_weight,
    gate_up_mean,
    gate_up_square,
    down_weight,
    down_mean,
    down_square,
    gains,
    gains_mean,
    gains_square,
):
    rows, width = tokens.shape
    heads = lax.axis_size("tp")
    ranks = decay_in_weight.shape[1]
    units = down_weight.shape[0]
    steps = rows // ROWS
    own = lax.axis_index("tp").astype(jnp.int32).reshape(1)
    gain_one = gains[:width].reshape(1, width)
    gain_two = gains[width : 2 * width].reshape(1, width)
    gain_head = gains[2 * width :].reshape(1, HV)

    mixer_pack = jnp.concatenate(
        [
            query_key_weight[0].T,
            query_key_weight[1].T,
            value_gate_weight[0].T,
            value_gate_weight[1].T,
            output_weight,
            decay_in_weight.T,
        ]
    ).astype(BF16)
    ffn_pack = jnp.concatenate(
        [gate_up_weight[0].T, gate_up_weight[1].T, down_weight]
    ).astype(BF16)
    small = jnp.concatenate([decay_out_weight, decay_bias.reshape(1, HK)])
    small_full = lax.all_gather(small, "tp")
    decay_out_full = small_full[:, :ranks]
    bias_full = small_full[:, ranks:]
    mixer = gather_pack(mixer_pack)
    ffn = gather_pack(ffn_pack)

    position = lax.axis_index("ctx") * rows + jnp.arange(rows, dtype=jnp.int32)
    back_ffn = jnp.where((position < lengths[0])[:, None], cotangent, jnp.zeros_like(cotangent))

    columns = 2 * HK + 2 * HV
    row_spec = pl.BlockSpec((ROWS, width), lambda i, *_: (i, 0))
    gain_spec = pl.BlockSpec((1, width), lambda i, *_: (0, 0))
    head_gain_spec = pl.BlockSpec((1, HV), lambda i, *_: (0, 0))
    weight_spec = pl.BlockSpec(
        (heads, columns, width), lambda i, *_: (0, 0, 0), pipeline_mode=pl.Buffered(1)
    )
    rank_weight_spec = pl.BlockSpec(
        (1, ranks, width), lambda i, *_: (0, (columns + HV) // ranks, 0)
    )
    out_weight_spec = pl.BlockSpec(
        (heads, HV, width), lambda i, *_: (0, columns // HV, 0), pipeline_mode=pl.Buffered(1)
    )
    decay_out_spec = pl.BlockSpec((heads, ranks, HK), lambda i, *_: (0, 0, 0))
    bias_spec = pl.BlockSpec((heads, 1, HK), lambda i, *_: (0, 0, 0))
    state_spec = pl.BlockSpec((heads, HV, HK), lambda i, *_: (0, 0, 0))

    def by_head(size, reverse=False):
        if reverse:
            return pl.BlockSpec((heads, ROWS, size), lambda i, *_: (0, steps - 1 - i, 0))
        return pl.BlockSpec((heads, ROWS, size), lambda i, *_: (0, i, 0))

    parts = ROWS // BLOCK
    normed, qkv, out_gate, rank, logits, cum, local_state, local_total = call(
        project_kernel,
        (steps,),
        [row_spec, gain_spec, weight_spec, rank_weight_spec, decay_out_spec, bias_spec],
        [
            row_spec,
            by_head(2 * HK + HV),
            by_head(HV),
            pl.BlockSpec((ROWS, ranks), lambda i, *_: (i, 0)),
            by_head(HK),
            by_head(HK),
            state_spec,
            bias_spec,
        ],
        [
            shaped((rows, width), BF16),
            shaped((heads, rows, 2 * HK + HV)),
            shaped((heads, rows, HV)),
            shaped((rows, ranks)),
            shaped((heads, rows, HK)),
            shaped((heads, rows, HK)),
            shaped((heads, HV, HK)),
            shaped((heads, 1, HK)),
        ],
        [],
        (tokens, gain_one, mixer, mixer, decay_out_full, bias_full),
        0,
        2 * rows * width * columns * heads,
        rows * heads * 4 * 1024,
    )
    device_decay = jnp.exp(local_total)
    start_state = carry(local_state, device_decay, 1)

    mixed, states, gated_own, middle, normed_two = call(
        mix_kernel,
        (steps,),
        [
            row_spec,
            by_head(2 * HK + HV),
            by_head(HV),
            by_head(HK),
            state_spec,
            out_weight_spec,
            head_gain_spec,
            gain_spec,
        ],
        [
            by_head(HV),
            pl.BlockSpec((parts, heads, HV, HK), lambda i, *_: (i, 0, 0, 0)),
            pl.BlockSpec((ROWS, HV), lambda i, *_: (i, 0)),
            row_spec,
            row_spec,
        ],
        [
            shaped((heads, rows, HV)),
            shaped((steps * parts, heads, HV, HK)),
            shaped((rows, HV), BF16),
            shaped((rows, width)),
            shaped((rows, width), BF16),
        ],
        [pltpu.VMEM((heads, HV, HK), F32), pltpu.VMEM((ROWS, heads * HV), BF16)],
        (own, tokens, qkv, out_gate, cum, start_state, mixer, gain_head, gain_two),
        1,
        2 * rows * width * HV * heads * 3,
        rows * heads * 4 * 1024,
    )

    wide_spec = pl.BlockSpec((FFN_ROWS, width), lambda i, j, *_: (i, 0))
    own_spec = pl.BlockSpec((FFN_ROWS, units), lambda i, j, *_: (i, 0))
    wide_gain_spec = pl.BlockSpec((1, width), lambda i, j, *_: (0, 0))
    active, back_gate, back_up, layer_out, back_middle, back_attn, gain_two_part = call(
        ffn_kernel,
        (rows // FFN_ROWS, heads),
        [
            wide_spec,
            wide_spec,
            wide_spec,
            pl.BlockSpec((1, 3 * units, width), lambda i, j, *_: (j, 0, 0)),
            wide_gain_spec,
        ],
        [own_spec, own_spec, own_spec, wide_spec, wide_spec, wide_spec, wide_gain_spec],
        [
            shaped((rows, units), BF16),
            shaped((rows, units), BF16),
            shaped((rows, units), BF16),
            shaped((rows, width), BF16),
            shaped((rows, width)),
            shaped((rows, width), BF16),
            shaped((1, width)),
        ],
        [pltpu.VMEM((FFN_ROWS, width), F32), pltpu.VMEM((FFN_ROWS, width), F32)],
        (own, normed_two, back_ffn, middle, ffn, gain_two),
        1,
        12 * rows * width * units * heads,
        rows * width * 24,
    )
    ffn_grad = jnp.concatenate(
        [
            dot(back_gate, normed_two, TN),
            dot(back_up, normed_two, TN),
            dot(active, back_ffn, TN),
        ]
    )
    ffn_share = lax.psum_scatter(ffn_grad, ("dp", "ctx"), scatter_dimension=1, tiled=True)
    output_grad = dot(gated_own, back_attn, TN)
    output_share = lax.psum_scatter(output_grad, ("dp", "ctx"), scatter_dimension=1, tiled=True)

    back_row_spec = pl.BlockSpec((ROWS, width), lambda i, *_: (steps - 1 - i, 0))
    back_mixed, back_out_gate, head_gain_part, collected = call(
        gate_back_kernel,
        (steps,),
        [
            back_row_spec,
            out_weight_spec,
            by_head(HV, True),
            by_head(HV, True),
            by_head(HK, True),
            by_head(HK, True),
            head_gain_spec,
        ],
        [by_head(HV, True), by_head(HV, True), head_gain_spec, state_spec],
        [
            shaped((heads, rows, HV)),
            shaped((heads, rows, HV), BF16),
            shaped((1, HV)),
            shaped((heads, HV, HK)),
        ],
        [],
        (back_attn, mixer, mixed, out_gate, qkv, cum, gain_head),
        0,
        2 * rows * width * HV * heads,
        rows * heads * 4 * 1024,
    )
    back_end = carry(collected, device_decay, -1)

    grad_columns = columns + ranks
    mixer_back, input_grad, decay_out_grad, bias_grad, gain_one_part = call(
        mix_back_kernel,
        (steps,),
        [
            back_row_spec,
            back_row_spec,
            by_head(2 * HK + HV, True),
            by_head(HK, True),
            by_head(HK, True),
            pl.BlockSpec((parts, heads, HV, HK), lambda i, *_: (steps - 1 - i, 0, 0, 0)),
            by_head(HV, True),
            by_head(HV, True),
            state_spec,
            weight_spec,
            rank_weight_spec,
            decay_out_spec,
            pl.BlockSpec((ROWS, ranks), lambda i, *_: (steps - 1 - i, 0)),
            gain_spec,
        ],
        [
            pl.BlockSpec((ROWS, grad_columns), lambda i, *_: (steps - 1 - i, 0)),
            back_row_spec,
            decay_out_spec,
            bias_spec,
            gain_spec,
        ],
        [
            shaped((rows, grad_columns), BF16),
            shaped((rows, width)),
            shaped((heads, ranks, HK)),
            shaped((heads, 1, HK)),
            shaped((1, width)),
        ],
        [pltpu.VMEM((heads, HV, HK), F32), pltpu.VMEM((heads, ROWS, columns), BF16)],
        (
            own, tokens, back_middle, qkv, cum, logits, states, back_mixed, back_out_gate, back_end,
            mixer, mixer, decay_out_full, rank, gain_one,
        ),
        1,
        2 * rows * width * columns * heads * 2,
        rows * heads * 4 * 2048,
    )
    mixer_grad = dot(mixer_back, normed, TN)
    mixer_share = lax.psum_scatter(mixer_grad, ("dp", "ctx"), scatter_dimension=1, tiled=True)
    decay_out_own = lax.dynamic_index_in_dim(decay_out_grad, own[0], 0, keepdims=False)
    bias_own = lax.dynamic_index_in_dim(bias_grad, own[0], 0, keepdims=False)
    sums = jnp.concatenate(
        [
            gain_one_part.reshape(-1),
            gain_two_part.reshape(-1),
            head_gain_part.reshape(-1),
            bias_own.reshape(-1),
            decay_out_own.reshape(-1),
        ]
    )
    sums = total_over(sums, ("dp", "ctx"))
    gain_count = gains.shape[0]
    gains_grad = sums[:gain_count]
    bias_total = sums[gain_count : gain_count + HK]
    decay_out_total = sums[gain_count + HK :].reshape(ranks, HK)

    query_key_share = jnp.stack([mixer_share[:HK].T, mixer_share[HK : 2 * HK].T])
    value_gate_share = jnp.stack(
        [mixer_share[2 * HK : 2 * HK + HV].T, mixer_share[2 * HK + HV : columns].T]
    )
    decay_in_share = mixer_share[columns:].T
    gate_up_share = jnp.stack([ffn_share[:units].T, ffn_share[units : 2 * units].T])
    down_share = ffn_share[2 * units :]

    updated = adamw(
        query_key_weight,
        query_key_share,
        query_key_mean,
        query_key_square,
        RATE_MATRIX,
        WEIGHT_DECAY,
    )
    updated = updated + adamw(
        value_gate_weight,
        value_gate_share,
        value_gate_mean,
        value_gate_square,
        RATE_MATRIX,
        WEIGHT_DECAY,
    )
    updated = updated + adamw(
        decay_in_weight, decay_in_share, decay_in_mean, decay_in_square, RATE_MATRIX, WEIGHT_DECAY
    )
    updated = updated + adamw(
        decay_out_weight, decay_out_total, decay_out_mean, decay_out_square, RATE_RANK, WEIGHT_DECAY
    )
    updated = updated + adamw(
        decay_bias, bias_total, decay_bias_mean, decay_bias_square, RATE_BIAS, 0.0
    )
    updated = updated + adamw(
        output_weight, output_share, output_mean, output_square, RATE_MATRIX, WEIGHT_DECAY
    )
    updated = updated + adamw(
        gate_up_weight, gate_up_share, gate_up_mean, gate_up_square, RATE_MATRIX, WEIGHT_DECAY
    )
    updated = updated + adamw(
        down_weight, down_share, down_mean, down_square, RATE_MATRIX, WEIGHT_DECAY
    )
    updated = updated + adamw(gains, gains_grad, gains_mean, gains_square, RATE_GAIN, 0.0)
    return (layer_out, input_grad) + updated


def solution(mesh):
    tokens_at = P(("dp", "ctx"), None)
    split_at = P(None, ("dp", "ctx"), "tp")
    deep_at = P("tp", ("dp", "ctx"))
    rank_out_at = P(None, "tp")
    kinds = (split_at, split_at, tokens_at, rank_out_at, P("tp"), deep_at, split_at, deep_at, P())
    params = tuple(kind for kind in kinds for _ in range(3))
    return jax.shard_map(
        body,
        mesh=mesh,
        in_specs=(tokens_at, tokens_at, P("dp")) + params,
        out_specs=(tokens_at, tokens_at) + params,
        check_vma=False,
    )
```

time: 1480 us -> 663 us (0.45)
  waiting for transfers between devices: 906 us -> 128 us
  Pallas kernels: 0 us -> 314 us
  matrix products: 193 us -> 25 us
  other arithmetic: 161 us -> 25.1 us
  local copies, waits for them, and re-layouts: 128 us -> 103 us
  blocking collectives: 64.5 us -> 39.6 us
    psum x3 -> x0, waiting for transfers between devices: 846 us -> none  [the longest x2 550 us: tensor_total(): return lax.psum(term_fn(0, row_count), 'tp')]
    pallas_call x0 -> x5, Pallas kernels: none -> 314 us  [call(): pl.pallas_call(kernel, grid_spec=pltpu.PrefetchScalarGridSpec(num_scalar_...]
    dot_general x44 -> x5, matrix products: 193 us -> 25 us  [dot(): return lax.dot_general(left, right, dims, preferred_element_type=F32)]
    reshape x0 -> x4, local copies, waits for them, and re-layouts: none -> 86 us  [the longest x2 46.1 us: gather_pack(): whole = whole.reshape(-1, lax.axis_size('tp'), rows, share)]
    dynamic_update_slice x128 -> x0, local copies, waits for them, and re-layouts: 59.4 us -> none  [gla_head(): lax.scan(advance, start_state, (block_total, update_terms))]
    add x35 -> x2, other arithmetic: 56.4 us -> 2.2 us  [carry(): incoming = from_behind(decay * incoming + local, 'ctx', steps)]
    reduce_sum x36 -> x0, other arithmetic: 48.9 us -> none  [the longest x32 32.6 us: advance(): return (jnp.exp(item[0])[:, None] * state + item[1], state)]
    reduce_scatter x5 -> x2, waiting for transfers between devices: 24.4 us -> 67.4 us  [the longest x1 67.4 us: body(): lax.psum_scatter(ffn_grad, ('dp', 'ctx'), scatter_dimension=1, tiled=True)]
  transfers between devices with their start and end apart: 14 -> 7, of which waited for: 6 -> 2; matrix products, arithmetic and copies ran while one was open for 23% -> 12% of each run, Pallas kernels for 0% -> 28%
where the time goes in v1:
time: 663 us; the launch traced here: 655 us
  Pallas kernels  314 us (47%)
  waiting for transfers between devices  128 us (19%)
  local copies, waits for them, and re-layouts  103 us (16%)
  blocking collectives  39.6 us (6%)
  other arithmetic  25.1 us (4%)
  matrix products  25 us (4%)
  between operations  15.6 us (2%)
    pallas_call x5, Pallas kernels, call(): pl.pallas_call(kernel, grid_spec=pltpu.PrefetchScalarGridSpec(num_scalar_...  314 us
    reduce_scatter x1, waiting for transfers between devices, body(): lax.psum_scatter(ffn_grad, ('dp', 'ctx'), scatter_dimension=1, tiled=True)  67.4 us
    all_gather x2, waiting for transfers between devices, gather_pack(): whole = lax.all_gather(pack, ('dp', 'ctx', 'tp'))  61 us
    reshape x2, local copies, waits for them, and re-layouts, gather_pack(): whole = whole.reshape(-1, lax.axis_size('tp'), rows, share)  46.1 us
    reshape x2, local copies, waits for them, and re-layouts, gather_pack(): return whole.transpose(1, 2, 0, 3).reshape(whole.shape[1], rows, -1)  39.9 us
    dot_general x5, matrix products, dot(): return lax.dot_general(left, right, dims, preferred_element_type=F32)  25 us
    psum x1, blocking collectives, total_over(): return lax.psum(value, axes)  24.9 us
    all_gather x1, blocking collectives, body(): small_full = lax.all_gather(small, 'tp')  14.7 us
  transfers between devices with their start and end apart: 7, of which 2 were waited for; matrix products, arithmetic and copies ran while one was open for 12% of the time, Pallas kernels for 28%

profile of v1, /device:TPU:0, one launch (start us, length us, event | category | flops | bytes accessed | tf_op | source)
XLA Modules:
  0.0 655.4 jit_solution(12470442024180958951)
XLA Ops:
  7.3 1.1 copy.77
  8.4 0.6 copy-done.6
  9.0 1.1 copy.78
  10.2 1.0 bitcast_dynamic-update-slice_fusion
  11.1 0.7 constant_dynamic-update-slice_fusion
  11.9 0.7 copy-done.10
  12.6 1.2 convert.53
  13.9 0.8 pad_maximum_fusion.2
  14.8 14.7 %all-gather.1 = f32[4,17,128]{2,1,0:T(8,128)S(1)} all-gather(f32[1,17,128]{2,1,0:T(8,128)S(1)} %maximum_bitcast_fusion), channel_id=2, replica_groups=mesh['dp'=4,'ctx'=2,'tp'=4] {'tp'}, dimensions={0}, use_global_device_ids=true | all-gather | bytes 43520 | tf_op jit(solution)/shard_map/all_gather | solution.py:491
  29.6 0.6 slice.109.decay_out
  30.2 0.6 slice.110.bias
  30.8 0.6 slice.89
  32.0 0.6 fusion.22
  32.6 61.0 %all-gather.5.cloned.1.call-done = bf16[32,1040,128]{2,1,0:T(8,128)(2,1)} async-done(((bf16[1,1040,128]{2,1,0:T(8,128)(2,1)}), bf16[32,1040,128]{2,1,0:T(8,128)(2,1)}) %all-gather.5.cloned.1.call-update) | async-done | bytes 8519696 | tf_op jit(solution)/shard_map/all_gather | solution.py:404
  93.5 14.0 %copy.98 = bf16[8,4,1040,128]{3,0,2,1:T(8,128)(2,1)} copy(bf16[8,4,1040,128]{3,2,1,0:T(8,128)(2,1)} %bitcast.134) | data formatting | bytes 17039360 | tf_op jit(solution)/shard_map/reshape | solution.py:405
  107.6 13.8 %reshape.253.weight.rank_weight.out_weight = bf16[4,1040,1024]{2,1,0:T(8,128)(2,1)} reshape(bf16[4,1040,8,128]{3,2,1,0:T(8,128)(2,1)} %bitcast.132) | data formatting | bytes 17039360 | tf_op jit(solution)/shard_map/reshape | solution.py:406
  121.3 43.6 %shard_map.509 = (bf16[2048,1024]{1,0:T(8,128)(2,1)}, f32[4,2048,512]{2,1,0:T(8,128)}, f32[4,2048,256]{2,1,0:T(8,128)}, f32[2048,16]{1,0:T(8,128)}, f32[4,2048,1...) custom-call(bf16[2048,1024]{1,0:T(8,128)(2,1)} %tokens.5, ...), custom_call_target="tpu_custom_call" | custom-call | flops 12884901888 | bytes 33554432 | tf_op jit(solution)/shard_map/pallas_call | solution.py:371
  165.0 0.7 exponential_multiply_fusion
  165.7 1.1 broadcast_add_fusion.1
  166.8 2.6 collective-permute-start
  169.4 4.0 broadcast_select_fusion.back
  173.4 0.8 copy-done.36
  174.2 54.2 %shard_map.510 = (f32[4,2048,256]{2,1,0:T(8,128)}, f32[16,4,256,128]{3,2,1,0:T(8,128)}, bf16[2048,256]{1,0:T(8,128)(2,1)}, f32[2048,1024]{1,0:T(8,128)}, bf16[2048,1024]{1,0:T(8,128)(2,1)}) custom-call(s32[1]{0:T(128)} %bitcast.own, bf16[2048,1024]{1,0:T(8,128)(2,1)} %tokens.5, f32[4,2048,512]{2,1,0:T(8,128)} %get-tuple-element.58.qkv.query_in, ...), custom_call_target="tpu_custom_call" | custom-call | flops 12884901888 | bytes 33554432 | tf_op jit(solution)/shard_map/pallas_call | solution.py:371
  228.4 32.1 %copy.97 = bf16[8,4,2112,128]{3,0,2,1:T(8,128)(2,1)} copy(bf16[8,4,2112,128]{3,2,1,0:T(8,128)(2,1)} %bitcast.133) | data formatting | bytes 34603008 | tf_op jit(solution)/shard_map/reshape | solution.py:405
  260.5 26.1 %reshape.258.weight = bf16[4,2112,1024]{2,1,0:T(8,128)(2,1)} reshape(bf16[4,2112,8,128]{3,2,1,0:T(8,128)(2,1)} %bitcast.131) | data formatting | bytes 34603008 | tf_op jit(solution)/shard_map/reshape | solution.py:406
  286.7 101.6 %shard_map.511 = (bf16[2048,704]{1,0:T(8,128)(2,1)}, bf16[2048,704]{1,0:T(8,128)(2,1)}, bf16[2048,704]{1,0:T(8,128)(2,1)}, bf16[2048,1024]{1,0:T(8,128)(2,1)}, f...) custom-call(s32[1]{0:T(128)} %bitcast.own, bf16[2048,1024]{1,0:T(8,128)(2,1)} %get-tuple-element.63.normed, ...), custom_call_target="tpu_custom_call" | custom-call | flops 70866960384 | bytes 50331648 | tf_op jit(solution)/shard_map/pallas_call | solution.py:371
  388.3 27.9 %shard_map.512 = (f32[4,2048,256]{2,1,0:T(8,128)}, bf16[4,2048,256]{2,1,0:T(8,128)(2,1)}, f32[1,256]{1,0:T(1,128)}, f32[4,256,128]{2,1,0:T(8,128)}) custom-call(bf16[2048,1024]{1,0:T(8,128)(2,1)} %get-tuple-element.69.back_attn, bf16[4,1040,1024]{2,1,0:T(8,128)(2,1)} %reshape.253.weight.rank_weight.out_weight, f32[4,2048,256]{2,1,0:T(8,128)} %get-tuple-element.70.mixed_in, ...), custom_call_target="tpu_custom_call" | custom-call | flops 4294967296 | bytes 33554432 | tf_op jit(solution)/shard_map/pallas_call | solution.py:371
  416.3 1.1 broadcast_add_fusion
  417.3 1.3 collective-permute-start.1
  418.6 4.5 fusion.24
  423.2 0.8 copy-done.35
  424.0 86.9 %shard_map.513 = (bf16[2048,784]{1,0:T(8,128)(2,1)}, f32[2048,1024]{1,0:T(8,128)}, f32[4,16,128]{2,1,0:T(8,128)}, f32[4,1,128]{2,1,0:T(1,128)}, f32[1,1024]{1,0:T(1,128)}) custom-call(s32[1]{0:T(128)} %bitcast.own, bf16[2048,1024]{1,0:T(8,128)(2,1)} %tokens.5, f32[2048,1024]{1,0:T(8,128)} %get-tuple-element.66.back_middle, ...), custom_call_target="tpu_custom_call" | custom-call | flops 25769803776 | bytes 67108864 | tf_op jit(solution)/shard_map/pallas_call | solution.py:371
  510.9 8.6 %fusion.23 = f32[784,1024]{1,0:T(8,128)} fusion(bf16[2048,784]{1,0:T(8,128)(2,1)} %get-tuple-element.76, bf16[2048,1024]{1,0:T(8,128)(2,1)} %get-tuple-element.77), kind=kOutput, calls=%fused_computation.76 | convolution fusion | flops 3288334336 | bytes 10616832 | tf_op jit(solution)/shard_map/dot_general | solution.py:39
  519.7 5.4 fusion.25
  525.1 3.3 fusion.26
  528.4 0.3 copy-done.39
  528.7 3.3 fusion.27
  532.0 4.0 pad_maximum_fusion
  536.2 0.7 copy-done.11
  537.0 0.1 copy.85
  537.1 0.1 copy.86
  537.2 0.1 copy.81
  537.4 0.1 copy.82
  537.5 0.7 constant_dynamic-update-slice_fusion.3
  538.2 0.7 bitcast_dynamic-update-slice_fusion.1
  538.9 24.9 %psum.7 = f32[4480]{0:T(1024)S(1)} all-reduce(f32[4480]{0:T(1024)S(1)} %bitcast_dynamic-update-slice_fusion.1), channel_id=1, replica_groups=mesh['dp'=4,'ctx'=2,'tp'=4] {'dp','ctx'}, use_global_device_ids=true, to_apply=%region_1.2 | all-reduce | flops 4480 | bytes 35840 | tf_op jit(solution)/shard_map/psum | solution.py:413
  563.8 0.5 multiply_subtract_fusion.8
  564.4 0.6 multiply_subtract_fusion.6
  565.0 0.6 multiply_subtract_fusion.5
  565.6 1.7 multiply_subtract_fusion.3
  567.3 1.0 slice_bitcast_fusion.5
  568.3 0.2 multiply_subtract_fusion.2
  568.6 0.8 copy.92
  569.4 0.8 copy.93
  570.3 0.8 copy.94
  571.1 0.9 slice_bitcast_fusion.7
  572.0 0.1 multiply_subtract_fusion.4
  572.1 0.8 copy.89
  572.9 0.8 copy.90
  573.6 0.8 copy.91
  574.4 1.3 multiply_subtract_fusion.7
  575.7 67.4 %reduce-scatter.8.cloned.1.call-done = f32[2112,128]{1,0:T(8,128)} async-done(((f32[2112,1024]{1,0:T(8,128)}), f32[2112,128]{1,0:T(8,128)}) %reduce-scatter.8.cloned.1.call-update) | async-done | bytes 1081360 | tf_op jit(solution)/shard_map/reduce_scatter | solution.py:626
  643.1 2.6 multiply_subtract_fusion.1
  645.6 2.8 multiply_subtract_fusion
  (106 shorter events, 0.7 us)
Async XLA Ops:
  7.2 6.6 %copy-start.4 = (f32[704,128]{1,0:T(8,128)S(1)}, f32[704,128]{1,0:T(8,128)}, u32[]{:S(2)}) copy-start(f32[704,128]{1,0:T(8,128)} %param.54) | copy-start | bytes 1081348
  7.2 7.6 %copy-start.30 = (f32[128]{0:T(128)S(1)}, f32[128]{0:T(128)}, u32[]{:S(2)}) copy-start(f32[128]{0:T(128)} %param.45) | copy-start | bytes 1540
  7.2 7.6 %copy-start.20 = (f32[16,128]{1,0:T(8,128)S(1)}, f32[16,128]{1,0:T(8,128)}, u32[]{:S(2)}) copy-start(f32[16,128]{1,0:T(8,128)} %param.42) | copy-start | bytes 24580
  7.2 23.5 %copy-start.17 = (f32[2304]{0:T(1024)S(1)}, f32[2304]{0:T(1024)}, u32[]{:S(2)}) copy-start(f32[2304]{0:T(1024)} %param.57) | copy-start | bytes 27652
  7.3 86.3 %all-gather.5.cloned.1.call-start = ((), (), s32[]{:S(2)}) async-start(), calls=%async_computation.3 | async-start | bytes 8785920 | tf_op jit(solution)/shard_map/all_gather | solution.py:404
  8.4 0.7 copy-start.6
  10.1 97.5 %copy-start.2 = (f32[2,128,256]{1,2,0:T(8,128)}, f32[2,128,256]{1,2,0:T(8,128)S(1)}, u32[]{:S(2)}) copy-start(f32[2,128,256]{1,2,0:T(8,128)S(1)} %copy.78) | copy-start | bytes 786436
  11.9 0.7 copy-start.10
  12.6 215.8 %all-gather.7.cloned.1.call-start = ((), (), s32[]{:S(2)}) async-start(), calls=%async_computation.4 | async-start | bytes 17842176 | tf_op jit(solution)/shard_map/all_gather | solution.py:404
  14.7 550.9 %reduce-scatter.6.cloned.1.call-start = ((), (), s32[]{:S(2)}) async-start(), calls=%async_computation.6 | async-start | bytes 1179648 | tf_op jit(solution)/shard_map/reduce_scatter | solution.py:628
  166.8 6.6 %collective-permute-start = (f32[4,256,128]{2,1,0:T(8,128)S(1)}, f32[4,256,128]{2,1,0:T(8,128)S(1)}, u32[]{:S(2)}, u32[]{:S(2)}) collective-permute-start(f32[4,256,128]{2,1,0:T(8,128)S(1)} %broadcast_add_fusion.1), channel_id=1, source_target_pairs={{0,4},{1,5},{2,6},{3,7},{8,12},{9,13},{10,14},{11,15},{16,20},{17,... | collective-permute-start | bytes 1572872 | tf_op jit(solution)/shard_map/ppermute | solution.py:391
  173.4 0.8 copy-start.36
  388.3 30.3 %copy-start.37 = (bf16[2048,256]{1,0:T(8,128)(2,1)S(1)}, bf16[2048,256]{1,0:T(8,128)(2,1)}, u32[]{:S(2)}) copy-start(bf16[2048,256]{1,0:T(8,128)(2,1)} %get-tuple-element.83) | copy-start | bytes 3145732
  417.3 5.9 collective-permute-start.1
  423.1 144.2 %reduce-scatter.4.cloned.1.call-start = ((), (), s32[]{:S(2)}) async-start(), calls=%async_computation.5 | async-start | bytes 3612672 | tf_op jit(solution)/shard_map/reduce_scatter | solution.py:702
  423.2 0.8 copy-start.35
  510.9 8.7 %copy-start.41 = (bf16[2048,704]{1,0:T(8,128)(2,1)S(1)}, bf16[2048,704]{1,0:T(8,128)(2,1)}, u32[]{:S(2)}) copy-start(bf16[2048,704]{1,0:T(8,128)(2,1)} %get-tuple-element.84) | copy-start | bytes 8650756
  519.6 123.4 %reduce-scatter.8.cloned.1.call-start = ((), (), s32[]{:S(2)}) async-start(), calls=%async_computation.7 | async-start | bytes 9732096 | tf_op jit(solution)/shard_map/reduce_scatter | solution.py:626
  519.7 5.4 copy-start.38
  519.7 5.4 copy-start.40
  525.1 3.3 copy-start
  525.1 3.6 copy-start.39
  536.0 0.9 copy-start.11
  536.0 1.1 copy-start.12
  536.0 1.2 copy-start.15
  536.0 1.3 copy-start.16
  536.0 1.5 copy-start.29
  536.0 1.5 copy-start.28
  536.0 1.5 copy-start.32
  536.0 27.7 %copy-start.31 = (f32[128]{0:T(128)S(1)}, f32[128]{0:T(128)}, u32[]{:S(2)}) copy-start(f32[128]{0:T(128)} %param.45) | copy-start | bytes 1540
  536.1 27.7 %copy-start.33 = (f32[128]{0:T(128)S(1)}, f32[128]{0:T(128)}, u32[]{:S(2)}) copy-start(f32[128]{0:T(128)} %param.47) | copy-start | bytes 1540
  536.1 27.7 %copy-start.34 = (f32[128]{0:T(128)S(1)}, f32[128]{0:T(128)}, u32[]{:S(2)}) copy-start(f32[128]{0:T(128)} %param.46) | copy-start | bytes 1540
  536.1 28.3 %copy-start.21 = (f32[16,128]{1,0:T(8,128)S(1)}, f32[16,128]{1,0:T(8,128)}, u32[]{:S(2)}) copy-start(f32[16,128]{1,0:T(8,128)} %param.42) | copy-start | bytes 24580
  536.1 28.3 %copy-start.24 = (f32[16,128]{1,0:T(8,128)S(1)}, f32[16,128]{1,0:T(8,128)}, u32[]{:S(2)}) copy-start(f32[16,128]{1,0:T(8,128)} %param.44) | copy-start | bytes 24580
  536.1 28.2 %copy-start.25 = (f32[16,128]{1,0:T(8,128)S(1)}, f32[16,128]{1,0:T(8,128)}, u32[]{:S(2)}) copy-start(f32[16,128]{1,0:T(8,128)} %param.43) | copy-start | bytes 24580
  536.1 28.9 %copy-start.18 = (f32[2304]{0:T(1024)S(1)}, f32[2304]{0:T(1024)}, u32[]{:S(2)}) copy-start(f32[2304]{0:T(1024)} %param.57) | copy-start | bytes 27652
  536.1 28.9 %copy-start.22 = (f32[2304]{0:T(1024)S(1)}, f32[2304]{0:T(1024)}, u32[]{:S(2)}) copy-start(f32[2304]{0:T(1024)} %param.59) | copy-start | bytes 27652
  536.1 28.8 %copy-start.23 = (f32[2304]{0:T(1024)S(1)}, f32[2304]{0:T(1024)}, u32[]{:S(2)}) copy-start(f32[2304]{0:T(1024)} %param.58) | copy-start | bytes 27652
  536.2 29.5 %copy-start.9 = (f32[256,128]{1,0:T(8,128)S(1)}, f32[256,128]{1,0:T(8,128)}, u32[]{:S(2)}) copy-start(f32[256,128]{1,0:T(8,128)} %param.48) | copy-start | bytes 393220
  536.2 29.5 %copy-start.13 = (f32[256,128]{1,0:T(8,128)S(1)}, f32[256,128]{1,0:T(8,128)}, u32[]{:S(2)}) copy-start(f32[256,128]{1,0:T(8,128)} %param.50) | copy-start | bytes 393220
  536.2 29.4 %copy-start.14 = (f32[256,128]{1,0:T(8,128)S(1)}, f32[256,128]{1,0:T(8,128)}, u32[]{:S(2)}) copy-start(f32[256,128]{1,0:T(8,128)} %param.49) | copy-start | bytes 393220
  536.2 32.1 %copy-start.3 = (f32[2,128,256]{1,2,0:T(8,128)S(1)}, f32[2,128,256]{1,2,0:T(8,128)}, u32[]{:S(2)}) copy-start(f32[2,128,256]{1,2,0:T(8,128)} %copy-done.2) | copy-start | bytes 786436
  536.2 35.7 %copy-start.7 = (f32[2,128,128]{1,2,0:T(8,128)S(1)}, f32[2,128,128]{1,2,0:T(8,128)}, u32[]{:S(2)}) copy-start(f32[2,128,128]{1,2,0:T(8,128)} %copy-done.6) | copy-start | bytes 393220
  536.9 37.4 %copy-start.19 = (f32[128,16]{0,1:T(8,128)S(1)}, f32[128,16]{0,1:T(8,128)}, u32[]{:S(2)}) copy-start(f32[128,16]{0,1:T(8,128)} %param.39) | copy-start | bytes 24580
  536.9 37.4 %copy-start.26 = (f32[128,16]{0,1:T(8,128)S(1)}, f32[128,16]{0,1:T(8,128)}, u32[]{:S(2)}) copy-start(f32[128,16]{0,1:T(8,128)} %param.41) | copy-start | bytes 24580
  537.0 37.4 %copy-start.27 = (f32[128,16]{0,1:T(8,128)S(1)}, f32[128,16]{0,1:T(8,128)}, u32[]{:S(2)}) copy-start(f32[128,16]{0,1:T(8,128)} %param.40) | copy-start | bytes 24580
  537.1 106.0 %copy-start.5 = (f32[704,128]{1,0:T(8,128)S(1)}, f32[704,128]{1,0:T(8,128)}, u32[]{:S(2)}) copy-start(f32[704,128]{1,0:T(8,128)} %param.54) | copy-start | bytes 1081348
  568.6 77.1 %copy-start.1 = (f32[2,128,704]{1,2,0:T(8,128)S(1)}, f32[2,128,704]{1,2,0:T(8,128)}, u32[]{:S(2)}) copy-start(f32[2,128,704]{1,2,0:T(8,128)} %param.51) | copy-start | bytes 2162692
  568.6 77.1 %copy-start.8 = (f32[2,128,704]{1,2,0:T(8,128)S(1)}, f32[2,128,704]{1,2,0:T(8,128)}, u32[]{:S(2)}) copy-start(f32[2,128,704]{1,2,0:T(8,128)} %param.53) | copy-start | bytes 2162692
Sparse Core Ops, SparseCore 0:
  12.7 80.7 all-gather.4
  96.9 115.8 all-gather.6
  423.3 35.4 reduce-scatter.5
  519.7 47.2 reduce-scatter.3
  570.4 72.5 reduce-scatter.7

commit v2 on v1

--- a/solution.py
+++ b/solution.py
@@ -10,9 +10,13 @@
 HK = 128
 HV = 256
 BLOCK = 128
+LANES = 128
+GROUPS = 8
 MID = 63
+DECAY_ROWS = 32
 ROWS = 256
 FFN_ROWS = 512
+FFN_PARTS = 2
 STEP = 10
 
 NORM_EPS = 1e-06
@@ -45,9 +49,10 @@
 
 
 def dot_split(left, right, dims=NN):
-    return (
-        dot(left[0], right[0], dims) + dot(left[0], right[1], dims) + dot(left[1], right[0], dims)
-    )
+    axis = 1 - dims[0][0][0]
+    size = left[0].shape[axis]
+    both = dot(jnp.concatenate(left, axis=axis), right[0], dims)
+    return both[:size] + both[size:] + dot(left[0], right[1], dims)
 
 
 def dot_exact(matrix, values):
@@ -79,41 +84,62 @@
 
 
 def sigmoid(values):
-    return 1.0 / (1.0 + jnp.exp(-values))
+    return 0.5 + 0.5 * jnp.tanh(0.5 * values)
+
+
+def fill(info, first, second, pieces):
+    heads = first.shape[1]
+    for head in range(heads):
+        slot = info[2 * GROUPS + head]
+        for group in range(GROUPS):
+            lanes = slice(group * LANES, (group + 1) * LANES)
+            place = info[GROUPS + group]
+            for source_index, source in enumerate((first, second)):
+
+                @pl.when(info[group] == source_index)
+                def _():
+                    for target, start, count in pieces:
+                        if target.shape[0] == count and head > 0:
+                            continue
+                        at = head * count
+                        target[at : at + count, lanes] = source[
+                            place, slot, start : start + count
+                        ]
 
 
 def project_kernel(
-    tokens, gain, weight, rank_weight, decay_out, bias,
-    normed_out, qkv_out, gate_out, rank_out, logits_out, cum_out, state_out, total_out,
+    info, tokens, gain, first, second, decay_out,
+    normed_out, kv_out, rank_out, logits_out, cum_out, state_out, total_out, weight, rank_weight,
 ):
-    heads = weight.shape[0]
+    heads = first.shape[1]
+    size = HK + HV
+    ranks = rank_out.shape[1]
 
     @pl.when(pl.program_id(0) == 0)
     def _():
         state_out[...] = jnp.zeros_like(state_out)
         total_out[...] = jnp.zeros_like(total_out)
+        fill(info, first, second, ((weight, 0, size), (rank_weight, size, ranks)))
 
     inputs = tokens[...].astype(F32)
     normed = (inputs * inverse_rms(inputs, NORM_EPS) * gain[...]).astype(BF16)
     normed_out[...] = normed
-    rank = dot(normed, rank_weight[0], NT)
+    rank = dot(normed, rank_weight[...], NT)
     rank_out[...] = rank
     lower = as_ones(lower_mask())
+    made = dot(normed, weight[...], NT)
     for head in range(heads):
-        made = dot(normed, weight[head], NT)
-        query = made[:, :HK] * HK ** (-0.5)
-        keys = made[:, HK : 2 * HK]
-        values = made[:, 2 * HK : 2 * HK + HV]
-        qkv_out[head, :, :HK] = query
-        qkv_out[head, :, HK : 2 * HK] = keys
-        qkv_out[head, :, 2 * HK :] = values
-        gate_out[head] = made[:, 2 * HK + HV :]
+        slot = info[2 * GROUPS + head]
+        keys = made[:, head * size : head * size + HK]
+        values = made[:, head * size + HK : (head + 1) * size]
+        kv_out[head, :, :HK] = keys
+        kv_out[head, :, HK:] = values
         logits = (
             lax.dot_general(
-                rank, decay_out[head], NN, precision=lax.Precision.HIGHEST,
+                rank, decay_out[slot, :ranks], NN, precision=lax.Precision.HIGHEST,
                 preferred_element_type=F32,
             )
-            + bias[head]
+            + decay_out[slot, ranks : ranks + 1]
         )
         logits_out[head] = logits
         log_decay = (
@@ -132,23 +158,29 @@
 
 
 def mix_kernel(
-    own, tokens, qkv, gate, cum_in, start, out_weight, head_gain, gain,
-    mixed_out, state_out, gated_out, middle_out, normed_out,
+    info, tokens, normed, kv, cum_in, start, first, second, head_gain, gain,
+    query_out, gate_out, mixed_out, state_out, gated_out, middle_out, normed_out, weight, out_weight,
     state_ref, gated_ref,
 ):
     heads = start.shape[0]
+    size = HK + HV
 
     @pl.when(pl.program_id(0) == 0)
     def _():
         state_ref[...] = start[...]
-
+        fill(info, first, second, ((weight, 0, size), (out_weight, size, HV)))
+
+    made = dot(normed[...], weight[...], NT)
     causal = lower_mask()
     for part in range(ROWS // BLOCK):
         span = slice(part * BLOCK, (part + 1) * BLOCK)
         for head in range(heads):
-            query = qkv[head, span, :HK]
-            keys = qkv[head, span, HK : 2 * HK]
-            values = split_two(qkv[head, span, 2 * HK :])
+            query = made[span, head * size : head * size + HK] * HK ** (-0.5)
+            out_gate = made[span, head * size + HK : (head + 1) * size]
+            query_out[head, span] = query
+            gate_out[head, span] = out_gate
+            keys = kv[head, span, :HK]
+            values = split_two(kv[head, span, HK:])
             cum = cum_in[head, span]
             center = cum[MID : MID + 1]
             total = cum[BLOCK - 1 :]
@@ -163,65 +195,69 @@
             carried = split_two(keys * jnp.exp(total - cum))
             state_ref[head] = state * jnp.exp(total) + dot_split(values, carried, TN)
             mixed_out[head, span] = mixed
-            out_gate = gate[head, span]
             gated = (
                 mixed * inverse_rms(mixed, HEAD_EPS) * head_gain[...] * (out_gate * sigmoid(out_gate))
             ).astype(BF16)
             gated_ref[span, head * HV : (head + 1) * HV] = gated
 
-            @pl.when(own[0] == head)
+            @pl.when(info[2 * GROUPS + heads] == head)
             def _():
                 gated_out[span] = gated
 
-    width = tokens.shape[1]
-    middle = tokens[...].astype(F32) + dot(
-        gated_ref[...], out_weight[...].reshape(heads * HV, width)
-    )
+    middle = tokens[...].astype(F32) + dot(gated_ref[...], out_weight[...])
     middle_out[...] = middle
     normed_out[...] = (middle * inverse_rms(middle, NORM_EPS) * gain[...]).astype(BF16)
 
 
 def ffn_kernel(
-    own, normed, back, middle, weight, gain,
+    weight_pieces, info, normed, back, middle, weight, gain,
     active_out, back_gate_out, back_up_out, layer_out, back_middle_out, back_attn_out, gain_out,
     ffn_ref, back_ref,
 ):
     step, piece = pl.program_id(0), pl.program_id(1)
-    units = weight.shape[1] // 3
+    units = weight.shape[2] // 3
 
     @pl.when((step == 0) & (piece == 0))
     def _():
+        ffn_ref[...] = jnp.zeros_like(ffn_ref)
+        back_ref[...] = jnp.zeros_like(back_ref)
         gain_out[...] = jnp.zeros_like(gain_out)
 
-    gate_weight = weight[0, :units]
-    up_weight = weight[0, units : 2 * units]
-    down_weight = weight[0, 2 * units :]
-    gate_values = dot(normed[...], gate_weight, NT)
-    upward = dot(normed[...], up_weight, NT)
-    back_active = dot(back[...], down_weight, NT)
-    share = sigmoid(gate_values)
-    silu = gate_values * share
-    active = (silu * upward).astype(BF16)
-    back_gate = (back_active * upward * (share * (1.0 + gate_values * (1.0 - share)))).astype(BF16)
-    back_up = (back_active * silu).astype(BF16)
-    ffn = dot(active, down_weight)
-    back_normed = dot(back_gate, gate_weight) + dot(back_up, up_weight)
-
-    @pl.when(piece == own[0])
-    def _():
-        active_out[...] = active
-        back_gate_out[...] = back_gate
-        back_up_out[...] = back_up
-
-    @pl.when(piece == 0)
-    def _():
-        ffn_ref[...] = ffn
-        back_ref[...] = back_normed
-
-    @pl.when(piece > 0)
-    def _():
-        ffn_ref[...] += ffn
-        back_ref[...] += back_normed
+    def rows_of(start):
+        return jnp.concatenate(
+            [weight[group, 0, start : start + units] for group in range(GROUPS)], axis=1
+        )
+
+    gate_weight, up_weight, down_weight = rows_of(0), rows_of(units), rows_of(2 * units)
+    count = normed.shape[0] // FFN_PARTS
+    spans = [slice(part * count, (part + 1) * count) for part in range(FFN_PARTS)]
+    made = [
+        (
+            dot(normed[span], gate_weight, NT),
+            dot(normed[span], up_weight, NT),
+            dot(back[span], down_weight, NT),
+        )
+        for span in spans
+    ]
+    for span, (gate_values, upward, back_active) in zip(spans, made):
+        share = sigmoid(gate_values)
+        silu = gate_values * share
+        active = (silu * upward).astype(BF16)
+        back_gate = (
+            back_active * upward * (share * (1.0 + gate_values * (1.0 - share)))
+        ).astype(BF16)
+        back_up = (back_active * silu).astype(BF16)
+        ffn = dot(active, down_weight)
+        back_normed = dot(back_gate, gate_weight) + dot(back_up, up_weight)
+        keep = jnp.where(piece > 0, 1.0, 0.0)
+        ffn_ref[span] = ffn_ref[span] * keep + ffn
+        back_ref[span] = back_ref[span] * keep + back_normed
+
+        @pl.when(piece == info[2 * GROUPS + weight_pieces])
+        def _():
+            active_out[span] = active
+            back_gate_out[span] = back_gate
+            back_up_out[span] = back_up
 
     @pl.when(piece == pl.num_programs(1) - 1)
     def _():
@@ -251,7 +287,7 @@
         state_out[...] = jnp.zeros_like(state_out)
 
     for head in range(heads):
-        back_gated = dot(back_attn[...], out_weight[head], NT)
+        back_gated = dot(back_attn[...], out_weight[head * HV : (head + 1) * HV], NT)
         mixed = mixed_in[head]
         out_gate = gate[head]
         inverse = inverse_rms(mixed, HEAD_EPS)
@@ -278,12 +314,14 @@
 
 
 def mix_back_kernel(
-    own, tokens, back_middle, qkv, cum_in, logits_in, states, back_mixed, back_gate, back_end,
-    weight, rank_weight, decay_out, rank, gain,
+    info, tokens, back_middle, query_in, kv, cum_in, logits_in, states, back_mixed, back_gate,
+    back_end, query_weight, key_weight, rank_weight, decay_out, rank, gain,
     grad_out, input_out, decay_grad_out, bias_out, gain_out,
-    state_ref, back_ref,
+    state_ref, query_ref, key_ref,
 ):
-    heads = weight.shape[0]
+    heads = back_end.shape[0]
+    size = HK + HV
+    ranks = rank.shape[1]
 
     @pl.when(pl.program_id(0) == 0)
     def _():
@@ -298,9 +336,10 @@
         span = slice(part * BLOCK, (part + 1) * BLOCK)
         rank_back = jnp.zeros((BLOCK, rank.shape[1]), F32)
         for head in range(heads):
-            query = qkv[head, span, :HK]
-            keys = qkv[head, span, HK : 2 * HK]
-            values = split_two(qkv[head, span, 2 * HK :])
+            slot = info[2 * GROUPS + head]
+            query = query_in[head, span]
+            keys = kv[head, span, :HK]
+            values = split_two(kv[head, span, HK:])
             cum = cum_in[head, span]
             center = cum[MID : MID + 1]
             total = cum[BLOCK - 1 :]
@@ -335,23 +374,28 @@
             back_logits = back_decay * sigmoid(-logits_in[head, span]) / GATE_SCALE
             bias_out[head] += jnp.sum(back_logits, axis=0, keepdims=True)
             rank_back += lax.dot_general(
-                back_logits, decay_out[head], NT, precision=lax.Precision.HIGHEST,
+                back_logits, decay_out[slot, :ranks], NT, precision=lax.Precision.HIGHEST,
                 preferred_element_type=F32,
             )
             decay_grad_out[head] += dot_split(split_two(rank[span]), split_two(back_logits), TN)
-            back_ref[head, span, :HK] = (back_query * HK ** (-0.5)).astype(BF16)
-            back_ref[head, span, HK : 2 * HK] = back_keys.astype(BF16)
-            back_ref[head, span, 2 * HK : 2 * HK + HV] = back_values.astype(BF16)
-            back_ref[head, span, 2 * HK + HV :] = back_gate[head, span]
-        grad_out[span, 2 * HK + 2 * HV :] = rank_back.astype(BF16)
-
-    back_normed = dot(grad_out[:, 2 * HK + 2 * HV :], rank_weight[0])
+            at = head * size
+            query_ref[span, at : at + HK] = (back_query * HK ** (-0.5)).astype(BF16)
+            query_ref[span, at + HK : at + size] = back_gate[head, span]
+            key_ref[span, at : at + HK] = back_keys.astype(BF16)
+            key_ref[span, at + HK : at + size] = back_values.astype(BF16)
+        grad_out[span, 2 * size :] = rank_back.astype(BF16)
+
+    back_normed = (
+        dot(grad_out[:, 2 * size :], rank_weight[...])
+        + dot(query_ref[...], query_weight[...])
+        + dot(key_ref[...], key_weight[...])
+    )
     for head in range(heads):
-        back_normed += dot(back_ref[head], weight[head])
-
-        @pl.when(own[0] == head)
+
+        @pl.when(info[2 * GROUPS + heads] == head)
         def _():
-            grad_out[:, : 2 * HK + 2 * HV] = back_ref[head]
+            grad_out[:, :size] = query_ref[:, head * size : (head + 1) * size]
+            grad_out[:, size : 2 * size] = key_ref[:, head * size : (head + 1) * size]
 
     inputs = tokens[...].astype(F32)
     inverse = inverse_rms(inputs, NORM_EPS)
@@ -398,19 +442,95 @@
     return incoming
 
 
-def gather_pack(pack):
-    rows, share = pack.shape
-    if share % 128 == 0:
+def staged():
+    return lax.axis_size("dp") == 4 and lax.axis_size("ctx") == 2
+
+
+def swap(value, axis, distance):
+    count = lax.axis_size(axis)
+    return lax.ppermute(value, axis, [(source, source ^ distance) for source in range(count)])
+
+
+def shift(value, axis, distance):
+    count = lax.axis_size(axis)
+    return lax.ppermute(
+        value, axis, [(source, (source + distance) % count) for source in range(count)]
+    )
+
+
+def gather_plain(pack):
+    rows = pack.shape[0]
+    whole = lax.all_gather(lax.all_gather(pack, "tp"), ("dp", "ctx"), axis=2, tiled=True)
+    return whole.reshape(whole.shape[0], rows, GROUPS, LANES).transpose(2, 0, 1, 3)
+
+
+def gather_slots(pack):
+    count = lax.axis_size("tp")
+    line = jnp.stack([pack] + [shift(pack, "tp", distance) for distance in range(1, count)])
+    across, beyond = swap(line, "dp", 1), swap(line, "dp", 2)
+    half = count // 2
+    far = jnp.concatenate([swap(across[:half], "dp", 2), swap(beyond[half:], "dp", 1)])
+    first = jnp.stack([line, across, beyond, far])
+    return first, swap(first, "ctx", 1)
+
+
+def gather_pair(pack):
+    if staged():
+        return gather_slots(pack)
+    whole = gather_plain(pack)
+    half = GROUPS // 2
+    return whole[:half], whole[half:]
+
+
+def gather_info():
+    count = lax.axis_size("tp")
+    own = lax.axis_index("tp")
+    group = jnp.arange(GROUPS, dtype=jnp.int32)
+    heads = jnp.arange(count, dtype=jnp.int32)
+    if staged():
+        which = (group % 2) ^ lax.axis_index("ctx")
+        place = (group // 2) ^ lax.axis_index("dp")
+        slot = lax.rem(own - heads + count, count)
+    else:
+        which, place, slot = group // (GROUPS // 2), group % (GROUPS // 2), heads
+    return jnp.concatenate([which, place, slot, own.reshape(1)]).astype(jnp.int32)
+
+
+def gather_whole(pack):
+    if staged():
+        rows, share = pack.shape
         whole = lax.all_gather(pack, ("dp", "ctx", "tp"))
-        whole = whole.reshape(-1, lax.axis_size("tp"), rows, share)
-        return whole.transpose(1, 2, 0, 3).reshape(whole.shape[1], rows, -1)
-    return lax.all_gather(
-        lax.all_gather(pack, "tp"), ("dp", "ctx"), axis=2, tiled=True
-    )
-
-
-def total_over(value, axes):
-    return lax.psum(value, axes)
+        return whole.reshape(-1, lax.axis_size("tp"), rows, share)
+    return gather_plain(pack)
+
+
+def scatter_rows(value):
+    if not staged():
+        return lax.psum_scatter(value, ("dp", "ctx"), scatter_dimension=0, tiled=True)
+    device, core = lax.axis_index("dp"), lax.axis_index("ctx")
+    row, column = device // 2, device % 2
+
+    def pick(array, axis, index):
+        return lax.dynamic_index_in_dim(array, index, axis, keepdims=False)
+
+    columns = value.shape[1]
+    value = value.reshape(2, 2, 2, -1, columns)
+    value = pick(value, 2, core) + swap(pick(value, 2, 1 - core), "ctx", 1)
+    half = value.shape[2] // 2
+    upper, lower = value[:, :, :half], value[:, :, half:]
+    upper = pick(upper, 1, column) + swap(pick(upper, 1, 1 - column), "dp", 1)
+    lower = pick(lower, 0, row) + swap(pick(lower, 0, 1 - row), "dp", 2)
+    upper = pick(upper, 0, row) + swap(pick(upper, 0, 1 - row), "dp", 2)
+    lower = pick(lower, 0, column) + swap(pick(lower, 0, 1 - column), "dp", 1)
+    return jnp.concatenate([upper, lower])
+
+
+def total_over(value):
+    if not staged():
+        return lax.psum(value, ("dp", "ctx"))
+    for axis, distance in (("ctx", 1), ("dp", 1), ("dp", 2)):
+        value = value + swap(value, axis, distance)
+    return value
 
 
 def adamw(weight_now, grad_now, mean_now, square_now, rate_value, decay_value):
@@ -469,121 +589,142 @@
     ranks = decay_in_weight.shape[1]
     units = down_weight.shape[0]
     steps = rows // ROWS
-    own = lax.axis_index("tp").astype(jnp.int32).reshape(1)
+    info = gather_info()
     gain_one = gains[:width].reshape(1, width)
     gain_two = gains[width : 2 * width].reshape(1, width)
     gain_head = gains[2 * width :].reshape(1, HV)
-
-    mixer_pack = jnp.concatenate(
-        [
-            query_key_weight[0].T,
-            query_key_weight[1].T,
-            value_gate_weight[0].T,
-            value_gate_weight[1].T,
-            output_weight,
-            decay_in_weight.T,
+    size = HK + HV
+
+    small = jnp.concatenate(
+        [
+            decay_out_weight,
+            decay_bias.reshape(1, HK),
+            jnp.zeros((DECAY_ROWS - ranks - 1, HK), F32),
         ]
-    ).astype(BF16)
-    ffn_pack = jnp.concatenate(
-        [gate_up_weight[0].T, gate_up_weight[1].T, down_weight]
-    ).astype(BF16)
-    small = jnp.concatenate([decay_out_weight, decay_bias.reshape(1, HK)])
-    small_full = lax.all_gather(small, "tp")
-    decay_out_full = small_full[:, :ranks]
-    bias_full = small_full[:, ranks:]
-    mixer = gather_pack(mixer_pack)
-    ffn = gather_pack(ffn_pack)
+    )
+    key_parts = [
+        query_key_weight[1].T.astype(BF16),
+        value_gate_weight[0].T.astype(BF16),
+        decay_in_weight.T.astype(BF16),
+    ]
+    if staged():
+        key_first, key_second = gather_pair(jnp.concatenate(key_parts + three_parts(small)))
+        sent = key_first[0, :, size + ranks :].astype(F32).reshape(heads, 3, DECAY_ROWS, HK)
+        decay_out_full = sent[:, 0] + sent[:, 1] + sent[:, 2]
+    else:
+        key_first, key_second = gather_pair(jnp.concatenate(key_parts))
+        decay_out_full = lax.all_gather(small, "tp")
+    query_first, query_second = gather_pair(
+        jnp.concatenate(
+            [query_key_weight[0].T, value_gate_weight[1].T, output_weight]
+        ).astype(BF16)
+    )
+    ffn = gather_whole(
+        jnp.concatenate([gate_up_weight[0].T, gate_up_weight[1].T, down_weight]).astype(BF16)
+    )
 
     position = lax.axis_index("ctx") * rows + jnp.arange(rows, dtype=jnp.int32)
     back_ffn = jnp.where((position < lengths[0])[:, None], cotangent, jnp.zeros_like(cotangent))
 
-    columns = 2 * HK + 2 * HV
+    columns = 2 * size
     row_spec = pl.BlockSpec((ROWS, width), lambda i, *_: (i, 0))
     gain_spec = pl.BlockSpec((1, width), lambda i, *_: (0, 0))
     head_gain_spec = pl.BlockSpec((1, HV), lambda i, *_: (0, 0))
-    weight_spec = pl.BlockSpec(
-        (heads, columns, width), lambda i, *_: (0, 0, 0), pipeline_mode=pl.Buffered(1)
-    )
-    rank_weight_spec = pl.BlockSpec(
-        (1, ranks, width), lambda i, *_: (0, (columns + HV) // ranks, 0)
-    )
-    out_weight_spec = pl.BlockSpec(
-        (heads, HV, width), lambda i, *_: (0, columns // HV, 0), pipeline_mode=pl.Buffered(1)
-    )
-    decay_out_spec = pl.BlockSpec((heads, ranks, HK), lambda i, *_: (0, 0, 0))
+    state_spec = pl.BlockSpec((heads, HV, HK), lambda i, *_: (0, 0, 0))
     bias_spec = pl.BlockSpec((heads, 1, HK), lambda i, *_: (0, 0, 0))
-    state_spec = pl.BlockSpec((heads, HV, HK), lambda i, *_: (0, 0, 0))
-
-    def by_head(size, reverse=False):
+
+    def fixed(array):
+        return pl.BlockSpec(
+            array.shape, lambda i, *_: (0,) * len(array.shape), pipeline_mode=pl.Buffered(1)
+        )
+
+    def by_head(length, reverse=False):
         if reverse:
-            return pl.BlockSpec((heads, ROWS, size), lambda i, *_: (0, steps - 1 - i, 0))
-        return pl.BlockSpec((heads, ROWS, size), lambda i, *_: (0, i, 0))
-
+            return pl.BlockSpec((heads, ROWS, length), lambda i, *_: (0, steps - 1 - i, 0))
+        return pl.BlockSpec((heads, ROWS, length), lambda i, *_: (0, i, 0))
+
+    weight_shape = shaped((heads * size, width), BF16)
+    rank_shape = shaped((ranks, width), BF16)
+    out_weight_shape = shaped((heads * HV, width), BF16)
     parts = ROWS // BLOCK
-    normed, qkv, out_gate, rank, logits, cum, local_state, local_total = call(
+    normed, kv, rank, logits, cum, local_state, local_total, key_weight, rank_weight = call(
         project_kernel,
         (steps,),
-        [row_spec, gain_spec, weight_spec, rank_weight_spec, decay_out_spec, bias_spec],
+        [row_spec, gain_spec, fixed(key_first), fixed(key_second), fixed(decay_out_full)],
         [
             row_spec,
-            by_head(2 * HK + HV),
-            by_head(HV),
+            by_head(size),
             pl.BlockSpec((ROWS, ranks), lambda i, *_: (i, 0)),
             by_head(HK),
             by_head(HK),
             state_spec,
             bias_spec,
+            fixed(weight_shape),
+            fixed(rank_shape),
         ],
         [
             shaped((rows, width), BF16),
-            shaped((heads, rows, 2 * HK + HV)),
-            shaped((heads, rows, HV)),
+            shaped((heads, rows, size)),
             shaped((rows, ranks)),
             shaped((heads, rows, HK)),
             shaped((heads, rows, HK)),
             shaped((heads, HV, HK)),
             shaped((heads, 1, HK)),
+            weight_shape,
+            rank_shape,
         ],
         [],
-        (tokens, gain_one, mixer, mixer, decay_out_full, bias_full),
-        0,
-        2 * rows * width * columns * heads,
+        (info, tokens, gain_one, key_first, key_second, decay_out_full),
+        1,
+        2 * rows * width * size * heads,
         rows * heads * 4 * 1024,
     )
     device_decay = jnp.exp(local_total)
     start_state = carry(local_state, device_decay, 1)
 
-    mixed, states, gated_own, middle, normed_two = call(
+    query, out_gate, mixed, states, gated_own, middle, normed_two, query_weight, out_weight = call(
         mix_kernel,
         (steps,),
         [
             row_spec,
-            by_head(2 * HK + HV),
-            by_head(HV),
+            row_spec,
+            by_head(size),
             by_head(HK),
             state_spec,
-            out_weight_spec,
+            fixed(query_first),
+            fixed(query_second),
             head_gain_spec,
             gain_spec,
         ],
         [
+            by_head(HK),
+            by_head(HV),
             by_head(HV),
             pl.BlockSpec((parts, heads, HV, HK), lambda i, *_: (i, 0, 0, 0)),
             pl.BlockSpec((ROWS, HV), lambda i, *_: (i, 0)),
             row_spec,
             row_spec,
-        ],
-        [
+            fixed(weight_shape),
+            fixed(out_weight_shape),
+        ],
+        [
+            shaped((heads, rows, HK)),
+            shaped((heads, rows, HV)),
             shaped((heads, rows, HV)),
             shaped((steps * parts, heads, HV, HK)),
             shaped((rows, HV), BF16),
             shaped((rows, width)),
             shaped((rows, width), BF16),
+            weight_shape,
+            out_weight_shape,
         ],
         [pltpu.VMEM((heads, HV, HK), F32), pltpu.VMEM((ROWS, heads * HV), BF16)],
-        (own, tokens, qkv, out_gate, cum, start_state, mixer, gain_head, gain_two),
+        (
+            info, tokens, normed, kv, cum, start_state, query_first, query_second,
+            gain_head, gain_two,
+        ),
         1,
-        2 * rows * width * HV * heads * 3,
+        2 * rows * width * (size + 2 * HV) * heads,
         rows * heads * 4 * 1024,
     )
 
@@ -591,13 +732,13 @@
     own_spec = pl.BlockSpec((FFN_ROWS, units), lambda i, j, *_: (i, 0))
     wide_gain_spec = pl.BlockSpec((1, width), lambda i, j, *_: (0, 0))
     active, back_gate, back_up, layer_out, back_middle, back_attn, gain_two_part = call(
-        ffn_kernel,
+        functools.partial(ffn_kernel, heads),
         (rows // FFN_ROWS, heads),
         [
             wide_spec,
             wide_spec,
             wide_spec,
-            pl.BlockSpec((1, 3 * units, width), lambda i, j, *_: (j, 0, 0)),
+            pl.BlockSpec((GROUPS, 1, 3 * units, LANES), lambda i, j, *_: (0, j, 0, 0)),
             wide_gain_spec,
         ],
         [own_spec, own_spec, own_spec, wide_spec, wide_spec, wide_spec, wide_gain_spec],
@@ -611,21 +752,21 @@
             shaped((1, width)),
         ],
         [pltpu.VMEM((FFN_ROWS, width), F32), pltpu.VMEM((FFN_ROWS, width), F32)],
-        (own, normed_two, back_ffn, middle, ffn, gain_two),
+        (info, normed_two, back_ffn, middle, ffn, gain_two),
         1,
         12 * rows * width * units * heads,
         rows * width * 24,
     )
-    ffn_grad = jnp.concatenate(
+    early_grad = jnp.concatenate(
         [
             dot(back_gate, normed_two, TN),
             dot(back_up, normed_two, TN),
             dot(active, back_ffn, TN),
+            dot(gated_own, back_attn, TN),
         ]
     )
-    ffn_share = lax.psum_scatter(ffn_grad, ("dp", "ctx"), scatter_dimension=1, tiled=True)
-    output_grad = dot(gated_own, back_attn, TN)
-    output_share = lax.psum_scatter(output_grad, ("dp", "ctx"), scatter_dimension=1, tiled=True)
+    early_grad, back_attn = lax.optimization_barrier((early_grad, back_attn))
+    early_share = lax.psum_scatter(early_grad, ("dp", "ctx"), scatter_dimension=1, tiled=True)
 
     back_row_spec = pl.BlockSpec((ROWS, width), lambda i, *_: (steps - 1 - i, 0))
     back_mixed, back_out_gate, head_gain_part, collected = call(
@@ -633,7 +774,7 @@
         (steps,),
         [
             back_row_spec,
-            out_weight_spec,
+            fixed(out_weight),
             by_head(HV, True),
             by_head(HV, True),
             by_head(HK, True),
@@ -648,7 +789,7 @@
             shaped((heads, HV, HK)),
         ],
         [],
-        (back_attn, mixer, mixed, out_gate, qkv, cum, gain_head),
+        (back_attn, out_weight, mixed, out_gate, query, cum, gain_head),
         0,
         2 * rows * width * HV * heads,
         rows * heads * 4 * 1024,
@@ -662,23 +803,25 @@
         [
             back_row_spec,
             back_row_spec,
-            by_head(2 * HK + HV, True),
+            by_head(HK, True),
+            by_head(size, True),
             by_head(HK, True),
             by_head(HK, True),
             pl.BlockSpec((parts, heads, HV, HK), lambda i, *_: (steps - 1 - i, 0, 0, 0)),
             by_head(HV, True),
             by_head(HV, True),
             state_spec,
-            weight_spec,
-            rank_weight_spec,
-            decay_out_spec,
+            fixed(query_weight),
+            fixed(key_weight),
+            fixed(rank_weight),
+            fixed(decay_out_full),
             pl.BlockSpec((ROWS, ranks), lambda i, *_: (steps - 1 - i, 0)),
             gain_spec,
         ],
         [
             pl.BlockSpec((ROWS, grad_columns), lambda i, *_: (steps - 1 - i, 0)),
             back_row_spec,
-            decay_out_spec,
+            pl.BlockSpec((heads, ranks, HK), lambda i, *_: (0, 0, 0)),
             bias_spec,
             gain_spec,
         ],
@@ -689,19 +832,22 @@
             shaped((heads, 1, HK)),
             shaped((1, width)),
         ],
-        [pltpu.VMEM((heads, HV, HK), F32), pltpu.VMEM((heads, ROWS, columns), BF16)],
+        [
+            pltpu.VMEM((heads, HV, HK), F32),
+            pltpu.VMEM((ROWS, heads * size), BF16),
+            pltpu.VMEM((ROWS, heads * size), BF16),
+        ],
         (
-            own, tokens, back_middle, qkv, cum, logits, states, back_mixed, back_out_gate, back_end,
-            mixer, mixer, decay_out_full, rank, gain_one,
+            info, tokens, back_middle, query, kv, cum, logits, states, back_mixed, back_out_gate,
+            back_end, query_weight, key_weight, rank_weight, decay_out_full, rank, gain_one,
         ),
         1,
         2 * rows * width * columns * heads * 2,
         rows * heads * 4 * 2048,
     )
-    mixer_grad = dot(mixer_back, normed, TN)
-    mixer_share = lax.psum_scatter(mixer_grad, ("dp", "ctx"), scatter_dimension=1, tiled=True)
-    decay_out_own = lax.dynamic_index_in_dim(decay_out_grad, own[0], 0, keepdims=False)
-    bias_own = lax.dynamic_index_in_dim(bias_grad, own[0], 0, keepdims=False)
+    own = info[-1]
+    decay_out_own = lax.dynamic_index_in_dim(decay_out_grad, own, 0, keepdims=False)
+    bias_own = lax.dynamic_index_in_dim(bias_grad, own, 0, keepdims=False)
     sums = jnp.concatenate(
         [
             gain_one_part.reshape(-1),
@@ -711,19 +857,19 @@
             decay_out_own.reshape(-1),
         ]
     )
-    sums = total_over(sums, ("dp", "ctx"))
+    sums = total_over(sums)
+    mixer_share = scatter_rows(dot(normed, mixer_back, TN))
     gain_count = gains.shape[0]
     gains_grad = sums[:gain_count]
     bias_total = sums[gain_count : gain_count + HK]
     decay_out_total = sums[gain_count + HK :].reshape(ranks, HK)
 
-    query_key_share = jnp.stack([mixer_share[:HK].T, mixer_share[HK : 2 * HK].T])
-    value_gate_share = jnp.stack(
-        [mixer_share[2 * HK : 2 * HK + HV].T, mixer_share[2 * HK + HV : columns].T]
-    )
-    decay_in_share = mixer_share[columns:].T
-    gate_up_share = jnp.stack([ffn_share[:units].T, ffn_share[units : 2 * units].T])
-    down_share = ffn_share[2 * units :]
+    query_key_share = jnp.stack([mixer_share[:, :HK], mixer_share[:, size : size + HK]])
+    value_gate_share = jnp.stack([mixer_share[:, size + HK : columns], mixer_share[:, HK:size]])
+    decay_in_share = mixer_share[:, columns:]
+    gate_up_share = jnp.stack([early_share[:units].T, early_share[units : 2 * units].T])
+    down_share = early_share[2 * units : 3 * units]
+    output_share = early_share[3 * units :]
 
     updated = adamw(
         query_key_weight,

time: 663 us -> 533 us (0.80)
  local copies, waits for them, and re-layouts: 103 us -> 34.4 us
  waiting for transfers between devices: 128 us -> 68.2 us
  blocking collectives: 39.6 us -> 0 us
  starting transfers between devices: 4.13 us -> 39.7 us
    reshape x4 -> x1, local copies, waits for them, and re-layouts: 86 us -> 4.6 us  [scatter_rows(): value = value.reshape(2, 2, 2, -1, columns)]
    reduce_scatter x3 -> x1, waiting for transfers between devices: 67.4 us -> 0.01 us  [body(): lax.psum_scatter(early_grad, ('dp', 'ctx'), scatter_dimension=1, tiled=True)]
    ppermute x0 -> x24, waiting for transfers between devices: none -> 65.6 us  [the longest x18 50.9 us: swap(): lax.ppermute(value, axis, [(source, source ^ distance) for source in rang...]
    all_gather x2 -> x1, waiting for transfers between devices: 61 us -> 0.02 us  [gather_whole(): whole = lax.all_gather(pack, ('dp', 'ctx', 'tp'))]
    ppermute x0 -> x24, starting transfers between devices: none -> 35.8 us  [the longest x6 19.5 us: shift(): lax.ppermute(value, axis, [(source, (source + distance) % count) for sour...]
    psum x1 -> x0, blocking collectives: 24.9 us -> none  [total_over(): return lax.psum(value, axes)]
    all_gather x1 -> x0, blocking collectives: 14.7 us -> none  [body(): small_full = lax.all_gather(small, 'tp')]
    dynamic_slice x0 -> x7, local copies, waits for them, and re-layouts: none -> 8.1 us  [pick(): return lax.dynamic_index_in_dim(array, index, axis, keepdims=False)]
  transfers between devices with their start and end apart: 7 -> 28, of which waited for: 2 -> 13; matrix products, arithmetic and copies ran while one was open for 12% -> 11% of each run, Pallas kernels for 28% -> 40%
where the time goes in v2:
time: 533 us; the launch traced here: 525 us
  Pallas kernels  313 us (59%)
  waiting for transfers between devices  68.2 us (13%)
  starting transfers between devices  39.7 us (7%)
  local copies, waits for them, and re-layouts  34.4 us (6%)
  other arithmetic  31.2 us (6%)
  matrix products  22.5 us (4%)
  between operations  16.2 us (3%)
    pallas_call x5, Pallas kernels, call(): pl.pallas_call(kernel, grid_spec=pltpu.PrefetchScalarGridSpec(num_scalar_...  313 us
    ppermute x18, waiting for transfers between devices, swap(): lax.ppermute(value, axis, [(source, source ^ distance) for source in rang...  50.9 us
    dot_general x5, matrix products, dot(): return lax.dot_general(left, right, dims, preferred_element_type=F32)  22.5 us
    ppermute x6, starting transfers between devices, shift(): lax.ppermute(value, axis, [(source, (source + distance) % count) for sour...  19.5 us
    unnamed x121, local copies, waits for them, and re-layouts  17.5 us
    ppermute x18, starting transfers between devices, swap(): lax.ppermute(value, axis, [(source, source ^ distance) for source in rang...  16.3 us
    ppermute x6, waiting for transfers between devices, shift(): lax.ppermute(value, axis, [(source, (source + distance) % count) for sour...  14.7 us
  transfers between devices with their start and end apart: 28, of which 13 were waited for; matrix products, arithmetic and copies ran while one was open for 11% of the time, Pallas kernels for 40%

profile of v2, /device:TPU:0, one launch (start us, length us, event | category | flops | bytes accessed | tf_op | source)
XLA Modules:
  0.0 525.1 jit_solution(664931103013520362)
XLA Ops:
  7.3 1.3 convert.43
  8.6 1.0 convert_bitcast_fusion
  11.2 4.1 collective-permute-start.1
  15.3 1.3 collective-permute-start.2
  17.4 5.7 %collective-permute-done.1 = bf16[496,128]{1,0:T(8,128)(2,1)S(1)} collective-permute-done((bf16[496,128]{1,0:T(8,128)(2,1)S(1)}, bf16[496,128]{1,0:T(8,128)(2,1)S(1)}, u32[]{:S(2)}, u32[]{:S(2)}) %collective-permute-start.1) | collective-permute-done | bytes 127008 | tf_op jit(solution)/shard_map/ppermute | solution.py:456
  23.1 2.3 collective-permute-done
  25.5 1.6 collective-permute-start.3
  27.0 1.5 collective-permute-start.4
  28.6 8.0 %collective-permute-start.9 = (bf16[640,128]{1,0:T(8,128)(2,1)S(1)}, bf16[640,128]{1,0:T(8,128)(2,1)S(1)}, u32[]{:S(2)}, u32[]{:S(2)}) collective-permute-start(bf16[640,128]{1,0:T(8,128)(2,1)S(1)} %pad_maximum_fusion.8), channel_id=1, source_target_pairs={{0,1},{1,2},{2,3},{3,0},{4,5},{5,6},{6,7},{7,4},{8,9},{9,10},{10,1... | collective-permute-start | bytes 491528 | tf_op jit(solution)/shard_map/ppermute | solution.py:456
  36.6 2.6 collective-permute-start.10
  39.2 2.8 collective-permute-start.11
  43.0 6.7 %collective-permute-done.10 = bf16[640,128]{1,0:T(8,128)(2,1)S(1)} collective-permute-done((bf16[640,128]{1,0:T(8,128)(2,1)S(1)}, bf16[640,128]{1,0:T(8,128)(2,1)S(1)}, u32[]{:S(2)}, u32[]{:S(2)}) %collective-permute-start.10) | collective-permute-done | bytes 163872 | tf_op jit(solution)/shard_map/ppermute | solution.py:456
  50.4 1.2 collective-permute-start.12
  51.6 1.4 collective-permute-start.13
  53.1 1.5 pad_maximum_fusion.2.first
  54.6 25.9 %collective-permute-done.12 = bf16[4,640,128]{2,1,0:T(8,128)(2,1)S(1)} collective-permute-done((bf16[4,640,128]{2,1,0:T(8,128)(2,1)S(1)}, bf16[4,640,128]{2,1,0:T(8,128)(2,1)S(1)}, u32[]{:S(2)}, u32[]{:S(2)}) %collective-permute-start.12) | collective-permute-done | bytes 655392 | tf_op jit(solution)/shard_map/ppermute | solution.py:451
  80.6 1.3 collective-permute-start.14
  82.7 1.6 collective-permute-start.15
  85.6 2.6 collective-permute-done.14
  88.2 2.2 collective-permute-done.15
  90.5 1.4 pad_maximum_fusion.1.first
  94.1 35.7 %shard_map.509 = (bf16[2048,1024]{1,0:T(8,128)(2,1)}, f32[4,2048,384]{2,1,0:T(8,128)}, f32[2048,16]{1,0:T(8,128)}, f32[4,2048,128]{2,1,0:T(8,128)}, f32[4,2048,1...) custom-call(s32[21]{0:T(128)} %pad_add_fusion.info, ...), custom_call_target="tpu_custom_call" | custom-call | flops 6442450944 | bytes 33554432 | tf_op jit(solution)/shard_map/pallas_call | solution.py:415
  130.4 1.1 broadcast_add_fusion.1
  131.5 2.5 collective-permute-start.8
  134.1 3.8 broadcast_select_fusion.back
  138.7 64.0 %shard_map.510 = (f32[4,2048,128]{2,1,0:T(8,128)}, f32[4,2048,256]{2,1,0:T(8,128)}, f32[4,2048,256]{2,1,0:T(8,128)}, f32[16,4,256,128]{3,2,1,0:T(8,128)}, bf16[2...) custom-call(s32[21]{0:T(128)} %pad_add_fusion.info, ...), custom_call_target="tpu_custom_call" | custom-call | flops 15032385536 | bytes 33554432 | tf_op jit(solution)/shard_map/pallas_call | solution.py:415
  202.7 100.6 %shard_map.511 = (bf16[2048,704]{1,0:T(8,128)(2,1)}, bf16[2048,704]{1,0:T(8,128)(2,1)}, bf16[2048,704]{1,0:T(8,128)(2,1)}, bf16[2048,1024]{1,0:T(8,128)(2,1)}, f...) custom-call(s32[21]{0:T(128)} %pad_add_fusion.info, ...), custom_call_target="tpu_custom_call" | custom-call | flops 70866960384 | bytes 50331648 | tf_op jit(solution)/shard_map/pallas_call | solution.py:415
  303.4 6.2 %fusion.39 = f32[704,1024]{1,0:T(8,128)S(1)} fusion(bf16[2048,704]{1,0:T(8,128)(2,1)} %get-tuple-element.77, bf16[2048,1024]{1,0:T(8,128)(2,1)} %get-tuple-element.70.normed), kind=kOutput, calls=%fused_computation.129 | convolution fusion | flops 2952790016 | bytes 9961472 | tf_op jit(solution)/shard_map/dot_general | solution.py:43
  309.7 3.2 fusion.40
  312.9 3.2 fusion.41
  316.2 1.3 fusion.42
  317.5 4.3 pad_maximum_fusion
  321.8 28.8 %shard_map.512 = (f32[4,2048,256]{2,1,0:T(8,128)}, bf16[4,2048,256]{2,1,0:T(8,128)(2,1)}, f32[1,256]{1,0:T(1,128)}, f32[4,256,128]{2,1,0:T(8,128)}) custom-call(bf16[2048,1024]{1,0:T(8,128)(2,1)} %get-tuple-element.82.back_attn, bf16[1024,1024]{1,0:T(8,128)(2,1)} %get-tuple-element.83.out_weight, f32[4,2048,256]{2,1,0:T(8,128)} %get-tuple-element.84.mixed_in, ...), custom_call_target="tpu_custom_call" | custom-call | flops 4294967296 | bytes 33554432 | tf_op jit(solution)/shard_map/pallas_call | solution.py:415
  350.6 1.1 broadcast_add_fusion
  351.7 1.3 collective-permute-start.17
  353.0 2.5 collective-permute-done.17.back_end
  356.3 83.9 %shard_map.513 = (bf16[2048,784]{1,0:T(8,128)(2,1)}, f32[2048,1024]{1,0:T(8,128)}, f32[4,16,128]{2,1,0:T(8,128)}, f32[4,1,128]{2,1,0:T(1,128)}, f32[1,1024]{1,0:T(1,128)}) custom-call(s32[21]{0:T(128)} %pad_add_fusion.info, bf16[2048,1024]{1,0:T(8,128)(2,1)} %tokens.5, f32[2048,1024]{1,0:T(8,128)} %get-tuple-element.73.back_middle, ...), custom_call_target="tpu_custom_call" | custom-call | flops 25769803776 | bytes 67108864 | tf_op jit(solution)/shard_map/pallas_call | solution.py:415
  440.2 8.6 %fusion.43 = f32[1024,784]{0,1:T(8,128)} fusion(bf16[2048,1024]{1,0:T(8,128)(2,1)} %get-tuple-element.65.normed, bf16[2048,784]{1,0:T(8,128)(2,1)} %get-tuple-element.94), kind=kOutput, calls=%fused_computation.133 | convolution fusion | flops 3288334336 | bytes 10616832 | tf_op jit(solution)/shard_map/dot_general | solution.py:43
  448.7 4.6 reshape.216
  453.3 4.0 constant_dynamic-slice_fusion.6
  457.3 1.3 copy.209
  460.5 1.6 collective-permute-done.23
  462.1 1.8 collective-permute-start.24
  463.9 2.0 collective-permute-done.24
  465.9 1.4 collective-permute-start.25
  467.2 1.1 copy.190
  468.3 1.8 copy.191
  470.1 1.7 copy.176
  471.8 1.7 copy.187
  474.3 1.1 copy.180
  475.4 2.0 collective-permute-start.19
  478.0 1.0 constant_dynamic-slice_fusion.2
  479.0 1.4 copy.184
  482.2 5.0 collective-permute-done.19
  487.2 1.1 bitcast_add_fusion.1
  489.0 4.6 collective-permute-done.21
  494.9 5.2 collective-permute-done.20
  500.1 1.8 collective-permute-done.22
  501.9 1.0 add.256
  506.9 1.8 copy.194
  508.7 1.7 copy.195
  511.8 2.6 multiply_subtract_fusion.1
  514.4 1.7 multiply_subtract_fusion
  516.1 1.7 multiply_subtract_fusion.3
  (200 shorter events, 22.4 us)
Async XLA Ops:
  7.2 3.4 copy-start.22
  7.2 3.5 copy-start.27
  7.2 3.7 copy-start.30
  7.2 3.7 copy-start.36
  7.2 3.7 copy-start.25
  7.3 10.1 %copy-start.9 = (f32[256,128]{1,0:T(8,128)S(1)}, f32[256,128]{1,0:T(8,128)}, u32[]{:S(2)}) copy-start(f32[256,128]{1,0:T(8,128)} %param.48) | copy-start | bytes 393220
  7.3 195.4 %all-gather.2.cloned.1.call-start = ((), (), s32[]{:S(2)}) async-start(), calls=%async_computation.1 | async-start | bytes 17842176 | tf_op jit(solution)/shard_map/all_gather | solution.py:502
  10.5 501.3 %reduce-scatter.2.cloned.1.call-start = ((), (), s32[]{:S(2)}) async-start(), calls=%async_computation.2 | async-start | bytes 10911744 | tf_op jit(solution)/shard_map/reduce_scatter | solution.py:769
  10.7 42.3 %copy-start.5 = (f32[2,128,256]{1,2,0:T(8,128)}, f32[2,128,256]{1,2,0:T(8,128)S(1)}, u32[]{:S(2)}) copy-start(f32[2,128,256]{1,2,0:T(8,128)S(1)} %copy.170) | copy-start | bytes 786436
  10.8 38.9 %copy-start.12 = (f32[2,128,128]{1,2,0:T(8,128)}, f32[2,128,128]{1,2,0:T(8,128)S(1)}, u32[]{:S(2)}) copy-start(f32[2,128,128]{1,2,0:T(8,128)S(1)} %copy.169) | copy-start | bytes 393220
  11.2 11.9 %collective-permute-start.1 = (bf16[496,128]{1,0:T(8,128)(2,1)S(1)}, bf16[496,128]{1,0:T(8,128)(2,1)S(1)}, u32[]{:S(2)}, u32[]{:S(2)}) collective-permute-start(bf16[496,128]{1,0:T(8,128)(2,1)S(1)} %constant_dynamic-update-slice_fusion), channel_id=1, source_target_pairs={{0,2},{1,3},{2,0},{3,1},{4,6},{5,7},{6,4},{7,5},{8,10},{9,11},{10,... | collective-permute-start | bytes 380936 | tf_op jit(solution)/shard_map/ppermute | solution.py:456
  15.3 7.8 %collective-permute-start.2 = (bf16[496,128]{1,0:T(8,128)(2,1)S(1)}, bf16[496,128]{1,0:T(8,128)(2,1)S(1)}, u32[]{:S(2)}, u32[]{:S(2)}) collective-permute-start(bf16[496,128]{1,0:T(8,128)(2,1)S(1)} %constant_dynamic-update-slice_fusion), channel_id=1, source_target_pairs={{0,3},{1,0},{2,1},{3,2},{4,7},{5,4},{6,5},{7,6},{8,11},{9,8},{10,9... | collective-permute-start | bytes 380936 | tf_op jit(solution)/shard_map/ppermute | solution.py:456
  16.7 8.7 %collective-permute-start = (bf16[496,128]{1,0:T(8,128)(2,1)S(1)}, bf16[496,128]{1,0:T(8,128)(2,1)S(1)}, u32[]{:S(2)}, u32[]{:S(2)}) collective-permute-start(bf16[496,128]{1,0:T(8,128)(2,1)S(1)} %constant_dynamic-update-slice_fusion), channel_id=1, source_target_pairs={{0,1},{1,2},{2,3},{3,0},{4,5},{5,6},{6,7},{7,4},{8,9},{9,10},{10,1... | collective-permute-start | bytes 380936 | tf_op jit(solution)/shard_map/ppermute | solution.py:456
  25.5 16.6 %collective-permute-start.3 = (bf16[4,496,128]{2,1,0:T(8,128)(2,1)S(1)}, bf16[4,496,128]{2,1,0:T(8,128)(2,1)S(1)}, u32[]{:S(2)}, u32[]{:S(2)}) collective-permute-start(bf16[4,496,128]{2,1,0:T(8,128)(2,1)S(1)} %get-tuple-element.317), channel_id=1, source_target_pairs={{0,8},{8,0},{16,24},{24,16},{1,9},{9,1},{17,25},{25,17},{2,10},{10... | collective-permute-start | bytes 1523720 | tf_op jit(solution)/shard_map/ppermute | solution.py:451
  27.0 15.1 %collective-permute-start.4 = (bf16[4,496,128]{2,1,0:T(8,128)(2,1)S(1)}, bf16[4,496,128]{2,1,0:T(8,128)(2,1)S(1)}, u32[]{:S(2)}, u32[]{:S(2)}) collective-permute-start(bf16[4,496,128]{2,1,0:T(8,128)(2,1)S(1)} %get-tuple-element.317), channel_id=1, source_target_pairs={{0,16},{8,24},{16,0},{24,8},{1,17},{9,25},{17,1},{25,9},{2,18},{10... | collective-permute-start | bytes 1523720 | tf_op jit(solution)/shard_map/ppermute | solution.py:451
  28.6 14.4 %collective-permute-start.9 = (bf16[640,128]{1,0:T(8,128)(2,1)S(1)}, bf16[640,128]{1,0:T(8,128)(2,1)S(1)}, u32[]{:S(2)}, u32[]{:S(2)}) collective-permute-start(bf16[640,128]{1,0:T(8,128)(2,1)S(1)} %pad_maximum_fusion.8), channel_id=1, source_target_pairs={{0,1},{1,2},{2,3},{3,0},{4,5},{5,6},{6,7},{7,4},{8,9},{9,10},{10,1... | collective-permute-start | bytes 491528 | tf_op jit(solution)/shard_map/ppermute | solution.py:456
  36.6 13.1 %collective-permute-start.10 = (bf16[640,128]{1,0:T(8,128)(2,1)S(1)}, bf16[640,128]{1,0:T(8,128)(2,1)S(1)}, u32[]{:S(2)}, u32[]{:S(2)}) collective-permute-start(bf16[640,128]{1,0:T(8,128)(2,1)S(1)} %pad_maximum_fusion.8), channel_id=1, source_target_pairs={{0,2},{1,3},{2,0},{3,1},{4,6},{5,7},{6,4},{7,5},{8,10},{9,11},{10,... | collective-permute-start | bytes 491528 | tf_op jit(solution)/shard_map/ppermute | solution.py:456
  39.2 10.5 %collective-permute-start.11 = (bf16[640,128]{1,0:T(8,128)(2,1)S(1)}, bf16[640,128]{1,0:T(8,128)(2,1)S(1)}, u32[]{:S(2)}, u32[]{:S(2)}) collective-permute-start(bf16[640,128]{1,0:T(8,128)(2,1)S(1)} %pad_maximum_fusion.8), channel_id=1, source_target_pairs={{0,3},{1,0},{2,1},{3,2},{4,7},{5,4},{6,5},{7,6},{8,11},{9,8},{10,9... | collective-permute-start | bytes 491528 | tf_op jit(solution)/shard_map/ppermute | solution.py:456
  42.1 10.9 %collective-permute-start.5 = (bf16[2,496,128]{2,1,0:T(8,128)(2,1)S(1)}, bf16[2,496,128]{2,1,0:T(8,128)(2,1)S(1)}, u32[]{:S(2)}, u32[]{:S(2)}) collective-permute-start(bf16[2,496,128]{2,1,0:T(8,128)(2,1)S(1)} %slice.141), channel_id=1, source_target_pairs={{0,16},{8,24},{16,0},{24,8},{1,17},{9,25},{17,1},{25,9},{2,18},{10... | collective-permute-start | bytes 761864 | tf_op jit(solution)/shard_map/ppermute | solution.py:451
  42.2 10.8 %collective-permute-start.6 = (bf16[2,496,128]{2,1,0:T(8,128)(2,1)S(1)}, bf16[2,496,128]{2,1,0:T(8,128)(2,1)S(1)}, u32[]{:S(2)}, u32[]{:S(2)}) collective-permute-start(bf16[2,496,128]{2,1,0:T(8,128)(2,1)S(1)} %slice.142), channel_id=1, source_target_pairs={{0,8},{8,0},{16,24},{24,16},{1,9},{9,1},{17,25},{25,17},{2,10},{10... | collective-permute-start | bytes 761864 | tf_op jit(solution)/shard_map/ppermute | solution.py:451
  43.0 6.8 %copy-start.18 = (bf16[1,256,128]{2,1,0:T(8,128)(2,1)}, bf16[1,256,128]{2,1,0:T(8,128)(2,1)S(1)}, u32[]{:S(2)}) copy-start(bf16[1,256,128]{2,1,0:T(8,128)(2,1)S(1)} %convert_bitcast_fusion.1) | copy-start | bytes 196612
  50.4 30.2 %collective-permute-start.12 = (bf16[4,640,128]{2,1,0:T(8,128)(2,1)S(1)}, bf16[4,640,128]{2,1,0:T(8,128)(2,1)S(1)}, u32[]{:S(2)}, u32[]{:S(2)}) collective-permute-start(bf16[4,640,128]{2,1,0:T(8,128)(2,1)S(1)} %pad_maximum_fusion.4), channel_id=1, source_target_pairs={{0,8},{8,0},{16,24},{24,16},{1,9},{9,1},{17,25},{25,17},{2,10},{10... | collective-permute-start | bytes 1966088 | tf_op jit(solution)/shard_map/ppermute | solution.py:451
  51.6 30.3 %collective-permute-start.13 = (bf16[4,640,128]{2,1,0:T(8,128)(2,1)S(1)}, bf16[4,640,128]{2,1,0:T(8,128)(2,1)S(1)}, u32[]{:S(2)}, u32[]{:S(2)}) collective-permute-start(bf16[4,640,128]{2,1,0:T(8,128)(2,1)S(1)} %pad_maximum_fusion.4), channel_id=1, source_target_pairs={{0,16},{8,24},{16,0},{24,8},{1,17},{9,25},{17,1},{25,9},{2,18},{10... | collective-permute-start | bytes 1966088 | tf_op jit(solution)/shard_map/ppermute | solution.py:451
  53.0 31.2 %copy-start.28 = (f32[2304]{0:T(1024)S(1)}, f32[2304]{0:T(1024)}, u32[]{:S(2)}) copy-start(f32[2304]{0:T(1024)} %param.57) | copy-start | bytes 27652
  53.0 32.4 %copy-start.17 = (bf16[640,128]{1,0:T(8,128)(2,1)S(1)}, bf16[640,128]{1,0:T(8,128)(2,1)}, u32[]{:S(2)}) copy-start(bf16[640,128]{1,0:T(8,128)(2,1)} %copy-done.16) | copy-start | bytes 491524
  53.1 32.4 %copy-start.19 = (bf16[1,256,128]{2,1,0:T(8,128)(2,1)S(1)}, bf16[1,256,128]{2,1,0:T(8,128)(2,1)}, u32[]{:S(2)}) copy-start(bf16[1,256,128]{2,1,0:T(8,128)(2,1)} %copy-done.18) | copy-start | bytes 196612
  54.6 39.5 %collective-permute-start.7 = (bf16[4,4,496,128]{3,2,1,0:T(8,128)(2,1)}, bf16[4,4,496,128]{3,2,1,0:T(8,128)(2,1)}, u32[]{:S(2)}, u32[]{:S(2)}) collective-permute-start(bf16[4,4,496,128]{3,2,1,0:T(8,128)(2,1)} %pad_maximum_fusion.2.first), channel_id=1, source_target_pairs={{0,4},{4,0},{1,5},{5,1},{2,6},{6,2},{3,7},{7,3},{8,12},{12,8},{9,1... | collective-permute-start | bytes 6094856 | tf_op jit(solution)/shard_map/ppermute | solution.py:451
  80.6 7.6 %collective-permute-start.14 = (bf16[2,640,128]{2,1,0:T(8,128)(2,1)S(1)}, bf16[2,640,128]{2,1,0:T(8,128)(2,1)S(1)}, u32[]{:S(2)}, u32[]{:S(2)}) collective-permute-start(bf16[2,640,128]{2,1,0:T(8,128)(2,1)S(1)} %slice.149), channel_id=1, source_target_pairs={{0,16},{8,24},{16,0},{24,8},{1,17},{9,25},{17,1},{25,9},{2,18},{10... | collective-permute-start | bytes 983048 | tf_op jit(solution)/shard_map/ppermute | solution.py:451
  81.9 8.6 %copy-start.7 = (bf16[4,640,128]{2,1,0:T(8,128)(2,1)}, bf16[4,640,128]{2,1,0:T(8,128)(2,1)S(1)}, u32[]{:S(2)}) copy-start(bf16[4,640,128]{2,1,0:T(8,128)(2,1)S(1)} %collective-permute-done.13) | copy-start | bytes 1966084
  82.7 7.7 %collective-permute-start.15 = (bf16[2,640,128]{2,1,0:T(8,128)(2,1)}, bf16[2,640,128]{2,1,0:T(8,128)(2,1)S(1)}, u32[]{:S(2)}, u32[]{:S(2)}) collective-permute-start(bf16[2,640,128]{2,1,0:T(8,128)(2,1)} %slice.150), channel_id=1, source_target_pairs={{0,8},{8,0},{16,24},{24,16},{1,9},{9,1},{17,25},{25,17},{2,10},{10... | collective-permute-start | bytes 983048 | tf_op jit(solution)/shard_map/ppermute | solution.py:451
  91.9 37.8 %copy-start.4 = (bf16[4,4,640,128]{3,2,1,0:T(8,128)(2,1)}, bf16[4,4,640,128]{3,2,1,0:T(8,128)(2,1)S(1)}, u32[]{:S(2)}) copy-start(bf16[4,4,640,128]{3,2,1,0:T(8,128)(2,1)S(1)} %pad_maximum_fusion.1.first) | copy-start | bytes 7864324
  91.9 46.0 %collective-permute-start.16 = (bf16[4,4,640,128]{3,2,1,0:T(8,128)(2,1)S(1)}, bf16[4,4,640,128]{3,2,1,0:T(8,128)(2,1)}, u32[]{:S(2)}, u32[]{:S(2)}) collective-permute-start(bf16[4,4,640,128]{3,2,1,0:T(8,128)(2,1)S(1)} %pad_maximum_fusion.1.first), channel_id=1, source_target_pairs={{0,4},{4,0},{1,5},{5,1},{2,6},{6,2},{3,7},{7,3},{8,12},{12,8},{9,1... | collective-permute-start | bytes 7864328 | tf_op jit(solution)/shard_map/ppermute | solution.py:451
  131.5 6.3 %collective-permute-start.8 = (f32[4,256,128]{2,1,0:T(8,128)S(1)}, f32[4,256,128]{2,1,0:T(8,128)S(1)}, u32[]{:S(2)}, u32[]{:S(2)}) collective-permute-start(f32[4,256,128]{2,1,0:T(8,128)S(1)} %broadcast_add_fusion.1), channel_id=1, source_target_pairs={{0,4},{1,5},{2,6},{3,7},{8,12},{9,13},{10,14},{11,15},{16,20},{17,... | collective-permute-start | bytes 1572872 | tf_op jit(solution)/shard_map/ppermute | solution.py:435
  303.4 6.3 %copy-start.48 = (bf16[2048,1024]{1,0:T(8,128)(2,1)S(1)}, bf16[2048,1024]{1,0:T(8,128)(2,1)}, u32[]{:S(2)}) copy-start(bf16[2048,1024]{1,0:T(8,128)(2,1)} %get-tuple-element.70.normed) | copy-start | bytes 12582916
  303.4 6.3 %copy-start.50 = (bf16[2048,704]{1,0:T(8,128)(2,1)S(1)}, bf16[2048,704]{1,0:T(8,128)(2,1)}, u32[]{:S(2)}) copy-start(bf16[2048,704]{1,0:T(8,128)(2,1)} %get-tuple-element.78) | copy-start | bytes 8650756
  309.6 3.3 copy-start.2
  309.7 3.3 copy-start.49
  312.9 3.3 copy-start.1
  312.9 3.3 copy-start.47
  351.7 3.8 collective-permute-start.17
  457.3 16.1 %copy-start = (f32[2,2,1,128,784]{3,2,1,0,4:T(1,128)S(1)}, f32[2,2,1,128,784]{3,2,1,0,4:T(1,128)}, u32[]{:S(2)}) copy-start(f32[2,2,1,128,784]{3,2,1,0,4:T(1,128)} %get-tuple-element.302) | copy-start | bytes 4816900
  458.6 14.8 %collective-permute-start.18 = (f32[2,2,128,784]{2,3,1,0:T(8,128)}, f32[2,2,128,784]{2,3,1,0:T(8,128)S(1)}, u32[]{:S(2)}, u32[]{:S(2)}) collective-permute-start(f32[2,2,128,784]{2,3,1,0:T(8,128)} %bitcast.156), channel_id=1, source_target_pairs={{0,4},{4,0},{1,5},{5,1},{2,6},{6,2},{3,7},{7,3},{8,12},{12,8},{9,1... | collective-permute-start | bytes 4816904 | tf_op jit(solution)/shard_map/ppermute | solution.py:451
  460.1 1.9 collective-permute-start.23
  462.1 3.8 collective-permute-start.24
  465.9 7.5 %collective-permute-start.25 = (f32[4480]{0:T(1024)S(1)}, f32[4480]{0:T(1024)S(1)}, u32[]{:S(2)}, u32[]{:S(2)}) collective-permute-start(f32[4480]{0:T(1024)S(1)} %add.274), channel_id=1, source_target_pairs={{0,16},{8,24},{16,0},{24,8},{1,17},{9,25},{17,1},{25,9},{2,18},{10... | collective-permute-start | bytes 53768 | tf_op jit(solution)/shard_map/ppermute | solution.py:451
  474.3 6.7 %copy-start.26 = (f32[16,128]{1,0:T(8,128)S(1)}, f32[16,128]{1,0:T(8,128)}, u32[]{:S(2)}) copy-start(f32[16,128]{1,0:T(8,128)} %param.42) | copy-start | bytes 24580
  474.3 6.7 %copy-start.34 = (f32[16,128]{1,0:T(8,128)S(1)}, f32[16,128]{1,0:T(8,128)}, u32[]{:S(2)}) copy-start(f32[16,128]{1,0:T(8,128)} %param.44) | copy-start | bytes 24580
  474.3 6.7 %copy-start.35 = (f32[16,128]{1,0:T(8,128)S(1)}, f32[16,128]{1,0:T(8,128)}, u32[]{:S(2)}) copy-start(f32[16,128]{1,0:T(8,128)} %param.43) | copy-start | bytes 24580
  475.4 11.8 %collective-permute-start.19 = (f32[2,64,784]{2,1,0:T(8,128)}, f32[2,64,784]{2,1,0:T(8,128)}, u32[]{:S(2)}, u32[]{:S(2)}) collective-permute-start(f32[2,64,784]{2,1,0:T(8,128)} %bitcast.169), channel_id=1, source_target_pairs={{0,8},{8,0},{16,24},{24,16},{1,9},{9,1},{17,25},{25,17},{2,10},{10... | collective-permute-start | bytes 1204232 | tf_op jit(solution)/shard_map/ppermute | solution.py:451
  480.4 13.1 %collective-permute-start.21 = (f32[2,64,784]{2,1,0:T(8,128)S(1)}, f32[2,64,784]{2,1,0:T(8,128)S(1)}, u32[]{:S(2)}, u32[]{:S(2)}) collective-permute-start(f32[2,64,784]{2,1,0:T(8,128)S(1)} %bitcast.168), channel_id=1, source_target_pairs={{0,16},{8,24},{16,0},{24,8},{1,17},{9,25},{17,1},{25,9},{2,18},{10... | collective-permute-start | bytes 1204232 | tf_op jit(solution)/shard_map/ppermute | solution.py:451
  482.2 11.8 %copy-start.37 = (f32[128]{0:T(128)S(1)}, f32[128]{0:T(128)}, u32[]{:S(2)}) copy-start(f32[128]{0:T(128)} %param.45) | copy-start | bytes 1540
  482.2 11.8 %copy-start.43 = (f32[128]{0:T(128)S(1)}, f32[128]{0:T(128)}, u32[]{:S(2)}) copy-start(f32[128]{0:T(128)} %param.47) | copy-start | bytes 1540
  482.2 11.8 %copy-start.44 = (f32[128]{0:T(128)S(1)}, f32[128]{0:T(128)}, u32[]{:S(2)}) copy-start(f32[128]{0:T(128)} %param.46) | copy-start | bytes 1540
  488.5 11.6 %collective-permute-start.20 = (f32[64,784]{0,1:T(8,128)S(1)}, f32[64,784]{0,1:T(8,128)S(1)}, u32[]{:S(2)}, u32[]{:S(2)}) collective-permute-start(f32[64,784]{0,1:T(8,128)S(1)} %copy.181), channel_id=1, source_target_pairs={{0,16},{8,24},{16,0},{24,8},{1,17},{9,25},{17,1},{25,9},{2,18},{10... | collective-permute-start | bytes 602120 | tf_op jit(solution)/shard_map/ppermute | solution.py:451
  493.7 9.5 %copy-start.6 = (f32[2,128,256]{1,2,0:T(8,128)S(1)}, f32[2,128,256]{1,2,0:T(8,128)}, u32[]{:S(2)}) copy-start(f32[2,128,256]{1,2,0:T(8,128)} %copy-done.5) | copy-start | bytes 786436
  493.7 9.5 %copy-start.11 = (f32[2,128,256]{1,2,0:T(8,128)S(1)}, f32[2,128,256]{1,2,0:T(8,128)}, u32[]{:S(2)}) copy-start(f32[2,128,256]{1,2,0:T(8,128)} %copy.191) | copy-start | bytes 786436
  493.9 8.0 %collective-permute-start.22 = (f32[64,784]{0,1:T(8,128)S(1)}, f32[64,784]{0,1:T(8,128)}, u32[]{:S(2)}, u32[]{:S(2)}) collective-permute-start(f32[64,784]{0,1:T(8,128)S(1)} %copy.185), channel_id=1, source_target_pairs={{0,8},{8,0},{16,24},{24,16},{1,9},{9,1},{17,25},{25,17},{2,10},{10... | collective-permute-start | bytes 602120 | tf_op jit(solution)/shard_map/ppermute | solution.py:451
  503.1 7.9 %copy-start.31 = (f32[128,16]{0,1:T(8,128)S(1)}, f32[128,16]{0,1:T(8,128)}, u32[]{:S(2)}) copy-start(f32[128,16]{0,1:T(8,128)} %param.39) | copy-start | bytes 24580
  503.2 7.9 %copy-start.38 = (f32[128,16]{0,1:T(8,128)S(1)}, f32[128,16]{0,1:T(8,128)}, u32[]{:S(2)}) copy-start(f32[128,16]{0,1:T(8,128)} %param.41) | copy-start | bytes 24580
  503.2 7.9 %copy-start.39 = (f32[128,16]{0,1:T(8,128)S(1)}, f32[128,16]{0,1:T(8,128)}, u32[]{:S(2)}) copy-start(f32[128,16]{0,1:T(8,128)} %param.40) | copy-start | bytes 24580
  503.4 8.4 %copy-start.8 = (f32[704,128]{1,0:T(8,128)S(1)}, f32[704,128]{1,0:T(8,128)}, u32[]{:S(2)}) copy-start(f32[704,128]{1,0:T(8,128)} %param.54) | copy-start | bytes 1081348
  506.9 7.5 %copy-start.3 = (f32[2,128,704]{1,2,0:T(8,128)S(1)}, f32[2,128,704]{1,2,0:T(8,128)}, u32[]{:S(2)}) copy-start(f32[2,128,704]{1,2,0:T(8,128)} %param.51) | copy-start | bytes 2162692
  506.9 7.5 %copy-start.14 = (f32[2,128,704]{1,2,0:T(8,128)S(1)}, f32[2,128,704]{1,2,0:T(8,128)}, u32[]{:S(2)}) copy-start(f32[2,128,704]{1,2,0:T(8,128)} %param.53) | copy-start | bytes 2162692
  506.9 7.5 %copy-start.15 = (f32[2,128,704]{1,2,0:T(8,128)S(1)}, f32[2,128,704]{1,2,0:T(8,128)}, u32[]{:S(2)}) copy-start(f32[2,128,704]{1,2,0:T(8,128)} %param.52) | copy-start | bytes 2162692
  (15 other events, 30.7 us)
Sparse Core Ops, SparseCore 0:
  11.5 141.9 all-gather.1
  321.9 82.6 reduce-scatter.1

commit v3 on v2

--- a/solution.py
+++ b/solution.py
@@ -128,33 +128,40 @@
     rank_out[...] = rank
     lower = as_ones(lower_mask())
     made = dot(normed, weight[...], NT)
-    for head in range(heads):
+    every = range(heads)
+    keys = [made[:, head * size : head * size + HK] for head in every]
+    values = [made[:, head * size + HK : (head + 1) * size] for head in every]
+    logits = []
+    for head in every:
         slot = info[2 * GROUPS + head]
-        keys = made[:, head * size : head * size + HK]
-        values = made[:, head * size + HK : (head + 1) * size]
-        kv_out[head, :, :HK] = keys
-        kv_out[head, :, HK:] = values
-        logits = (
+        logits.append(
             lax.dot_general(
                 rank, decay_out[slot, :ranks], NN, precision=lax.Precision.HIGHEST,
                 preferred_element_type=F32,
             )
             + decay_out[slot, ranks : ranks + 1]
         )
-        logits_out[head] = logits
-        log_decay = (
-            jnp.minimum(logits, 0.0) - jnp.log1p(jnp.exp(-jnp.abs(logits)))
-        ) / GATE_SCALE
-        state = state_out[head]
-        for part in range(ROWS // BLOCK):
-            span = slice(part * BLOCK, (part + 1) * BLOCK)
-            cum = dot_exact(lower, log_decay[span])
-            cum_out[head, span] = cum
-            total = cum[BLOCK - 1 :]
-            carried = split_two(keys[span] * jnp.exp(total - cum))
-            state = state * jnp.exp(total) + dot_split(split_two(values[span]), carried, TN)
-            total_out[head] += total
-        state_out[head] = state
+    for head in every:
+        kv_out[head, :, :HK] = keys[head]
+        kv_out[head, :, HK:] = values[head]
+        logits_out[head] = logits[head]
+    log_decay = [
+        (jnp.minimum(item, 0.0) - jnp.log1p(jnp.exp(-jnp.abs(item)))) / GATE_SCALE
+        for item in logits
+    ]
+    for part in range(ROWS // BLOCK):
+        span = slice(part * BLOCK, (part + 1) * BLOCK)
+        cum = [dot_exact(lower, log_decay[head][span]) for head in every]
+        total = [item[BLOCK - 1 :] for item in cum]
+        carried = [
+            split_two(keys[head][span] * jnp.exp(total[head] - cum[head])) for head in every
+        ]
+        value_parts = [split_two(values[head][span]) for head in every]
+        added = [dot_split(value_parts[head], carried[head], TN) for head in every]
+        for head in every:
+            cum_out[head, span] = cum[head]
+            state_out[head] = state_out[head] * jnp.exp(total[head]) + added[head]
+            total_out[head] += total[head]
 
 
 def mix_kernel(
@@ -172,37 +179,45 @@
 
     made = dot(normed[...], weight[...], NT)
     causal = lower_mask()
+    every = range(heads)
     for part in range(ROWS // BLOCK):
         span = slice(part * BLOCK, (part + 1) * BLOCK)
-        for head in range(heads):
-            query = made[span, head * size : head * size + HK] * HK ** (-0.5)
-            out_gate = made[span, head * size + HK : (head + 1) * size]
-            query_out[head, span] = query
-            gate_out[head, span] = out_gate
-            keys = kv[head, span, :HK]
-            values = split_two(kv[head, span, HK:])
-            cum = cum_in[head, span]
-            center = cum[MID : MID + 1]
-            total = cum[BLOCK - 1 :]
-            query_mid = split_two(query * jnp.exp(cum - center))
-            key_mid = split_two(keys * jnp.exp(center - cum))
-            scores = split_two(jnp.where(causal, dot_split(query_mid, key_mid, NT), 0.0))
-            state = state_ref[head]
-            state_out[part, head] = state
-            mixed = dot_split(scores, values) + dot_split(
-                split_two(query * jnp.exp(cum)), split_two(state), NT
-            )
-            carried = split_two(keys * jnp.exp(total - cum))
-            state_ref[head] = state * jnp.exp(total) + dot_split(values, carried, TN)
-            mixed_out[head, span] = mixed
-            gated = (
-                mixed * inverse_rms(mixed, HEAD_EPS) * head_gain[...] * (out_gate * sigmoid(out_gate))
+        query = [made[span, head * size : head * size + HK] * HK ** (-0.5) for head in every]
+        out_gate = [made[span, head * size + HK : (head + 1) * size] for head in every]
+        keys = [kv[head, span, :HK] for head in every]
+        cum = [cum_in[head, span] for head in every]
+        center = [item[MID : MID + 1] for item in cum]
+        total = [item[BLOCK - 1 :] for item in cum]
+        query_mid = [split_two(query[head] * jnp.exp(cum[head] - center[head])) for head in every]
+        key_mid = [split_two(keys[head] * jnp.exp(center[head] - cum[head])) for head in every]
+        scores = [dot_split(query_mid[head], key_mid[head], NT) for head in every]
+        since = [split_two(query[head] * jnp.exp(cum[head])) for head in every]
+        states = [state_ref[head] for head in every]
+        carried = [split_two(keys[head] * jnp.exp(total[head] - cum[head])) for head in every]
+        values = [split_two(kv[head, span, HK:]) for head in every]
+        outer = [dot_split(since[head], split_two(states[head]), NT) for head in every]
+        added = [dot_split(values[head], carried[head], TN) for head in every]
+        scores = [split_two(jnp.where(causal, item, 0.0)) for item in scores]
+        mixed = [dot_split(scores[head], values[head]) + outer[head] for head in every]
+        for head in every:
+            query_out[head, span] = query[head]
+            gate_out[head, span] = out_gate[head]
+            state_out[part, head] = states[head]
+            state_ref[head] = states[head] * jnp.exp(total[head]) + added[head]
+            mixed_out[head, span] = mixed[head]
+        for head in every:
+            gated_ref[span, head * HV : (head + 1) * HV] = (
+                mixed[head]
+                * inverse_rms(mixed[head], HEAD_EPS)
+                * head_gain[...]
+                * (out_gate[head] * sigmoid(out_gate[head]))
             ).astype(BF16)
-            gated_ref[span, head * HV : (head + 1) * HV] = gated
-
-            @pl.when(info[2 * GROUPS + heads] == head)
-            def _():
-                gated_out[span] = gated
+
+    for head in every:
+
+        @pl.when(info[2 * GROUPS + heads] == head)
+        def _():
+            gated_out[...] = gated_ref[:, head * HV : (head + 1) * HV]
 
     middle = tokens[...].astype(F32) + dot(gated_ref[...], out_weight[...])
     middle_out[...] = middle
@@ -212,7 +227,7 @@
 def ffn_kernel(
     weight_pieces, info, normed, back, middle, weight, gain,
     active_out, back_gate_out, back_up_out, layer_out, back_middle_out, back_attn_out, gain_out,
-    ffn_ref, back_ref,
+    ffn_ref, back_ref, active_ref, back_gate_ref, back_up_ref,
 ):
     step, piece = pl.program_id(0), pl.program_id(1)
     units = weight.shape[2] // 3
@@ -252,12 +267,15 @@
         keep = jnp.where(piece > 0, 1.0, 0.0)
         ffn_ref[span] = ffn_ref[span] * keep + ffn
         back_ref[span] = back_ref[span] * keep + back_normed
-
-        @pl.when(piece == info[2 * GROUPS + weight_pieces])
-        def _():
-            active_out[span] = active
-            back_gate_out[span] = back_gate
-            back_up_out[span] = back_up
+        active_ref[span] = active
+        back_gate_ref[span] = back_gate
+        back_up_ref[span] = back_up
+
+    @pl.when(piece == info[2 * GROUPS + weight_pieces])
+    def _():
+        active_out[...] = active_ref[...]
+        back_gate_out[...] = back_gate_ref[...]
+        back_up_out[...] = back_up_ref[...]
 
     @pl.when(piece == pl.num_programs(1) - 1)
     def _():
@@ -286,8 +304,13 @@
         gain_out[...] = jnp.zeros_like(gain_out)
         state_out[...] = jnp.zeros_like(state_out)
 
-    for head in range(heads):
-        back_gated = dot(back_attn[...], out_weight[head * HV : (head + 1) * HV], NT)
+    every = range(heads)
+    back_gated = [
+        dot(back_attn[...], out_weight[head * HV : (head + 1) * HV], NT) for head in every
+    ]
+    scaled = [query_in[head] * jnp.exp(cum_in[head]) for head in every]
+    back_mixed = []
+    for head in every:
         mixed = mixed_in[head]
         out_gate = gate[head]
         inverse = inverse_rms(mixed, HEAD_EPS)
@@ -295,29 +318,29 @@
         share = sigmoid(out_gate)
         silu = out_gate * share
         slope = share * (1.0 + out_gate * (1.0 - share))
-        back_gate_out[head] = (back_gated * unit * head_gain[...] * slope).astype(BF16)
-        gain_out[...] += jnp.sum(back_gated * unit * silu, axis=0, keepdims=True)
-        weighted = back_gated * head_gain[...] * silu
-        back_mixed = inverse * (
-            weighted - unit * jnp.mean(weighted * unit, axis=-1, keepdims=True)
-        )
-        back_mixed_out[head] = back_mixed
-        state = state_out[head]
-        for part in reversed(range(ROWS // BLOCK)):
-            span = slice(part * BLOCK, (part + 1) * BLOCK)
-            cum = cum_in[head, span]
-            scaled = split_two(query_in[head, span] * jnp.exp(cum))
-            state = state * jnp.exp(cum[BLOCK - 1 :]) + dot_split(
-                split_two(back_mixed[span]), scaled, TN
-            )
-        state_out[head] = state
+        shaped_back = back_gated[head] * unit
+        back_gate_out[head] = (shaped_back * head_gain[...] * slope).astype(BF16)
+        gain_out[...] += jnp.sum(shaped_back * silu, axis=0, keepdims=True)
+        weighted = back_gated[head] * head_gain[...] * silu
+        item = inverse * (weighted - unit * jnp.mean(weighted * unit, axis=-1, keepdims=True))
+        back_mixed_out[head] = item
+        back_mixed.append(item)
+    for part in reversed(range(ROWS // BLOCK)):
+        span = slice(part * BLOCK, (part + 1) * BLOCK)
+        added = [
+            dot_split(split_two(back_mixed[head][span]), split_two(scaled[head][span]), TN)
+            for head in every
+        ]
+        for head in every:
+            last = cum_in[head, (part + 1) * BLOCK - 1 : (part + 1) * BLOCK]
+            state_out[head] = state_out[head] * jnp.exp(last) + added[head]
 
 
 def mix_back_kernel(
-    info, tokens, back_middle, query_in, kv, cum_in, logits_in, states, back_mixed, back_gate,
+    homes, info, tokens, back_middle, query_in, kv, cum_in, logits_in, states, back_mixed, back_gate,
     back_end, query_weight, key_weight, rank_weight, decay_out, rank, gain,
     grad_out, input_out, decay_grad_out, bias_out, gain_out,
-    state_ref, query_ref, key_ref,
+    state_ref, query_ref, key_ref, grad_ref,
 ):
     heads = back_end.shape[0]
     size = HK + HV
@@ -326,80 +349,108 @@
     @pl.when(pl.program_id(0) == 0)
     def _():
         state_ref[...] = back_end[...]
+        grad_out[...] = jnp.zeros_like(grad_out)
         decay_grad_out[...] = jnp.zeros_like(decay_grad_out)
         bias_out[...] = jnp.zeros_like(bias_out)
         gain_out[...] = jnp.zeros_like(gain_out)
 
     causal = lower_mask()
     upper = as_ones(upper_mask())
+    every = range(heads)
     for part in reversed(range(ROWS // BLOCK)):
         span = slice(part * BLOCK, (part + 1) * BLOCK)
-        rank_back = jnp.zeros((BLOCK, rank.shape[1]), F32)
-        for head in range(heads):
+        query = [query_in[head, span] for head in every]
+        keys = [kv[head, span, :HK] for head in every]
+        cum = [cum_in[head, span] for head in every]
+        center = [item[MID : MID + 1] for item in cum]
+        total = [item[BLOCK - 1 :] for item in cum]
+        grow = [jnp.exp(cum[head] - center[head]) for head in every]
+        shrink = [jnp.exp(center[head] - cum[head]) for head in every]
+        query_mid = [split_two(query[head] * grow[head]) for head in every]
+        key_mid = [split_two(keys[head] * shrink[head]) for head in every]
+        values = [split_two(kv[head, span, HK:]) for head in every]
+        back = [split_two(back_mixed[head, span]) for head in every]
+        scores = [dot_split(query_mid[head], key_mid[head], NT) for head in every]
+        back_scores = [dot_split(back[head], values[head], NT) for head in every]
+        since = [jnp.exp(cum[head]) for head in every]
+        until = [jnp.exp(total[head] - cum[head]) for head in every]
+        carried = [keys[head] * until[head] for head in every]
+        back_state = [state_ref[head] for head in every]
+        back_state_parts = [split_two(item) for item in back_state]
+        back_carried = [dot_split(values[head], back_state_parts[head]) for head in every]
+        back_since = [dot_split(back[head], split_two(states[part, head])) for head in every]
+        added = [
+            dot_split(back[head], split_two(query[head] * since[head]), TN) for head in every
+        ]
+        outer = [
+            dot_split(split_two(carried[head]), back_state_parts[head], NT) for head in every
+        ]
+        scores = [split_two(jnp.where(causal, item, 0.0)) for item in scores]
+        back_scores = [split_two(jnp.where(causal, item, 0.0)) for item in back_scores]
+        back_query = [
+            dot_split(back_scores[head], key_mid[head]) * grow[head]
+            + back_since[head] * since[head]
+            for head in every
+        ]
+        back_keys = [
+            dot_split(back_scores[head], query_mid[head], TN) * shrink[head]
+            + back_carried[head] * until[head]
+            for head in every
+        ]
+        back_values = [dot_split(scores[head], back[head], TN) + outer[head] for head in every]
+        back_total = []
+        for head in every:
+            decayed = back_state[head] * jnp.exp(total[head])
+            back_total.append(
+                jnp.sum(back_carried[head] * carried[head], axis=0, keepdims=True)
+                + jnp.sum(decayed * states[part, head], axis=0, keepdims=True)
+            )
+            state_ref[head] = decayed + added[head]
+        back_logits = [
+            (
+                dot_exact(upper, query[head] * back_query[head] - keys[head] * back_keys[head])
+                + back_total[head]
+            )
+            * sigmoid(-logits_in[head, span])
+            / GATE_SCALE
+            for head in every
+        ]
+        rank_parts = split_two(rank[span])
+        rank_back = jnp.zeros((BLOCK, ranks), F32)
+        for head in every:
             slot = info[2 * GROUPS + head]
-            query = query_in[head, span]
-            keys = kv[head, span, :HK]
-            values = split_two(kv[head, span, HK:])
-            cum = cum_in[head, span]
-            center = cum[MID : MID + 1]
-            total = cum[BLOCK - 1 :]
-            grow, shrink = jnp.exp(cum - center), jnp.exp(center - cum)
-            since, until = jnp.exp(cum), jnp.exp(total - cum)
-            query_mid, key_mid = split_two(query * grow), split_two(keys * shrink)
-            carried = keys * until
-            carried_split = split_two(carried)
-            back = split_two(back_mixed[head, span])
-            scores = split_two(jnp.where(causal, dot_split(query_mid, key_mid, NT), 0.0))
-            back_scores = split_two(jnp.where(causal, dot_split(back, values, NT), 0.0))
-            state = states[part, head]
-            back_state = state_ref[head]
-            back_state_split = split_two(back_state)
-            back_values = dot_split(scores, back, TN) + dot_split(
-                carried_split, back_state_split, NT
-            )
-            back_query = (
-                dot_split(back_scores, key_mid) * grow
-                + dot_split(back, split_two(state)) * since
-            )
-            back_carried = dot_split(values, back_state_split)
-            back_keys = dot_split(back_scores, query_mid, TN) * shrink + back_carried * until
-            decayed = back_state * jnp.exp(total)
-            back_total = jnp.sum(back_carried * carried, axis=0, keepdims=True) + jnp.sum(
-                decayed * state, axis=0, keepdims=True
-            )
-            state_ref[head] = decayed + dot_split(back, split_two(query * since), TN)
-            back_decay = (
-                dot_exact(upper, query * back_query - keys * back_keys) + back_total
-            )
-            back_logits = back_decay * sigmoid(-logits_in[head, span]) / GATE_SCALE
-            bias_out[head] += jnp.sum(back_logits, axis=0, keepdims=True)
             rank_back += lax.dot_general(
-                back_logits, decay_out[slot, :ranks], NT, precision=lax.Precision.HIGHEST,
+                back_logits[head], decay_out[slot, :ranks], NT, precision=lax.Precision.HIGHEST,
                 preferred_element_type=F32,
             )
-            decay_grad_out[head] += dot_split(split_two(rank[span]), split_two(back_logits), TN)
+            bias_out[head] += jnp.sum(back_logits[head], axis=0, keepdims=True)
+            decay_grad_out[head] += dot_split(rank_parts, split_two(back_logits[head]), TN)
             at = head * size
-            query_ref[span, at : at + HK] = (back_query * HK ** (-0.5)).astype(BF16)
+            query_ref[span, at : at + HK] = (back_query[head] * HK ** (-0.5)).astype(BF16)
             query_ref[span, at + HK : at + size] = back_gate[head, span]
-            key_ref[span, at : at + HK] = back_keys.astype(BF16)
-            key_ref[span, at + HK : at + size] = back_values.astype(BF16)
-        grad_out[span, 2 * size :] = rank_back.astype(BF16)
+            key_ref[span, at : at + HK] = back_keys[head].astype(BF16)
+            key_ref[span, at + HK : at + size] = back_values[head].astype(BF16)
+        grad_ref[span, 2 * size :] = rank_back.astype(BF16)
+
+    for head in every:
+
+        @pl.when(info[2 * GROUPS + heads] == head)
+        def _():
+            grad_ref[:, :size] = query_ref[:, head * size : (head + 1) * size]
+            grad_ref[:, size : 2 * size] = key_ref[:, head * size : (head + 1) * size]
 
     back_normed = (
-        dot(grad_out[:, 2 * size :], rank_weight[...])
+        dot(grad_ref[:, 2 * size :], rank_weight[...])
         + dot(query_ref[...], query_weight[...])
         + dot(key_ref[...], key_weight[...])
     )
-    for head in range(heads):
-
-        @pl.when(info[2 * GROUPS + heads] == head)
-        def _():
-            grad_out[:, :size] = query_ref[:, head * size : (head + 1) * size]
-            grad_out[:, size : 2 * size] = key_ref[:, head * size : (head + 1) * size]
-
     inputs = tokens[...].astype(F32)
     inverse = inverse_rms(inputs, NORM_EPS)
     unit = inputs * inverse
+    normed = (unit * gain[...]).astype(BF16)
+    weight_grad = dot(normed, grad_ref[...], TN)
+    for group in range(GROUPS):
+        grad_out[info[group], homes[group]] += weight_grad[group * LANES : (group + 1) * LANES]
     weighted = back_normed * gain[...]
     input_out[...] = back_middle[...] + inverse * (
         weighted - unit * jnp.mean(weighted * unit, axis=-1, keepdims=True)
@@ -464,22 +515,40 @@
     return whole.reshape(whole.shape[0], rows, GROUPS, LANES).transpose(2, 0, 1, 3)
 
 
-def gather_slots(pack):
+def gather_line(pack):
     count = lax.axis_size("tp")
-    line = jnp.stack([pack] + [shift(pack, "tp", distance) for distance in range(1, count)])
-    across, beyond = swap(line, "dp", 1), swap(line, "dp", 2)
-    half = count // 2
-    far = jnp.concatenate([swap(across[:half], "dp", 2), swap(beyond[half:], "dp", 1)])
-    first = jnp.stack([line, across, beyond, far])
-    return first, swap(first, "ctx", 1)
+    return jnp.stack([pack] + [shift(pack, "tp", distance) for distance in range(1, count)])
+
+
+def gather_square(line):
+    return jnp.stack([line] + [swap(line, "dp", distance) for distance in range(1, 4)])
+
+
+def gather_slots(key_pack, query_pack):
+    key_line = gather_line(key_pack)
+    query_pack, key_line = lax.optimization_barrier((query_pack, key_line))
+    key_first = gather_square(key_line)
+    query_line = gather_line(query_pack)
+    query_line, key_first = lax.optimization_barrier((query_line, key_first))
+    query_first = gather_square(query_line)
+    return (
+        key_first,
+        swap(key_first, "ctx", 1),
+        query_first,
+        swap(query_first, "ctx", 1),
+    )
 
 
 def gather_pair(pack):
-    if staged():
-        return gather_slots(pack)
     whole = gather_plain(pack)
     half = GROUPS // 2
     return whole[:half], whole[half:]
+
+
+def gather_homes():
+    if staged():
+        return [group // 2 for group in range(GROUPS)]
+    return [group % (GROUPS // 2) for group in range(GROUPS)]
 
 
 def gather_info():
@@ -505,18 +574,19 @@
 
 
 def scatter_rows(value):
+    columns = value.shape[-1]
     if not staged():
-        return lax.psum_scatter(value, ("dp", "ctx"), scatter_dimension=0, tiled=True)
-    device, core = lax.axis_index("dp"), lax.axis_index("ctx")
+        return lax.psum_scatter(
+            value.reshape(-1, columns), ("dp", "ctx"), scatter_dimension=0, tiled=True
+        )
+    device = lax.axis_index("dp")
     row, column = device // 2, device % 2
 
     def pick(array, axis, index):
         return lax.dynamic_index_in_dim(array, index, axis, keepdims=False)
 
-    columns = value.shape[1]
-    value = value.reshape(2, 2, 2, -1, columns)
-    value = pick(value, 2, core) + swap(pick(value, 2, 1 - core), "ctx", 1)
-    half = value.shape[2] // 2
+    value = (value[0] + swap(value[1], "ctx", 1)).reshape(2, 2, LANES, columns)
+    half = LANES // 2
     upper, lower = value[:, :, :half], value[:, :, half:]
     upper = pick(upper, 1, column) + swap(pick(upper, 1, 1 - column), "dp", 1)
     lower = pick(lower, 0, row) + swap(pick(lower, 0, 1 - row), "dp", 2)
@@ -607,18 +677,19 @@
         value_gate_weight[0].T.astype(BF16),
         decay_in_weight.T.astype(BF16),
     ]
+    query_pack = jnp.concatenate(
+        [query_key_weight[0].T, value_gate_weight[1].T, output_weight]
+    ).astype(BF16)
     if staged():
-        key_first, key_second = gather_pair(jnp.concatenate(key_parts + three_parts(small)))
+        key_first, key_second, query_first, query_second = gather_slots(
+            jnp.concatenate(key_parts + three_parts(small)), query_pack
+        )
         sent = key_first[0, :, size + ranks :].astype(F32).reshape(heads, 3, DECAY_ROWS, HK)
         decay_out_full = sent[:, 0] + sent[:, 1] + sent[:, 2]
     else:
         key_first, key_second = gather_pair(jnp.concatenate(key_parts))
+        query_first, query_second = gather_pair(query_pack)
         decay_out_full = lax.all_gather(small, "tp")
-    query_first, query_second = gather_pair(
-        jnp.concatenate(
-            [query_key_weight[0].T, value_gate_weight[1].T, output_weight]
-        ).astype(BF16)
-    )
     ffn = gather_whole(
         jnp.concatenate([gate_up_weight[0].T, gate_up_weight[1].T, down_weight]).astype(BF16)
     )
@@ -751,7 +822,13 @@
             shaped((rows, width), BF16),
             shaped((1, width)),
         ],
-        [pltpu.VMEM((FFN_ROWS, width), F32), pltpu.VMEM((FFN_ROWS, width), F32)],
+        [
+            pltpu.VMEM((FFN_ROWS, width), F32),
+            pltpu.VMEM((FFN_ROWS, width), F32),
+            pltpu.VMEM((FFN_ROWS, units), BF16),
+            pltpu.VMEM((FFN_ROWS, units), BF16),
+            pltpu.VMEM((FFN_ROWS, units), BF16),
+        ],
         (info, normed_two, back_ffn, middle, ffn, gain_two),
         1,
         12 * rows * width * units * heads,
@@ -797,8 +874,9 @@
     back_end = carry(collected, device_decay, -1)
 
     grad_columns = columns + ranks
+    grad_shape = shaped((2, GROUPS // 2, LANES, grad_columns))
     mixer_back, input_grad, decay_out_grad, bias_grad, gain_one_part = call(
-        mix_back_kernel,
+        functools.partial(mix_back_kernel, gather_homes()),
         (steps,),
         [
             back_row_spec,
@@ -819,14 +897,14 @@
             gain_spec,
         ],
         [
-            pl.BlockSpec((ROWS, grad_columns), lambda i, *_: (steps - 1 - i, 0)),
+            fixed(grad_shape),
             back_row_spec,
             pl.BlockSpec((heads, ranks, HK), lambda i, *_: (0, 0, 0)),
             bias_spec,
             gain_spec,
         ],
         [
-            shaped((rows, grad_columns), BF16),
+            grad_shape,
             shaped((rows, width)),
             shaped((heads, ranks, HK)),
             shaped((heads, 1, HK)),
@@ -836,6 +914,7 @@
             pltpu.VMEM((heads, HV, HK), F32),
             pltpu.VMEM((ROWS, heads * size), BF16),
             pltpu.VMEM((ROWS, heads * size), BF16),
+            pltpu.VMEM((ROWS, grad_columns), BF16),
         ],
         (
             info, tokens, back_middle, query, kv, cum, logits, states, back_mixed, back_out_gate,
@@ -858,7 +937,7 @@
         ]
     )
     sums = total_over(sums)
-    mixer_share = scatter_rows(dot(normed, mixer_back, TN))
+    mixer_share = scatter_rows(mixer_back)
     gain_count = gains.shape[0]
     gains_grad = sums[:gain_count]
     bias_total = sums[gain_count : gain_count + HK]

time: 533 us -> 475 us (0.89)
  Pallas kernels: 313 us -> 262 us
  waiting for transfers between devices: 68.2 us -> 80.4 us
  local copies, waits for them, and re-layouts: 34.4 us -> 25.2 us
  matrix products: 22.5 us -> 13.8 us
    pallas_call x5, Pallas kernels: 313 us -> 262 us  [call(): pl.pallas_call(kernel, grid_spec=pltpu.PrefetchScalarGridSpec(num_scalar_...]
    dot_general x5 -> x4, matrix products: 22.5 us -> 13.8 us  [dot(): return lax.dot_general(left, right, dims, preferred_element_type=F32)]
    dynamic_slice x7 -> x0, local copies, waits for them, and re-layouts: 8.1 us -> none  [pick(): return lax.dynamic_index_in_dim(array, index, axis, keepdims=False)]
    ppermute x18 -> x16, waiting for transfers between devices: 50.9 us -> 58.4 us  [swap(): lax.ppermute(value, axis, [(source, source ^ distance) for source in rang...]
    ppermute x18 -> x16, starting transfers between devices: 16.3 us -> 15.1 us  [swap(): lax.ppermute(value, axis, [(source, source ^ distance) for source in rang...]
    unnamed x121 -> x104, local copies, waits for them, and re-layouts: 17.5 us -> 16.9 us
  transfers between devices with their start and end apart: 28 -> 26, of which waited for: 13 -> 14; matrix products, arithmetic and copies ran while one was open for 11% -> 9% of each run, Pallas kernels for 40% -> 35%
where the time goes in v3:
time: 475 us; the launch traced here: 469 us
  Pallas kernels  262 us (55%)
  waiting for transfers between devices  80.4 us (17%)
  starting transfers between devices  36.4 us (8%)
  other arithmetic  34.8 us (7%)
  local copies, waits for them, and re-layouts  25.2 us (5%)
  between operations  16.1 us (3%)
  matrix products  13.8 us (3%)
    pallas_call x5, Pallas kernels, call(): pl.pallas_call(kernel, grid_spec=pltpu.PrefetchScalarGridSpec(num_scalar_...  262 us
    ppermute x16, waiting for transfers between devices, swap(): lax.ppermute(value, axis, [(source, source ^ distance) for source in rang...  58.4 us
    ppermute x6, waiting for transfers between devices, shift(): lax.ppermute(value, axis, [(source, (source + distance) % count) for sour...  19.4 us
    ppermute x6, starting transfers between devices, shift(): lax.ppermute(value, axis, [(source, (source + distance) % count) for sour...  17.4 us
    unnamed x104, local copies, waits for them, and re-layouts  16.9 us
    ppermute x16, starting transfers between devices, swap(): lax.ppermute(value, axis, [(source, source ^ distance) for source in rang...  15.1 us
    dot_general x4, matrix products, dot(): return lax.dot_general(left, right, dims, preferred_element_type=F32)  13.8 us
    sub x9, other arithmetic, adamw(): weight_now - rate_value * (mean_hat / (jnp.sqrt(square_hat) + ADAM_EPS) +...  10.6 us
  transfers between devices with their start and end apart: 26, of which 14 were waited for; matrix products, arithmetic and copies ran while one was open for 9% of the time, Pallas kernels for 35%

profile of v3, /device:TPU:0, one launch (start us, length us, event | category | flops | bytes accessed | tf_op | source)
XLA Modules:
  0.0 468.8 jit_solution(9504538618781133267)
XLA Ops:
  7.3 1.3 convert.37
  8.6 1.0 convert_bitcast_fusion
  11.3 3.0 collective-permute-start
  14.3 2.6 collective-permute-start.1
  16.9 1.3 collective-permute-start.2
  18.3 2.4 collective-permute-done
  20.7 4.6 collective-permute-done.1
  25.4 1.6 collective-permute-start.6
  26.9 1.5 collective-permute-start.7
  28.9 6.0 %collective-permute-start.3 = (bf16[640,128]{1,0:T(8,128)(2,1)S(1)}, bf16[640,128]{1,0:T(8,128)(2,1)S(1)}, u32[]{:S(2)}, u32[]{:S(2)}) collective-permute-start(bf16[640,128]{1,0:T(8,128)(2,1)S(1)} %pad_maximum_fusion.8), channel_id=1, source_target_pairs={{0,1},{1,2},{2,3},{3,0},{4,5},{5,6},{6,7},{7,4},{8,9},{9,10},{10,1... | collective-permute-start | bytes 491528 | tf_op jit(solution)/shard_map/ppermute | solution.py:507
  34.9 4.2 collective-permute-start.4
  39.1 5.7 %collective-permute-done.3 = bf16[640,128]{1,0:T(8,128)(2,1)S(1)} collective-permute-done((bf16[640,128]{1,0:T(8,128)(2,1)S(1)}, bf16[640,128]{1,0:T(8,128)(2,1)S(1)}, u32[]{:S(2)}, u32[]{:S(2)}) %collective-permute-start.3) | collective-permute-done | bytes 163872 | tf_op jit(solution)/shard_map/ppermute | solution.py:507
  45.1 5.4 %collective-permute-done.4 = bf16[640,128]{1,0:T(8,128)(2,1)S(1)} collective-permute-done((bf16[640,128]{1,0:T(8,128)(2,1)S(1)}, bf16[640,128]{1,0:T(8,128)(2,1)S(1)}, u32[]{:S(2)}, u32[]{:S(2)}) %collective-permute-start.4) | collective-permute-done | bytes 163872 | tf_op jit(solution)/shard_map/ppermute | solution.py:507
  50.5 1.3 collective-permute-done.5
  52.1 1.5 pad_maximum_fusion.2.first
  53.6 1.4 collective-permute-start.11
  55.0 1.5 collective-permute-start.12
  58.3 26.2 %collective-permute-done.11 = bf16[4,640,128]{2,1,0:T(8,128)(2,1)} collective-permute-done((bf16[4,640,128]{2,1,0:T(8,128)(2,1)S(1)}, bf16[4,640,128]{2,1,0:T(8,128)(2,1)}, u32[]{:S(2)}, u32[]{:S(2)}) %collective-permute-start.11) | collective-permute-done | bytes 655392 | tf_op jit(solution)/shard_map/ppermute | solution.py:502
  84.5 14.7 %collective-permute-done.13 = bf16[4,640,128]{2,1,0:T(8,128)(2,1)S(1)} collective-permute-done((bf16[4,640,128]{2,1,0:T(8,128)(2,1)S(1)}, bf16[4,640,128]{2,1,0:T(8,128)(2,1)S(1)}, u32[]{:S(2)}, u32[]{:S(2)}) %collective-permute-start.13) | collective-permute-done | bytes 655392 | tf_op jit(solution)/shard_map/ppermute | solution.py:502
  100.0 2.3 pad_maximum_fusion.1.first
  103.8 0.9 slice.108
  105.4 28.8 %shard_map.509 = (bf16[2048,1024]{1,0:T(8,128)(2,1)}, f32[4,2048,384]{2,1,0:T(8,128)}, f32[2048,16]{1,0:T(8,128)}, f32[4,2048,128]{2,1,0:T(8,128)}, f32[4,2048,1...) custom-call(s32[21]{0:T(128)} %pad_add_fusion.info, ...), custom_call_target="tpu_custom_call" | custom-call | flops 6442450944 | bytes 33554432 | tf_op jit(solution)/shard_map/pallas_call | solution.py:466
  134.9 1.1 broadcast_add_fusion.1
  136.0 2.6 collective-permute-start.10
  138.6 4.0 broadcast_select_fusion.back
  143.3 40.4 %shard_map.510 = (f32[4,2048,128]{2,1,0:T(8,128)}, f32[4,2048,256]{2,1,0:T(8,128)}, f32[4,2048,256]{2,1,0:T(8,128)}, f32[16,4,256,128]{3,2,1,0:T(8,128)}, bf16[2...) custom-call(s32[21]{0:T(128)} %pad_add_fusion.info, ...), custom_call_target="tpu_custom_call" | custom-call | flops 15032385536 | bytes 33554432 | tf_op jit(solution)/shard_map/pallas_call | solution.py:466
  183.8 99.7 %shard_map.511 = (bf16[2048,704]{1,0:T(8,128)(2,1)}, bf16[2048,704]{1,0:T(8,128)(2,1)}, bf16[2048,704]{1,0:T(8,128)(2,1)}, bf16[2048,1024]{1,0:T(8,128)(2,1)}, f...) custom-call(s32[21]{0:T(128)} %pad_add_fusion.info, ...), custom_call_target="tpu_custom_call" | custom-call | flops 70866960384 | bytes 50331648 | tf_op jit(solution)/shard_map/pallas_call | solution.py:466
  283.5 6.1 %fusion.31 = f32[704,1024]{1,0:T(8,128)S(1)} fusion(bf16[2048,704]{1,0:T(8,128)(2,1)} %get-tuple-element.85, bf16[2048,1024]{1,0:T(8,128)(2,1)} %get-tuple-element.78.normed), kind=kOutput, calls=%fused_computation.115 | convolution fusion | flops 2952790016 | bytes 9961472 | tf_op jit(solution)/shard_map/dot_general | solution.py:43
  289.6 3.2 fusion.32
  292.9 3.2 fusion.33
  296.1 1.3 fusion.34
  297.4 4.3 pad_maximum_fusion
  301.8 23.5 %shard_map.512 = (f32[4,2048,256]{2,1,0:T(8,128)}, bf16[4,2048,256]{2,1,0:T(8,128)(2,1)}, f32[1,256]{1,0:T(1,128)}, f32[4,256,128]{2,1,0:T(8,128)}) custom-call(bf16[2048,1024]{1,0:T(8,128)(2,1)} %get-tuple-element.90.back_attn, bf16[1024,1024]{1,0:T(8,128)(2,1)} %get-tuple-element.91.out_weight, f32[4,2048,256]{2,1,0:T(8,128)} %get-tuple-element.92.mixed_in, ...), custom_call_target="tpu_custom_call" | custom-call | flops 4294967296 | bytes 33554432 | tf_op jit(solution)/shard_map/pallas_call | solution.py:466
  325.2 1.1 broadcast_add_fusion
  326.3 1.3 collective-permute-start.15
  327.6 2.5 collective-permute-done.15.back_end
  330.9 69.8 %shard_map.513 = (f32[2,4,128,784]{3,2,1,0:T(8,128)}, f32[2048,1024]{1,0:T(8,128)}, f32[4,16,128]{2,1,0:T(8,128)}, f32[4,1,128]{2,1,0:T(1,128)}, f32[1,1024]{1,0:T(1,128)}) custom-call(s32[21]{0:T(128)} %pad_add_fusion.info, bf16[2048,1024]{1,0:T(8,128)(2,1)} %tokens.5, f32[2048,1024]{1,0:T(8,128)} %get-tuple-element.81.back_middle, ...), custom_call_target="tpu_custom_call" | custom-call | flops 25769803776 | bytes 67108864 | tf_op jit(solution)/shard_map/pallas_call | solution.py:466
  400.7 1.6 slice_bitcast_fusion
  405.1 1.6 collective-permute-done.21
  406.7 1.4 collective-permute-start.22
  408.1 2.4 collective-permute-done.22
  410.5 1.4 collective-permute-start.23
  411.9 1.1 copy.145
  413.0 1.1 copy.146
  414.1 1.7 copy.134
  415.7 1.7 copy.142
  417.4 2.1 copy.136
  419.5 1.7 bitcast_add_fusion
  422.6 1.6 collective-permute-start.19
  424.9 7.8 %collective-permute-done.17 = f32[2,64,784]{2,1,0:T(8,128)S(1)} collective-permute-done((f32[2,64,784]{2,1,0:T(8,128)S(1)}, f32[2,64,784]{2,1,0:T(8,128)S(1)}, u32[]{:S(2)}, u32[]{:S(2)}) %collective-permute-start.17) | collective-permute-done | bytes 401440 | tf_op jit(solution)/shard_map/ppermute | solution.py:502
  434.5 2.2 collective-permute-start.20
  437.5 5.1 %collective-permute-done.18 = f32[64,784]{0,1:T(8,128)} collective-permute-done((f32[64,784]{0,1:T(8,128)S(1)}, f32[64,784]{0,1:T(8,128)}, u32[]{:S(2)}, u32[]{:S(2)}) %collective-permute-start.18) | collective-permute-done | bytes 200736 | tf_op jit(solution)/shard_map/ppermute | solution.py:502
  442.6 1.1 add.244
  443.7 1.1 add.246
  445.2 0.8 copy.152
  446.0 0.8 copy.153
  446.9 0.8 copy.154
  447.9 1.9 multiply_subtract_fusion.4
  449.8 1.7 copy.149
  451.4 1.7 copy.150
  453.1 1.7 copy.151
  455.5 2.6 multiply_subtract_fusion.1
  458.1 1.7 multiply_subtract_fusion
  459.8 1.7 multiply_subtract_fusion.3
  (169 shorter events, 17.7 us)
Async XLA Ops:
  7.2 3.4 copy-start.14
  7.2 3.5 copy-start.19
  7.2 3.8 copy-start.22
  7.2 3.8 copy-start.28
  7.2 3.8 copy-start.17
  7.3 11.0 %copy-start.12 = (f32[256,128]{1,0:T(8,128)S(1)}, f32[256,128]{1,0:T(8,128)}, u32[]{:S(2)}) copy-start(f32[256,128]{1,0:T(8,128)} %param.48) | copy-start | bytes 393220
  7.3 176.5 %all-gather.2.cloned.1.call-start = ((), (), s32[]{:S(2)}) async-start(), calls=%async_computation.1 | async-start | bytes 17842176 | tf_op jit(solution)/shard_map/all_gather | solution.py:571
  10.5 444.9 %reduce-scatter.2.cloned.1.call-start = ((), (), s32[]{:S(2)}) async-start(), calls=%async_computation.2 | async-start | bytes 10911744 | tf_op jit(solution)/shard_map/reduce_scatter | solution.py:846
  10.7 41.1 %copy-start.4 = (f32[2,128,256]{1,2,0:T(8,128)}, f32[2,128,256]{1,2,0:T(8,128)S(1)}, u32[]{:S(2)}) copy-start(f32[2,128,256]{1,2,0:T(8,128)S(1)} %copy.130) | copy-start | bytes 786436
  10.9 41.0 %copy-start.7 = (f32[2,128,128]{1,2,0:T(8,128)}, f32[2,128,128]{1,2,0:T(8,128)S(1)}, u32[]{:S(2)}) copy-start(f32[2,128,128]{1,2,0:T(8,128)S(1)} %copy.129) | copy-start | bytes 393220
  11.3 9.4 %collective-permute-start = (bf16[496,128]{1,0:T(8,128)(2,1)S(1)}, bf16[496,128]{1,0:T(8,128)(2,1)S(1)}, u32[]{:S(2)}, u32[]{:S(2)}) collective-permute-start(bf16[496,128]{1,0:T(8,128)(2,1)S(1)} %constant_dynamic-update-slice_fusion), channel_id=1, source_target_pairs={{0,1},{1,2},{2,3},{3,0},{4,5},{5,6},{6,7},{7,4},{8,9},{9,10},{10,1... | collective-permute-start | bytes 380936 | tf_op jit(solution)/shard_map/ppermute | solution.py:507
  14.3 11.0 %collective-permute-start.1 = (bf16[496,128]{1,0:T(8,128)(2,1)S(1)}, bf16[496,128]{1,0:T(8,128)(2,1)S(1)}, u32[]{:S(2)}, u32[]{:S(2)}) collective-permute-start(bf16[496,128]{1,0:T(8,128)(2,1)S(1)} %constant_dynamic-update-slice_fusion), channel_id=1, source_target_pairs={{0,2},{1,3},{2,0},{3,1},{4,6},{5,7},{6,4},{7,5},{8,10},{9,11},{10,... | collective-permute-start | bytes 380936 | tf_op jit(solution)/shard_map/ppermute | solution.py:507
  16.9 8.4 %collective-permute-start.2 = (bf16[496,128]{1,0:T(8,128)(2,1)S(1)}, bf16[496,128]{1,0:T(8,128)(2,1)S(1)}, u32[]{:S(2)}, u32[]{:S(2)}) collective-permute-start(bf16[496,128]{1,0:T(8,128)(2,1)S(1)} %constant_dynamic-update-slice_fusion), channel_id=1, source_target_pairs={{0,3},{1,0},{2,1},{3,2},{4,7},{5,4},{6,5},{7,6},{8,11},{9,8},{10,9... | collective-permute-start | bytes 380936 | tf_op jit(solution)/shard_map/ppermute | solution.py:507
  25.3 31.8 %copy-start.20 = (f32[2304]{0:T(1024)S(1)}, f32[2304]{0:T(1024)}, u32[]{:S(2)}) copy-start(f32[2304]{0:T(1024)} %param.57) | copy-start | bytes 27652
  25.4 26.5 %collective-permute-start.6 = (bf16[4,496,128]{2,1,0:T(8,128)(2,1)S(1)}, bf16[4,496,128]{2,1,0:T(8,128)(2,1)S(1)}, u32[]{:S(2)}, u32[]{:S(2)}) collective-permute-start(bf16[4,496,128]{2,1,0:T(8,128)(2,1)S(1)} %pad_maximum_fusion.6), channel_id=1, source_target_pairs={{0,8},{8,0},{16,24},{24,16},{1,9},{9,1},{17,25},{25,17},{2,10},{10... | collective-permute-start | bytes 1523720 | tf_op jit(solution)/shard_map/ppermute | solution.py:502
  26.9 25.0 %collective-permute-start.7 = (bf16[4,496,128]{2,1,0:T(8,128)(2,1)S(1)}, bf16[4,496,128]{2,1,0:T(8,128)(2,1)S(1)}, u32[]{:S(2)}, u32[]{:S(2)}) collective-permute-start(bf16[4,496,128]{2,1,0:T(8,128)(2,1)S(1)} %pad_maximum_fusion.6), channel_id=1, source_target_pairs={{0,16},{8,24},{16,0},{24,8},{1,17},{9,25},{17,1},{25,9},{2,18},{10... | collective-permute-start | bytes 1523720 | tf_op jit(solution)/shard_map/ppermute | solution.py:502
  28.5 23.6 %collective-permute-start.8 = (bf16[4,496,128]{2,1,0:T(8,128)(2,1)S(1)}, bf16[4,496,128]{2,1,0:T(8,128)(2,1)S(1)}, u32[]{:S(2)}, u32[]{:S(2)}) collective-permute-start(bf16[4,496,128]{2,1,0:T(8,128)(2,1)S(1)} %pad_maximum_fusion.6), channel_id=1, source_target_pairs={{0,24},{8,16},{16,8},{24,0},{1,25},{9,17},{17,9},{25,1},{2,26},{10... | collective-permute-start | bytes 1523720 | tf_op jit(solution)/shard_map/ppermute | solution.py:502
  28.9 15.9 %collective-permute-start.3 = (bf16[640,128]{1,0:T(8,128)(2,1)S(1)}, bf16[640,128]{1,0:T(8,128)(2,1)S(1)}, u32[]{:S(2)}, u32[]{:S(2)}) collective-permute-start(bf16[640,128]{1,0:T(8,128)(2,1)S(1)} %pad_maximum_fusion.8), channel_id=1, source_target_pairs={{0,1},{1,2},{2,3},{3,0},{4,5},{5,6},{6,7},{7,4},{8,9},{9,10},{10,1... | collective-permute-start | bytes 491528 | tf_op jit(solution)/shard_map/ppermute | solution.py:507
  34.9 15.6 %collective-permute-start.4 = (bf16[640,128]{1,0:T(8,128)(2,1)S(1)}, bf16[640,128]{1,0:T(8,128)(2,1)S(1)}, u32[]{:S(2)}, u32[]{:S(2)}) collective-permute-start(bf16[640,128]{1,0:T(8,128)(2,1)S(1)} %pad_maximum_fusion.8), channel_id=1, source_target_pairs={{0,2},{1,3},{2,0},{3,1},{4,6},{5,7},{6,4},{7,5},{8,10},{9,11},{10,... | collective-permute-start | bytes 491528 | tf_op jit(solution)/shard_map/ppermute | solution.py:507
  44.9 6.9 %collective-permute-start.5 = (bf16[640,128]{1,0:T(8,128)(2,1)S(1)}, bf16[640,128]{1,0:T(8,128)(2,1)S(1)}, u32[]{:S(2)}, u32[]{:S(2)}) collective-permute-start(bf16[640,128]{1,0:T(8,128)(2,1)S(1)} %pad_maximum_fusion.8), channel_id=1, source_target_pairs={{0,3},{1,0},{2,1},{3,2},{4,7},{5,4},{6,5},{7,6},{8,11},{9,8},{10,9... | collective-permute-start | bytes 491528 | tf_op jit(solution)/shard_map/ppermute | solution.py:507
  53.6 51.8 %collective-permute-start.9 = (bf16[4,4,496,128]{3,2,1,0:T(8,128)(2,1)}, bf16[4,4,496,128]{3,2,1,0:T(8,128)(2,1)}, u32[]{:S(2)}, u32[]{:S(2)}) collective-permute-start(bf16[4,4,496,128]{3,2,1,0:T(8,128)(2,1)} %pad_maximum_fusion.2.first), channel_id=1, source_target_pairs={{0,4},{4,0},{1,5},{5,1},{2,6},{6,2},{3,7},{7,3},{8,12},{12,8},{9,1... | collective-permute-start | bytes 6094856 | tf_op jit(solution)/shard_map/ppermute | solution.py:502
  53.6 30.9 %collective-permute-start.11 = (bf16[4,640,128]{2,1,0:T(8,128)(2,1)S(1)}, bf16[4,640,128]{2,1,0:T(8,128)(2,1)}, u32[]{:S(2)}, u32[]{:S(2)}) collective-permute-start(bf16[4,640,128]{2,1,0:T(8,128)(2,1)S(1)} %pad_maximum_fusion.4), channel_id=1, source_target_pairs={{0,8},{8,0},{16,24},{24,16},{1,9},{9,1},{17,25},{25,17},{2,10},{10... | collective-permute-start | bytes 1966088 | tf_op jit(solution)/shard_map/ppermute | solution.py:502
  55.0 29.5 %collective-permute-start.12 = (bf16[4,640,128]{2,1,0:T(8,128)(2,1)S(1)}, bf16[4,640,128]{2,1,0:T(8,128)(2,1)}, u32[]{:S(2)}, u32[]{:S(2)}) collective-permute-start(bf16[4,640,128]{2,1,0:T(8,128)(2,1)S(1)} %pad_maximum_fusion.4), channel_id=1, source_target_pairs={{0,16},{8,24},{16,0},{24,8},{1,17},{9,25},{17,1},{25,9},{2,18},{10... | collective-permute-start | bytes 1966088 | tf_op jit(solution)/shard_map/ppermute | solution.py:502
  56.5 42.7 %collective-permute-start.13 = (bf16[4,640,128]{2,1,0:T(8,128)(2,1)S(1)}, bf16[4,640,128]{2,1,0:T(8,128)(2,1)S(1)}, u32[]{:S(2)}, u32[]{:S(2)}) collective-permute-start(bf16[4,640,128]{2,1,0:T(8,128)(2,1)S(1)} %pad_maximum_fusion.4), channel_id=1, source_target_pairs={{0,24},{8,16},{16,8},{24,0},{1,25},{9,17},{17,9},{25,1},{2,26},{10... | collective-permute-start | bytes 1966088 | tf_op jit(solution)/shard_map/ppermute | solution.py:502
  99.2 0.8 copy-start.11
  102.3 31.9 %copy-start.3 = (bf16[4,4,640,128]{3,2,1,0:T(8,128)(2,1)}, bf16[4,4,640,128]{3,2,1,0:T(8,128)(2,1)S(1)}, u32[]{:S(2)}) copy-start(bf16[4,4,640,128]{3,2,1,0:T(8,128)(2,1)S(1)} %pad_maximum_fusion.1.first) | copy-start | bytes 7864324
  102.3 40.2 %collective-permute-start.14 = (bf16[4,4,640,128]{3,2,1,0:T(8,128)(2,1)S(1)}, bf16[4,4,640,128]{3,2,1,0:T(8,128)(2,1)}, u32[]{:S(2)}, u32[]{:S(2)}) collective-permute-start(bf16[4,4,640,128]{3,2,1,0:T(8,128)(2,1)S(1)} %pad_maximum_fusion.1.first), channel_id=1, source_target_pairs={{0,4},{4,0},{1,5},{5,1},{2,6},{6,2},{3,7},{7,3},{8,12},{12,8},{9,1... | collective-permute-start | bytes 7864328 | tf_op jit(solution)/shard_map/ppermute | solution.py:502
  136.0 6.6 %collective-permute-start.10 = (f32[4,256,128]{2,1,0:T(8,128)S(1)}, f32[4,256,128]{2,1,0:T(8,128)S(1)}, u32[]{:S(2)}, u32[]{:S(2)}) collective-permute-start(f32[4,256,128]{2,1,0:T(8,128)S(1)} %broadcast_add_fusion.1), channel_id=1, source_target_pairs={{0,4},{1,5},{2,6},{3,7},{8,12},{9,13},{10,14},{11,15},{16,20},{17,... | collective-permute-start | bytes 1572872 | tf_op jit(solution)/shard_map/ppermute | solution.py:486
  283.5 6.1 %copy-start.40 = (bf16[2048,1024]{1,0:T(8,128)(2,1)S(1)}, bf16[2048,1024]{1,0:T(8,128)(2,1)}, u32[]{:S(2)}) copy-start(bf16[2048,1024]{1,0:T(8,128)(2,1)} %get-tuple-element.78.normed) | copy-start | bytes 12582916
  283.5 6.1 %copy-start.42 = (bf16[2048,704]{1,0:T(8,128)(2,1)S(1)}, bf16[2048,704]{1,0:T(8,128)(2,1)}, u32[]{:S(2)}) copy-start(bf16[2048,704]{1,0:T(8,128)(2,1)} %get-tuple-element.86) | copy-start | bytes 8650756
  289.6 3.3 copy-start.1
  289.6 3.3 copy-start.41
  292.9 3.3 copy-start
  292.9 3.3 copy-start.39
  326.3 3.8 collective-permute-start.15
  400.7 2.8 copy-start.33
  400.7 2.7 copy-start.32
  400.7 2.7 copy-start.34
  403.2 14.2 %collective-permute-start.16 = (f32[4,128,784]{1,2,0:T(8,128)S(1)}, f32[4,128,784]{1,2,0:T(8,128)}, u32[]{:S(2)}, u32[]{:S(2)}) collective-permute-start(f32[4,128,784]{1,2,0:T(8,128)S(1)} %copy.135), channel_id=1, source_target_pairs={{0,4},{4,0},{1,5},{5,1},{2,6},{6,2},{3,7},{7,3},{8,12},{12,8},{9,1... | collective-permute-start | bytes 4816904 | tf_op jit(solution)/shard_map/ppermute | solution.py:502
  404.8 1.9 collective-permute-start.21
  406.7 3.8 collective-permute-start.22
  410.5 6.9 %collective-permute-start.23 = (f32[4480]{0:T(1024)S(1)}, f32[4480]{0:T(1024)S(1)}, u32[]{:S(2)}, u32[]{:S(2)}) collective-permute-start(f32[4480]{0:T(1024)S(1)} %add.264), channel_id=1, source_target_pairs={{0,16},{8,24},{16,0},{24,8},{1,17},{9,25},{17,1},{25,9},{2,18},{10... | collective-permute-start | bytes 53768 | tf_op jit(solution)/shard_map/ppermute | solution.py:502
  421.2 3.0 copy-start.18
  421.2 3.0 copy-start.26
  421.2 3.0 copy-start.27
  421.4 11.3 %collective-permute-start.17 = (f32[2,64,784]{2,1,0:T(8,128)S(1)}, f32[2,64,784]{2,1,0:T(8,128)S(1)}, u32[]{:S(2)}, u32[]{:S(2)}) collective-permute-start(f32[2,64,784]{2,1,0:T(8,128)S(1)} %dynamic-slice_bitcast_fusion.1), channel_id=1, source_target_pairs={{0,8},{8,0},{16,24},{24,16},{1,9},{9,1},{17,25},{25,17},{2,10},{10... | collective-permute-start | bytes 1204232 | tf_op jit(solution)/shard_map/ppermute | solution.py:502
  422.6 14.1 %copy-start.29 = (f32[128]{0:T(128)S(1)}, f32[128]{0:T(128)}, u32[]{:S(2)}) copy-start(f32[128]{0:T(128)} %param.45) | copy-start | bytes 1540
  422.6 14.1 %copy-start.35 = (f32[128]{0:T(128)S(1)}, f32[128]{0:T(128)}, u32[]{:S(2)}) copy-start(f32[128]{0:T(128)} %param.47) | copy-start | bytes 1540
  422.6 14.1 %copy-start.36 = (f32[128]{0:T(128)S(1)}, f32[128]{0:T(128)}, u32[]{:S(2)}) copy-start(f32[128]{0:T(128)} %param.46) | copy-start | bytes 1540
  422.6 11.6 %collective-permute-start.19 = (f32[2,64,784]{2,1,0:T(8,128)S(1)}, f32[2,64,784]{2,1,0:T(8,128)S(1)}, u32[]{:S(2)}, u32[]{:S(2)}) collective-permute-start(f32[2,64,784]{2,1,0:T(8,128)S(1)} %dynamic-slice_bitcast_fusion), channel_id=1, source_target_pairs={{0,16},{8,24},{16,0},{24,8},{1,17},{9,25},{17,1},{25,9},{2,18},{10... | collective-permute-start | bytes 1204232 | tf_op jit(solution)/shard_map/ppermute | solution.py:502
  433.0 9.6 %collective-permute-start.18 = (f32[64,784]{0,1:T(8,128)S(1)}, f32[64,784]{0,1:T(8,128)}, u32[]{:S(2)}, u32[]{:S(2)}) collective-permute-start(f32[64,784]{0,1:T(8,128)S(1)} %copy.138), channel_id=1, source_target_pairs={{0,16},{8,24},{16,0},{24,8},{1,17},{9,25},{17,1},{25,9},{2,18},{10... | collective-permute-start | bytes 602120 | tf_op jit(solution)/shard_map/ppermute | solution.py:502
  434.2 10.7 %copy-start.5 = (f32[2,128,256]{1,2,0:T(8,128)S(1)}, f32[2,128,256]{1,2,0:T(8,128)}, u32[]{:S(2)}) copy-start(f32[2,128,256]{1,2,0:T(8,128)} %copy-done.4) | copy-start | bytes 786436
  434.5 9.2 %collective-permute-start.20 = (f32[64,784]{0,1:T(8,128)S(1)}, f32[64,784]{0,1:T(8,128)}, u32[]{:S(2)}, u32[]{:S(2)}) collective-permute-start(f32[64,784]{0,1:T(8,128)S(1)} %copy.140), channel_id=1, source_target_pairs={{0,8},{8,0},{16,24},{24,16},{1,9},{9,1},{17,25},{25,17},{2,10},{10... | collective-permute-start | bytes 602120 | tf_op jit(solution)/shard_map/ppermute | solution.py:502
  443.7 4.1 copy-start.8
  444.9 9.8 %copy-start.23 = (f32[128,16]{0,1:T(8,128)S(1)}, f32[128,16]{0,1:T(8,128)}, u32[]{:S(2)}) copy-start(f32[128,16]{0,1:T(8,128)} %param.39) | copy-start | bytes 24580
  444.9 9.8 %copy-start.30 = (f32[128,16]{0,1:T(8,128)S(1)}, f32[128,16]{0,1:T(8,128)}, u32[]{:S(2)}) copy-start(f32[128,16]{0,1:T(8,128)} %param.41) | copy-start | bytes 24580
  444.9 9.8 %copy-start.31 = (f32[128,16]{0,1:T(8,128)S(1)}, f32[128,16]{0,1:T(8,128)}, u32[]{:S(2)}) copy-start(f32[128,16]{0,1:T(8,128)} %param.40) | copy-start | bytes 24580
  445.0 10.5 %copy-start.6 = (f32[704,128]{1,0:T(8,128)S(1)}, f32[704,128]{1,0:T(8,128)}, u32[]{:S(2)}) copy-start(f32[704,128]{1,0:T(8,128)} %param.54) | copy-start | bytes 1081348
  447.8 10.2 %copy-start.2 = (f32[2,128,704]{1,2,0:T(8,128)S(1)}, f32[2,128,704]{1,2,0:T(8,128)}, u32[]{:S(2)}) copy-start(f32[2,128,704]{1,2,0:T(8,128)} %param.51) | copy-start | bytes 2162692
  447.8 10.2 %copy-start.9 = (f32[2,128,704]{1,2,0:T(8,128)S(1)}, f32[2,128,704]{1,2,0:T(8,128)}, u32[]{:S(2)}) copy-start(f32[2,128,704]{1,2,0:T(8,128)} %param.53) | copy-start | bytes 2162692
  447.8 10.2 %copy-start.10 = (f32[2,128,704]{1,2,0:T(8,128)S(1)}, f32[2,128,704]{1,2,0:T(8,128)}, u32[]{:S(2)}) copy-start(f32[2,128,704]{1,2,0:T(8,128)} %param.52) | copy-start | bytes 2162692
  458.0 1.7 copy-start.13
  458.0 1.7 copy-start.15
  458.0 1.7 copy-start.16
  (5 other events, 3.7 us)
Sparse Core Ops, SparseCore 0:
  11.5 141.9 all-gather.1
  301.9 76.9 reduce-scatter.1

commit v4 on v3

--- a/solution.py
+++ b/solution.py
@@ -16,7 +16,7 @@
 DECAY_ROWS = 32
 ROWS = 256
 FFN_ROWS = 512
-FFN_PARTS = 2
+FFN_CUTS = 8
 STEP = 10
 
 NORM_EPS = 1e-06
@@ -234,9 +234,12 @@
 
     @pl.when((step == 0) & (piece == 0))
     def _():
+        gain_out[...] = jnp.zeros_like(gain_out)
+
+    @pl.when(piece == 0)
+    def _():
         ffn_ref[...] = jnp.zeros_like(ffn_ref)
         back_ref[...] = jnp.zeros_like(back_ref)
-        gain_out[...] = jnp.zeros_like(gain_out)
 
     def rows_of(start):
         return jnp.concatenate(
@@ -244,32 +247,47 @@
         )
 
     gate_weight, up_weight, down_weight = rows_of(0), rows_of(units), rows_of(2 * units)
-    count = normed.shape[0] // FFN_PARTS
-    spans = [slice(part * count, (part + 1) * count) for part in range(FFN_PARTS)]
-    made = [
-        (
-            dot(normed[span], gate_weight, NT),
-            dot(normed[span], up_weight, NT),
-            dot(back[span], down_weight, NT),
-        )
-        for span in spans
-    ]
-    for span, (gate_values, upward, back_active) in zip(spans, made):
+    half = normed.shape[0] // 2
+    third = half // FFN_CUTS
+
+    def made(part):
+        span = slice(part * half, (part + 1) * half)
+        yield dot(normed[span], gate_weight, NT)
+        yield dot(normed[span], up_weight, NT)
+        yield dot(back[span], down_weight, NT)
+
+    def elementwise(part, values, cut):
+        span = slice(cut * third, (cut + 1) * third)
+        target = slice(part * half + cut * third, part * half + (cut + 1) * third)
+        gate_values, upward, back_active = [item[span] for item in values]
         share = sigmoid(gate_values)
         silu = gate_values * share
-        active = (silu * upward).astype(BF16)
-        back_gate = (
+        active_ref[target] = (silu * upward).astype(BF16)
+        back_gate_ref[target] = (
             back_active * upward * (share * (1.0 + gate_values * (1.0 - share)))
         ).astype(BF16)
-        back_up = (back_active * silu).astype(BF16)
-        ffn = dot(active, down_weight)
-        back_normed = dot(back_gate, gate_weight) + dot(back_up, up_weight)
-        keep = jnp.where(piece > 0, 1.0, 0.0)
-        ffn_ref[span] = ffn_ref[span] * keep + ffn
-        back_ref[span] = back_ref[span] * keep + back_normed
-        active_ref[span] = active
-        back_gate_ref[span] = back_gate
-        back_up_ref[span] = back_up
+        back_up_ref[target] = (back_active * silu).astype(BF16)
+
+    def added(part):
+        span = slice(part * half, (part + 1) * half)
+        ffn_ref[span] += dot(active_ref[span], down_weight)
+        yield
+        back_ref[span] += dot(back_gate_ref[span], gate_weight)
+        yield
+        back_ref[span] += dot(back_up_ref[span], up_weight)
+        yield
+
+    first = list(made(0))
+    second = []
+    for index, item in enumerate(made(1)):
+        second.append(item)
+        for cut in range(index * FFN_CUTS // 3, (index + 1) * FFN_CUTS // 3):
+            elementwise(0, first, cut)
+    for index, _ in enumerate(added(0)):
+        for cut in range(index * FFN_CUTS // 3, (index + 1) * FFN_CUTS // 3):
+            elementwise(1, second, cut)
+    for _ in added(1):
+        pass
 
     @pl.when(piece == info[2 * GROUPS + weight_pieces])
     def _():
@@ -339,8 +357,8 @@
 def mix_back_kernel(
     homes, info, tokens, back_middle, query_in, kv, cum_in, logits_in, states, back_mixed, back_gate,
     back_end, query_weight, key_weight, rank_weight, decay_out, rank, gain,
-    grad_out, input_out, decay_grad_out, bias_out, gain_out,
-    state_ref, query_ref, key_ref, grad_ref,
+    kept_out, sent_out, rank_grad_out, input_out, decay_grad_out, bias_out, gain_out,
+    state_ref, query_ref, key_ref, grad_ref, rank_ref, sum_ref,
 ):
     heads = back_end.shape[0]
     size = HK + HV
@@ -349,7 +367,8 @@
     @pl.when(pl.program_id(0) == 0)
     def _():
         state_ref[...] = back_end[...]
-        grad_out[...] = jnp.zeros_like(grad_out)
+        sum_ref[...] = jnp.zeros_like(sum_ref)
+        rank_grad_out[...] = jnp.zeros_like(rank_grad_out)
         decay_grad_out[...] = jnp.zeros_like(decay_grad_out)
         bias_out[...] = jnp.zeros_like(bias_out)
         gain_out[...] = jnp.zeros_like(gain_out)
@@ -430,17 +449,17 @@
             query_ref[span, at + HK : at + size] = back_gate[head, span]
             key_ref[span, at : at + HK] = back_keys[head].astype(BF16)
             key_ref[span, at + HK : at + size] = back_values[head].astype(BF16)
-        grad_ref[span, 2 * size :] = rank_back.astype(BF16)
+        rank_ref[span] = rank_back.astype(BF16)
 
     for head in every:
 
         @pl.when(info[2 * GROUPS + heads] == head)
         def _():
             grad_ref[:, :size] = query_ref[:, head * size : (head + 1) * size]
-            grad_ref[:, size : 2 * size] = key_ref[:, head * size : (head + 1) * size]
+            grad_ref[:, size:] = key_ref[:, head * size : (head + 1) * size]
 
     back_normed = (
-        dot(grad_ref[:, 2 * size :], rank_weight[...])
+        dot(rank_ref[...], rank_weight[...])
         + dot(query_ref[...], query_weight[...])
         + dot(key_ref[...], key_weight[...])
     )
@@ -448,14 +467,23 @@
     inverse = inverse_rms(inputs, NORM_EPS)
     unit = inputs * inverse
     normed = (unit * gain[...]).astype(BF16)
-    weight_grad = dot(normed, grad_ref[...], TN)
-    for group in range(GROUPS):
-        grad_out[info[group], homes[group]] += weight_grad[group * LANES : (group + 1) * LANES]
+    sum_ref[...] += dot(normed, grad_ref[...], TN)
+    rank_grad_out[...] += dot(rank_ref[...], normed, TN)
     weighted = back_normed * gain[...]
     input_out[...] = back_middle[...] + inverse * (
         weighted - unit * jnp.mean(weighted * unit, axis=-1, keepdims=True)
     )
     gain_out[...] += jnp.sum(back_normed * unit, axis=0, keepdims=True)
+
+    @pl.when(pl.program_id(0) == pl.num_programs(0) - 1)
+    def _():
+        for group in range(GROUPS):
+            found = slice(group * LANES, (group + 1) * LANES)
+            for index, target in enumerate((kept_out, sent_out)):
+
+                @pl.when(info[group] == index)
+                def _():
+                    target[homes[group]] = sum_ref[found]
 
 
 def shaped(shape, kind=F32):
@@ -521,22 +549,16 @@
 
 
 def gather_square(line):
-    return jnp.stack([line] + [swap(line, "dp", distance) for distance in range(1, 4)])
+    return [line] + [swap(line, "dp", distance) for distance in range(1, 4)]
 
 
 def gather_slots(key_pack, query_pack):
     key_line = gather_line(key_pack)
     query_pack, key_line = lax.optimization_barrier((query_pack, key_line))
-    key_first = gather_square(key_line)
+    key_first = jnp.stack(gather_square(key_line))
     query_line = gather_line(query_pack)
     query_line, key_first = lax.optimization_barrier((query_line, key_first))
-    query_first = gather_square(query_line)
-    return (
-        key_first,
-        swap(key_first, "ctx", 1),
-        query_first,
-        swap(query_first, "ctx", 1),
-    )
+    return key_first, swap(key_first, "ctx", 1), gather_square(query_line)
 
 
 def gather_pair(pack):
@@ -573,26 +595,27 @@
     return gather_plain(pack)
 
 
-def scatter_rows(value):
-    columns = value.shape[-1]
+def scatter_rows(kept, sent, early):
+    columns = kept.shape[-1]
     if not staged():
-        return lax.psum_scatter(
-            value.reshape(-1, columns), ("dp", "ctx"), scatter_dimension=0, tiled=True
-        )
+        whole = jnp.concatenate([kept, sent]).reshape(-1, columns)
+        return lax.psum_scatter(whole, ("dp", "ctx"), scatter_dimension=0, tiled=True), early
     device = lax.axis_index("dp")
     row, column = device // 2, device % 2
 
     def pick(array, axis, index):
         return lax.dynamic_index_in_dim(array, index, axis, keepdims=False)
 
-    value = (value[0] + swap(value[1], "ctx", 1)).reshape(2, 2, LANES, columns)
+    value = kept + swap(sent, "ctx", 1)
+    value, early = lax.optimization_barrier((value, early))
+    value = value.reshape(2, 2, LANES, columns)
     half = LANES // 2
     upper, lower = value[:, :, :half], value[:, :, half:]
     upper = pick(upper, 1, column) + swap(pick(upper, 1, 1 - column), "dp", 1)
     lower = pick(lower, 0, row) + swap(pick(lower, 0, 1 - row), "dp", 2)
     upper = pick(upper, 0, row) + swap(pick(upper, 0, 1 - row), "dp", 2)
     lower = pick(lower, 0, column) + swap(pick(lower, 0, 1 - column), "dp", 1)
-    return jnp.concatenate([upper, lower])
+    return jnp.concatenate([upper, lower]), early
 
 
 def total_over(value):
@@ -681,7 +704,7 @@
         [query_key_weight[0].T, value_gate_weight[1].T, output_weight]
     ).astype(BF16)
     if staged():
-        key_first, key_second, query_first, query_second = gather_slots(
+        key_first, key_second, query_square = gather_slots(
             jnp.concatenate(key_parts + three_parts(small)), query_pack
         )
         sent = key_first[0, :, size + ranks :].astype(F32).reshape(heads, 3, DECAY_ROWS, HK)
@@ -750,6 +773,10 @@
         2 * rows * width * size * heads,
         rows * heads * 4 * 1024,
     )
+    if staged():
+        query_square, local_state = lax.optimization_barrier((query_square, local_state))
+        query_first = jnp.stack(query_square)
+        query_second = swap(query_first, "ctx", 1)
     device_decay = jnp.exp(local_total)
     start_state = carry(local_state, device_decay, 1)
 
@@ -873,9 +900,9 @@
     )
     back_end = carry(collected, device_decay, -1)
 
-    grad_columns = columns + ranks
-    grad_shape = shaped((2, GROUPS // 2, LANES, grad_columns))
-    mixer_back, input_grad, decay_out_grad, bias_grad, gain_one_part = call(
+    grad_shape = shaped((GROUPS // 2, LANES, columns))
+    rank_grad_shape = shaped((ranks, width))
+    kept, sent_away, rank_grad, input_grad, decay_out_grad, bias_grad, gain_one_part = call(
         functools.partial(mix_back_kernel, gather_homes()),
         (steps,),
         [
@@ -898,6 +925,8 @@
         ],
         [
             fixed(grad_shape),
+            fixed(grad_shape),
+            fixed(rank_grad_shape),
             back_row_spec,
             pl.BlockSpec((heads, ranks, HK), lambda i, *_: (0, 0, 0)),
             bias_spec,
@@ -905,6 +934,8 @@
         ],
         [
             grad_shape,
+            grad_shape,
+            rank_grad_shape,
             shaped((rows, width)),
             shaped((heads, ranks, HK)),
             shaped((heads, 1, HK)),
@@ -914,7 +945,9 @@
             pltpu.VMEM((heads, HV, HK), F32),
             pltpu.VMEM((ROWS, heads * size), BF16),
             pltpu.VMEM((ROWS, heads * size), BF16),
-            pltpu.VMEM((ROWS, grad_columns), BF16),
+            pltpu.VMEM((ROWS, columns), BF16),
+            pltpu.VMEM((ROWS, ranks), BF16),
+            pltpu.VMEM((width, columns), F32),
         ],
         (
             info, tokens, back_middle, query, kv, cum, logits, states, back_mixed, back_out_gate,
@@ -924,28 +957,36 @@
         2 * rows * width * columns * heads * 2,
         rows * heads * 4 * 2048,
     )
+    mixer_share, early_share = scatter_rows(kept, sent_away, early_share)
     own = info[-1]
     decay_out_own = lax.dynamic_index_in_dim(decay_out_grad, own, 0, keepdims=False)
     bias_own = lax.dynamic_index_in_dim(bias_grad, own, 0, keepdims=False)
-    sums = jnp.concatenate(
-        [
-            gain_one_part.reshape(-1),
-            gain_two_part.reshape(-1),
-            head_gain_part.reshape(-1),
-            bias_own.reshape(-1),
-            decay_out_own.reshape(-1),
-        ]
-    )
-    sums = total_over(sums)
-    mixer_share = scatter_rows(mixer_back)
+    sums = total_over(
+        jnp.concatenate(
+            [
+                gain_one_part.reshape(-1),
+                gain_two_part.reshape(-1),
+                head_gain_part.reshape(-1),
+                bias_own.reshape(-1),
+                decay_out_own.reshape(-1),
+                rank_grad.reshape(-1),
+            ]
+        )
+    )
     gain_count = gains.shape[0]
+    decay_start = gain_count + HK
+    rank_start = decay_start + ranks * HK
     gains_grad = sums[:gain_count]
-    bias_total = sums[gain_count : gain_count + HK]
-    decay_out_total = sums[gain_count + HK :].reshape(ranks, HK)
+    bias_total = sums[gain_count:decay_start]
+    decay_out_total = sums[decay_start:rank_start].reshape(ranks, HK)
+    share = decay_in_weight.shape[0]
+    place = (lax.axis_index("dp") * lax.axis_size("ctx") + lax.axis_index("ctx")) * share
+    decay_in_share = lax.dynamic_slice_in_dim(
+        sums[rank_start:].reshape(ranks, width), place, share, axis=1
+    ).T
 
     query_key_share = jnp.stack([mixer_share[:, :HK], mixer_share[:, size : size + HK]])
     value_gate_share = jnp.stack([mixer_share[:, size + HK : columns], mixer_share[:, HK:size]])
-    decay_in_share = mixer_share[:, columns:]
     gate_up_share = jnp.stack([early_share[:units].T, early_share[units : 2 * units].T])
     down_share = early_share[2 * units : 3 * units]
     output_share = early_share[3 * units :]

time: 475 us -> 421 us (0.89)
  waiting for transfers between devices: 80.4 us -> 52.5 us
  local copies, waits for them, and re-layouts: 25.2 us -> 6.68 us
  other arithmetic: 34.8 us -> 27.9 us
    ppermute x16, waiting for transfers between devices: 58.4 us -> 29.3 us  [swap(): lax.ppermute(value, axis, [(source, source ^ distance) for source in rang...]
    unnamed x104 -> x108, local copies, waits for them, and re-layouts: 16.9 us -> 5 us
  transfers between devices with their start and end apart: 26 -> 26, of which waited for: 14 -> 16; matrix products, arithmetic and copies ran while one was open for 9% -> 6% of each run, Pallas kernels for 35% -> 39%
where the time goes in v4:
time: 421 us; the launch traced here: 415 us
  Pallas kernels  261 us (62%)
  waiting for transfers between devices  52.5 us (12%)
  starting transfers between devices  36.6 us (9%)
  other arithmetic  27.9 us (7%)
  between operations  15.9 us (4%)
  matrix products  14 us (3%)
  local copies, waits for them, and re-layouts  6.68 us (2%)
    pallas_call x5, Pallas kernels, call(): pl.pallas_call(kernel, grid_spec=pltpu.PrefetchScalarGridSpec(num_scalar_...  261 us
    ppermute x16, waiting for transfers between devices, swap(): lax.ppermute(value, axis, [(source, source ^ distance) for source in rang...  29.3 us
    ppermute x6, waiting for transfers between devices, shift(): lax.ppermute(value, axis, [(source, (source + distance) % count) for sour...  19.4 us
    ppermute x6, starting transfers between devices, shift(): lax.ppermute(value, axis, [(source, (source + distance) % count) for sour...  17.5 us
    ppermute x16, starting transfers between devices, swap(): lax.ppermute(value, axis, [(source, source ^ distance) for source in rang...  14.8 us
    dot_general x4, matrix products, dot(): return lax.dot_general(left, right, dims, preferred_element_type=F32)  14 us
  transfers between devices with their start and end apart: 26, of which 16 were waited for; matrix products, arithmetic and copies ran while one was open for 6% of the time, Pallas kernels for 39%

profile of v4, /device:TPU:0, one launch (start us, length us, event | category | flops | bytes accessed | tf_op | source)
XLA Modules:
  0.0 414.8 jit_solution(4960116516554252407)
XLA Ops:
  7.3 1.3 convert.37
  8.7 1.0 convert_bitcast_fusion
  9.7 0.8 pad_maximum_fusion.5
  11.2 3.0 collective-permute-start
  14.3 2.6 collective-permute-start.1
  16.9 1.3 collective-permute-start.2
  18.3 2.4 collective-permute-done
  20.6 4.6 %collective-permute-done.1 = bf16[496,128]{1,0:T(8,128)(2,1)S(1)} collective-permute-done((bf16[496,128]{1,0:T(8,128)(2,1)S(1)}, bf16[496,128]{1,0:T(8,128)(2,1)S(1)}, u32[]{:S(2)}, u32[]{:S(2)}) %collective-permute-start.1) | collective-permute-done | bytes 127008 | tf_op jit(solution)/shard_map/ppermute | solution.py:535
  25.3 1.6 collective-permute-start.6
  26.9 1.5 collective-permute-start.7
  28.9 6.0 %collective-permute-start.3 = (bf16[640,128]{1,0:T(8,128)(2,1)S(1)}, bf16[640,128]{1,0:T(8,128)(2,1)S(1)}, u32[]{:S(2)}, u32[]{:S(2)}) collective-permute-start(bf16[640,128]{1,0:T(8,128)(2,1)S(1)} %pad_maximum_fusion.8), channel_id=1, source_target_pairs={{0,1},{1,2},{2,3},{3,0},{4,5},{5,6},{6,7},{7,4},{8,9},{9,10},{10,1... | collective-permute-start | bytes 491528 | tf_op jit(solution)/shard_map/ppermute | solution.py:535
  34.9 4.1 collective-permute-start.4
  39.0 5.7 %collective-permute-done.3 = bf16[640,128]{1,0:T(8,128)(2,1)S(1)} collective-permute-done((bf16[640,128]{1,0:T(8,128)(2,1)S(1)}, bf16[640,128]{1,0:T(8,128)(2,1)S(1)}, u32[]{:S(2)}, u32[]{:S(2)}) %collective-permute-start.3) | collective-permute-done | bytes 163872 | tf_op jit(solution)/shard_map/ppermute | solution.py:535
  45.0 5.4 %collective-permute-done.4 = bf16[640,128]{1,0:T(8,128)(2,1)S(1)} collective-permute-done((bf16[640,128]{1,0:T(8,128)(2,1)S(1)}, bf16[640,128]{1,0:T(8,128)(2,1)S(1)}, u32[]{:S(2)}, u32[]{:S(2)}) %collective-permute-start.4) | collective-permute-done | bytes 163872 | tf_op jit(solution)/shard_map/ppermute | solution.py:535
  50.5 1.3 collective-permute-done.5
  52.4 0.8 pad_add_fusion.info
  53.8 1.4 collective-permute-start.10
  55.2 1.5 collective-permute-start.11
  56.7 0.7 collective-permute-start.12
  57.4 0.6 fusion.7.decay_out
  58.0 28.7 %shard_map.509 = (bf16[2048,1024]{1,0:T(8,128)(2,1)}, f32[4,2048,384]{2,1,0:T(8,128)}, f32[2048,16]{1,0:T(8,128)}, f32[4,2048,128]{2,1,0:T(8,128)}, f32[4,2048,1...) custom-call(s32[21]{0:T(128)} %pad_add_fusion.info, ...), custom_call_target="tpu_custom_call" | custom-call | flops 6442450944 | bytes 33554432 | tf_op jit(solution)/shard_map/pallas_call | solution.py:494
  86.8 12.5 %collective-permute-done.12 = bf16[4,640,128]{2,1,0:T(8,128)(2,1)} collective-permute-done((bf16[4,640,128]{2,1,0:T(8,128)(2,1)S(1)}, bf16[4,640,128]{2,1,0:T(8,128)(2,1)}, u32[]{:S(2)}, u32[]{:S(2)}) %collective-permute-start.12) | collective-permute-done | bytes 655392 | tf_op jit(solution)/shard_map/ppermute | solution.py:530
  99.3 2.4 pad_maximum_fusion.1.first
  101.8 0.7 slice.106
  103.2 1.1 broadcast_add_fusion.1
  104.3 3.0 collective-permute-start.13
  107.3 4.0 broadcast_select_fusion.back
  111.2 0.8 copy-done.44
  112.0 40.1 %shard_map.510 = (f32[4,2048,128]{2,1,0:T(8,128)}, f32[4,2048,256]{2,1,0:T(8,128)}, f32[4,2048,256]{2,1,0:T(8,128)}, f32[16,4,256,128]{3,2,1,0:T(8,128)}, bf16[2...) custom-call(s32[21]{0:T(128)} %pad_add_fusion.info, ...), custom_call_target="tpu_custom_call" | custom-call | flops 15032385536 | bytes 33554432 | tf_op jit(solution)/shard_map/pallas_call | solution.py:494
  152.1 1.3 all-gather.2.cloned.1.call-done
  153.5 99.5 %shard_map.511 = (bf16[2048,704]{1,0:T(8,128)(2,1)}, bf16[2048,704]{1,0:T(8,128)(2,1)}, bf16[2048,704]{1,0:T(8,128)(2,1)}, bf16[2048,1024]{1,0:T(8,128)(2,1)}, f...) custom-call(s32[21]{0:T(128)} %pad_add_fusion.info, ...), custom_call_target="tpu_custom_call" | custom-call | flops 70866960384 | bytes 50331648 | tf_op jit(solution)/shard_map/pallas_call | solution.py:494
  253.0 6.3 %fusion.34 = f32[704,1024]{1,0:T(8,128)S(1)} fusion(bf16[2048,704]{1,0:T(8,128)(2,1)} %get-tuple-element.99, bf16[2048,1024]{1,0:T(8,128)(2,1)} %get-tuple-element.92.normed), kind=kOutput, calls=%fused_computation.115 | convolution fusion | flops 2952790016 | bytes 9961472 | tf_op jit(solution)/shard_map/dot_general | solution.py:43
  259.4 3.2 fusion.35
  262.6 3.2 fusion.36
  265.9 1.3 fusion.37
  267.2 4.3 %pad_maximum_fusion = f32[2368,1024]{1,0:T(8,128)} fusion(f32[256,1024]{1,0:T(8,128)S(1)} %fusion.37, f32[704,1024]{1,0:T(8,128)S(1)} %fusion.36, f32[704,1024]{1,0:T(8,128)S(1)} %fusion.35, f32[704,1024]{1,0:T(8,128)S(1)} %fusion.34), kind=kLoop, calls=%fused_computation | loop fusion | flops 7274496 | bytes 19398656 | tf_op jit(solution)/shard_map/concatenate | solution.py:864
  271.5 24.3 %shard_map.512 = (f32[4,2048,256]{2,1,0:T(8,128)}, bf16[4,2048,256]{2,1,0:T(8,128)(2,1)}, f32[1,256]{1,0:T(1,128)}, f32[4,256,128]{2,1,0:T(8,128)}) custom-call(bf16[2048,1024]{1,0:T(8,128)(2,1)} %get-tuple-element.104.back_attn, bf16[1024,1024]{1,0:T(8,128)(2,1)} %get-tuple-element.105.out_weight, f32[4,2048,256]{2,1,0:T(8,128)} %get-tuple-element.106.mixed_in, ...), custom_call_target="tpu_custom_call" | custom-call | flops 4294967296 | bytes 33554432 | tf_op jit(solution)/shard_map/pallas_call | solution.py:494
  295.8 1.2 broadcast_add_fusion
  297.0 1.3 collective-permute-start.15
  298.3 2.5 collective-permute-done.15.back_end
  300.8 0.8 copy-done.43
  301.8 68.5 %shard_map.513 = (f32[4,128,768]{2,1,0:T(8,128)}, f32[4,128,768]{2,1,0:T(8,128)}, f32[16,1024]{1,0:T(8,128)}, f32[2048,1024]{1,0:T(8,128)}, f32[4,16,128]{2,1,0:...) custom-call(s32[21]{0:T(128)} %pad_add_fusion.info, bf16[2048,1024]{1,0:T(8,128)(2,1)} %tokens.5, ...), custom_call_target="tpu_custom_call" | custom-call | flops 25769803776 | bytes 67108864 | tf_op jit(solution)/shard_map/pallas_call | solution.py:494
  370.4 0.9 copy.74
  371.2 0.7 constant_dynamic-update-slice_fusion.4
  371.9 0.7 constant_dynamic-update-slice_fusion.6
  372.6 0.7 bitcast_dynamic-update-slice_fusion
  373.8 0.9 collective-permute-done.21
  374.8 1.3 collective-permute-start.22
  376.1 3.5 collective-permute-done.22
  379.6 1.6 collective-permute-start.23
  381.2 3.0 collective-permute-done.23
  384.8 0.6 multiply_subtract_fusion.7
  385.5 0.6 multiply_subtract_fusion.6
  386.7 1.6 add.243
  388.7 1.3 collective-permute-start.17
  390.6 1.2 multiply_subtract_fusion.1
  391.8 1.7 multiply_subtract_fusion
  393.6 0.8 multiply_subtract_fusion.3
  394.4 3.8 collective-permute-done.17
  398.3 1.6 collective-permute-start.18
  400.5 3.5 collective-permute-done.18
  404.0 1.7 collective-permute-done.20
  405.9 1.0 multiply_subtract_fusion.2
  406.9 0.8 multiply_subtract_fusion.4
  (166 shorter events, 6.8 us)
Async XLA Ops:
  7.2 3.4 copy-start.14
  7.2 3.5 copy-start.7
  7.2 3.7 copy-start.28
  7.2 3.7 copy-start.36
  7.3 3.7 copy-start.24
  7.3 11.0 %copy-start.12 = (f32[256,128]{1,0:T(8,128)S(1)}, f32[256,128]{1,0:T(8,128)}, u32[]{:S(2)}) copy-start(f32[256,128]{1,0:T(8,128)} %param.48) | copy-start | bytes 393220
  7.3 146.2 %all-gather.2.cloned.1.call-start = ((), (), s32[]{:S(2)}) async-start(), calls=%async_computation.1 | async-start | bytes 17842176 | tf_op jit(solution)/shard_map/all_gather | solution.py:593
  10.5 377.9 %reduce-scatter.2.cloned.1.call-start = ((), (), s32[]{:S(2)}) async-start(), calls=%async_computation.2 | async-start | bytes 10911744 | tf_op jit(solution)/shard_map/reduce_scatter | solution.py:873
  11.2 9.4 %collective-permute-start = (bf16[496,128]{1,0:T(8,128)(2,1)S(1)}, bf16[496,128]{1,0:T(8,128)(2,1)S(1)}, u32[]{:S(2)}, u32[]{:S(2)}) collective-permute-start(bf16[496,128]{1,0:T(8,128)(2,1)S(1)} %constant_dynamic-update-slice_fusion), channel_id=1, source_target_pairs={{0,1},{1,2},{2,3},{3,0},{4,5},{5,6},{6,7},{7,4},{8,9},{9,10},{10,1... | collective-permute-start | bytes 380936 | tf_op jit(solution)/shard_map/ppermute | solution.py:535
  14.3 11.0 %collective-permute-start.1 = (bf16[496,128]{1,0:T(8,128)(2,1)S(1)}, bf16[496,128]{1,0:T(8,128)(2,1)S(1)}, u32[]{:S(2)}, u32[]{:S(2)}) collective-permute-start(bf16[496,128]{1,0:T(8,128)(2,1)S(1)} %constant_dynamic-update-slice_fusion), channel_id=1, source_target_pairs={{0,2},{1,3},{2,0},{3,1},{4,6},{5,7},{6,4},{7,5},{8,10},{9,11},{10,... | collective-permute-start | bytes 380936 | tf_op jit(solution)/shard_map/ppermute | solution.py:535
  16.9 8.4 %collective-permute-start.2 = (bf16[496,128]{1,0:T(8,128)(2,1)S(1)}, bf16[496,128]{1,0:T(8,128)(2,1)S(1)}, u32[]{:S(2)}, u32[]{:S(2)}) collective-permute-start(bf16[496,128]{1,0:T(8,128)(2,1)S(1)} %constant_dynamic-update-slice_fusion), channel_id=1, source_target_pairs={{0,3},{1,0},{2,1},{3,2},{4,7},{5,4},{6,5},{7,6},{8,11},{9,8},{10,9... | collective-permute-start | bytes 380936 | tf_op jit(solution)/shard_map/ppermute | solution.py:535
  25.3 27.9 %copy-start.26 = (f32[2304]{0:T(1024)S(1)}, f32[2304]{0:T(1024)}, u32[]{:S(2)}) copy-start(f32[2304]{0:T(1024)} %param.57) | copy-start | bytes 27652
  25.3 26.5 %collective-permute-start.6 = (bf16[4,496,128]{2,1,0:T(8,128)(2,1)S(1)}, bf16[4,496,128]{2,1,0:T(8,128)(2,1)S(1)}, u32[]{:S(2)}, u32[]{:S(2)}) collective-permute-start(bf16[4,496,128]{2,1,0:T(8,128)(2,1)S(1)} %pad_maximum_fusion.6), channel_id=1, source_target_pairs={{0,8},{8,0},{16,24},{24,16},{1,9},{9,1},{17,25},{25,17},{2,10},{10... | collective-permute-start | bytes 1523720 | tf_op jit(solution)/shard_map/ppermute | solution.py:530
  26.9 25.0 %collective-permute-start.7 = (bf16[4,496,128]{2,1,0:T(8,128)(2,1)S(1)}, bf16[4,496,128]{2,1,0:T(8,128)(2,1)S(1)}, u32[]{:S(2)}, u32[]{:S(2)}) collective-permute-start(bf16[4,496,128]{2,1,0:T(8,128)(2,1)S(1)} %pad_maximum_fusion.6), channel_id=1, source_target_pairs={{0,16},{8,24},{16,0},{24,8},{1,17},{9,25},{17,1},{25,9},{2,18},{10... | collective-permute-start | bytes 1523720 | tf_op jit(solution)/shard_map/ppermute | solution.py:530
  28.4 23.7 %collective-permute-start.8 = (bf16[4,496,128]{2,1,0:T(8,128)(2,1)S(1)}, bf16[4,496,128]{2,1,0:T(8,128)(2,1)S(1)}, u32[]{:S(2)}, u32[]{:S(2)}) collective-permute-start(bf16[4,496,128]{2,1,0:T(8,128)(2,1)S(1)} %pad_maximum_fusion.6), channel_id=1, source_target_pairs={{0,24},{8,16},{16,8},{24,0},{1,25},{9,17},{17,9},{25,1},{2,26},{10... | collective-permute-start | bytes 1523720 | tf_op jit(solution)/shard_map/ppermute | solution.py:530
  28.9 15.8 %collective-permute-start.3 = (bf16[640,128]{1,0:T(8,128)(2,1)S(1)}, bf16[640,128]{1,0:T(8,128)(2,1)S(1)}, u32[]{:S(2)}, u32[]{:S(2)}) collective-permute-start(bf16[640,128]{1,0:T(8,128)(2,1)S(1)} %pad_maximum_fusion.8), channel_id=1, source_target_pairs={{0,1},{1,2},{2,3},{3,0},{4,5},{5,6},{6,7},{7,4},{8,9},{9,10},{10,1... | collective-permute-start | bytes 491528 | tf_op jit(solution)/shard_map/ppermute | solution.py:535
  34.9 15.5 %collective-permute-start.4 = (bf16[640,128]{1,0:T(8,128)(2,1)S(1)}, bf16[640,128]{1,0:T(8,128)(2,1)S(1)}, u32[]{:S(2)}, u32[]{:S(2)}) collective-permute-start(bf16[640,128]{1,0:T(8,128)(2,1)S(1)} %pad_maximum_fusion.8), channel_id=1, source_target_pairs={{0,2},{1,3},{2,0},{3,1},{4,6},{5,7},{6,4},{7,5},{8,10},{9,11},{10,... | collective-permute-start | bytes 491528 | tf_op jit(solution)/shard_map/ppermute | solution.py:535
  44.7 7.1 %collective-permute-start.5 = (bf16[640,128]{1,0:T(8,128)(2,1)S(1)}, bf16[640,128]{1,0:T(8,128)(2,1)S(1)}, u32[]{:S(2)}, u32[]{:S(2)}) collective-permute-start(bf16[640,128]{1,0:T(8,128)(2,1)S(1)} %pad_maximum_fusion.8), channel_id=1, source_target_pairs={{0,3},{1,0},{2,1},{3,2},{4,7},{5,4},{6,5},{7,6},{8,11},{9,8},{10,9... | collective-permute-start | bytes 491528 | tf_op jit(solution)/shard_map/ppermute | solution.py:535
  52.3 5.7 %copy-start.4 = (bf16[4,4,496,128]{3,2,1,0:T(8,128)(2,1)}, bf16[4,4,496,128]{3,2,1,0:T(8,128)(2,1)S(1)}, u32[]{:S(2)}) copy-start(bf16[4,4,496,128]{3,2,1,0:T(8,128)(2,1)S(1)} %pad_maximum_fusion.2.first) | copy-start | bytes 6094852
  52.3 5.7 %collective-permute-start.9 = (bf16[4,4,496,128]{3,2,1,0:T(8,128)(2,1)S(1)}, bf16[4,4,496,128]{3,2,1,0:T(8,128)(2,1)}, u32[]{:S(2)}, u32[]{:S(2)}) collective-permute-start(bf16[4,4,496,128]{3,2,1,0:T(8,128)(2,1)S(1)} %pad_maximum_fusion.2.first), channel_id=1, source_target_pairs={{0,4},{4,0},{1,5},{5,1},{2,6},{6,2},{3,7},{7,3},{8,12},{12,8},{9,1... | collective-permute-start | bytes 6094856 | tf_op jit(solution)/shard_map/ppermute | solution.py:530
  53.8 33.0 %collective-permute-start.10 = (bf16[4,640,128]{2,1,0:T(8,128)(2,1)S(1)}, bf16[4,640,128]{2,1,0:T(8,128)(2,1)S(1)}, u32[]{:S(2)}, u32[]{:S(2)}) collective-permute-start(bf16[4,640,128]{2,1,0:T(8,128)(2,1)S(1)} %pad_maximum_fusion.4), channel_id=1, source_target_pairs={{0,8},{8,0},{16,24},{24,16},{1,9},{9,1},{17,25},{25,17},{2,10},{10... | collective-permute-start | bytes 1966088 | tf_op jit(solution)/shard_map/ppermute | solution.py:530
  55.2 31.6 %collective-permute-start.11 = (bf16[4,640,128]{2,1,0:T(8,128)(2,1)S(1)}, bf16[4,640,128]{2,1,0:T(8,128)(2,1)}, u32[]{:S(2)}, u32[]{:S(2)}) collective-permute-start(bf16[4,640,128]{2,1,0:T(8,128)(2,1)S(1)} %pad_maximum_fusion.4), channel_id=1, source_target_pairs={{0,16},{8,24},{16,0},{24,8},{1,17},{9,25},{17,1},{25,9},{2,18},{10... | collective-permute-start | bytes 1966088 | tf_op jit(solution)/shard_map/ppermute | solution.py:530
  56.7 42.6 %collective-permute-start.12 = (bf16[4,640,128]{2,1,0:T(8,128)(2,1)S(1)}, bf16[4,640,128]{2,1,0:T(8,128)(2,1)}, u32[]{:S(2)}, u32[]{:S(2)}) collective-permute-start(bf16[4,640,128]{2,1,0:T(8,128)(2,1)S(1)} %pad_maximum_fusion.4), channel_id=1, source_target_pairs={{0,24},{8,16},{16,8},{24,0},{1,25},{9,17},{17,9},{25,1},{2,26},{10... | collective-permute-start | bytes 1966088 | tf_op jit(solution)/shard_map/ppermute | solution.py:530
  86.8 16.4 %copy-start.39 = (f32[4,1,128]{2,1,0:T(1,128)S(1)}, f32[4,1,128]{2,1,0:T(1,128)}, u32[]{:S(2)}) copy-start(f32[4,1,128]{2,1,0:T(1,128)} %get-tuple-element.84) | copy-start | bytes 6148
  86.8 12.5 %copy-start.11 = (bf16[4,640,128]{2,1,0:T(8,128)(2,1)}, bf16[4,640,128]{2,1,0:T(8,128)(2,1)S(1)}, u32[]{:S(2)}) copy-start(bf16[4,640,128]{2,1,0:T(8,128)(2,1)S(1)} %collective-permute-done.10) | copy-start | bytes 1966084
  101.7 9.5 %copy-start.3 = (bf16[4,4,640,128]{3,2,1,0:T(8,128)(2,1)}, bf16[4,4,640,128]{3,2,1,0:T(8,128)(2,1)S(1)}, u32[]{:S(2)}) copy-start(bf16[4,4,640,128]{3,2,1,0:T(8,128)(2,1)S(1)} %pad_maximum_fusion.1.first) | copy-start | bytes 7864324
  101.7 9.5 %collective-permute-start.14 = (bf16[4,4,640,128]{3,2,1,0:T(8,128)(2,1)S(1)}, bf16[4,4,640,128]{3,2,1,0:T(8,128)(2,1)}, u32[]{:S(2)}, u32[]{:S(2)}) collective-permute-start(bf16[4,4,640,128]{3,2,1,0:T(8,128)(2,1)S(1)} %pad_maximum_fusion.1.first), channel_id=1, source_target_pairs={{0,4},{4,0},{1,5},{5,1},{2,6},{6,2},{3,7},{7,3},{8,12},{12,8},{9,1... | collective-permute-start | bytes 7864328 | tf_op jit(solution)/shard_map/ppermute | solution.py:530
  104.3 7.0 %collective-permute-start.13 = (f32[4,256,128]{2,1,0:T(8,128)S(1)}, f32[4,256,128]{2,1,0:T(8,128)S(1)}, u32[]{:S(2)}, u32[]{:S(2)}) collective-permute-start(f32[4,256,128]{2,1,0:T(8,128)S(1)} %broadcast_add_fusion.1), channel_id=1, source_target_pairs={{0,4},{1,5},{2,6},{3,7},{8,12},{9,13},{10,14},{11,15},{16,20},{17,... | collective-permute-start | bytes 1572872 | tf_op jit(solution)/shard_map/ppermute | solution.py:514
  253.0 6.3 %copy-start.46 = (bf16[2048,1024]{1,0:T(8,128)(2,1)S(1)}, bf16[2048,1024]{1,0:T(8,128)(2,1)}, u32[]{:S(2)}) copy-start(bf16[2048,1024]{1,0:T(8,128)(2,1)} %get-tuple-element.92.normed) | copy-start | bytes 12582916
  253.0 6.3 %copy-start.48 = (bf16[2048,704]{1,0:T(8,128)(2,1)S(1)}, bf16[2048,704]{1,0:T(8,128)(2,1)}, u32[]{:S(2)}) copy-start(bf16[2048,704]{1,0:T(8,128)(2,1)} %get-tuple-element.100) | copy-start | bytes 8650756
  259.3 3.3 copy-start.1
  259.3 3.3 copy-start.47
  262.6 3.3 copy-start
  262.6 3.3 copy-start.45
  297.0 3.8 collective-permute-start.15
  301.6 70.3 %copy-start.38 = (f32[1,1024]{1,0:T(1,128)S(1)}, f32[1,1024]{1,0:T(1,128)}, u32[]{:S(2)}) copy-start(f32[1,1024]{1,0:T(1,128)} %get-tuple-element.121) | copy-start | bytes 12292
  301.6 70.3 %copy-start.40 = (f32[1,256]{1,0:T(1,128)S(1)}, f32[1,256]{1,0:T(1,128)}, u32[]{:S(2)}) copy-start(f32[1,256]{1,0:T(1,128)} %get-tuple-element.122) | copy-start | bytes 3076
  301.6 82.6 %copy-start.37 = (f32[128]{0:T(128)S(1)}, f32[128]{0:T(128)}, u32[]{:S(2)}) copy-start(f32[128]{0:T(128)} %param.45) | copy-start | bytes 1540
  301.6 82.6 %copy-start.41 = (f32[128]{0:T(128)S(1)}, f32[128]{0:T(128)}, u32[]{:S(2)}) copy-start(f32[128]{0:T(128)} %param.47) | copy-start | bytes 1540
  301.6 82.6 %copy-start.42 = (f32[128]{0:T(128)S(1)}, f32[128]{0:T(128)}, u32[]{:S(2)}) copy-start(f32[128]{0:T(128)} %param.46) | copy-start | bytes 1540
  301.7 83.2 %copy-start.29 = (f32[128,16]{0,1:T(8,128)S(1)}, f32[128,16]{0,1:T(8,128)}, u32[]{:S(2)}) copy-start(f32[128,16]{0,1:T(8,128)} %param.39) | copy-start | bytes 24580
  301.7 83.2 %copy-start.32 = (f32[128,16]{0,1:T(8,128)S(1)}, f32[128,16]{0,1:T(8,128)}, u32[]{:S(2)}) copy-start(f32[128,16]{0,1:T(8,128)} %param.41) | copy-start | bytes 24580
  301.7 83.1 %copy-start.33 = (f32[128,16]{0,1:T(8,128)S(1)}, f32[128,16]{0,1:T(8,128)}, u32[]{:S(2)}) copy-start(f32[128,16]{0,1:T(8,128)} %param.40) | copy-start | bytes 24580
  301.7 83.8 %copy-start.25 = (f32[16,128]{1,0:T(8,128)S(1)}, f32[16,128]{1,0:T(8,128)}, u32[]{:S(2)}) copy-start(f32[16,128]{1,0:T(8,128)} %param.42) | copy-start | bytes 24580
  301.7 83.8 %copy-start.34 = (f32[16,128]{1,0:T(8,128)S(1)}, f32[16,128]{1,0:T(8,128)}, u32[]{:S(2)}) copy-start(f32[16,128]{1,0:T(8,128)} %param.44) | copy-start | bytes 24580
  301.7 83.8 %copy-start.35 = (f32[16,128]{1,0:T(8,128)S(1)}, f32[16,128]{1,0:T(8,128)}, u32[]{:S(2)}) copy-start(f32[16,128]{1,0:T(8,128)} %param.43) | copy-start | bytes 24580
  301.7 84.4 %copy-start.27 = (f32[2304]{0:T(1024)S(1)}, f32[2304]{0:T(1024)}, u32[]{:S(2)}) copy-start(f32[2304]{0:T(1024)} %param.57) | copy-start | bytes 27652
  301.7 84.4 %copy-start.30 = (f32[2304]{0:T(1024)S(1)}, f32[2304]{0:T(1024)}, u32[]{:S(2)}) copy-start(f32[2304]{0:T(1024)} %param.59) | copy-start | bytes 27652
  301.8 84.4 %copy-start.31 = (f32[2304]{0:T(1024)S(1)}, f32[2304]{0:T(1024)}, u32[]{:S(2)}) copy-start(f32[2304]{0:T(1024)} %param.58) | copy-start | bytes 27652
  370.2 16.5 %collective-permute-start.16 = (f32[4,128,768]{2,1,0:T(8,128)}, f32[4,128,768]{2,1,0:T(8,128)S(1)}, u32[]{:S(2)}, u32[]{:S(2)}) collective-permute-start(f32[4,128,768]{2,1,0:T(8,128)} %get-tuple-element.117), channel_id=1, source_target_pairs={{0,4},{4,0},{1,5},{5,1},{2,6},{6,2},{3,7},{7,3},{8,12},{12,8},{9,1... | collective-permute-start | bytes 4718600 | tf_op jit(solution)/shard_map/ppermute | solution.py:530
  373.3 1.4 collective-permute-start.21
  374.8 4.9 %collective-permute-start.22 = (f32[20864]{0:T(1024)S(1)}, f32[20864]{0:T(1024)S(1)}, u32[]{:S(2)}, u32[]{:S(2)}) collective-permute-start(f32[20864]{0:T(1024)S(1)} %add.264), channel_id=1, source_target_pairs={{0,8},{8,0},{16,24},{24,16},{1,9},{9,1},{17,25},{25,17},{2,10},{10... | collective-permute-start | bytes 250376 | tf_op jit(solution)/shard_map/ppermute | solution.py:530
  379.6 4.6 %collective-permute-start.23 = (f32[20864]{0:T(1024)S(1)}, f32[20864]{0:T(1024)S(1)}, u32[]{:S(2)}, u32[]{:S(2)}) collective-permute-start(f32[20864]{0:T(1024)S(1)} %add.265), channel_id=1, source_target_pairs={{0,16},{8,24},{16,0},{24,8},{1,17},{9,25},{17,1},{25,9},{2,18},{10... | collective-permute-start | bytes 250376 | tf_op jit(solution)/shard_map/ppermute | solution.py:530
  388.6 3.2 copy-start.2
  388.7 9.5 %collective-permute-start.17 = (f32[2,64,768]{2,1,0:T(8,128)S(1)}, f32[2,64,768]{2,1,0:T(8,128)S(1)}, u32[]{:S(2)}, u32[]{:S(2)}) collective-permute-start(f32[2,64,768]{2,1,0:T(8,128)S(1)} %dynamic-slice_bitcast_fusion.1), channel_id=1, source_target_pairs={{0,8},{8,0},{16,24},{24,16},{1,9},{9,1},{17,25},{25,17},{2,10},{10... | collective-permute-start | bytes 1179656 | tf_op jit(solution)/shard_map/ppermute | solution.py:530
  390.0 9.9 %collective-permute-start.19 = (f32[2,64,768]{2,1,0:T(8,128)S(1)}, f32[2,64,768]{2,1,0:T(8,128)S(1)}, u32[]{:S(2)}, u32[]{:S(2)}) collective-permute-start(f32[2,64,768]{2,1,0:T(8,128)S(1)} %dynamic-slice_bitcast_fusion), channel_id=1, source_target_pairs={{0,16},{8,24},{16,0},{24,8},{1,17},{9,25},{17,1},{25,9},{2,18},{10... | collective-permute-start | bytes 1179656 | tf_op jit(solution)/shard_map/ppermute | solution.py:530
  393.5 12.3 %copy-start.8 = (f32[2,128,256]{2,1,0:T(8,128)S(1)}, f32[2,128,256]{2,1,0:T(8,128)}, u32[]{:S(2)}) copy-start(f32[2,128,256]{2,1,0:T(8,128)} %param.36) | copy-start | bytes 786436
  393.5 12.3 %copy-start.18 = (f32[2,128,256]{2,1,0:T(8,128)S(1)}, f32[2,128,256]{2,1,0:T(8,128)}, u32[]{:S(2)}) copy-start(f32[2,128,256]{2,1,0:T(8,128)} %param.38) | copy-start | bytes 786436
  393.6 12.3 %copy-start.19 = (f32[2,128,256]{2,1,0:T(8,128)S(1)}, f32[2,128,256]{2,1,0:T(8,128)}, u32[]{:S(2)}) copy-start(f32[2,128,256]{2,1,0:T(8,128)} %param.37) | copy-start | bytes 786436
  398.2 8.7 %copy-start.15 = (f32[2,128,128]{2,1,0:T(8,128)S(1)}, f32[2,128,128]{2,1,0:T(8,128)}, u32[]{:S(2)}) copy-start(f32[2,128,128]{2,1,0:T(8,128)} %param.33) | copy-start | bytes 393220
  398.2 8.7 %copy-start.22 = (f32[2,128,128]{2,1,0:T(8,128)S(1)}, f32[2,128,128]{2,1,0:T(8,128)}, u32[]{:S(2)}) copy-start(f32[2,128,128]{2,1,0:T(8,128)} %param.35) | copy-start | bytes 393220
  398.2 8.6 %copy-start.23 = (f32[2,128,128]{2,1,0:T(8,128)S(1)}, f32[2,128,128]{2,1,0:T(8,128)}, u32[]{:S(2)}) copy-start(f32[2,128,128]{2,1,0:T(8,128)} %param.34) | copy-start | bytes 393220
  398.3 5.7 %collective-permute-start.18 = (f32[64,768]{1,0:T(8,128)S(1)}, f32[64,768]{1,0:T(8,128)S(1)}, u32[]{:S(2)}, u32[]{:S(2)}) collective-permute-start(f32[64,768]{1,0:T(8,128)S(1)} %dynamic-slice_bitcast_fusion.3), channel_id=1, source_target_pairs={{0,16},{8,24},{16,0},{24,8},{1,17},{9,25},{17,1},{25,9},{2,18},{10... | collective-permute-start | bytes 589832 | tf_op jit(solution)/shard_map/ppermute | solution.py:530
  400.0 5.7 %collective-permute-start.20 = (f32[64,768]{1,0:T(8,128)S(1)}, f32[64,768]{1,0:T(8,128)S(1)}, u32[]{:S(2)}, u32[]{:S(2)}) collective-permute-start(f32[64,768]{1,0:T(8,128)S(1)} %dynamic-slice_bitcast_fusion.2), channel_id=1, source_target_pairs={{0,8},{8,0},{16,24},{24,16},{1,9},{9,1},{17,25},{25,17},{2,10},{10... | collective-permute-start | bytes 589832 | tf_op jit(solution)/shard_map/ppermute | solution.py:530
  (11 other events, 22.2 us)
Sparse Core Ops, SparseCore 0:
  11.5 141.9 all-gather.1
  271.6 75.9 reduce-scatter.1

commit v5 on v4

--- a/solution.py
+++ b/solution.py
@@ -16,7 +16,6 @@
 DECAY_ROWS = 32
 ROWS = 256
 FFN_ROWS = 512
-FFN_CUTS = 8
 STEP = 10
 
 NORM_EPS = 1e-06
@@ -30,7 +29,7 @@
 RATE_RANK = 0.1
 RATE_BIAS = 1.5
 RATE_GAIN = 0.3
-VMEM_LIMIT = 60 * 1024 * 1024
+VMEM_LIMIT = 62 * 1024 * 1024
 
 F32 = jnp.float32
 BF16 = jnp.bfloat16
@@ -225,83 +224,61 @@
 
 
 def ffn_kernel(
-    weight_pieces, info, normed, back, middle, weight, gain,
+    info, normed, back, middle, weight, gain,
     active_out, back_gate_out, back_up_out, layer_out, back_middle_out, back_attn_out, gain_out,
-    ffn_ref, back_ref, active_ref, back_gate_ref, back_up_ref,
+    ffn_ref, back_ref, turned_ref, active_ref, back_gate_ref, back_up_ref,
 ):
-    step, piece = pl.program_id(0), pl.program_id(1)
+    piece, step = pl.program_id(0), pl.program_id(1)
+    pieces = pl.num_programs(0)
     units = weight.shape[2] // 3
+    count = normed.shape[0]
+    rows = pl.ds(pl.multiple_of(step * count, count), count)
 
     @pl.when((step == 0) & (piece == 0))
     def _():
         gain_out[...] = jnp.zeros_like(gain_out)
-
-    @pl.when(piece == 0)
-    def _():
         ffn_ref[...] = jnp.zeros_like(ffn_ref)
         back_ref[...] = jnp.zeros_like(back_ref)
+
+    @pl.when(step == 0)
+    def _():
+        for kind in range(3):
+            for group in range(GROUPS):
+                turned_ref[kind, group * LANES : (group + 1) * LANES] = weight[
+                    group, 0, kind * units : (kind + 1) * units
+                ].T
 
     def rows_of(start):
         return jnp.concatenate(
             [weight[group, 0, start : start + units] for group in range(GROUPS)], axis=1
         )
 
-    gate_weight, up_weight, down_weight = rows_of(0), rows_of(units), rows_of(2 * units)
-    half = normed.shape[0] // 2
-    third = half // FFN_CUTS
-
-    def made(part):
-        span = slice(part * half, (part + 1) * half)
-        yield dot(normed[span], gate_weight, NT)
-        yield dot(normed[span], up_weight, NT)
-        yield dot(back[span], down_weight, NT)
-
-    def elementwise(part, values, cut):
-        span = slice(cut * third, (cut + 1) * third)
-        target = slice(part * half + cut * third, part * half + (cut + 1) * third)
-        gate_values, upward, back_active = [item[span] for item in values]
-        share = sigmoid(gate_values)
-        silu = gate_values * share
-        active_ref[target] = (silu * upward).astype(BF16)
-        back_gate_ref[target] = (
-            back_active * upward * (share * (1.0 + gate_values * (1.0 - share)))
-        ).astype(BF16)
-        back_up_ref[target] = (back_active * silu).astype(BF16)
-
-    def added(part):
-        span = slice(part * half, (part + 1) * half)
-        ffn_ref[span] += dot(active_ref[span], down_weight)
-        yield
-        back_ref[span] += dot(back_gate_ref[span], gate_weight)
-        yield
-        back_ref[span] += dot(back_up_ref[span], up_weight)
-        yield
-
-    first = list(made(0))
-    second = []
-    for index, item in enumerate(made(1)):
-        second.append(item)
-        for cut in range(index * FFN_CUTS // 3, (index + 1) * FFN_CUTS // 3):
-            elementwise(0, first, cut)
-    for index, _ in enumerate(added(0)):
-        for cut in range(index * FFN_CUTS // 3, (index + 1) * FFN_CUTS // 3):
-            elementwise(1, second, cut)
-    for _ in added(1):
-        pass
-
-    @pl.when(piece == info[2 * GROUPS + weight_pieces])
+    gate_values = dot(normed[...], turned_ref[0])
+    upward = dot(normed[...], turned_ref[1])
+    back_active = dot(back[...], turned_ref[2])
+    share = sigmoid(gate_values)
+    silu = gate_values * share
+    active_ref[...] = (silu * upward).astype(BF16)
+    back_gate_ref[...] = (
+        back_active * upward * (share * (1.0 + gate_values * (1.0 - share)))
+    ).astype(BF16)
+    back_up_ref[...] = (back_active * silu).astype(BF16)
+    ffn_ref[rows] += dot(active_ref[...], rows_of(2 * units))
+    back_ref[rows] += dot(back_gate_ref[...], rows_of(0)) + dot(back_up_ref[...], rows_of(units))
+
+    @pl.when(piece == info[2 * GROUPS + pieces])
     def _():
         active_out[...] = active_ref[...]
         back_gate_out[...] = back_gate_ref[...]
         back_up_out[...] = back_up_ref[...]
 
-    @pl.when(piece == pl.num_programs(1) - 1)
+    @pl.when(piece == pieces - 1)
     def _():
         mid = middle[...]
-        layer_out[...] = (mid + ffn_ref[...]).astype(BF16)
+        layer_out[...] = (mid + ffn_ref[rows]).astype(BF16)
         inverse = inverse_rms(mid, NORM_EPS)
         unit = mid * inverse
-        total = back_ref[...]
+        total = back_ref[rows]
         weighted = total * gain[...]
         back_middle = back[...].astype(F32) + inverse * (
             weighted - unit * jnp.mean(weighted * unit, axis=-1, keepdims=True)
@@ -595,11 +572,12 @@
     return gather_plain(pack)
 
 
-def scatter_rows(kept, sent, early):
+def finish_sums(kept, sent, sums, early):
     columns = kept.shape[-1]
     if not staged():
         whole = jnp.concatenate([kept, sent]).reshape(-1, columns)
-        return lax.psum_scatter(whole, ("dp", "ctx"), scatter_dimension=0, tiled=True), early
+        share = lax.psum_scatter(whole, ("dp", "ctx"), scatter_dimension=0, tiled=True)
+        return share, lax.psum(sums, ("dp", "ctx")), early
     device = lax.axis_index("dp")
     row, column = device // 2, device % 2
 
@@ -607,23 +585,19 @@
         return lax.dynamic_index_in_dim(array, index, axis, keepdims=False)
 
     value = kept + swap(sent, "ctx", 1)
-    value, early = lax.optimization_barrier((value, early))
+    sums = sums + swap(sums, "ctx", 1)
+    value, sums, early = lax.optimization_barrier((value, sums, early))
     value = value.reshape(2, 2, LANES, columns)
     half = LANES // 2
     upper, lower = value[:, :, :half], value[:, :, half:]
     upper = pick(upper, 1, column) + swap(pick(upper, 1, 1 - column), "dp", 1)
     lower = pick(lower, 0, row) + swap(pick(lower, 0, 1 - row), "dp", 2)
+    sums = sums + swap(sums, "dp", 1)
+    upper, lower, sums = lax.optimization_barrier((upper, lower, sums))
     upper = pick(upper, 0, row) + swap(pick(upper, 0, 1 - row), "dp", 2)
     lower = pick(lower, 0, column) + swap(pick(lower, 0, 1 - column), "dp", 1)
-    return jnp.concatenate([upper, lower]), early
-
-
-def total_over(value):
-    if not staged():
-        return lax.psum(value, ("dp", "ctx"))
-    for axis, distance in (("ctx", 1), ("dp", 1), ("dp", 2)):
-        value = value + swap(value, axis, distance)
-    return value
+    sums = sums + swap(sums, "dp", 2)
+    return jnp.concatenate([upper, lower]), sums, early
 
 
 def adamw(weight_now, grad_now, mean_now, square_now, rate_value, decay_value):
@@ -826,20 +800,30 @@
         rows * heads * 4 * 1024,
     )
 
-    wide_spec = pl.BlockSpec((FFN_ROWS, width), lambda i, j, *_: (i, 0))
-    own_spec = pl.BlockSpec((FFN_ROWS, units), lambda i, j, *_: (i, 0))
-    wide_gain_spec = pl.BlockSpec((1, width), lambda i, j, *_: (0, 0))
+    tiles = rows // FFN_ROWS
+
+    def last_only(j, i, info):
+        return (jnp.where(j == heads - 1, i, 0), 0)
+
+    def own_only(j, i, info):
+        own = info[2 * GROUPS + heads]
+        return (jnp.where(j < own, 0, jnp.where(j > own, tiles - 1, i)), 0)
+
+    tile_spec = pl.BlockSpec((FFN_ROWS, width), lambda j, i, *_: (i, 0))
+    last_spec = pl.BlockSpec((FFN_ROWS, width), last_only, pipeline_mode=pl.Buffered(1))
+    own_spec = pl.BlockSpec((FFN_ROWS, units), own_only, pipeline_mode=pl.Buffered(1))
+    tile_gain_spec = pl.BlockSpec((1, width), lambda j, i, *_: (0, 0))
     active, back_gate, back_up, layer_out, back_middle, back_attn, gain_two_part = call(
-        functools.partial(ffn_kernel, heads),
-        (rows // FFN_ROWS, heads),
-        [
-            wide_spec,
-            wide_spec,
-            wide_spec,
-            pl.BlockSpec((GROUPS, 1, 3 * units, LANES), lambda i, j, *_: (0, j, 0, 0)),
-            wide_gain_spec,
-        ],
-        [own_spec, own_spec, own_spec, wide_spec, wide_spec, wide_spec, wide_gain_spec],
+        ffn_kernel,
+        (heads, tiles),
+        [
+            tile_spec,
+            tile_spec,
+            last_spec,
+            pl.BlockSpec((GROUPS, 1, 3 * units, LANES), lambda j, i, *_: (0, j, 0, 0)),
+            tile_gain_spec,
+        ],
+        [own_spec, own_spec, own_spec, last_spec, last_spec, last_spec, tile_gain_spec],
         [
             shaped((rows, units), BF16),
             shaped((rows, units), BF16),
@@ -850,8 +834,9 @@
             shaped((1, width)),
         ],
         [
-            pltpu.VMEM((FFN_ROWS, width), F32),
-            pltpu.VMEM((FFN_ROWS, width), F32),
+            pltpu.VMEM((rows, width), F32),
+            pltpu.VMEM((rows, width), F32),
+            pltpu.VMEM((3, width, units), BF16),
             pltpu.VMEM((FFN_ROWS, units), BF16),
             pltpu.VMEM((FFN_ROWS, units), BF16),
             pltpu.VMEM((FFN_ROWS, units), BF16),
@@ -957,22 +942,20 @@
         2 * rows * width * columns * heads * 2,
         rows * heads * 4 * 2048,
     )
-    mixer_share, early_share = scatter_rows(kept, sent_away, early_share)
     own = info[-1]
     decay_out_own = lax.dynamic_index_in_dim(decay_out_grad, own, 0, keepdims=False)
     bias_own = lax.dynamic_index_in_dim(bias_grad, own, 0, keepdims=False)
-    sums = total_over(
-        jnp.concatenate(
-            [
-                gain_one_part.reshape(-1),
-                gain_two_part.reshape(-1),
-                head_gain_part.reshape(-1),
-                bias_own.reshape(-1),
-                decay_out_own.reshape(-1),
-                rank_grad.reshape(-1),
-            ]
-        )
-    )
+    sums = jnp.concatenate(
+        [
+            gain_one_part.reshape(-1),
+            gain_two_part.reshape(-1),
+            head_gain_part.reshape(-1),
+            bias_own.reshape(-1),
+            decay_out_own.reshape(-1),
+            rank_grad.reshape(-1),
+        ]
+    )
+    mixer_share, sums, early_share = finish_sums(kept, sent_away, sums, early_share)
     gain_count = gains.shape[0]
     decay_start = gain_count + HK
     rank_start = decay_start + ranks * HK

time: 421 us -> 428 us (1.017)
  Pallas kernels: 261 us -> 278 us
  waiting for transfers between devices: 52.5 us -> 44 us
    pallas_call x5, Pallas kernels: 261 us -> 278 us  [call(): pl.pallas_call(kernel, grid_spec=pltpu.PrefetchScalarGridSpec(num_scalar_...]
    ppermute x16, waiting for transfers between devices: 29.3 us -> 21.5 us  [swap(): lax.ppermute(value, axis, [(source, source ^ distance) for source in rang...]
  transfers between devices with their start and end apart: 26 -> 26, of which waited for: 16 -> 14; matrix products, arithmetic and copies ran while one was open for 6% -> 6% of each run, Pallas kernels for 39% -> 38%
where the time goes in v5:
time: 428 us; the launch traced here: 422 us
  Pallas kernels  278 us (65%)
  waiting for transfers between devices  44 us (10%)
  starting transfers between devices  34.5 us (8%)
  other arithmetic  28.4 us (7%)
  between operations  15.9 us (4%)
  matrix products  14 us (3%)
  local copies, waits for them, and re-layouts  7.45 us (2%)
    pallas_call x5, Pallas kernels, call(): pl.pallas_call(kernel, grid_spec=pltpu.PrefetchScalarGridSpec(num_scalar_...  278 us
    ppermute x16, waiting for transfers between devices, swap(): lax.ppermute(value, axis, [(source, source ^ distance) for source in rang...  21.5 us
    ppermute x6, waiting for transfers between devices, shift(): lax.ppermute(value, axis, [(source, (source + distance) % count) for sour...  19.4 us
    ppermute x6, starting transfers between devices, shift(): lax.ppermute(value, axis, [(source, (source + distance) % count) for sour...  17.5 us
    dot_general x4, matrix products, dot(): return lax.dot_general(left, right, dims, preferred_element_type=F32)  14 us
    ppermute x16, starting transfers between devices, swap(): lax.ppermute(value, axis, [(source, source ^ distance) for source in rang...  12.7 us
  transfers between devices with their start and end apart: 26, of which 14 were waited for; matrix products, arithmetic and copies ran while one was open for 6% of the time, Pallas kernels for 38%

profile of v5, /device:TPU:0, one launch (start us, length us, event | category | flops | bytes accessed | tf_op | source)
XLA Modules:
  0.0 422.2 jit_solution(707414597994177982)
XLA Ops:
  7.3 1.3 convert.37
  8.7 1.0 convert_bitcast_fusion
  9.7 0.8 pad_maximum_fusion.5
  11.2 3.0 collective-permute-start
  14.3 2.6 collective-permute-start.1
  16.9 1.3 collective-permute-start.2
  18.3 2.4 collective-permute-done
  20.6 4.6 %collective-permute-done.1 = bf16[496,128]{1,0:T(8,128)(2,1)S(1)} collective-permute-done((bf16[496,128]{1,0:T(8,128)(2,1)S(1)}, bf16[496,128]{1,0:T(8,128)(2,1)S(1)}, u32[]{:S(2)}, u32[]{:S(2)}) %collective-permute-start.1) | collective-permute-done | bytes 127008 | tf_op jit(solution)/shard_map/ppermute | solution.py:512
  25.3 1.6 collective-permute-start.6
  26.9 1.5 collective-permute-start.7
  28.9 6.1 %collective-permute-start.3 = (bf16[640,128]{1,0:T(8,128)(2,1)S(1)}, bf16[640,128]{1,0:T(8,128)(2,1)S(1)}, u32[]{:S(2)}, u32[]{:S(2)}) collective-permute-start(bf16[640,128]{1,0:T(8,128)(2,1)S(1)} %pad_maximum_fusion.8), channel_id=1, source_target_pairs={{0,1},{1,2},{2,3},{3,0},{4,5},{5,6},{6,7},{7,4},{8,9},{9,10},{10,1... | collective-permute-start | bytes 491528 | tf_op jit(solution)/shard_map/ppermute | solution.py:512
  34.9 4.1 collective-permute-start.4
  39.0 5.7 %collective-permute-done.3 = bf16[640,128]{1,0:T(8,128)(2,1)S(1)} collective-permute-done((bf16[640,128]{1,0:T(8,128)(2,1)S(1)}, bf16[640,128]{1,0:T(8,128)(2,1)S(1)}, u32[]{:S(2)}, u32[]{:S(2)}) %collective-permute-start.3) | collective-permute-done | bytes 163872 | tf_op jit(solution)/shard_map/ppermute | solution.py:512
  45.0 5.4 %collective-permute-done.4 = bf16[640,128]{1,0:T(8,128)(2,1)S(1)} collective-permute-done((bf16[640,128]{1,0:T(8,128)(2,1)S(1)}, bf16[640,128]{1,0:T(8,128)(2,1)S(1)}, u32[]{:S(2)}, u32[]{:S(2)}) %collective-permute-start.4) | collective-permute-done | bytes 163872 | tf_op jit(solution)/shard_map/ppermute | solution.py:512
  50.4 1.3 collective-permute-done.5
  52.1 1.5 pad_maximum_fusion.2.first
  53.6 0.6 pad_add_fusion.info
  54.2 0.6 fusion.33
  54.8 0.9 slice.102
  55.7 1.3 collective-permute-start.10
  57.0 1.5 collective-permute-start.11
  58.5 0.7 collective-permute-start.12
  59.2 0.6 fusion.7.decay_out
  59.9 28.7 %shard_map.509 = (bf16[2048,1024]{1,0:T(8,128)(2,1)}, f32[4,2048,384]{2,1,0:T(8,128)}, f32[2048,16]{1,0:T(8,128)}, f32[4,2048,128]{2,1,0:T(8,128)}, f32[4,2048,1...) custom-call(s32[21]{0:T(128)} %pad_add_fusion.info, ...), custom_call_target="tpu_custom_call" | custom-call | flops 6442450944 | bytes 33554432 | tf_op jit(solution)/shard_map/pallas_call | solution.py:471
  88.7 10.7 %collective-permute-done.12 = bf16[4,640,128]{2,1,0:T(8,128)(2,1)} collective-permute-done((bf16[4,640,128]{2,1,0:T(8,128)(2,1)S(1)}, bf16[4,640,128]{2,1,0:T(8,128)(2,1)}, u32[]{:S(2)}, u32[]{:S(2)}) %collective-permute-start.12) | collective-permute-done | bytes 655392 | tf_op jit(solution)/shard_map/ppermute | solution.py:507
  99.4 2.9 pad_maximum_fusion.1.first
  102.3 0.6 slice.106
  103.6 3.0 collective-permute-start.13
  106.6 3.9 broadcast_select_fusion.back
  110.5 0.8 copy-done.42
  111.3 40.3 %shard_map.510 = (f32[4,2048,128]{2,1,0:T(8,128)}, f32[4,2048,256]{2,1,0:T(8,128)}, f32[4,2048,256]{2,1,0:T(8,128)}, f32[16,4,256,128]{3,2,1,0:T(8,128)}, bf16[2...) custom-call(s32[21]{0:T(128)} %pad_add_fusion.info, ...), custom_call_target="tpu_custom_call" | custom-call | flops 15032385536 | bytes 33554432 | tf_op jit(solution)/shard_map/pallas_call | solution.py:471
  151.6 0.6 all-gather.2.cloned.1.call-done
  152.2 115.9 %shard_map.511 = (bf16[2048,704]{1,0:T(8,128)(2,1)}, bf16[2048,704]{1,0:T(8,128)(2,1)}, bf16[2048,704]{1,0:T(8,128)(2,1)}, bf16[2048,1024]{1,0:T(8,128)(2,1)}, f...) custom-call(s32[21]{0:T(128)} %pad_add_fusion.info, ...), custom_call_target="tpu_custom_call" | custom-call | flops 70866960384 | bytes 50331648 | tf_op jit(solution)/shard_map/pallas_call | solution.py:471
  268.1 6.3 %fusion.34 = f32[704,1024]{1,0:T(8,128)S(1)} fusion(bf16[2048,704]{1,0:T(8,128)(2,1)} %get-tuple-element.103, bf16[2048,1024]{1,0:T(8,128)(2,1)} %get-tuple-element.96.normed), kind=kOutput, calls=%fused_computation.115 | convolution fusion | flops 2952790016 | bytes 9961472 | tf_op jit(solution)/shard_map/dot_general | solution.py:42
  274.5 3.2 fusion.35
  277.7 3.2 fusion.36
  281.0 1.3 fusion.37
  282.3 4.3 %pad_maximum_fusion = f32[2368,1024]{1,0:T(8,128)} fusion(f32[256,1024]{1,0:T(8,128)S(1)} %fusion.37, f32[704,1024]{1,0:T(8,128)S(1)} %fusion.36, f32[704,1024]{1,0:T(8,128)S(1)} %fusion.35, f32[704,1024]{1,0:T(8,128)S(1)} %fusion.34), kind=kLoop, calls=%fused_computation | loop fusion | flops 7274496 | bytes 19398656 | tf_op jit(solution)/shard_map/concatenate | solution.py:849
  286.6 24.5 %shard_map.512 = (f32[4,2048,256]{2,1,0:T(8,128)}, bf16[4,2048,256]{2,1,0:T(8,128)(2,1)}, f32[1,256]{1,0:T(1,128)}, f32[4,256,128]{2,1,0:T(8,128)}) custom-call(bf16[2048,1024]{1,0:T(8,128)(2,1)} %get-tuple-element.108.back_attn, bf16[1024,1024]{1,0:T(8,128)(2,1)} %get-tuple-element.109.out_weight, f32[4,2048,256]{2,1,0:T(8,128)} %get-tuple-element.110.mixed_in, ...), custom_call_target="tpu_custom_call" | custom-call | flops 4294967296 | bytes 33554432 | tf_op jit(solution)/shard_map/pallas_call | solution.py:471
  311.2 1.1 broadcast_add_fusion
  312.3 1.3 collective-permute-start.15
  313.6 2.5 collective-permute-done.15.back_end
  316.1 0.8 copy-done.41
  316.9 68.4 %shard_map.513 = (f32[4,128,768]{2,1,0:T(8,128)}, f32[4,128,768]{2,1,0:T(8,128)}, f32[16,1024]{1,0:T(8,128)}, f32[2048,1024]{1,0:T(8,128)}, f32[4,16,128]{2,1,0:...) custom-call(s32[21]{0:T(128)} %pad_add_fusion.info, bf16[2048,1024]{1,0:T(8,128)(2,1)} %tokens.5, ...), custom_call_target="tpu_custom_call" | custom-call | flops 25769803776 | bytes 67108864 | tf_op jit(solution)/shard_map/pallas_call | solution.py:471
  385.4 0.9 copy.74
  386.3 0.7 constant_dynamic-update-slice_fusion.4
  387.0 0.7 constant_dynamic-update-slice_fusion.6
  387.7 0.7 bitcast_dynamic-update-slice_fusion
  388.9 0.9 collective-permute-done.17
  389.8 1.6 add.243
  392.0 0.6 collective-permute-start.19
  392.6 1.6 collective-permute-start.18
  394.3 1.2 multiply_subtract_fusion.1
  395.5 1.7 multiply_subtract_fusion
  397.3 0.8 multiply_subtract_fusion.3
  398.2 5.1 %collective-permute-done.19 = f32[2,64,768]{2,1,0:T(8,128)S(1)} collective-permute-done((f32[2,64,768]{2,1,0:T(8,128)S(1)}, f32[2,64,768]{2,1,0:T(8,128)S(1)}, u32[]{:S(2)}, u32[]{:S(2)}) %collective-permute-start.19) | collective-permute-done | bytes 393248 | tf_op jit(solution)/shard_map/ppermute | solution.py:507
  403.3 1.5 collective-permute-done.18
  405.3 1.8 collective-permute-start.21
  407.4 2.9 collective-permute-done.23
  410.5 0.6 multiply_subtract_fusion.5
  411.1 0.6 multiply_subtract_fusion.6
  411.7 0.6 multiply_subtract_fusion.7
  413.3 1.0 multiply_subtract_fusion.2
  414.3 0.8 multiply_subtract_fusion.4
  (162 shorter events, 5.3 us)
Async XLA Ops:
  7.2 3.4 copy-start.11
  7.2 3.5 copy-start.5
  7.2 3.7 copy-start.26
  7.2 3.7 copy-start.34
  7.3 3.7 copy-start.22
  7.3 11.0 %copy-start.9 = (f32[256,128]{1,0:T(8,128)S(1)}, f32[256,128]{1,0:T(8,128)}, u32[]{:S(2)}) copy-start(f32[256,128]{1,0:T(8,128)} %param.48) | copy-start | bytes 393220
  7.3 144.9 %all-gather.2.cloned.1.call-start = ((), (), s32[]{:S(2)}) async-start(), calls=%async_computation.1 | async-start | bytes 17842176 | tf_op jit(solution)/shard_map/all_gather | solution.py:570
  10.5 380.9 %reduce-scatter.2.cloned.1.call-start = ((), (), s32[]{:S(2)}) async-start(), calls=%async_computation.2 | async-start | bytes 10911744 | tf_op jit(solution)/shard_map/reduce_scatter | solution.py:858
  11.2 9.4 %collective-permute-start = (bf16[496,128]{1,0:T(8,128)(2,1)S(1)}, bf16[496,128]{1,0:T(8,128)(2,1)S(1)}, u32[]{:S(2)}, u32[]{:S(2)}) collective-permute-start(bf16[496,128]{1,0:T(8,128)(2,1)S(1)} %constant_dynamic-update-slice_fusion), channel_id=1, source_target_pairs={{0,1},{1,2},{2,3},{3,0},{4,5},{5,6},{6,7},{7,4},{8,9},{9,10},{10,1... | collective-permute-start | bytes 380936 | tf_op jit(solution)/shard_map/ppermute | solution.py:512
  14.3 11.0 %collective-permute-start.1 = (bf16[496,128]{1,0:T(8,128)(2,1)S(1)}, bf16[496,128]{1,0:T(8,128)(2,1)S(1)}, u32[]{:S(2)}, u32[]{:S(2)}) collective-permute-start(bf16[496,128]{1,0:T(8,128)(2,1)S(1)} %constant_dynamic-update-slice_fusion), channel_id=1, source_target_pairs={{0,2},{1,3},{2,0},{3,1},{4,6},{5,7},{6,4},{7,5},{8,10},{9,11},{10,... | collective-permute-start | bytes 380936 | tf_op jit(solution)/shard_map/ppermute | solution.py:512
  16.9 8.4 %collective-permute-start.2 = (bf16[496,128]{1,0:T(8,128)(2,1)S(1)}, bf16[496,128]{1,0:T(8,128)(2,1)S(1)}, u32[]{:S(2)}, u32[]{:S(2)}) collective-permute-start(bf16[496,128]{1,0:T(8,128)(2,1)S(1)} %constant_dynamic-update-slice_fusion), channel_id=1, source_target_pairs={{0,3},{1,0},{2,1},{3,2},{4,7},{5,4},{6,5},{7,6},{8,11},{9,8},{10,9... | collective-permute-start | bytes 380936 | tf_op jit(solution)/shard_map/ppermute | solution.py:512
  25.2 29.0 %copy-start.24 = (f32[2304]{0:T(1024)S(1)}, f32[2304]{0:T(1024)}, u32[]{:S(2)}) copy-start(f32[2304]{0:T(1024)} %param.57) | copy-start | bytes 27652
  25.3 26.5 %collective-permute-start.6 = (bf16[4,496,128]{2,1,0:T(8,128)(2,1)S(1)}, bf16[4,496,128]{2,1,0:T(8,128)(2,1)S(1)}, u32[]{:S(2)}, u32[]{:S(2)}) collective-permute-start(bf16[4,496,128]{2,1,0:T(8,128)(2,1)S(1)} %pad_maximum_fusion.6), channel_id=1, source_target_pairs={{0,8},{8,0},{16,24},{24,16},{1,9},{9,1},{17,25},{25,17},{2,10},{10... | collective-permute-start | bytes 1523720 | tf_op jit(solution)/shard_map/ppermute | solution.py:507
  26.9 25.0 %collective-permute-start.7 = (bf16[4,496,128]{2,1,0:T(8,128)(2,1)S(1)}, bf16[4,496,128]{2,1,0:T(8,128)(2,1)S(1)}, u32[]{:S(2)}, u32[]{:S(2)}) collective-permute-start(bf16[4,496,128]{2,1,0:T(8,128)(2,1)S(1)} %pad_maximum_fusion.6), channel_id=1, source_target_pairs={{0,16},{8,24},{16,0},{24,8},{1,17},{9,25},{17,1},{25,9},{2,18},{10... | collective-permute-start | bytes 1523720 | tf_op jit(solution)/shard_map/ppermute | solution.py:507
  28.4 23.7 %collective-permute-start.8 = (bf16[4,496,128]{2,1,0:T(8,128)(2,1)S(1)}, bf16[4,496,128]{2,1,0:T(8,128)(2,1)S(1)}, u32[]{:S(2)}, u32[]{:S(2)}) collective-permute-start(bf16[4,496,128]{2,1,0:T(8,128)(2,1)S(1)} %pad_maximum_fusion.6), channel_id=1, source_target_pairs={{0,24},{8,16},{16,8},{24,0},{1,25},{9,17},{17,9},{25,1},{2,26},{10... | collective-permute-start | bytes 1523720 | tf_op jit(solution)/shard_map/ppermute | solution.py:507
  28.9 15.8 %collective-permute-start.3 = (bf16[640,128]{1,0:T(8,128)(2,1)S(1)}, bf16[640,128]{1,0:T(8,128)(2,1)S(1)}, u32[]{:S(2)}, u32[]{:S(2)}) collective-permute-start(bf16[640,128]{1,0:T(8,128)(2,1)S(1)} %pad_maximum_fusion.8), channel_id=1, source_target_pairs={{0,1},{1,2},{2,3},{3,0},{4,5},{5,6},{6,7},{7,4},{8,9},{9,10},{10,1... | collective-permute-start | bytes 491528 | tf_op jit(solution)/shard_map/ppermute | solution.py:512
  34.9 15.5 %collective-permute-start.4 = (bf16[640,128]{1,0:T(8,128)(2,1)S(1)}, bf16[640,128]{1,0:T(8,128)(2,1)S(1)}, u32[]{:S(2)}, u32[]{:S(2)}) collective-permute-start(bf16[640,128]{1,0:T(8,128)(2,1)S(1)} %pad_maximum_fusion.8), channel_id=1, source_target_pairs={{0,2},{1,3},{2,0},{3,1},{4,6},{5,7},{6,4},{7,5},{8,10},{9,11},{10,... | collective-permute-start | bytes 491528 | tf_op jit(solution)/shard_map/ppermute | solution.py:512
  44.7 7.1 %collective-permute-start.5 = (bf16[640,128]{1,0:T(8,128)(2,1)S(1)}, bf16[640,128]{1,0:T(8,128)(2,1)S(1)}, u32[]{:S(2)}, u32[]{:S(2)}) collective-permute-start(bf16[640,128]{1,0:T(8,128)(2,1)S(1)} %pad_maximum_fusion.8), channel_id=1, source_target_pairs={{0,3},{1,0},{2,1},{3,2},{4,7},{5,4},{6,5},{7,6},{8,11},{9,8},{10,9... | collective-permute-start | bytes 491528 | tf_op jit(solution)/shard_map/ppermute | solution.py:512
  53.6 6.3 %collective-permute-start.9 = (bf16[4,4,496,128]{3,2,1,0:T(8,128)(2,1)}, bf16[4,4,496,128]{3,2,1,0:T(8,128)(2,1)}, u32[]{:S(2)}, u32[]{:S(2)}) collective-permute-start(bf16[4,4,496,128]{3,2,1,0:T(8,128)(2,1)} %pad_maximum_fusion.2.first), channel_id=1, source_target_pairs={{0,4},{4,0},{1,5},{5,1},{2,6},{6,2},{3,7},{7,3},{8,12},{12,8},{9,1... | collective-permute-start | bytes 6094856 | tf_op jit(solution)/shard_map/ppermute | solution.py:507
  55.7 32.9 %collective-permute-start.10 = (bf16[4,640,128]{2,1,0:T(8,128)(2,1)S(1)}, bf16[4,640,128]{2,1,0:T(8,128)(2,1)S(1)}, u32[]{:S(2)}, u32[]{:S(2)}) collective-permute-start(bf16[4,640,128]{2,1,0:T(8,128)(2,1)S(1)} %pad_maximum_fusion.4), channel_id=1, source_target_pairs={{0,8},{8,0},{16,24},{24,16},{1,9},{9,1},{17,25},{25,17},{2,10},{10... | collective-permute-start | bytes 1966088 | tf_op jit(solution)/shard_map/ppermute | solution.py:507
  57.0 31.6 %collective-permute-start.11 = (bf16[4,640,128]{2,1,0:T(8,128)(2,1)S(1)}, bf16[4,640,128]{2,1,0:T(8,128)(2,1)S(1)}, u32[]{:S(2)}, u32[]{:S(2)}) collective-permute-start(bf16[4,640,128]{2,1,0:T(8,128)(2,1)S(1)} %pad_maximum_fusion.4), channel_id=1, source_target_pairs={{0,16},{8,24},{16,0},{24,8},{1,17},{9,25},{17,1},{25,9},{2,18},{10... | collective-permute-start | bytes 1966088 | tf_op jit(solution)/shard_map/ppermute | solution.py:507
  58.5 40.8 %collective-permute-start.12 = (bf16[4,640,128]{2,1,0:T(8,128)(2,1)S(1)}, bf16[4,640,128]{2,1,0:T(8,128)(2,1)}, u32[]{:S(2)}, u32[]{:S(2)}) collective-permute-start(bf16[4,640,128]{2,1,0:T(8,128)(2,1)S(1)} %pad_maximum_fusion.4), channel_id=1, source_target_pairs={{0,24},{8,16},{16,8},{24,0},{1,25},{9,17},{17,9},{25,1},{2,26},{10... | collective-permute-start | bytes 1966088 | tf_op jit(solution)/shard_map/ppermute | solution.py:507
  88.6 14.9 %copy-start.37 = (f32[4,1,128]{2,1,0:T(1,128)S(1)}, f32[4,1,128]{2,1,0:T(1,128)}, u32[]{:S(2)}) copy-start(f32[4,1,128]{2,1,0:T(1,128)} %get-tuple-element.88) | copy-start | bytes 6148
  88.6 14.9 %copy-start.13 = (f32[4,256,128]{2,1,0:T(8,128)S(1)}, f32[4,256,128]{2,1,0:T(8,128)}, u32[]{:S(2)}) copy-start(f32[4,256,128]{2,1,0:T(8,128)} %get-tuple-element.91) | copy-start | bytes 1572868
  102.3 8.2 %collective-permute-start.14 = (bf16[4,4,640,128]{3,2,1,0:T(8,128)(2,1)}, bf16[4,4,640,128]{3,2,1,0:T(8,128)(2,1)}, u32[]{:S(2)}, u32[]{:S(2)}) collective-permute-start(bf16[4,4,640,128]{3,2,1,0:T(8,128)(2,1)} %pad_maximum_fusion.1.first), channel_id=1, source_target_pairs={{0,4},{4,0},{1,5},{5,1},{2,6},{6,2},{3,7},{7,3},{8,12},{12,8},{9,1... | collective-permute-start | bytes 7864328 | tf_op jit(solution)/shard_map/ppermute | solution.py:507
  103.6 6.9 %collective-permute-start.13 = (f32[4,256,128]{2,1,0:T(8,128)S(1)}, f32[4,256,128]{2,1,0:T(8,128)S(1)}, u32[]{:S(2)}, u32[]{:S(2)}) collective-permute-start(f32[4,256,128]{2,1,0:T(8,128)S(1)} %broadcast_add_fusion.1), channel_id=1, source_target_pairs={{0,4},{1,5},{2,6},{3,7},{8,12},{9,13},{10,14},{11,15},{16,20},{17,... | collective-permute-start | bytes 1572872 | tf_op jit(solution)/shard_map/ppermute | solution.py:491
  268.1 6.3 %copy-start.44 = (bf16[2048,1024]{1,0:T(8,128)(2,1)S(1)}, bf16[2048,1024]{1,0:T(8,128)(2,1)}, u32[]{:S(2)}) copy-start(bf16[2048,1024]{1,0:T(8,128)(2,1)} %get-tuple-element.96.normed) | copy-start | bytes 12582916
  268.1 6.3 %copy-start.46 = (bf16[2048,704]{1,0:T(8,128)(2,1)S(1)}, bf16[2048,704]{1,0:T(8,128)(2,1)}, u32[]{:S(2)}) copy-start(bf16[2048,704]{1,0:T(8,128)(2,1)} %get-tuple-element.104) | copy-start | bytes 8650756
  274.4 3.3 copy-start.1
  274.5 3.3 copy-start.45
  277.7 3.3 copy-start
  277.7 3.3 copy-start.43
  312.3 3.8 collective-permute-start.15
  316.9 70.1 %copy-start.36 = (f32[1,1024]{1,0:T(1,128)S(1)}, f32[1,1024]{1,0:T(1,128)}, u32[]{:S(2)}) copy-start(f32[1,1024]{1,0:T(1,128)} %get-tuple-element.123) | copy-start | bytes 12292
  316.9 70.1 %copy-start.38 = (f32[1,256]{1,0:T(1,128)S(1)}, f32[1,256]{1,0:T(1,128)}, u32[]{:S(2)}) copy-start(f32[1,256]{1,0:T(1,128)} %get-tuple-element.124) | copy-start | bytes 3076
  385.3 4.5 %collective-permute-start.16 = (f32[4,128,768]{2,1,0:T(8,128)}, f32[4,128,768]{2,1,0:T(8,128)S(1)}, u32[]{:S(2)}, u32[]{:S(2)}) collective-permute-start(f32[4,128,768]{2,1,0:T(8,128)} %get-tuple-element.121), channel_id=1, source_target_pairs={{0,4},{4,0},{1,5},{5,1},{2,6},{6,2},{3,7},{7,3},{8,12},{12,8},{9,1... | collective-permute-start | bytes 4718600 | tf_op jit(solution)/shard_map/ppermute | solution.py:507
  388.4 1.4 collective-permute-start.17
  391.5 6.6 %collective-permute-start.20 = (f32[20864]{0:T(1024)S(1)}, f32[20864]{0:T(1024)S(1)}, u32[]{:S(2)}, u32[]{:S(2)}) collective-permute-start(f32[20864]{0:T(1024)S(1)} %add.245), channel_id=1, source_target_pairs={{0,8},{8,0},{16,24},{24,16},{1,9},{9,1},{17,25},{25,17},{2,10},{10... | collective-permute-start | bytes 250376 | tf_op jit(solution)/shard_map/ppermute | solution.py:507
  391.9 3.5 copy-start.2
  391.9 3.5 copy-start.7
  391.9 3.5 copy-start.8
  392.0 11.3 %collective-permute-start.19 = (f32[2,64,768]{2,1,0:T(8,128)S(1)}, f32[2,64,768]{2,1,0:T(8,128)S(1)}, u32[]{:S(2)}, u32[]{:S(2)}) collective-permute-start(f32[2,64,768]{2,1,0:T(8,128)S(1)} %dynamic-slice_bitcast_fusion), channel_id=1, source_target_pairs={{0,16},{8,24},{16,0},{24,8},{1,17},{9,25},{17,1},{25,9},{2,18},{10... | collective-permute-start | bytes 1179656 | tf_op jit(solution)/shard_map/ppermute | solution.py:507
  392.6 12.1 %collective-permute-start.18 = (f32[2,64,768]{2,1,0:T(8,128)S(1)}, f32[2,64,768]{2,1,0:T(8,128)S(1)}, u32[]{:S(2)}, u32[]{:S(2)}) collective-permute-start(f32[2,64,768]{2,1,0:T(8,128)S(1)} %dynamic-slice_bitcast_fusion.1), channel_id=1, source_target_pairs={{0,8},{8,0},{16,24},{24,16},{1,9},{9,1},{17,25},{25,17},{2,10},{10... | collective-permute-start | bytes 1179656 | tf_op jit(solution)/shard_map/ppermute | solution.py:507
  397.2 13.3 %copy-start.25 = (f32[2304]{0:T(1024)S(1)}, f32[2304]{0:T(1024)}, u32[]{:S(2)}) copy-start(f32[2304]{0:T(1024)} %param.57) | copy-start | bytes 27652
  397.2 13.3 %copy-start.28 = (f32[2304]{0:T(1024)S(1)}, f32[2304]{0:T(1024)}, u32[]{:S(2)}) copy-start(f32[2304]{0:T(1024)} %param.59) | copy-start | bytes 27652
  397.2 13.3 %copy-start.29 = (f32[2304]{0:T(1024)S(1)}, f32[2304]{0:T(1024)}, u32[]{:S(2)}) copy-start(f32[2304]{0:T(1024)} %param.58) | copy-start | bytes 27652
  397.2 13.9 %copy-start.23 = (f32[16,128]{1,0:T(8,128)S(1)}, f32[16,128]{1,0:T(8,128)}, u32[]{:S(2)}) copy-start(f32[16,128]{1,0:T(8,128)} %param.42) | copy-start | bytes 24580
  397.2 13.9 %copy-start.30 = (f32[16,128]{1,0:T(8,128)S(1)}, f32[16,128]{1,0:T(8,128)}, u32[]{:S(2)}) copy-start(f32[16,128]{1,0:T(8,128)} %param.44) | copy-start | bytes 24580
  397.2 13.9 %copy-start.31 = (f32[16,128]{1,0:T(8,128)S(1)}, f32[16,128]{1,0:T(8,128)}, u32[]{:S(2)}) copy-start(f32[16,128]{1,0:T(8,128)} %param.43) | copy-start | bytes 24580
  397.2 14.5 %copy-start.27 = (f32[128,16]{0,1:T(8,128)S(1)}, f32[128,16]{0,1:T(8,128)}, u32[]{:S(2)}) copy-start(f32[128,16]{0,1:T(8,128)} %param.39) | copy-start | bytes 24580
  397.2 14.5 %copy-start.32 = (f32[128,16]{0,1:T(8,128)S(1)}, f32[128,16]{0,1:T(8,128)}, u32[]{:S(2)}) copy-start(f32[128,16]{0,1:T(8,128)} %param.41) | copy-start | bytes 24580
  397.3 14.5 %copy-start.33 = (f32[128,16]{0,1:T(8,128)S(1)}, f32[128,16]{0,1:T(8,128)}, u32[]{:S(2)}) copy-start(f32[128,16]{0,1:T(8,128)} %param.40) | copy-start | bytes 24580
  397.3 15.1 %copy-start.35 = (f32[128]{0:T(128)S(1)}, f32[128]{0:T(128)}, u32[]{:S(2)}) copy-start(f32[128]{0:T(128)} %param.45) | copy-start | bytes 1540
  397.3 15.1 %copy-start.39 = (f32[128]{0:T(128)S(1)}, f32[128]{0:T(128)}, u32[]{:S(2)}) copy-start(f32[128]{0:T(128)} %param.47) | copy-start | bytes 1540
  397.3 15.1 %copy-start.40 = (f32[128]{0:T(128)S(1)}, f32[128]{0:T(128)}, u32[]{:S(2)}) copy-start(f32[128]{0:T(128)} %param.46) | copy-start | bytes 1540
  398.1 15.1 %copy-start.6 = (f32[2,128,256]{2,1,0:T(8,128)S(1)}, f32[2,128,256]{2,1,0:T(8,128)}, u32[]{:S(2)}) copy-start(f32[2,128,256]{2,1,0:T(8,128)} %param.36) | copy-start | bytes 786436
  398.1 15.1 %copy-start.16 = (f32[2,128,256]{2,1,0:T(8,128)S(1)}, f32[2,128,256]{2,1,0:T(8,128)}, u32[]{:S(2)}) copy-start(f32[2,128,256]{2,1,0:T(8,128)} %param.38) | copy-start | bytes 786436
  398.1 15.1 %copy-start.17 = (f32[2,128,256]{2,1,0:T(8,128)S(1)}, f32[2,128,256]{2,1,0:T(8,128)}, u32[]{:S(2)}) copy-start(f32[2,128,256]{2,1,0:T(8,128)} %param.37) | copy-start | bytes 786436
  404.8 9.4 %copy-start.12 = (f32[2,128,128]{2,1,0:T(8,128)S(1)}, f32[2,128,128]{2,1,0:T(8,128)}, u32[]{:S(2)}) copy-start(f32[2,128,128]{2,1,0:T(8,128)} %param.33) | copy-start | bytes 393220
  404.8 9.4 %copy-start.20 = (f32[2,128,128]{2,1,0:T(8,128)S(1)}, f32[2,128,128]{2,1,0:T(8,128)}, u32[]{:S(2)}) copy-start(f32[2,128,128]{2,1,0:T(8,128)} %param.35) | copy-start | bytes 393220
  404.8 9.4 %copy-start.21 = (f32[2,128,128]{2,1,0:T(8,128)S(1)}, f32[2,128,128]{2,1,0:T(8,128)}, u32[]{:S(2)}) copy-start(f32[2,128,128]{2,1,0:T(8,128)} %param.34) | copy-start | bytes 393220
  404.9 5.5 %collective-permute-start.23 = (f32[20864]{0:T(1024)S(1)}, f32[20864]{0:T(1024)S(1)}, u32[]{:S(2)}, u32[]{:S(2)}) collective-permute-start(f32[20864]{0:T(1024)S(1)} %add.253), channel_id=1, source_target_pairs={{0,16},{8,24},{16,0},{24,8},{1,17},{9,25},{17,1},{25,9},{2,18},{10... | collective-permute-start | bytes 250376 | tf_op jit(solution)/shard_map/ppermute | solution.py:507
  405.3 7.9 %collective-permute-start.21 = (f32[64,768]{1,0:T(8,128)S(1)}, f32[64,768]{1,0:T(8,128)S(1)}, u32[]{:S(2)}, u32[]{:S(2)}) collective-permute-start(f32[64,768]{1,0:T(8,128)S(1)} %dynamic-slice_bitcast_fusion.3), channel_id=1, source_target_pairs={{0,16},{8,24},{16,0},{24,8},{1,17},{9,25},{17,1},{25,9},{2,18},{10... | collective-permute-start | bytes 589832 | tf_op jit(solution)/shard_map/ppermute | solution.py:507
  407.0 6.1 %collective-permute-start.22 = (f32[64,768]{1,0:T(8,128)S(1)}, f32[64,768]{1,0:T(8,128)S(1)}, u32[]{:S(2)}, u32[]{:S(2)}) collective-permute-start(f32[64,768]{1,0:T(8,128)S(1)} %dynamic-slice_bitcast_fusion.2), channel_id=1, source_target_pairs={{0,8},{8,0},{16,24},{24,16},{1,9},{9,1},{17,25},{25,17},{2,10},{10... | collective-permute-start | bytes 589832 | tf_op jit(solution)/shard_map/ppermute | solution.py:507
  (9 other events, 18.0 us)
Sparse Core Ops, SparseCore 0:
  11.5 140.6 all-gather.1
  286.7 75.4 reduce-scatter.1

commit v6 on v5

--- a/solution.py
+++ b/solution.py
@@ -15,7 +15,7 @@
 MID = 63
 DECAY_ROWS = 32
 ROWS = 256
-FFN_ROWS = 512
+FFN_CUT = 256
 STEP = 10
 
 NORM_EPS = 1e-06
@@ -54,12 +54,24 @@
     return both[:size] + both[size:] + dot(left[0], right[1], dims)
 
 
-def dot_exact(matrix, values):
-    high = values.astype(BF16)
-    rest = values - high.astype(F32)
-    middle = rest.astype(BF16)
-    low = (rest - middle.astype(F32)).astype(BF16)
-    return dot(matrix, high) + dot(matrix, middle) + dot(matrix, low)
+def dot_sum(matrix, values):
+    high, low = split_two(values)
+    both = dot(matrix, jnp.concatenate([high, low], axis=1))
+    return both[:, : values.shape[1]] + both[:, values.shape[1] :]
+
+
+def dot_two(left, right, dims=NN):
+    axis = 1 - dims[0][0][0]
+    size = left[0].shape[axis]
+    both = dot(jnp.concatenate(left, axis=axis), right, dims)
+    return both[:size] + both[size:]
+
+
+def heads_side_by_side(info, decay_out, start, stop):
+    heads = decay_out.shape[0]
+    return jnp.concatenate(
+        [decay_out[info[2 * GROUPS + head], start:stop] for head in range(heads)], axis=1
+    )
 
 
 def lower_mask():
@@ -130,16 +142,11 @@
     every = range(heads)
     keys = [made[:, head * size : head * size + HK] for head in every]
     values = [made[:, head * size + HK : (head + 1) * size] for head in every]
-    logits = []
-    for head in every:
-        slot = info[2 * GROUPS + head]
-        logits.append(
-            lax.dot_general(
-                rank, decay_out[slot, :ranks], NN, precision=lax.Precision.HIGHEST,
-                preferred_element_type=F32,
-            )
-            + decay_out[slot, ranks : ranks + 1]
-        )
+    all_logits = lax.dot_general(
+        rank, heads_side_by_side(info, decay_out, 0, ranks), NN,
+        precision=lax.Precision.HIGHEST, preferred_element_type=F32,
+    ) + heads_side_by_side(info, decay_out, ranks, ranks + 1)
+    logits = [all_logits[:, head * HK : (head + 1) * HK] for head in every]
     for head in every:
         kv_out[head, :, :HK] = keys[head]
         kv_out[head, :, HK:] = values[head]
@@ -150,7 +157,7 @@
     ]
     for part in range(ROWS // BLOCK):
         span = slice(part * BLOCK, (part + 1) * BLOCK)
-        cum = [dot_exact(lower, log_decay[head][span]) for head in every]
+        cum = [dot_sum(lower, log_decay[head][span]) for head in every]
         total = [item[BLOCK - 1 :] for item in cum]
         carried = [
             split_two(keys[head][span] * jnp.exp(total[head] - cum[head])) for head in every
@@ -226,59 +233,73 @@
 def ffn_kernel(
     info, normed, back, middle, weight, gain,
     active_out, back_gate_out, back_up_out, layer_out, back_middle_out, back_attn_out, gain_out,
-    ffn_ref, back_ref, turned_ref, active_ref, back_gate_ref, back_up_ref,
+    ffn_ref, back_ref, active_ref, back_gate_ref, back_up_ref,
 ):
-    piece, step = pl.program_id(0), pl.program_id(1)
-    pieces = pl.num_programs(0)
+    step, piece = pl.program_id(0), pl.program_id(1)
+    pieces = pl.num_programs(1)
+    own = info[2 * GROUPS + pieces]
     units = weight.shape[2] // 3
-    count = normed.shape[0]
-    rows = pl.ds(pl.multiple_of(step * count, count), count)
 
     @pl.when((step == 0) & (piece == 0))
     def _():
         gain_out[...] = jnp.zeros_like(gain_out)
+
+    @pl.when(piece == 0)
+    def _():
         ffn_ref[...] = jnp.zeros_like(ffn_ref)
         back_ref[...] = jnp.zeros_like(back_ref)
 
-    @pl.when(step == 0)
+    def rows_of(start, stop):
+        return jnp.concatenate([weight[group, 0, start:stop] for group in range(GROUPS)], axis=1)
+
+    cuts = [(start, min(start + FFN_CUT, units)) for start in range(0, units, FFN_CUT)]
+
+    def elementwise(cut, gate_values, upward, back_active):
+        at = slice(*cut)
+        share = sigmoid(gate_values)
+        silu = gate_values * share
+        active_ref[:, at] = (silu * upward).astype(BF16)
+        back_gate_ref[:, at] = (
+            back_active * upward * (share * (1.0 + gate_values * (1.0 - share)))
+        ).astype(BF16)
+        back_up_ref[:, at] = (back_active * silu).astype(BF16)
+
+    waiting = None
+    for cut in cuts:
+        start, stop = cut
+        made = (
+            dot(normed[...], rows_of(start, stop), NT),
+            dot(normed[...], rows_of(units + start, units + stop), NT),
+            dot(back[...], rows_of(2 * units + start, 2 * units + stop), NT),
+        )
+        if waiting is not None:
+            elementwise(*waiting)
+        waiting = (cut,) + made
+    elementwise(*waiting)
+    back_ref[...] += dot(back_gate_ref[...], rows_of(0, units)) + dot(
+        back_up_ref[...], rows_of(units, 2 * units)
+    )
+
+    @pl.when(step == own)
     def _():
-        for kind in range(3):
-            for group in range(GROUPS):
-                turned_ref[kind, group * LANES : (group + 1) * LANES] = weight[
-                    group, 0, kind * units : (kind + 1) * units
-                ].T
-
-    def rows_of(start):
-        return jnp.concatenate(
-            [weight[group, 0, start : start + units] for group in range(GROUPS)], axis=1
-        )
-
-    gate_values = dot(normed[...], turned_ref[0])
-    upward = dot(normed[...], turned_ref[1])
-    back_active = dot(back[...], turned_ref[2])
-    share = sigmoid(gate_values)
-    silu = gate_values * share
-    active_ref[...] = (silu * upward).astype(BF16)
-    back_gate_ref[...] = (
-        back_active * upward * (share * (1.0 + gate_values * (1.0 - share)))
-    ).astype(BF16)
-    back_up_ref[...] = (back_active * silu).astype(BF16)
-    ffn_ref[rows] += dot(active_ref[...], rows_of(2 * units))
-    back_ref[rows] += dot(back_gate_ref[...], rows_of(0)) + dot(back_up_ref[...], rows_of(units))
-
-    @pl.when(piece == info[2 * GROUPS + pieces])
+        ffn_ref[...] += dot(active_ref[...], rows_of(2 * units, 3 * units))
+
+    @pl.when(piece == own)
     def _():
         active_out[...] = active_ref[...]
         back_gate_out[...] = back_gate_ref[...]
         back_up_out[...] = back_up_ref[...]
 
+    @pl.when((piece == pieces - 1) & (step == own))
+    def _():
+        layer_out[...] = (middle[...] + ffn_ref[...]).astype(BF16)
+
     @pl.when(piece == pieces - 1)
     def _():
         mid = middle[...]
-        layer_out[...] = (mid + ffn_ref[rows]).astype(BF16)
         inverse = inverse_rms(mid, NORM_EPS)
         unit = mid * inverse
-        total = back_ref[rows]
+        total = back_ref[...]
         weighted = total * gain[...]
         back_middle = back[...].astype(F32) + inverse * (
             weighted - unit * jnp.mean(weighted * unit, axis=-1, keepdims=True)
@@ -366,7 +387,7 @@
         key_mid = [split_two(keys[head] * shrink[head]) for head in every]
         values = [split_two(kv[head, span, HK:]) for head in every]
         back = [split_two(back_mixed[head, span]) for head in every]
-        scores = [dot_split(query_mid[head], key_mid[head], NT) for head in every]
+        scores = [dot_two(query_mid[head], key_mid[head][0], NT) for head in every]
         back_scores = [dot_split(back[head], values[head], NT) for head in every]
         since = [jnp.exp(cum[head]) for head in every]
         until = [jnp.exp(total[head] - cum[head]) for head in every]
@@ -379,7 +400,7 @@
             dot_split(back[head], split_two(query[head] * since[head]), TN) for head in every
         ]
         outer = [
-            dot_split(split_two(carried[head]), back_state_parts[head], NT) for head in every
+            dot_two(split_two(carried[head]), back_state_parts[head][0], NT) for head in every
         ]
         scores = [split_two(jnp.where(causal, item, 0.0)) for item in scores]
         back_scores = [split_two(jnp.where(causal, item, 0.0)) for item in back_scores]
@@ -393,7 +414,7 @@
             + back_carried[head] * until[head]
             for head in every
         ]
-        back_values = [dot_split(scores[head], back[head], TN) + outer[head] for head in every]
+        back_values = [dot_two(scores[head], back[head][0], TN) + outer[head] for head in every]
         back_total = []
         for head in every:
             decayed = back_state[head] * jnp.exp(total[head])
@@ -404,23 +425,21 @@
             state_ref[head] = decayed + added[head]
         back_logits = [
             (
-                dot_exact(upper, query[head] * back_query[head] - keys[head] * back_keys[head])
+                dot_sum(upper, query[head] * back_query[head] - keys[head] * back_keys[head])
                 + back_total[head]
             )
             * sigmoid(-logits_in[head, span])
             / GATE_SCALE
             for head in every
         ]
-        rank_parts = split_two(rank[span])
-        rank_back = jnp.zeros((BLOCK, ranks), F32)
+        together = jnp.concatenate(back_logits, axis=1)
+        rank_back = lax.dot_general(
+            together, heads_side_by_side(info, decay_out, 0, ranks), NT,
+            precision=lax.Precision.HIGHEST, preferred_element_type=F32,
+        )
+        decay_grad_out[...] += dot_split(split_two(rank[span]), split_two(together), TN)
+        bias_out[...] += jnp.sum(together, axis=0, keepdims=True)
         for head in every:
-            slot = info[2 * GROUPS + head]
-            rank_back += lax.dot_general(
-                back_logits[head], decay_out[slot, :ranks], NT, precision=lax.Precision.HIGHEST,
-                preferred_element_type=F32,
-            )
-            bias_out[head] += jnp.sum(back_logits[head], axis=0, keepdims=True)
-            decay_grad_out[head] += dot_split(rank_parts, split_two(back_logits[head]), TN)
             at = head * size
             query_ref[span, at : at + HK] = (back_query[head] * HK ** (-0.5)).astype(BF16)
             query_ref[span, at + HK : at + size] = back_gate[head, span]
@@ -572,12 +591,12 @@
     return gather_plain(pack)
 
 
-def finish_sums(kept, sent, sums, early):
+def finish_sums(kept, sent, sums, early, late):
     columns = kept.shape[-1]
     if not staged():
         whole = jnp.concatenate([kept, sent]).reshape(-1, columns)
         share = lax.psum_scatter(whole, ("dp", "ctx"), scatter_dimension=0, tiled=True)
-        return share, lax.psum(sums, ("dp", "ctx")), early
+        return share, lax.psum(sums, ("dp", "ctx")), early, late
     device = lax.axis_index("dp")
     row, column = device // 2, device % 2
 
@@ -586,7 +605,7 @@
 
     value = kept + swap(sent, "ctx", 1)
     sums = sums + swap(sums, "ctx", 1)
-    value, sums, early = lax.optimization_barrier((value, sums, early))
+    value, sums, early, late = lax.optimization_barrier((value, sums, early, late))
     value = value.reshape(2, 2, LANES, columns)
     half = LANES // 2
     upper, lower = value[:, :, :half], value[:, :, half:]
@@ -597,7 +616,7 @@
     upper = pick(upper, 0, row) + swap(pick(upper, 0, 1 - row), "dp", 2)
     lower = pick(lower, 0, column) + swap(pick(lower, 0, 1 - column), "dp", 1)
     sums = sums + swap(sums, "dp", 2)
-    return jnp.concatenate([upper, lower]), sums, early
+    return jnp.concatenate([upper, lower]), sums, early, late
 
 
 def adamw(weight_now, grad_now, mean_now, square_now, rate_value, decay_value):
@@ -800,52 +819,51 @@
         rows * heads * 4 * 1024,
     )
 
-    tiles = rows // FFN_ROWS
-
-    def last_only(j, i, info):
-        return (jnp.where(j == heads - 1, i, 0), 0)
-
-    def own_only(j, i, info):
-        own = info[2 * GROUPS + heads]
-        return (jnp.where(j < own, 0, jnp.where(j > own, tiles - 1, i)), 0)
-
-    tile_spec = pl.BlockSpec((FFN_ROWS, width), lambda j, i, *_: (i, 0))
-    last_spec = pl.BlockSpec((FFN_ROWS, width), last_only, pipeline_mode=pl.Buffered(1))
-    own_spec = pl.BlockSpec((FFN_ROWS, units), own_only, pipeline_mode=pl.Buffered(1))
-    tile_gain_spec = pl.BlockSpec((1, width), lambda j, i, *_: (0, 0))
-    active, back_gate, back_up, layer_out, back_middle, back_attn, gain_two_part = call(
+    tile = rows // heads
+    wide_spec = pl.BlockSpec((tile, width), lambda i, j, *_: (i, 0))
+    own_spec = pl.BlockSpec((tile, units), lambda i, j, *_: (i, 0))
+    wide_gain_spec = pl.BlockSpec((1, width), lambda i, j, *_: (0, 0))
+    active, back_gate, back_up, layer_own, back_middle, back_attn, gain_two_part = call(
         ffn_kernel,
-        (heads, tiles),
-        [
-            tile_spec,
-            tile_spec,
-            last_spec,
-            pl.BlockSpec((GROUPS, 1, 3 * units, LANES), lambda j, i, *_: (0, j, 0, 0)),
-            tile_gain_spec,
-        ],
-        [own_spec, own_spec, own_spec, last_spec, last_spec, last_spec, tile_gain_spec],
+        (heads, heads),
+        [
+            wide_spec,
+            wide_spec,
+            wide_spec,
+            pl.BlockSpec((GROUPS, 1, 3 * units, LANES), lambda i, j, *_: (0, j, 0, 0)),
+            wide_gain_spec,
+        ],
+        [
+            own_spec,
+            own_spec,
+            own_spec,
+            pl.BlockSpec((tile, width), lambda i, j, *_: (0, 0)),
+            wide_spec,
+            wide_spec,
+            wide_gain_spec,
+        ],
         [
             shaped((rows, units), BF16),
             shaped((rows, units), BF16),
             shaped((rows, units), BF16),
-            shaped((rows, width), BF16),
+            shaped((tile, width), BF16),
             shaped((rows, width)),
             shaped((rows, width), BF16),
             shaped((1, width)),
         ],
         [
-            pltpu.VMEM((rows, width), F32),
-            pltpu.VMEM((rows, width), F32),
-            pltpu.VMEM((3, width, units), BF16),
-            pltpu.VMEM((FFN_ROWS, units), BF16),
-            pltpu.VMEM((FFN_ROWS, units), BF16),
-            pltpu.VMEM((FFN_ROWS, units), BF16),
+            pltpu.VMEM((tile, width), F32),
+            pltpu.VMEM((tile, width), F32),
+            pltpu.VMEM((tile, units), BF16),
+            pltpu.VMEM((tile, units), BF16),
+            pltpu.VMEM((tile, units), BF16),
         ],
         (info, normed_two, back_ffn, middle, ffn, gain_two),
         1,
-        12 * rows * width * units * heads,
+        10 * rows * width * units * heads,
         rows * width * 24,
     )
+    layer_parts = [layer_own] + [shift(layer_own, "tp", distance) for distance in range(1, heads)]
     early_grad = jnp.concatenate(
         [
             dot(back_gate, normed_two, TN),
@@ -913,8 +931,8 @@
             fixed(grad_shape),
             fixed(rank_grad_shape),
             back_row_spec,
-            pl.BlockSpec((heads, ranks, HK), lambda i, *_: (0, 0, 0)),
-            bias_spec,
+            pl.BlockSpec((ranks, heads * HK), lambda i, *_: (0, 0)),
+            pl.BlockSpec((1, heads * HK), lambda i, *_: (0, 0)),
             gain_spec,
         ],
         [
@@ -922,8 +940,8 @@
             grad_shape,
             rank_grad_shape,
             shaped((rows, width)),
-            shaped((heads, ranks, HK)),
-            shaped((heads, 1, HK)),
+            shaped((ranks, heads * HK)),
+            shaped((1, heads * HK)),
             shaped((1, width)),
         ],
         [
@@ -943,8 +961,8 @@
         rows * heads * 4 * 2048,
     )
     own = info[-1]
-    decay_out_own = lax.dynamic_index_in_dim(decay_out_grad, own, 0, keepdims=False)
-    bias_own = lax.dynamic_index_in_dim(bias_grad, own, 0, keepdims=False)
+    decay_out_own = lax.dynamic_slice_in_dim(decay_out_grad, own * HK, HK, axis=1)
+    bias_own = lax.dynamic_slice_in_dim(bias_grad, own * HK, HK, axis=1)
     sums = jnp.concatenate(
         [
             gain_one_part.reshape(-1),
@@ -955,7 +973,18 @@
             rank_grad.reshape(-1),
         ]
     )
-    mixer_share, sums, early_share = finish_sums(kept, sent_away, sums, early_share)
+    mixer_share, sums, early_share, layer_parts = finish_sums(
+        kept, sent_away, sums, early_share, layer_parts
+    )
+    layer_order = jnp.stack(layer_parts)
+    layer_out = jnp.concatenate(
+        [
+            lax.dynamic_index_in_dim(
+                layer_order, lax.rem(own - head + heads, heads), 0, keepdims=False
+            )
+            for head in range(heads)
+        ]
+    )
     gain_count = gains.shape[0]
     decay_start = gain_count + HK
     rank_start = decay_start + ranks * HK

time: 428 us -> 508 us (1.19)
  the two profiles are of different devices: /device:TPU:0 before, /device:TPU:26 now
where the time goes in v6:
time: 508 us; the launch traced here: 502 us
  Pallas kernels  268 us (53%)
  waiting for transfers between devices  133 us (26%)
  other arithmetic  33.8 us (7%)
  starting transfers between devices  29 us (6%)
  between operations  15.9 us (3%)
  matrix products  14 us (3%)
  local copies, waits for them, and re-layouts  8.84 us (2%)
    pallas_call x5, Pallas kernels, call(): pl.pallas_call(kernel, grid_spec=pltpu.PrefetchScalarGridSpec(num_scalar_...  268 us
    ppermute x9, waiting for transfers between devices, shift(): lax.ppermute(value, axis, [(source, (source + distance) % count) for sour...  115 us
    ppermute x16, waiting for transfers between devices, swap(): lax.ppermute(value, axis, [(source, source ^ distance) for source in rang...  15.6 us
    dot_general x4, matrix products, dot(): return lax.dot_general(left, right, dims, preferred_element_type=F32)  14 us
    ppermute x16, starting transfers between devices, swap(): lax.ppermute(value, axis, [(source, source ^ distance) for source in rang...  12.3 us
    ppermute x9, starting transfers between devices, shift(): lax.ppermute(value, axis, [(source, (source + distance) % count) for sour...  12.3 us
  transfers between devices with their start and end apart: 29, of which 12 were waited for; matrix products, arithmetic and copies ran while one was open for 6% of the time, Pallas kernels for 31%

profile of v6, /device:TPU:26, one launch (start us, length us, event | category | flops | bytes accessed | tf_op | source)
XLA Modules:
  0.0 502.3 jit_solution(17406902913778896824)
XLA Ops:
  7.3 1.2 convert.37
  8.6 1.0 convert_bitcast_fusion
  9.6 0.8 pad_maximum_fusion.7
  10.5 1.0 copy.66
  12.3 1.7 collective-permute-start.1
  14.5 3.3 collective-permute-done
  17.8 13.9 %collective-permute-done.1 = bf16[496,128]{1,0:T(8,128)(2,1)S(1)} collective-permute-done((bf16[496,128]{1,0:T(8,128)(2,1)S(1)}, bf16[496,128]{1,0:T(8,128)(2,1)S(1)}, u32[]{:S(2)}, u32[]{:S(2)}) %collective-permute-start.1) | collective-permute-done | bytes 127008 | tf_op jit(solution)/shard_map/ppermute | solution.py:531
  31.8 0.9 collective-permute-start.6
  32.7 1.2 collective-permute-start.7
  33.9 1.4 collective-permute-start.8
  35.3 5.8 %collective-permute-done.3 = bf16[640,128]{1,0:T(8,128)(2,1)S(1)} collective-permute-done((bf16[640,128]{1,0:T(8,128)(2,1)S(1)}, bf16[640,128]{1,0:T(8,128)(2,1)S(1)}, u32[]{:S(2)}, u32[]{:S(2)}) %collective-permute-start.3) | collective-permute-done | bytes 163872 | tf_op jit(solution)/shard_map/ppermute | solution.py:531
  41.7 9.3 %collective-permute-done.4 = bf16[640,128]{1,0:T(8,128)(2,1)S(1)} collective-permute-done((bf16[640,128]{1,0:T(8,128)(2,1)S(1)}, bf16[640,128]{1,0:T(8,128)(2,1)S(1)}, u32[]{:S(2)}, u32[]{:S(2)}) %collective-permute-start.4) | collective-permute-done | bytes 163872 | tf_op jit(solution)/shard_map/ppermute | solution.py:531
  51.1 1.5 collective-permute-done.8
  52.6 1.5 pad_maximum_fusion.4.first
  54.7 0.6 fusion.33
  55.3 0.9 slice.102
  56.2 1.3 collective-permute-start.10
  57.5 2.5 collective-permute-start.11
  60.0 0.6 fusion.7.decay_out
  60.7 29.0 %shard_map.509 = (bf16[2048,1024]{1,0:T(8,128)(2,1)}, f32[4,2048,384]{2,1,0:T(8,128)}, f32[2048,16]{1,0:T(8,128)}, f32[4,2048,128]{2,1,0:T(8,128)}, f32[4,2048,1...) custom-call(s32[21]{0:T(128)} %pad_add_fusion.info, ...), custom_call_target="tpu_custom_call" | custom-call | flops 6442450944 | bytes 33554432 | tf_op jit(solution)/shard_map/pallas_call | solution.py:490
  89.7 8.6 %collective-permute-done.12 = bf16[4,640,128]{2,1,0:T(8,128)(2,1)} collective-permute-done((bf16[4,640,128]{2,1,0:T(8,128)(2,1)S(1)}, bf16[4,640,128]{2,1,0:T(8,128)(2,1)}, u32[]{:S(2)}, u32[]{:S(2)}) %collective-permute-start.12) | collective-permute-done | bytes 655392 | tf_op jit(solution)/shard_map/ppermute | solution.py:526
  98.3 3.0 pad_maximum_fusion.3.first
  102.5 3.0 collective-permute-start.13
  105.5 3.9 broadcast_select_fusion.back
  109.5 0.8 copy-done.42
  110.2 40.2 %shard_map.510 = (f32[4,2048,128]{2,1,0:T(8,128)}, f32[4,2048,256]{2,1,0:T(8,128)}, f32[4,2048,256]{2,1,0:T(8,128)}, f32[16,4,256,128]{3,2,1,0:T(8,128)}, bf16[2...) custom-call(s32[21]{0:T(128)} %pad_add_fusion.info, ...), custom_call_target="tpu_custom_call" | custom-call | flops 15032385536 | bytes 33554432 | tf_op jit(solution)/shard_map/pallas_call | solution.py:490
  150.5 109.8 %shard_map.511 = (bf16[2048,704]{1,0:T(8,128)(2,1)}, bf16[2048,704]{1,0:T(8,128)(2,1)}, bf16[2048,704]{1,0:T(8,128)(2,1)}, bf16[512,1024]{1,0:T(8,128)(2,1)}, f3...) custom-call(s32[21]{0:T(128)} %pad_add_fusion.info, ...), custom_call_target="tpu_custom_call" | custom-call | flops 59055800320 | bytes 50331648 | tf_op jit(solution)/shard_map/pallas_call | solution.py:490
  260.3 6.3 %fusion.34 = f32[704,1024]{1,0:T(8,128)S(1)} fusion(bf16[2048,704]{1,0:T(8,128)(2,1)} %get-tuple-element.106, bf16[2048,1024]{1,0:T(8,128)(2,1)} %get-tuple-element.100.normed), kind=kOutput, calls=%fused_computation.121 | convolution fusion | flops 2952790016 | bytes 9961472 | tf_op jit(solution)/shard_map/dot_general | solution.py:42
  266.6 3.2 fusion.35
  269.9 3.2 fusion.36
  273.2 1.3 fusion.37
  274.4 4.3 pad_maximum_fusion
  278.8 23.8 %shard_map.512 = (f32[4,2048,256]{2,1,0:T(8,128)}, bf16[4,2048,256]{2,1,0:T(8,128)(2,1)}, f32[1,256]{1,0:T(1,128)}, f32[4,256,128]{2,1,0:T(8,128)}) custom-call(bf16[2048,1024]{1,0:T(8,128)(2,1)} %get-tuple-element.111.back_attn, bf16[1024,1024]{1,0:T(8,128)(2,1)} %get-tuple-element.112.out_weight, f32[4,2048,256]{2,1,0:T(8,128)} %get-tuple-element.113.mixed_in, ...), custom_call_target="tpu_custom_call" | custom-call | flops 4294967296 | bytes 33554432 | tf_op jit(solution)/shard_map/pallas_call | solution.py:490
  302.6 1.1 broadcast_add_fusion
  303.7 1.3 collective-permute-start.15
  305.0 2.5 collective-permute-done.15.back_end
  307.5 0.8 copy-done.41
  308.3 64.7 %shard_map.513 = (f32[4,128,768]{2,1,0:T(8,128)}, f32[4,128,768]{2,1,0:T(8,128)}, f32[16,1024]{1,0:T(8,128)}, f32[2048,1024]{1,0:T(8,128)}, f32[16,512]{1,0:T(8,...) custom-call(s32[21]{0:T(128)} %pad_add_fusion.info, bf16[2048,1024]{1,0:T(8,128)(2,1)} %tokens.5, ...), custom_call_target="tpu_custom_call" | custom-call | flops 25769803776 | bytes 67108864 | tf_op jit(solution)/shard_map/pallas_call | solution.py:490
  373.6 7.2 %collective-permute-start.19 = (bf16[512,1024]{1,0:T(8,128)(2,1)}, bf16[512,1024]{1,0:T(8,128)(2,1)}, u32[]{:S(2)}, u32[]{:S(2)}) collective-permute-start(bf16[512,1024]{1,0:T(8,128)(2,1)} %get-tuple-element.132), channel_id=1, source_target_pairs={{0,2},{1,3},{2,0},{3,1},{4,6},{5,7},{6,4},{7,5},{8,10},{9,11},{10,... | collective-permute-start | bytes 3145736 | tf_op jit(solution)/shard_map/ppermute | solution.py:531
  380.7 2.0 collective-permute-start.20
  382.7 0.9 copy.74
  383.6 0.7 constant_dynamic-update-slice_fusion.4
  384.3 0.7 constant_dynamic-update-slice_fusion.6
  384.9 0.7 bitcast_dynamic-update-slice_fusion
  385.8 1.2 collective-permute-done.17
  387.0 0.6 add.277
  387.7 1.6 add.275
  389.3 9.6 %collective-permute-done.18 = bf16[512,1024]{1,0:T(8,128)(2,1)} collective-permute-done((bf16[512,1024]{1,0:T(8,128)(2,1)}, bf16[512,1024]{1,0:T(8,128)(2,1)}, u32[]{:S(2)}, u32[]{:S(2)}) %collective-permute-start.18) | collective-permute-done | bytes 1048608 | tf_op jit(solution)/shard_map/ppermute | solution.py:531
  399.0 73.2 %collective-permute-done.19 = bf16[512,1024]{1,0:T(8,128)(2,1)} collective-permute-done((bf16[512,1024]{1,0:T(8,128)(2,1)}, bf16[512,1024]{1,0:T(8,128)(2,1)}, u32[]{:S(2)}, u32[]{:S(2)}) %collective-permute-start.19) | collective-permute-done | bytes 1048608 | tf_op jit(solution)/shard_map/ppermute | solution.py:531
  472.5 2.1 collective-permute-start.21
  474.6 1.1 multiply_subtract_fusion.1
  475.8 2.4 pad_maximum_fusion.1
  478.7 2.3 pad_maximum_fusion.2
  481.2 1.7 multiply_subtract_fusion
  482.9 0.8 multiply_subtract_fusion.3
  483.8 1.3 collective-permute-done.21
  485.2 0.8 collective-permute-start.26
  486.0 1.4 collective-permute-start.24
  487.7 3.0 collective-permute-done.26
  490.8 0.6 multiply_subtract_fusion.5
  491.4 0.6 multiply_subtract_fusion.6
  492.1 0.6 multiply_subtract_fusion.7
  493.4 1.0 multiply_subtract_fusion.2
  494.4 0.8 multiply_subtract_fusion.4
  (171 shorter events, 6.2 us)
Async XLA Ops:
  7.2 4.3 copy-start.5
  7.2 4.6 copy-start.26
  7.2 4.6 copy-start.34
  7.2 4.6 copy-start.22
  7.3 7.2 %copy-start.9 = (f32[256,128]{1,0:T(8,128)S(1)}, f32[256,128]{1,0:T(8,128)}, u32[]{:S(2)}) copy-start(f32[256,128]{1,0:T(8,128)} %param.48) | copy-start | bytes 393220
  7.3 143.3 %all-gather.2.cloned.1.call-start = ((), (), s32[]{:S(2)}) async-start(), calls=%async_computation.1 | async-start | bytes 17842176 | tf_op jit(solution)/shard_map/all_gather | solution.py:589
  10.4 44.3 %copy-start.24 = (f32[2304]{0:T(1024)S(1)}, f32[2304]{0:T(1024)}, u32[]{:S(2)}) copy-start(f32[2304]{0:T(1024)} %param.57) | copy-start | bytes 27652
  10.5 461.7 %reduce-scatter.2.cloned.1.call-start = ((), (), s32[]{:S(2)}) async-start(), calls=%async_computation.2 | async-start | bytes 10911744 | tf_op jit(solution)/shard_map/reduce_scatter | solution.py:876
  12.1 5.7 %collective-permute-start = (bf16[496,128]{1,0:T(8,128)(2,1)S(1)}, bf16[496,128]{1,0:T(8,128)(2,1)S(1)}, u32[]{:S(2)}, u32[]{:S(2)}) collective-permute-start(bf16[496,128]{1,0:T(8,128)(2,1)S(1)} %constant_dynamic-update-slice_fusion), channel_id=1, source_target_pairs={{0,1},{1,2},{2,3},{3,0},{4,5},{5,6},{6,7},{7,4},{8,9},{9,10},{10,1... | collective-permute-start | bytes 380936 | tf_op jit(solution)/shard_map/ppermute | solution.py:531
  12.3 19.4 %collective-permute-start.1 = (bf16[496,128]{1,0:T(8,128)(2,1)S(1)}, bf16[496,128]{1,0:T(8,128)(2,1)S(1)}, u32[]{:S(2)}, u32[]{:S(2)}) collective-permute-start(bf16[496,128]{1,0:T(8,128)(2,1)S(1)} %constant_dynamic-update-slice_fusion), channel_id=1, source_target_pairs={{0,2},{1,3},{2,0},{3,1},{4,6},{5,7},{6,4},{7,5},{8,10},{9,11},{10,... | collective-permute-start | bytes 380936 | tf_op jit(solution)/shard_map/ppermute | solution.py:531
  14.0 17.7 %collective-permute-start.2 = (bf16[496,128]{1,0:T(8,128)(2,1)S(1)}, bf16[496,128]{1,0:T(8,128)(2,1)S(1)}, u32[]{:S(2)}, u32[]{:S(2)}) collective-permute-start(bf16[496,128]{1,0:T(8,128)(2,1)S(1)} %constant_dynamic-update-slice_fusion), channel_id=1, source_target_pairs={{0,3},{1,0},{2,1},{3,2},{4,7},{5,4},{6,5},{7,6},{8,11},{9,8},{10,9... | collective-permute-start | bytes 380936 | tf_op jit(solution)/shard_map/ppermute | solution.py:531
  31.8 19.3 %collective-permute-start.6 = (bf16[4,496,128]{2,1,0:T(8,128)(2,1)S(1)}, bf16[4,496,128]{2,1,0:T(8,128)(2,1)S(1)}, u32[]{:S(2)}, u32[]{:S(2)}) collective-permute-start(bf16[4,496,128]{2,1,0:T(8,128)(2,1)S(1)} %pad_maximum_fusion.8), channel_id=1, source_target_pairs={{0,8},{8,0},{16,24},{24,16},{1,9},{9,1},{17,25},{25,17},{2,10},{10... | collective-permute-start | bytes 1523720 | tf_op jit(solution)/shard_map/ppermute | solution.py:526
  32.7 18.4 %collective-permute-start.7 = (bf16[4,496,128]{2,1,0:T(8,128)(2,1)S(1)}, bf16[4,496,128]{2,1,0:T(8,128)(2,1)S(1)}, u32[]{:S(2)}, u32[]{:S(2)}) collective-permute-start(bf16[4,496,128]{2,1,0:T(8,128)(2,1)S(1)} %pad_maximum_fusion.8), channel_id=1, source_target_pairs={{0,16},{8,24},{16,0},{24,8},{1,17},{9,25},{17,1},{25,9},{2,18},{10... | collective-permute-start | bytes 1523720 | tf_op jit(solution)/shard_map/ppermute | solution.py:526
  33.9 18.6 %collective-permute-start.8 = (bf16[4,496,128]{2,1,0:T(8,128)(2,1)S(1)}, bf16[4,496,128]{2,1,0:T(8,128)(2,1)S(1)}, u32[]{:S(2)}, u32[]{:S(2)}) collective-permute-start(bf16[4,496,128]{2,1,0:T(8,128)(2,1)S(1)} %pad_maximum_fusion.8), channel_id=1, source_target_pairs={{0,24},{8,16},{16,8},{24,0},{1,25},{9,17},{17,9},{25,1},{2,26},{10... | collective-permute-start | bytes 1523720 | tf_op jit(solution)/shard_map/ppermute | solution.py:526
  35.3 5.8 %collective-permute-start.3 = (bf16[640,128]{1,0:T(8,128)(2,1)S(1)}, bf16[640,128]{1,0:T(8,128)(2,1)S(1)}, u32[]{:S(2)}, u32[]{:S(2)}) collective-permute-start(bf16[640,128]{1,0:T(8,128)(2,1)S(1)} %pad_maximum_fusion.10), channel_id=1, source_target_pairs={{0,1},{1,2},{2,3},{3,0},{4,5},{5,6},{6,7},{7,4},{8,9},{9,10},{10,1... | collective-permute-start | bytes 491528 | tf_op jit(solution)/shard_map/ppermute | solution.py:531
  35.3 15.6 %collective-permute-start.4 = (bf16[640,128]{1,0:T(8,128)(2,1)S(1)}, bf16[640,128]{1,0:T(8,128)(2,1)S(1)}, u32[]{:S(2)}, u32[]{:S(2)}) collective-permute-start(bf16[640,128]{1,0:T(8,128)(2,1)S(1)} %pad_maximum_fusion.10), channel_id=1, source_target_pairs={{0,2},{1,3},{2,0},{3,1},{4,6},{5,7},{6,4},{7,5},{8,10},{9,11},{10,... | collective-permute-start | bytes 491528 | tf_op jit(solution)/shard_map/ppermute | solution.py:531
  41.2 9.8 %collective-permute-start.5 = (bf16[640,128]{1,0:T(8,128)(2,1)S(1)}, bf16[640,128]{1,0:T(8,128)(2,1)S(1)}, u32[]{:S(2)}, u32[]{:S(2)}) collective-permute-start(bf16[640,128]{1,0:T(8,128)(2,1)S(1)} %pad_maximum_fusion.10), channel_id=1, source_target_pairs={{0,3},{1,0},{2,1},{3,2},{4,7},{5,4},{6,5},{7,6},{8,11},{9,8},{10,9... | collective-permute-start | bytes 491528 | tf_op jit(solution)/shard_map/ppermute | solution.py:531
  54.1 6.5 %collective-permute-start.9 = (bf16[4,4,496,128]{3,2,1,0:T(8,128)(2,1)}, bf16[4,4,496,128]{3,2,1,0:T(8,128)(2,1)}, u32[]{:S(2)}, u32[]{:S(2)}) collective-permute-start(bf16[4,4,496,128]{3,2,1,0:T(8,128)(2,1)} %pad_maximum_fusion.4.first), channel_id=1, source_target_pairs={{0,4},{4,0},{1,5},{5,1},{2,6},{6,2},{3,7},{7,3},{8,12},{12,8},{9,1... | collective-permute-start | bytes 6094856 | tf_op jit(solution)/shard_map/ppermute | solution.py:526
  56.2 33.5 %collective-permute-start.10 = (bf16[4,640,128]{2,1,0:T(8,128)(2,1)S(1)}, bf16[4,640,128]{2,1,0:T(8,128)(2,1)S(1)}, u32[]{:S(2)}, u32[]{:S(2)}) collective-permute-start(bf16[4,640,128]{2,1,0:T(8,128)(2,1)S(1)} %pad_maximum_fusion.6), channel_id=1, source_target_pairs={{0,8},{8,0},{16,24},{24,16},{1,9},{9,1},{17,25},{25,17},{2,10},{10... | collective-permute-start | bytes 1966088 | tf_op jit(solution)/shard_map/ppermute | solution.py:526
  57.5 32.2 %collective-permute-start.11 = (bf16[4,640,128]{2,1,0:T(8,128)(2,1)S(1)}, bf16[4,640,128]{2,1,0:T(8,128)(2,1)S(1)}, u32[]{:S(2)}, u32[]{:S(2)}) collective-permute-start(bf16[4,640,128]{2,1,0:T(8,128)(2,1)S(1)} %pad_maximum_fusion.6), channel_id=1, source_target_pairs={{0,16},{8,24},{16,0},{24,8},{1,17},{9,25},{17,1},{25,9},{2,18},{10... | collective-permute-start | bytes 1966088 | tf_op jit(solution)/shard_map/ppermute | solution.py:526
  60.0 38.3 %collective-permute-start.12 = (bf16[4,640,128]{2,1,0:T(8,128)(2,1)S(1)}, bf16[4,640,128]{2,1,0:T(8,128)(2,1)}, u32[]{:S(2)}, u32[]{:S(2)}) collective-permute-start(bf16[4,640,128]{2,1,0:T(8,128)(2,1)S(1)} %pad_maximum_fusion.6), channel_id=1, source_target_pairs={{0,24},{8,16},{16,8},{24,0},{1,25},{9,17},{17,9},{25,1},{2,26},{10... | collective-permute-start | bytes 1966088 | tf_op jit(solution)/shard_map/ppermute | solution.py:526
  89.7 12.8 %copy-start.37 = (f32[4,1,128]{2,1,0:T(1,128)S(1)}, f32[4,1,128]{2,1,0:T(1,128)}, u32[]{:S(2)}) copy-start(f32[4,1,128]{2,1,0:T(1,128)} %get-tuple-element.92) | copy-start | bytes 6148
  89.7 12.8 %copy-start.12 = (f32[4,256,128]{2,1,0:T(8,128)S(1)}, f32[4,256,128]{2,1,0:T(8,128)}, u32[]{:S(2)}) copy-start(f32[4,256,128]{2,1,0:T(8,128)} %get-tuple-element.95) | copy-start | bytes 1572868
  101.2 8.2 %collective-permute-start.14 = (bf16[4,4,640,128]{3,2,1,0:T(8,128)(2,1)}, bf16[4,4,640,128]{3,2,1,0:T(8,128)(2,1)}, u32[]{:S(2)}, u32[]{:S(2)}) collective-permute-start(bf16[4,4,640,128]{3,2,1,0:T(8,128)(2,1)} %pad_maximum_fusion.3.first), channel_id=1, source_target_pairs={{0,4},{4,0},{1,5},{5,1},{2,6},{6,2},{3,7},{7,3},{8,12},{12,8},{9,1... | collective-permute-start | bytes 7864328 | tf_op jit(solution)/shard_map/ppermute | solution.py:526
  102.5 6.9 %collective-permute-start.13 = (f32[4,256,128]{2,1,0:T(8,128)S(1)}, f32[4,256,128]{2,1,0:T(8,128)S(1)}, u32[]{:S(2)}, u32[]{:S(2)}) collective-permute-start(f32[4,256,128]{2,1,0:T(8,128)S(1)} %broadcast_add_fusion.1), channel_id=1, source_target_pairs={{0,4},{1,5},{2,6},{3,7},{8,12},{9,13},{10,14},{11,15},{16,20},{17,... | collective-permute-start | bytes 1572872 | tf_op jit(solution)/shard_map/ppermute | solution.py:510
  260.3 6.3 %copy-start.44 = (bf16[2048,1024]{1,0:T(8,128)(2,1)S(1)}, bf16[2048,1024]{1,0:T(8,128)(2,1)}, u32[]{:S(2)}) copy-start(bf16[2048,1024]{1,0:T(8,128)(2,1)} %get-tuple-element.100.normed) | copy-start | bytes 12582916
  260.3 6.3 %copy-start.46 = (bf16[2048,704]{1,0:T(8,128)(2,1)S(1)}, bf16[2048,704]{1,0:T(8,128)(2,1)}, u32[]{:S(2)}) copy-start(bf16[2048,704]{1,0:T(8,128)(2,1)} %get-tuple-element.107) | copy-start | bytes 8650756
  266.6 3.3 copy-start.1
  269.9 3.3 copy-start
  303.7 3.8 collective-permute-start.15
  308.3 76.0 %copy-start.36 = (f32[1,1024]{1,0:T(1,128)S(1)}, f32[1,1024]{1,0:T(1,128)}, u32[]{:S(2)}) copy-start(f32[1,1024]{1,0:T(1,128)} %get-tuple-element.125) | copy-start | bytes 12292
  308.3 76.0 %copy-start.38 = (f32[1,256]{1,0:T(1,128)S(1)}, f32[1,256]{1,0:T(1,128)}, u32[]{:S(2)}) copy-start(f32[1,256]{1,0:T(1,128)} %get-tuple-element.126) | copy-start | bytes 3076
  373.0 14.6 %collective-permute-start.16 = (f32[4,128,768]{2,1,0:T(8,128)}, f32[4,128,768]{2,1,0:T(8,128)S(1)}, u32[]{:S(2)}, u32[]{:S(2)}) collective-permute-start(f32[4,128,768]{2,1,0:T(8,128)} %get-tuple-element.123), channel_id=1, source_target_pairs={{0,4},{4,0},{1,5},{5,1},{2,6},{6,2},{3,7},{7,3},{8,12},{12,8},{9,1... | collective-permute-start | bytes 4718600 | tf_op jit(solution)/shard_map/ppermute | solution.py:526
  373.3 25.7 %collective-permute-start.18 = (bf16[512,1024]{1,0:T(8,128)(2,1)}, bf16[512,1024]{1,0:T(8,128)(2,1)}, u32[]{:S(2)}, u32[]{:S(2)}) collective-permute-start(bf16[512,1024]{1,0:T(8,128)(2,1)} %get-tuple-element.132), channel_id=1, source_target_pairs={{0,1},{1,2},{2,3},{3,0},{4,5},{5,6},{6,7},{7,4},{8,9},{9,10},{10,1... | collective-permute-start | bytes 3145736 | tf_op jit(solution)/shard_map/ppermute | solution.py:531
  373.6 98.6 %collective-permute-start.19 = (bf16[512,1024]{1,0:T(8,128)(2,1)}, bf16[512,1024]{1,0:T(8,128)(2,1)}, u32[]{:S(2)}, u32[]{:S(2)}) collective-permute-start(bf16[512,1024]{1,0:T(8,128)(2,1)} %get-tuple-element.132), channel_id=1, source_target_pairs={{0,2},{1,3},{2,0},{3,1},{4,6},{5,7},{6,4},{7,5},{8,10},{9,11},{10,... | collective-permute-start | bytes 3145736 | tf_op jit(solution)/shard_map/ppermute | solution.py:531
  380.7 91.4 %collective-permute-start.20 = (bf16[512,1024]{1,0:T(8,128)(2,1)}, bf16[512,1024]{1,0:T(8,128)(2,1)}, u32[]{:S(2)}, u32[]{:S(2)}) collective-permute-start(bf16[512,1024]{1,0:T(8,128)(2,1)} %get-tuple-element.132), channel_id=1, source_target_pairs={{0,3},{1,0},{2,1},{3,2},{4,7},{5,4},{6,5},{7,6},{8,11},{9,8},{10,9... | collective-permute-start | bytes 3145736 | tf_op jit(solution)/shard_map/ppermute | solution.py:531
  385.7 1.3 collective-permute-start.17
  387.7 87.0 %copy-start.3 = (f32[704,128]{1,0:T(8,128)S(1)}, f32[704,128]{1,0:T(8,128)}, u32[]{:S(2)}) copy-start(f32[704,128]{1,0:T(8,128)} %param.54) | copy-start | bytes 1081348
  389.3 85.3 %copy-start.13 = (f32[704,128]{1,0:T(8,128)S(1)}, f32[704,128]{1,0:T(8,128)}, u32[]{:S(2)}) copy-start(f32[704,128]{1,0:T(8,128)} %param.56) | copy-start | bytes 1081348
  389.3 85.3 %copy-start.14 = (f32[704,128]{1,0:T(8,128)S(1)}, f32[704,128]{1,0:T(8,128)}, u32[]{:S(2)}) copy-start(f32[704,128]{1,0:T(8,128)} %param.55) | copy-start | bytes 1081348
  472.2 11.6 %collective-permute-start.23 = (f32[20864]{0:T(1024)}, f32[20864]{0:T(1024)S(1)}, u32[]{:S(2)}, u32[]{:S(2)}) collective-permute-start(f32[20864]{0:T(1024)} %add.277), channel_id=1, source_target_pairs={{0,8},{8,0},{16,24},{24,16},{1,9},{9,1},{17,25},{25,17},{2,10},{10... | collective-permute-start | bytes 250376 | tf_op jit(solution)/shard_map/ppermute | solution.py:526
  472.4 11.3 %collective-permute-start.22 = (f32[2,64,768]{2,1,0:T(8,128)S(1)}, f32[2,64,768]{2,1,0:T(8,128)S(1)}, u32[]{:S(2)}, u32[]{:S(2)}) collective-permute-start(f32[2,64,768]{2,1,0:T(8,128)S(1)} %dynamic-slice_bitcast_fusion.4), channel_id=1, source_target_pairs={{0,16},{8,24},{16,0},{24,8},{1,17},{9,25},{17,1},{25,9},{2,18},{10... | collective-permute-start | bytes 1179656 | tf_op jit(solution)/shard_map/ppermute | solution.py:526
  472.5 12.6 %collective-permute-start.21 = (f32[2,64,768]{2,1,0:T(8,128)S(1)}, f32[2,64,768]{2,1,0:T(8,128)S(1)}, u32[]{:S(2)}, u32[]{:S(2)}) collective-permute-start(f32[2,64,768]{2,1,0:T(8,128)S(1)} %dynamic-slice_bitcast_fusion.5), channel_id=1, source_target_pairs={{0,8},{8,0},{16,24},{24,16},{1,9},{9,1},{17,25},{25,17},{2,10},{10... | collective-permute-start | bytes 1179656 | tf_op jit(solution)/shard_map/ppermute | solution.py:526
  481.1 9.7 %copy-start.25 = (f32[2304]{0:T(1024)S(1)}, f32[2304]{0:T(1024)}, u32[]{:S(2)}) copy-start(f32[2304]{0:T(1024)} %param.57) | copy-start | bytes 27652
  481.1 9.7 %copy-start.28 = (f32[2304]{0:T(1024)S(1)}, f32[2304]{0:T(1024)}, u32[]{:S(2)}) copy-start(f32[2304]{0:T(1024)} %param.59) | copy-start | bytes 27652
  481.1 9.7 %copy-start.29 = (f32[2304]{0:T(1024)S(1)}, f32[2304]{0:T(1024)}, u32[]{:S(2)}) copy-start(f32[2304]{0:T(1024)} %param.58) | copy-start | bytes 27652
  481.1 10.3 %copy-start.23 = (f32[16,128]{1,0:T(8,128)S(1)}, f32[16,128]{1,0:T(8,128)}, u32[]{:S(2)}) copy-start(f32[16,128]{1,0:T(8,128)} %param.42) | copy-start | bytes 24580
  481.1 10.3 %copy-start.30 = (f32[16,128]{1,0:T(8,128)S(1)}, f32[16,128]{1,0:T(8,128)}, u32[]{:S(2)}) copy-start(f32[16,128]{1,0:T(8,128)} %param.44) | copy-start | bytes 24580
  481.1 10.3 %copy-start.31 = (f32[16,128]{1,0:T(8,128)S(1)}, f32[16,128]{1,0:T(8,128)}, u32[]{:S(2)}) copy-start(f32[16,128]{1,0:T(8,128)} %param.43) | copy-start | bytes 24580
  481.1 10.9 %copy-start.27 = (f32[128,16]{0,1:T(8,128)S(1)}, f32[128,16]{0,1:T(8,128)}, u32[]{:S(2)}) copy-start(f32[128,16]{0,1:T(8,128)} %param.39) | copy-start | bytes 24580
  481.1 10.9 %copy-start.32 = (f32[128,16]{0,1:T(8,128)S(1)}, f32[128,16]{0,1:T(8,128)}, u32[]{:S(2)}) copy-start(f32[128,16]{0,1:T(8,128)} %param.41) | copy-start | bytes 24580
  481.1 10.9 %copy-start.33 = (f32[128,16]{0,1:T(8,128)S(1)}, f32[128,16]{0,1:T(8,128)}, u32[]{:S(2)}) copy-start(f32[128,16]{0,1:T(8,128)} %param.40) | copy-start | bytes 24580
  481.2 11.6 %copy-start.35 = (f32[128]{0:T(128)S(1)}, f32[128]{0:T(128)}, u32[]{:S(2)}) copy-start(f32[128]{0:T(128)} %param.45) | copy-start | bytes 1540
  481.2 11.5 %copy-start.39 = (f32[128]{0:T(128)S(1)}, f32[128]{0:T(128)}, u32[]{:S(2)}) copy-start(f32[128]{0:T(128)} %param.47) | copy-start | bytes 1540
  481.2 11.5 %copy-start.40 = (f32[128]{0:T(128)S(1)}, f32[128]{0:T(128)}, u32[]{:S(2)}) copy-start(f32[128]{0:T(128)} %param.46) | copy-start | bytes 1540
  482.9 10.5 %copy-start.6 = (f32[2,128,256]{2,1,0:T(8,128)S(1)}, f32[2,128,256]{2,1,0:T(8,128)}, u32[]{:S(2)}) copy-start(f32[2,128,256]{2,1,0:T(8,128)} %param.36) | copy-start | bytes 786436
  482.9 10.5 %copy-start.16 = (f32[2,128,256]{2,1,0:T(8,128)S(1)}, f32[2,128,256]{2,1,0:T(8,128)}, u32[]{:S(2)}) copy-start(f32[2,128,256]{2,1,0:T(8,128)} %param.38) | copy-start | bytes 786436
  482.9 10.5 %copy-start.17 = (f32[2,128,256]{2,1,0:T(8,128)S(1)}, f32[2,128,256]{2,1,0:T(8,128)}, u32[]{:S(2)}) copy-start(f32[2,128,256]{2,1,0:T(8,128)} %param.37) | copy-start | bytes 786436
  483.7 10.7 %copy-start.11 = (f32[2,128,128]{2,1,0:T(8,128)S(1)}, f32[2,128,128]{2,1,0:T(8,128)}, u32[]{:S(2)}) copy-start(f32[2,128,128]{2,1,0:T(8,128)} %param.33) | copy-start | bytes 393220
  483.7 10.7 %copy-start.20 = (f32[2,128,128]{2,1,0:T(8,128)S(1)}, f32[2,128,128]{2,1,0:T(8,128)}, u32[]{:S(2)}) copy-start(f32[2,128,128]{2,1,0:T(8,128)} %param.35) | copy-start | bytes 393220
  483.7 10.7 %copy-start.21 = (f32[2,128,128]{2,1,0:T(8,128)S(1)}, f32[2,128,128]{2,1,0:T(8,128)}, u32[]{:S(2)}) copy-start(f32[2,128,128]{2,1,0:T(8,128)} %param.34) | copy-start | bytes 393220
  485.2 5.5 %collective-permute-start.26 = (f32[20864]{0:T(1024)S(1)}, f32[20864]{0:T(1024)S(1)}, u32[]{:S(2)}, u32[]{:S(2)}) collective-permute-start(f32[20864]{0:T(1024)S(1)} %add.293), channel_id=1, source_target_pairs={{0,16},{8,24},{16,0},{24,8},{1,17},{9,25},{17,1},{25,9},{2,18},{10... | collective-permute-start | bytes 250376 | tf_op jit(solution)/shard_map/ppermute | solution.py:526
  486.0 7.3 %collective-permute-start.24 = (f32[64,768]{1,0:T(8,128)S(1)}, f32[64,768]{1,0:T(8,128)S(1)}, u32[]{:S(2)}, u32[]{:S(2)}) collective-permute-start(f32[64,768]{1,0:T(8,128)S(1)} %dynamic-slice_bitcast_fusion.7), channel_id=1, source_target_pairs={{0,16},{8,24},{16,0},{24,8},{1,17},{9,25},{17,1},{25,9},{2,18},{10... | collective-permute-start | bytes 589832 | tf_op jit(solution)/shard_map/ppermute | solution.py:526
  487.4 5.9 %collective-permute-start.25 = (f32[64,768]{1,0:T(8,128)S(1)}, f32[64,768]{1,0:T(8,128)S(1)}, u32[]{:S(2)}, u32[]{:S(2)}) collective-permute-start(f32[64,768]{1,0:T(8,128)S(1)} %dynamic-slice_bitcast_fusion.6), channel_id=1, source_target_pairs={{0,8},{8,0},{16,24},{24,16},{1,9},{9,1},{17,25},{25,17},{2,10},{10... | collective-permute-start | bytes 589832 | tf_op jit(solution)/shard_map/ppermute | solution.py:526
  (12 other events, 25.9 us)
Sparse Core Ops, SparseCore 0:
  11.5 137.0 all-gather.1
  278.9 82.2 reduce-scatter.1

commit v7 on v4

--- a/solution.py
+++ b/solution.py
@@ -30,7 +30,7 @@
 RATE_RANK = 0.1
 RATE_BIAS = 1.5
 RATE_GAIN = 0.3
-VMEM_LIMIT = 60 * 1024 * 1024
+VMEM_LIMIT = 62 * 1024 * 1024
 
 F32 = jnp.float32
 BF16 = jnp.bfloat16
@@ -55,12 +55,24 @@
     return both[:size] + both[size:] + dot(left[0], right[1], dims)
 
 
-def dot_exact(matrix, values):
-    high = values.astype(BF16)
-    rest = values - high.astype(F32)
-    middle = rest.astype(BF16)
-    low = (rest - middle.astype(F32)).astype(BF16)
-    return dot(matrix, high) + dot(matrix, middle) + dot(matrix, low)
+def dot_sum(matrix, values):
+    high, low = split_two(values)
+    both = dot(matrix, jnp.concatenate([high, low], axis=1))
+    return both[:, : values.shape[1]] + both[:, values.shape[1] :]
+
+
+def dot_two(left, right, dims=NN):
+    axis = 1 - dims[0][0][0]
+    size = left[0].shape[axis]
+    both = dot(jnp.concatenate(left, axis=axis), right, dims)
+    return both[:size] + both[size:]
+
+
+def heads_side_by_side(info, decay_out, start, stop):
+    heads = decay_out.shape[0]
+    return jnp.concatenate(
+        [decay_out[info[2 * GROUPS + head], start:stop] for head in range(heads)], axis=1
+    )
 
 
 def lower_mask():
@@ -131,16 +143,11 @@
     every = range(heads)
     keys = [made[:, head * size : head * size + HK] for head in every]
     values = [made[:, head * size + HK : (head + 1) * size] for head in every]
-    logits = []
-    for head in every:
-        slot = info[2 * GROUPS + head]
-        logits.append(
-            lax.dot_general(
-                rank, decay_out[slot, :ranks], NN, precision=lax.Precision.HIGHEST,
-                preferred_element_type=F32,
-            )
-            + decay_out[slot, ranks : ranks + 1]
-        )
+    all_logits = lax.dot_general(
+        rank, heads_side_by_side(info, decay_out, 0, ranks), NN,
+        precision=lax.Precision.HIGHEST, preferred_element_type=F32,
+    ) + heads_side_by_side(info, decay_out, ranks, ranks + 1)
+    logits = [all_logits[:, head * HK : (head + 1) * HK] for head in every]
     for head in every:
         kv_out[head, :, :HK] = keys[head]
         kv_out[head, :, HK:] = values[head]
@@ -151,7 +158,7 @@
     ]
     for part in range(ROWS // BLOCK):
         span = slice(part * BLOCK, (part + 1) * BLOCK)
-        cum = [dot_exact(lower, log_decay[head][span]) for head in every]
+        cum = [dot_sum(lower, log_decay[head][span]) for head in every]
         total = [item[BLOCK - 1 :] for item in cum]
         carried = [
             split_two(keys[head][span] * jnp.exp(total[head] - cum[head])) for head in every
@@ -389,7 +396,7 @@
         key_mid = [split_two(keys[head] * shrink[head]) for head in every]
         values = [split_two(kv[head, span, HK:]) for head in every]
         back = [split_two(back_mixed[head, span]) for head in every]
-        scores = [dot_split(query_mid[head], key_mid[head], NT) for head in every]
+        scores = [dot_two(query_mid[head], key_mid[head][0], NT) for head in every]
         back_scores = [dot_split(back[head], values[head], NT) for head in every]
         since = [jnp.exp(cum[head]) for head in every]
         until = [jnp.exp(total[head] - cum[head]) for head in every]
@@ -402,7 +409,7 @@
             dot_split(back[head], split_two(query[head] * since[head]), TN) for head in every
         ]
         outer = [
-            dot_split(split_two(carried[head]), back_state_parts[head], NT) for head in every
+            dot_two(split_two(carried[head]), back_state_parts[head][0], NT) for head in every
         ]
         scores = [split_two(jnp.where(causal, item, 0.0)) for item in scores]
         back_scores = [split_two(jnp.where(causal, item, 0.0)) for item in back_scores]
@@ -416,7 +423,7 @@
             + back_carried[head] * until[head]
             for head in every
         ]
-        back_values = [dot_split(scores[head], back[head], TN) + outer[head] for head in every]
+        back_values = [dot_two(scores[head], back[head][0], TN) + outer[head] for head in every]
         back_total = []
         for head in every:
             decayed = back_state[head] * jnp.exp(total[head])
@@ -427,23 +434,21 @@
             state_ref[head] = decayed + added[head]
         back_logits = [
             (
-                dot_exact(upper, query[head] * back_query[head] - keys[head] * back_keys[head])
+                dot_sum(upper, query[head] * back_query[head] - keys[head] * back_keys[head])
                 + back_total[head]
             )
             * sigmoid(-logits_in[head, span])
             / GATE_SCALE
             for head in every
         ]
-        rank_parts = split_two(rank[span])
-        rank_back = jnp.zeros((BLOCK, ranks), F32)
+        together = jnp.concatenate(back_logits, axis=1)
+        rank_back = lax.dot_general(
+            together, heads_side_by_side(info, decay_out, 0, ranks), NT,
+            precision=lax.Precision.HIGHEST, preferred_element_type=F32,
+        )
+        decay_grad_out[...] += dot_split(split_two(rank[span]), split_two(together), TN)
+        bias_out[...] += jnp.sum(together, axis=0, keepdims=True)
         for head in every:
-            slot = info[2 * GROUPS + head]
-            rank_back += lax.dot_general(
-                back_logits[head], decay_out[slot, :ranks], NT, precision=lax.Precision.HIGHEST,
-                preferred_element_type=F32,
-            )
-            bias_out[head] += jnp.sum(back_logits[head], axis=0, keepdims=True)
-            decay_grad_out[head] += dot_split(rank_parts, split_two(back_logits[head]), TN)
             at = head * size
             query_ref[span, at : at + HK] = (back_query[head] * HK ** (-0.5)).astype(BF16)
             query_ref[span, at + HK : at + size] = back_gate[head, span]
@@ -595,11 +600,12 @@
     return gather_plain(pack)
 
 
-def scatter_rows(kept, sent, early):
+def finish_sums(kept, sent, sums, early):
     columns = kept.shape[-1]
     if not staged():
         whole = jnp.concatenate([kept, sent]).reshape(-1, columns)
-        return lax.psum_scatter(whole, ("dp", "ctx"), scatter_dimension=0, tiled=True), early
+        share = lax.psum_scatter(whole, ("dp", "ctx"), scatter_dimension=0, tiled=True)
+        return share, lax.psum(sums, ("dp", "ctx")), early
     device = lax.axis_index("dp")
     row, column = device // 2, device % 2
 
@@ -607,23 +613,19 @@
         return lax.dynamic_index_in_dim(array, index, axis, keepdims=False)
 
     value = kept + swap(sent, "ctx", 1)
-    value, early = lax.optimization_barrier((value, early))
+    sums = sums + swap(sums, "ctx", 1)
+    value, sums, early = lax.optimization_barrier((value, sums, early))
     value = value.reshape(2, 2, LANES, columns)
     half = LANES // 2
     upper, lower = value[:, :, :half], value[:, :, half:]
     upper = pick(upper, 1, column) + swap(pick(upper, 1, 1 - column), "dp", 1)
     lower = pick(lower, 0, row) + swap(pick(lower, 0, 1 - row), "dp", 2)
+    sums = sums + swap(sums, "dp", 1)
+    upper, lower, sums = lax.optimization_barrier((upper, lower, sums))
     upper = pick(upper, 0, row) + swap(pick(upper, 0, 1 - row), "dp", 2)
     lower = pick(lower, 0, column) + swap(pick(lower, 0, 1 - column), "dp", 1)
-    return jnp.concatenate([upper, lower]), early
-
-
-def total_over(value):
-    if not staged():
-        return lax.psum(value, ("dp", "ctx"))
-    for axis, distance in (("ctx", 1), ("dp", 1), ("dp", 2)):
-        value = value + swap(value, axis, distance)
-    return value
+    sums = sums + swap(sums, "dp", 2)
+    return jnp.concatenate([upper, lower]), sums, early
 
 
 def adamw(weight_now, grad_now, mean_now, square_now, rate_value, decay_value):
@@ -928,8 +930,8 @@
             fixed(grad_shape),
             fixed(rank_grad_shape),
             back_row_spec,
-            pl.BlockSpec((heads, ranks, HK), lambda i, *_: (0, 0, 0)),
-            bias_spec,
+            pl.BlockSpec((ranks, heads * HK), lambda i, *_: (0, 0)),
+            pl.BlockSpec((1, heads * HK), lambda i, *_: (0, 0)),
             gain_spec,
         ],
         [
@@ -937,8 +939,8 @@
             grad_shape,
             rank_grad_shape,
             shaped((rows, width)),
-            shaped((heads, ranks, HK)),
-            shaped((heads, 1, HK)),
+            shaped((ranks, heads * HK)),
+            shaped((1, heads * HK)),
             shaped((1, width)),
         ],
         [
@@ -957,22 +959,20 @@
         2 * rows * width * columns * heads * 2,
         rows * heads * 4 * 2048,
     )
-    mixer_share, early_share = scatter_rows(kept, sent_away, early_share)
     own = info[-1]
-    decay_out_own = lax.dynamic_index_in_dim(decay_out_grad, own, 0, keepdims=False)
-    bias_own = lax.dynamic_index_in_dim(bias_grad, own, 0, keepdims=False)
-    sums = total_over(
-        jnp.concatenate(
-            [
-                gain_one_part.reshape(-1),
-                gain_two_part.reshape(-1),
-                head_gain_part.reshape(-1),
-                bias_own.reshape(-1),
-                decay_out_own.reshape(-1),
-                rank_grad.reshape(-1),
-            ]
-        )
-    )
+    decay_out_own = lax.dynamic_slice_in_dim(decay_out_grad, own * HK, HK, axis=1)
+    bias_own = lax.dynamic_slice_in_dim(bias_grad, own * HK, HK, axis=1)
+    sums = jnp.concatenate(
+        [
+            gain_one_part.reshape(-1),
+            gain_two_part.reshape(-1),
+            head_gain_part.reshape(-1),
+            bias_own.reshape(-1),
+            decay_out_own.reshape(-1),
+            rank_grad.reshape(-1),
+        ]
+    )
+    mixer_share, sums, early_share = finish_sums(kept, sent_away, sums, early_share)
     gain_count = gains.shape[0]
     decay_start = gain_count + HK
     rank_start = decay_start + ranks * HK

time: 421 us -> 408 us (0.969)
  waiting for transfers between devices: 52.5 us -> 43.2 us
    ppermute x16, waiting for transfers between devices: 29.3 us -> 20.7 us  [swap(): lax.ppermute(value, axis, [(source, source ^ distance) for source in rang...]
  transfers between devices with their start and end apart: 26 -> 26, of which waited for: 16 -> 13; matrix products, arithmetic and copies ran while one was open for 6% -> 6% of each run, Pallas kernels for 39% -> 39%
where the time goes in v7:
time: 408 us; the launch traced here: 401 us
  Pallas kernels  257 us (63%)
  waiting for transfers between devices  43.2 us (11%)
  starting transfers between devices  34.9 us (9%)
  other arithmetic  28.5 us (7%)
  between operations  15.9 us (4%)
  matrix products  14 us (3%)
  local copies, waits for them, and re-layouts  7.46 us (2%)
    pallas_call x5, Pallas kernels, call(): pl.pallas_call(kernel, grid_spec=pltpu.PrefetchScalarGridSpec(num_scalar_...  257 us
    ppermute x16, waiting for transfers between devices, swap(): lax.ppermute(value, axis, [(source, source ^ distance) for source in rang...  20.7 us
    ppermute x6, waiting for transfers between devices, shift(): lax.ppermute(value, axis, [(source, (source + distance) % count) for sour...  19.4 us
    ppermute x6, starting transfers between devices, shift(): lax.ppermute(value, axis, [(source, (source + distance) % count) for sour...  17.5 us
    dot_general x4, matrix products, dot(): return lax.dot_general(left, right, dims, preferred_element_type=F32)  14 us
    ppermute x16, starting transfers between devices, swap(): lax.ppermute(value, axis, [(source, source ^ distance) for source in rang...  13.1 us
  transfers between devices with their start and end apart: 26, of which 13 were waited for; matrix products, arithmetic and copies ran while one was open for 6% of the time, Pallas kernels for 39%

profile of v7, /device:TPU:0, one launch (start us, length us, event | category | flops | bytes accessed | tf_op | source)
XLA Modules:
  0.0 401.1 jit_solution(10824343391736414117)
XLA Ops:
  7.3 1.3 convert.37
  8.7 1.0 convert_bitcast_fusion
  9.7 0.8 pad_maximum_fusion.5
  11.2 3.0 collective-permute-start
  14.3 2.6 collective-permute-start.1
  16.9 1.3 collective-permute-start.2
  18.3 2.4 collective-permute-done
  20.6 4.6 %collective-permute-done.1 = bf16[496,128]{1,0:T(8,128)(2,1)S(1)} collective-permute-done((bf16[496,128]{1,0:T(8,128)(2,1)S(1)}, bf16[496,128]{1,0:T(8,128)(2,1)S(1)}, u32[]{:S(2)}, u32[]{:S(2)}) %collective-permute-start.1) | collective-permute-done | bytes 127008 | tf_op jit(solution)/shard_map/ppermute | solution.py:540
  25.3 1.6 collective-permute-start.6
  26.9 1.5 collective-permute-start.7
  28.9 6.1 %collective-permute-start.3 = (bf16[640,128]{1,0:T(8,128)(2,1)S(1)}, bf16[640,128]{1,0:T(8,128)(2,1)S(1)}, u32[]{:S(2)}, u32[]{:S(2)}) collective-permute-start(bf16[640,128]{1,0:T(8,128)(2,1)S(1)} %pad_maximum_fusion.8), channel_id=1, source_target_pairs={{0,1},{1,2},{2,3},{3,0},{4,5},{5,6},{6,7},{7,4},{8,9},{9,10},{10,1... | collective-permute-start | bytes 491528 | tf_op jit(solution)/shard_map/ppermute | solution.py:540
  34.9 4.1 %collective-permute-start.4 = (bf16[640,128]{1,0:T(8,128)(2,1)S(1)}, bf16[640,128]{1,0:T(8,128)(2,1)S(1)}, u32[]{:S(2)}, u32[]{:S(2)}) collective-permute-start(bf16[640,128]{1,0:T(8,128)(2,1)S(1)} %pad_maximum_fusion.8), channel_id=1, source_target_pairs={{0,2},{1,3},{2,0},{3,1},{4,6},{5,7},{6,4},{7,5},{8,10},{9,11},{10,... | collective-permute-start | bytes 491528 | tf_op jit(solution)/shard_map/ppermute | solution.py:540
  39.0 5.7 %collective-permute-done.3 = bf16[640,128]{1,0:T(8,128)(2,1)S(1)} collective-permute-done((bf16[640,128]{1,0:T(8,128)(2,1)S(1)}, bf16[640,128]{1,0:T(8,128)(2,1)S(1)}, u32[]{:S(2)}, u32[]{:S(2)}) %collective-permute-start.3) | collective-permute-done | bytes 163872 | tf_op jit(solution)/shard_map/ppermute | solution.py:540
  45.0 5.4 %collective-permute-done.4 = bf16[640,128]{1,0:T(8,128)(2,1)S(1)} collective-permute-done((bf16[640,128]{1,0:T(8,128)(2,1)S(1)}, bf16[640,128]{1,0:T(8,128)(2,1)S(1)}, u32[]{:S(2)}, u32[]{:S(2)}) %collective-permute-start.4) | collective-permute-done | bytes 163872 | tf_op jit(solution)/shard_map/ppermute | solution.py:540
  50.4 1.3 collective-permute-done.5
  52.1 1.5 pad_maximum_fusion.2.first
  53.6 0.6 pad_add_fusion.info
  54.2 0.6 fusion.33
  54.8 0.9 slice.102
  55.7 1.3 collective-permute-start.10
  57.0 1.5 collective-permute-start.11
  58.5 0.7 collective-permute-start.12
  59.2 0.6 fusion.7.decay_out
  59.9 29.0 %shard_map.509 = (bf16[2048,1024]{1,0:T(8,128)(2,1)}, f32[4,2048,384]{2,1,0:T(8,128)}, f32[2048,16]{1,0:T(8,128)}, f32[4,2048,128]{2,1,0:T(8,128)}, f32[4,2048,1...) custom-call(s32[21]{0:T(128)} %pad_add_fusion.info, ...), custom_call_target="tpu_custom_call" | custom-call | flops 6442450944 | bytes 33554432 | tf_op jit(solution)/shard_map/pallas_call | solution.py:499
  88.9 10.4 %collective-permute-done.12 = bf16[4,640,128]{2,1,0:T(8,128)(2,1)} collective-permute-done((bf16[4,640,128]{2,1,0:T(8,128)(2,1)S(1)}, bf16[4,640,128]{2,1,0:T(8,128)(2,1)}, u32[]{:S(2)}, u32[]{:S(2)}) %collective-permute-start.12) | collective-permute-done | bytes 655392 | tf_op jit(solution)/shard_map/ppermute | solution.py:535
  99.4 2.9 pad_maximum_fusion.1.first
  103.6 3.0 collective-permute-start.13
  106.6 3.9 broadcast_select_fusion.back
  110.5 0.8 copy-done.42
  111.3 40.3 %shard_map.510 = (f32[4,2048,128]{2,1,0:T(8,128)}, f32[4,2048,256]{2,1,0:T(8,128)}, f32[4,2048,256]{2,1,0:T(8,128)}, f32[16,4,256,128]{3,2,1,0:T(8,128)}, bf16[2...) custom-call(s32[21]{0:T(128)} %pad_add_fusion.info, ...), custom_call_target="tpu_custom_call" | custom-call | flops 15032385536 | bytes 33554432 | tf_op jit(solution)/shard_map/pallas_call | solution.py:499
  151.6 0.6 all-gather.2.cloned.1.call-done
  152.2 99.6 %shard_map.511 = (bf16[2048,704]{1,0:T(8,128)(2,1)}, bf16[2048,704]{1,0:T(8,128)(2,1)}, bf16[2048,704]{1,0:T(8,128)(2,1)}, bf16[2048,1024]{1,0:T(8,128)(2,1)}, f...) custom-call(s32[21]{0:T(128)} %pad_add_fusion.info, ...), custom_call_target="tpu_custom_call" | custom-call | flops 70866960384 | bytes 50331648 | tf_op jit(solution)/shard_map/pallas_call | solution.py:499
  251.8 6.3 %fusion.34 = f32[704,1024]{1,0:T(8,128)S(1)} fusion(bf16[2048,704]{1,0:T(8,128)(2,1)} %get-tuple-element.103, bf16[2048,1024]{1,0:T(8,128)(2,1)} %get-tuple-element.96.normed), kind=kOutput, calls=%fused_computation.115 | convolution fusion | flops 2952790016 | bytes 9961472 | tf_op jit(solution)/shard_map/dot_general | solution.py:43
  258.1 3.2 fusion.35
  261.4 3.2 fusion.36
  264.6 1.3 fusion.37
  265.9 4.3 %pad_maximum_fusion = f32[2368,1024]{1,0:T(8,128)} fusion(f32[256,1024]{1,0:T(8,128)S(1)} %fusion.37, f32[704,1024]{1,0:T(8,128)S(1)} %fusion.36, f32[704,1024]{1,0:T(8,128)S(1)} %fusion.35, f32[704,1024]{1,0:T(8,128)S(1)} %fusion.34), kind=kLoop, calls=%fused_computation | loop fusion | flops 7274496 | bytes 19398656 | tf_op jit(solution)/shard_map/concatenate | solution.py:866
  270.2 23.8 %shard_map.512 = (f32[4,2048,256]{2,1,0:T(8,128)}, bf16[4,2048,256]{2,1,0:T(8,128)(2,1)}, f32[1,256]{1,0:T(1,128)}, f32[4,256,128]{2,1,0:T(8,128)}) custom-call(bf16[2048,1024]{1,0:T(8,128)(2,1)} %get-tuple-element.108.back_attn, bf16[1024,1024]{1,0:T(8,128)(2,1)} %get-tuple-element.109.out_weight, f32[4,2048,256]{2,1,0:T(8,128)} %get-tuple-element.110.mixed_in, ...), custom_call_target="tpu_custom_call" | custom-call | flops 4294967296 | bytes 33554432 | tf_op jit(solution)/shard_map/pallas_call | solution.py:499
  294.0 1.1 broadcast_add_fusion
  295.2 1.3 collective-permute-start.15
  296.5 2.5 collective-permute-done.15.back_end
  299.0 0.8 copy-done.41
  299.8 64.5 %shard_map.513 = (f32[4,128,768]{2,1,0:T(8,128)}, f32[4,128,768]{2,1,0:T(8,128)}, f32[16,1024]{1,0:T(8,128)}, f32[2048,1024]{1,0:T(8,128)}, f32[16,512]{1,0:T(8,...) custom-call(s32[21]{0:T(128)} %pad_add_fusion.info, bf16[2048,1024]{1,0:T(8,128)(2,1)} %tokens.5, ...), custom_call_target="tpu_custom_call" | custom-call | flops 25769803776 | bytes 67108864 | tf_op jit(solution)/shard_map/pallas_call | solution.py:499
  364.5 0.9 copy.74
  365.3 0.7 constant_dynamic-update-slice_fusion.4
  366.0 0.7 constant_dynamic-update-slice_fusion.6
  366.7 0.7 bitcast_dynamic-update-slice_fusion
  367.9 0.9 collective-permute-done.17
  368.9 1.6 add.241
  370.6 0.6 collective-permute-start.20
  371.4 1.4 collective-permute-start.19
  372.8 0.9 collective-permute-start.18
  373.6 1.2 multiply_subtract_fusion.1
  374.8 1.7 multiply_subtract_fusion
  376.7 0.8 multiply_subtract_fusion.3
  377.5 4.8 %collective-permute-done.19 = f32[2,64,768]{2,1,0:T(8,128)S(1)} collective-permute-done((f32[2,64,768]{2,1,0:T(8,128)S(1)}, f32[2,64,768]{2,1,0:T(8,128)S(1)}, u32[]{:S(2)}, u32[]{:S(2)}) %collective-permute-start.19) | collective-permute-done | bytes 393248 | tf_op jit(solution)/shard_map/ppermute | solution.py:535
  382.4 1.4 collective-permute-done.18
  384.4 1.7 collective-permute-start.21
  386.6 2.9 collective-permute-done.23
  389.6 0.6 multiply_subtract_fusion.5
  390.2 0.6 multiply_subtract_fusion.6
  390.8 0.6 multiply_subtract_fusion.7
  392.2 1.0 multiply_subtract_fusion.2
  393.2 0.8 multiply_subtract_fusion.4
  (162 shorter events, 5.5 us)
Async XLA Ops:
  7.2 3.4 copy-start.11
  7.2 3.5 copy-start.5
  7.2 3.7 copy-start.26
  7.2 3.7 copy-start.34
  7.3 3.7 copy-start.22
  7.3 11.0 %copy-start.9 = (f32[256,128]{1,0:T(8,128)S(1)}, f32[256,128]{1,0:T(8,128)}, u32[]{:S(2)}) copy-start(f32[256,128]{1,0:T(8,128)} %param.48) | copy-start | bytes 393220
  7.3 144.9 %all-gather.2.cloned.1.call-start = ((), (), s32[]{:S(2)}) async-start(), calls=%async_computation.1 | async-start | bytes 17842176 | tf_op jit(solution)/shard_map/all_gather | solution.py:598
  10.5 360.0 %reduce-scatter.2.cloned.1.call-start = ((), (), s32[]{:S(2)}) async-start(), calls=%async_computation.2 | async-start | bytes 10911744 | tf_op jit(solution)/shard_map/reduce_scatter | solution.py:875
  11.2 9.4 %collective-permute-start = (bf16[496,128]{1,0:T(8,128)(2,1)S(1)}, bf16[496,128]{1,0:T(8,128)(2,1)S(1)}, u32[]{:S(2)}, u32[]{:S(2)}) collective-permute-start(bf16[496,128]{1,0:T(8,128)(2,1)S(1)} %constant_dynamic-update-slice_fusion), channel_id=1, source_target_pairs={{0,1},{1,2},{2,3},{3,0},{4,5},{5,6},{6,7},{7,4},{8,9},{9,10},{10,1... | collective-permute-start | bytes 380936 | tf_op jit(solution)/shard_map/ppermute | solution.py:540
  14.3 11.0 %collective-permute-start.1 = (bf16[496,128]{1,0:T(8,128)(2,1)S(1)}, bf16[496,128]{1,0:T(8,128)(2,1)S(1)}, u32[]{:S(2)}, u32[]{:S(2)}) collective-permute-start(bf16[496,128]{1,0:T(8,128)(2,1)S(1)} %constant_dynamic-update-slice_fusion), channel_id=1, source_target_pairs={{0,2},{1,3},{2,0},{3,1},{4,6},{5,7},{6,4},{7,5},{8,10},{9,11},{10,... | collective-permute-start | bytes 380936 | tf_op jit(solution)/shard_map/ppermute | solution.py:540
  16.9 8.4 %collective-permute-start.2 = (bf16[496,128]{1,0:T(8,128)(2,1)S(1)}, bf16[496,128]{1,0:T(8,128)(2,1)S(1)}, u32[]{:S(2)}, u32[]{:S(2)}) collective-permute-start(bf16[496,128]{1,0:T(8,128)(2,1)S(1)} %constant_dynamic-update-slice_fusion), channel_id=1, source_target_pairs={{0,3},{1,0},{2,1},{3,2},{4,7},{5,4},{6,5},{7,6},{8,11},{9,8},{10,9... | collective-permute-start | bytes 380936 | tf_op jit(solution)/shard_map/ppermute | solution.py:540
  25.2 29.0 %copy-start.24 = (f32[2304]{0:T(1024)S(1)}, f32[2304]{0:T(1024)}, u32[]{:S(2)}) copy-start(f32[2304]{0:T(1024)} %param.57) | copy-start | bytes 27652
  25.3 26.5 %collective-permute-start.6 = (bf16[4,496,128]{2,1,0:T(8,128)(2,1)S(1)}, bf16[4,496,128]{2,1,0:T(8,128)(2,1)S(1)}, u32[]{:S(2)}, u32[]{:S(2)}) collective-permute-start(bf16[4,496,128]{2,1,0:T(8,128)(2,1)S(1)} %pad_maximum_fusion.6), channel_id=1, source_target_pairs={{0,8},{8,0},{16,24},{24,16},{1,9},{9,1},{17,25},{25,17},{2,10},{10... | collective-permute-start | bytes 1523720 | tf_op jit(solution)/shard_map/ppermute | solution.py:535
  26.9 25.0 %collective-permute-start.7 = (bf16[4,496,128]{2,1,0:T(8,128)(2,1)S(1)}, bf16[4,496,128]{2,1,0:T(8,128)(2,1)S(1)}, u32[]{:S(2)}, u32[]{:S(2)}) collective-permute-start(bf16[4,496,128]{2,1,0:T(8,128)(2,1)S(1)} %pad_maximum_fusion.6), channel_id=1, source_target_pairs={{0,16},{8,24},{16,0},{24,8},{1,17},{9,25},{17,1},{25,9},{2,18},{10... | collective-permute-start | bytes 1523720 | tf_op jit(solution)/shard_map/ppermute | solution.py:535
  28.4 23.7 %collective-permute-start.8 = (bf16[4,496,128]{2,1,0:T(8,128)(2,1)S(1)}, bf16[4,496,128]{2,1,0:T(8,128)(2,1)S(1)}, u32[]{:S(2)}, u32[]{:S(2)}) collective-permute-start(bf16[4,496,128]{2,1,0:T(8,128)(2,1)S(1)} %pad_maximum_fusion.6), channel_id=1, source_target_pairs={{0,24},{8,16},{16,8},{24,0},{1,25},{9,17},{17,9},{25,1},{2,26},{10... | collective-permute-start | bytes 1523720 | tf_op jit(solution)/shard_map/ppermute | solution.py:535
  28.9 15.8 %collective-permute-start.3 = (bf16[640,128]{1,0:T(8,128)(2,1)S(1)}, bf16[640,128]{1,0:T(8,128)(2,1)S(1)}, u32[]{:S(2)}, u32[]{:S(2)}) collective-permute-start(bf16[640,128]{1,0:T(8,128)(2,1)S(1)} %pad_maximum_fusion.8), channel_id=1, source_target_pairs={{0,1},{1,2},{2,3},{3,0},{4,5},{5,6},{6,7},{7,4},{8,9},{9,10},{10,1... | collective-permute-start | bytes 491528 | tf_op jit(solution)/shard_map/ppermute | solution.py:540
  34.9 15.5 %collective-permute-start.4 = (bf16[640,128]{1,0:T(8,128)(2,1)S(1)}, bf16[640,128]{1,0:T(8,128)(2,1)S(1)}, u32[]{:S(2)}, u32[]{:S(2)}) collective-permute-start(bf16[640,128]{1,0:T(8,128)(2,1)S(1)} %pad_maximum_fusion.8), channel_id=1, source_target_pairs={{0,2},{1,3},{2,0},{3,1},{4,6},{5,7},{6,4},{7,5},{8,10},{9,11},{10,... | collective-permute-start | bytes 491528 | tf_op jit(solution)/shard_map/ppermute | solution.py:540
  44.7 7.1 %collective-permute-start.5 = (bf16[640,128]{1,0:T(8,128)(2,1)S(1)}, bf16[640,128]{1,0:T(8,128)(2,1)S(1)}, u32[]{:S(2)}, u32[]{:S(2)}) collective-permute-start(bf16[640,128]{1,0:T(8,128)(2,1)S(1)} %pad_maximum_fusion.8), channel_id=1, source_target_pairs={{0,3},{1,0},{2,1},{3,2},{4,7},{5,4},{6,5},{7,6},{8,11},{9,8},{10,9... | collective-permute-start | bytes 491528 | tf_op jit(solution)/shard_map/ppermute | solution.py:540
  53.6 6.3 %collective-permute-start.9 = (bf16[4,4,496,128]{3,2,1,0:T(8,128)(2,1)}, bf16[4,4,496,128]{3,2,1,0:T(8,128)(2,1)}, u32[]{:S(2)}, u32[]{:S(2)}) collective-permute-start(bf16[4,4,496,128]{3,2,1,0:T(8,128)(2,1)} %pad_maximum_fusion.2.first), channel_id=1, source_target_pairs={{0,4},{4,0},{1,5},{5,1},{2,6},{6,2},{3,7},{7,3},{8,12},{12,8},{9,1... | collective-permute-start | bytes 6094856 | tf_op jit(solution)/shard_map/ppermute | solution.py:535
  55.7 33.2 %collective-permute-start.10 = (bf16[4,640,128]{2,1,0:T(8,128)(2,1)S(1)}, bf16[4,640,128]{2,1,0:T(8,128)(2,1)S(1)}, u32[]{:S(2)}, u32[]{:S(2)}) collective-permute-start(bf16[4,640,128]{2,1,0:T(8,128)(2,1)S(1)} %pad_maximum_fusion.4), channel_id=1, source_target_pairs={{0,8},{8,0},{16,24},{24,16},{1,9},{9,1},{17,25},{25,17},{2,10},{10... | collective-permute-start | bytes 1966088 | tf_op jit(solution)/shard_map/ppermute | solution.py:535
  57.0 31.9 %collective-permute-start.11 = (bf16[4,640,128]{2,1,0:T(8,128)(2,1)S(1)}, bf16[4,640,128]{2,1,0:T(8,128)(2,1)S(1)}, u32[]{:S(2)}, u32[]{:S(2)}) collective-permute-start(bf16[4,640,128]{2,1,0:T(8,128)(2,1)S(1)} %pad_maximum_fusion.4), channel_id=1, source_target_pairs={{0,16},{8,24},{16,0},{24,8},{1,17},{9,25},{17,1},{25,9},{2,18},{10... | collective-permute-start | bytes 1966088 | tf_op jit(solution)/shard_map/ppermute | solution.py:535
  58.5 40.8 %collective-permute-start.12 = (bf16[4,640,128]{2,1,0:T(8,128)(2,1)S(1)}, bf16[4,640,128]{2,1,0:T(8,128)(2,1)}, u32[]{:S(2)}, u32[]{:S(2)}) collective-permute-start(bf16[4,640,128]{2,1,0:T(8,128)(2,1)S(1)} %pad_maximum_fusion.4), channel_id=1, source_target_pairs={{0,24},{8,16},{16,8},{24,0},{1,25},{9,17},{17,9},{25,1},{2,26},{10... | collective-permute-start | bytes 1966088 | tf_op jit(solution)/shard_map/ppermute | solution.py:535
  88.9 14.6 %copy-start.37 = (f32[4,1,128]{2,1,0:T(1,128)S(1)}, f32[4,1,128]{2,1,0:T(1,128)}, u32[]{:S(2)}) copy-start(f32[4,1,128]{2,1,0:T(1,128)} %get-tuple-element.88) | copy-start | bytes 6148
  88.9 14.7 %copy-start.13 = (f32[4,256,128]{2,1,0:T(8,128)S(1)}, f32[4,256,128]{2,1,0:T(8,128)}, u32[]{:S(2)}) copy-start(f32[4,256,128]{2,1,0:T(8,128)} %get-tuple-element.91) | copy-start | bytes 1572868
  102.3 8.2 %collective-permute-start.14 = (bf16[4,4,640,128]{3,2,1,0:T(8,128)(2,1)}, bf16[4,4,640,128]{3,2,1,0:T(8,128)(2,1)}, u32[]{:S(2)}, u32[]{:S(2)}) collective-permute-start(bf16[4,4,640,128]{3,2,1,0:T(8,128)(2,1)} %pad_maximum_fusion.1.first), channel_id=1, source_target_pairs={{0,4},{4,0},{1,5},{5,1},{2,6},{6,2},{3,7},{7,3},{8,12},{12,8},{9,1... | collective-permute-start | bytes 7864328 | tf_op jit(solution)/shard_map/ppermute | solution.py:535
  103.6 6.9 %collective-permute-start.13 = (f32[4,256,128]{2,1,0:T(8,128)S(1)}, f32[4,256,128]{2,1,0:T(8,128)S(1)}, u32[]{:S(2)}, u32[]{:S(2)}) collective-permute-start(f32[4,256,128]{2,1,0:T(8,128)S(1)} %broadcast_add_fusion.1), channel_id=1, source_target_pairs={{0,4},{1,5},{2,6},{3,7},{8,12},{9,13},{10,14},{11,15},{16,20},{17,... | collective-permute-start | bytes 1572872 | tf_op jit(solution)/shard_map/ppermute | solution.py:519
  251.8 6.3 %copy-start.44 = (bf16[2048,1024]{1,0:T(8,128)(2,1)S(1)}, bf16[2048,1024]{1,0:T(8,128)(2,1)}, u32[]{:S(2)}) copy-start(bf16[2048,1024]{1,0:T(8,128)(2,1)} %get-tuple-element.96.normed) | copy-start | bytes 12582916
  251.8 6.3 %copy-start.46 = (bf16[2048,704]{1,0:T(8,128)(2,1)S(1)}, bf16[2048,704]{1,0:T(8,128)(2,1)}, u32[]{:S(2)}) copy-start(bf16[2048,704]{1,0:T(8,128)(2,1)} %get-tuple-element.104) | copy-start | bytes 8650756
  258.1 3.3 copy-start.1
  258.1 3.3 copy-start.45
  261.4 3.3 copy-start
  261.4 3.3 copy-start.43
  295.2 3.8 collective-permute-start.15
  299.8 66.2 %copy-start.36 = (f32[1,1024]{1,0:T(1,128)S(1)}, f32[1,1024]{1,0:T(1,128)}, u32[]{:S(2)}) copy-start(f32[1,1024]{1,0:T(1,128)} %get-tuple-element.123) | copy-start | bytes 12292
  299.8 66.2 %copy-start.38 = (f32[1,256]{1,0:T(1,128)S(1)}, f32[1,256]{1,0:T(1,128)}, u32[]{:S(2)}) copy-start(f32[1,256]{1,0:T(1,128)} %get-tuple-element.124) | copy-start | bytes 3076
  364.3 4.5 %collective-permute-start.16 = (f32[4,128,768]{2,1,0:T(8,128)}, f32[4,128,768]{2,1,0:T(8,128)S(1)}, u32[]{:S(2)}, u32[]{:S(2)}) collective-permute-start(f32[4,128,768]{2,1,0:T(8,128)} %get-tuple-element.121), channel_id=1, source_target_pairs={{0,4},{4,0},{1,5},{5,1},{2,6},{6,2},{3,7},{7,3},{8,12},{12,8},{9,1... | collective-permute-start | bytes 4718600 | tf_op jit(solution)/shard_map/ppermute | solution.py:535
  367.4 1.4 collective-permute-start.17
  370.6 6.9 %collective-permute-start.20 = (f32[20864]{0:T(1024)S(1)}, f32[20864]{0:T(1024)S(1)}, u32[]{:S(2)}, u32[]{:S(2)}) collective-permute-start(f32[20864]{0:T(1024)S(1)} %add.243), channel_id=1, source_target_pairs={{0,8},{8,0},{16,24},{24,16},{1,9},{9,1},{17,25},{25,17},{2,10},{10... | collective-permute-start | bytes 250376 | tf_op jit(solution)/shard_map/ppermute | solution.py:535
  371.3 3.5 copy-start.2
  371.3 3.5 copy-start.7
  371.3 3.5 copy-start.8
  371.4 11.0 %collective-permute-start.19 = (f32[2,64,768]{2,1,0:T(8,128)S(1)}, f32[2,64,768]{2,1,0:T(8,128)S(1)}, u32[]{:S(2)}, u32[]{:S(2)}) collective-permute-start(f32[2,64,768]{2,1,0:T(8,128)S(1)} %dynamic-slice_bitcast_fusion), channel_id=1, source_target_pairs={{0,16},{8,24},{16,0},{24,8},{1,17},{9,25},{17,1},{25,9},{2,18},{10... | collective-permute-start | bytes 1179656 | tf_op jit(solution)/shard_map/ppermute | solution.py:535
  372.8 11.1 %collective-permute-start.18 = (f32[2,64,768]{2,1,0:T(8,128)S(1)}, f32[2,64,768]{2,1,0:T(8,128)S(1)}, u32[]{:S(2)}, u32[]{:S(2)}) collective-permute-start(f32[2,64,768]{2,1,0:T(8,128)S(1)} %dynamic-slice_bitcast_fusion.1), channel_id=1, source_target_pairs={{0,8},{8,0},{16,24},{24,16},{1,9},{9,1},{17,25},{25,17},{2,10},{10... | collective-permute-start | bytes 1179656 | tf_op jit(solution)/shard_map/ppermute | solution.py:535
  376.5 13.0 %copy-start.25 = (f32[2304]{0:T(1024)S(1)}, f32[2304]{0:T(1024)}, u32[]{:S(2)}) copy-start(f32[2304]{0:T(1024)} %param.57) | copy-start | bytes 27652
  376.5 13.0 %copy-start.28 = (f32[2304]{0:T(1024)S(1)}, f32[2304]{0:T(1024)}, u32[]{:S(2)}) copy-start(f32[2304]{0:T(1024)} %param.59) | copy-start | bytes 27652
  376.6 13.0 %copy-start.29 = (f32[2304]{0:T(1024)S(1)}, f32[2304]{0:T(1024)}, u32[]{:S(2)}) copy-start(f32[2304]{0:T(1024)} %param.58) | copy-start | bytes 27652
  376.6 13.6 %copy-start.23 = (f32[16,128]{1,0:T(8,128)S(1)}, f32[16,128]{1,0:T(8,128)}, u32[]{:S(2)}) copy-start(f32[16,128]{1,0:T(8,128)} %param.42) | copy-start | bytes 24580
  376.6 13.6 %copy-start.30 = (f32[16,128]{1,0:T(8,128)S(1)}, f32[16,128]{1,0:T(8,128)}, u32[]{:S(2)}) copy-start(f32[16,128]{1,0:T(8,128)} %param.44) | copy-start | bytes 24580
  376.6 13.6 %copy-start.31 = (f32[16,128]{1,0:T(8,128)S(1)}, f32[16,128]{1,0:T(8,128)}, u32[]{:S(2)}) copy-start(f32[16,128]{1,0:T(8,128)} %param.43) | copy-start | bytes 24580
  376.6 14.2 %copy-start.27 = (f32[128,16]{0,1:T(8,128)S(1)}, f32[128,16]{0,1:T(8,128)}, u32[]{:S(2)}) copy-start(f32[128,16]{0,1:T(8,128)} %param.39) | copy-start | bytes 24580
  376.6 14.2 %copy-start.32 = (f32[128,16]{0,1:T(8,128)S(1)}, f32[128,16]{0,1:T(8,128)}, u32[]{:S(2)}) copy-start(f32[128,16]{0,1:T(8,128)} %param.41) | copy-start | bytes 24580
  376.6 14.2 %copy-start.33 = (f32[128,16]{0,1:T(8,128)S(1)}, f32[128,16]{0,1:T(8,128)}, u32[]{:S(2)}) copy-start(f32[128,16]{0,1:T(8,128)} %param.40) | copy-start | bytes 24580
  376.6 14.8 %copy-start.35 = (f32[128]{0:T(128)S(1)}, f32[128]{0:T(128)}, u32[]{:S(2)}) copy-start(f32[128]{0:T(128)} %param.45) | copy-start | bytes 1540
  376.7 14.8 %copy-start.39 = (f32[128]{0:T(128)S(1)}, f32[128]{0:T(128)}, u32[]{:S(2)}) copy-start(f32[128]{0:T(128)} %param.47) | copy-start | bytes 1540
  376.7 14.8 %copy-start.40 = (f32[128]{0:T(128)S(1)}, f32[128]{0:T(128)}, u32[]{:S(2)}) copy-start(f32[128]{0:T(128)} %param.46) | copy-start | bytes 1540
  377.5 14.6 %copy-start.6 = (f32[2,128,256]{2,1,0:T(8,128)S(1)}, f32[2,128,256]{2,1,0:T(8,128)}, u32[]{:S(2)}) copy-start(f32[2,128,256]{2,1,0:T(8,128)} %param.36) | copy-start | bytes 786436
  377.5 14.6 %copy-start.16 = (f32[2,128,256]{2,1,0:T(8,128)S(1)}, f32[2,128,256]{2,1,0:T(8,128)}, u32[]{:S(2)}) copy-start(f32[2,128,256]{2,1,0:T(8,128)} %param.38) | copy-start | bytes 786436
  377.5 14.6 %copy-start.17 = (f32[2,128,256]{2,1,0:T(8,128)S(1)}, f32[2,128,256]{2,1,0:T(8,128)}, u32[]{:S(2)}) copy-start(f32[2,128,256]{2,1,0:T(8,128)} %param.37) | copy-start | bytes 786436
  383.9 9.3 %copy-start.12 = (f32[2,128,128]{2,1,0:T(8,128)S(1)}, f32[2,128,128]{2,1,0:T(8,128)}, u32[]{:S(2)}) copy-start(f32[2,128,128]{2,1,0:T(8,128)} %param.33) | copy-start | bytes 393220
  383.9 9.3 %copy-start.20 = (f32[2,128,128]{2,1,0:T(8,128)S(1)}, f32[2,128,128]{2,1,0:T(8,128)}, u32[]{:S(2)}) copy-start(f32[2,128,128]{2,1,0:T(8,128)} %param.35) | copy-start | bytes 393220
  383.9 9.2 %copy-start.21 = (f32[2,128,128]{2,1,0:T(8,128)S(1)}, f32[2,128,128]{2,1,0:T(8,128)}, u32[]{:S(2)}) copy-start(f32[2,128,128]{2,1,0:T(8,128)} %param.34) | copy-start | bytes 393220
  383.9 5.5 %collective-permute-start.23 = (f32[20864]{0:T(1024)S(1)}, f32[20864]{0:T(1024)S(1)}, u32[]{:S(2)}, u32[]{:S(2)}) collective-permute-start(f32[20864]{0:T(1024)S(1)} %add.251), channel_id=1, source_target_pairs={{0,16},{8,24},{16,0},{24,8},{1,17},{9,25},{17,1},{25,9},{2,18},{10... | collective-permute-start | bytes 250376 | tf_op jit(solution)/shard_map/ppermute | solution.py:535
  384.4 7.6 %collective-permute-start.21 = (f32[64,768]{1,0:T(8,128)S(1)}, f32[64,768]{1,0:T(8,128)S(1)}, u32[]{:S(2)}, u32[]{:S(2)}) collective-permute-start(f32[64,768]{1,0:T(8,128)S(1)} %dynamic-slice_bitcast_fusion.3), channel_id=1, source_target_pairs={{0,16},{8,24},{16,0},{24,8},{1,17},{9,25},{17,1},{25,9},{2,18},{10... | collective-permute-start | bytes 589832 | tf_op jit(solution)/shard_map/ppermute | solution.py:535
  386.1 5.9 %collective-permute-start.22 = (f32[64,768]{1,0:T(8,128)S(1)}, f32[64,768]{1,0:T(8,128)S(1)}, u32[]{:S(2)}, u32[]{:S(2)}) collective-permute-start(f32[64,768]{1,0:T(8,128)S(1)} %dynamic-slice_bitcast_fusion.2), channel_id=1, source_target_pairs={{0,8},{8,0},{16,24},{24,16},{1,9},{9,1},{17,25},{25,17},{2,10},{10... | collective-permute-start | bytes 589832 | tf_op jit(solution)/shard_map/ppermute | solution.py:535
  (9 other events, 19.2 us)
Sparse Core Ops, SparseCore 0:
  11.5 140.6 all-gather.1
  270.4 76.3 reduce-scatter.1
